TPU v7x, 32 devices: a whole 2x2x4 slice. The times are simulated.
32 devices in a mesh: blk: 32 (over z, y, x, core).
Axes of the slice: x: 2, y: 2, z: 4, core: 2. Of those that a mesh axis runs over, the one named last changes fastest.
Arguments:
- probe_vecs: bfloat16 [4096, 16, 128], P('blk'), may hold values from -6 to 6
- coeffs: bfloat16 [4096, 4, 128, 128], P('blk'), may hold values from -0.25 to 0.25
- cond_prec: bfloat16 [4096, 128, 128], P('blk'), may hold values from -1 to 5, as said below
- neighbours: int32 [4096, 4], P('blk'), may hold values from 0 to 4095, as said below
Outputs:
- qv: float32 [4096, 16, 128], P('blk')
Inputs may be any that keep to these rules, and one draw needn't show every extreme that they name: `neighbours`: columns 0 to 2 name three different blocks 1 to 16 places before the block, counting cyclically over all 4096 blocks. Column 3 names a block outside the block's own group of 128 consecutive blocks; it may coincide with a near neighbour. Of the blocks of one group, at most 5 name column-3 blocks in one same other group, and in every group some other group is named exactly 5 times. No two blocks of one group name the same column-3 block; blocks of different groups may name the same block, and all their far terms are added. `cond_prec`: each block is a diagonal matrix with entries between 0.25 and 4 plus off-diagonal noise (also on the diagonal) of magnitude at most 1.8 / sqrt(128).
All inputs are finite; a program needn't handle non-finite values.
Results may differ from a plain program's by a relative error of at most 0.0035.
Values may be sent and summed in bfloat16 or wider, within the bound.
No kernel may reach another device: no remote copies, remote signals or barrier semaphores. Data moves between devices by JAX's collectives and lax.ppermute only.
A program may use at most 128 MiB of HBM per device.

v0:
```python
import jax
import jax.numpy as jnp
from jax import lax
from jax.sharding import PartitionSpec as P


def passed_along(block, axis, distance):
    devices = range(lax.axis_size(axis))
    route = [((i - distance) % len(devices), i) for i in devices]
    return lax.ppermute(block, axis, route)


def per_device(probe_vecs, coeffs, cond_prec, neighbours):
    blocks, probes, points = probe_vecs.shape
    groups = lax.axis_size("blk")
    device_pos = lax.axis_index("blk")
    block_count = groups * blocks
    first_block = device_pos * blocks
    near_ids = neighbours[:, :3]
    near_rel = (near_ids - first_block + blocks) % block_count
    previous = passed_along(probe_vecs, "blk", 1)
    ext_pos = near_rel - (blocks - blocks)
    extended = jnp.concatenate([previous, probe_vecs], axis=0)
    near_tiles = extended[ext_pos]
    capacity = max(2, blocks // (groups - 1) + 1)
    far_block = neighbours[:, 3]
    owner_dev = far_block // blocks
    local_pos = far_block % blocks
    same_owner = owner_dev[:, None] == owner_dev[None, :]
    earlier = jnp.arange(blocks)[None, :] < jnp.arange(blocks)[:, None]
    slot_rank = jnp.sum(same_owner & earlier, axis=1)
    slot_pos = owner_dev * capacity + slot_rank
    wanted = (
        jnp.zeros((groups * capacity,), jnp.int32)
        .at[slot_pos]
        .set(local_pos + 1)
        .reshape(groups, capacity)
    )
    asked_for = lax.all_to_all(wanted, "blk", split_axis=0, concat_axis=0, tiled=True)
    picked = jnp.maximum(asked_for - 1, 0)
    outgoing = probe_vecs[picked]
    arrived = lax.all_to_all(outgoing, "blk", split_axis=0, concat_axis=0, tiled=True)
    far_tiles = arrived.reshape(groups * capacity, probes, points)[slot_pos]
    all_tiles = jnp.concatenate([near_tiles, far_tiles[:, None]], axis=1)
    mixed_sums = jnp.einsum("bkpn,bknm->bpm", all_tiles, coeffs, preferred_element_type=jnp.float32)
    whitened = (probe_vecs.astype(jnp.float32) - mixed_sums).astype(jnp.bfloat16)
    scaled = jnp.einsum(
        "bpm,bmn->bpn", whitened, cond_prec, preferred_element_type=jnp.float32
    ).astype(jnp.bfloat16)
    back_terms = jnp.einsum("bpn,bkmn->bkpm", scaled, coeffs, preferred_element_type=jnp.float32)
    near_sum = jax.ops.segment_sum(
        back_terms[:, :3].reshape(-1, probes, points),
        ext_pos.reshape(-1),
        num_segments=blocks + blocks,
    )
    returned_near = passed_along(near_sum[:blocks], "blk", -1)
    far_out = back_terms[:, 3].astype(jnp.bfloat16)
    parcel = jnp.zeros((groups * capacity, probes, points), jnp.bfloat16).at[slot_pos].set(far_out)
    parcel = parcel.reshape(groups, capacity, probes, points)
    returned = lax.all_to_all(parcel, "blk", split_axis=0, concat_axis=0, tiled=True)
    target = jnp.where(asked_for > 0, asked_for - 1, blocks).reshape(-1)
    far_sum = jax.ops.segment_sum(
        returned.reshape(-1, probes, points).astype(jnp.float32), target, num_segments=blocks + 1
    )[:blocks]
    result = scaled.astype(jnp.float32) - near_sum[blocks:] - returned_near - far_sum
    return result


def solution(mesh):
    in_specs = (
        P("blk", None, None),
        P("blk", None, None, None),
        P("blk", None, None),
        P("blk", None),
    )
    out_specs = P("blk", None, None)
    return jax.shard_map(
        per_device, mesh=mesh, in_specs=in_specs, out_specs=out_specs, check_vma=False
    )
```

profile of v0, /device:TPU:0, one launch (start us, length us, event | category | flops | bytes accessed | tf_op | source)
XLA Modules:
  0.0 150.1 jit_solution(15343199979386683668)
XLA Ops:
  0.0 0.8 fusion.21
  0.8 0.7 fusion.30
  1.5 0.7 and_select_fusion.1
  2.3 0.7 fusion.22
  3.0 1.0 scatter_custom_fusion
  4.1 14.3 %all_to_all.19 = s32[32,1,5]{2,1,0:T(1,128)S(1)} all-to-all(s32[32,1,5]{2,1,0:T(1,128)S(1)} %bitcast.54), channel_id=1, replica_groups=mesh['blk'=32] {'blk'}, dimensions={0} | all-to-all | bytes 1280 | tf_op jit(solution)/shard_map/all_to_all | solution.py:39
  18.6 2.6 %gather_fusion.1 = bf16[160,16,128]{2,1,0:T(8,128)(2,1)} fusion(bf16[128,16,128]{2,1,0:T(8,128)(2,1)} %param.4, s32[1024]{0:T(1024)S(1)} %pad_clamp_fusion.1), kind=kCustom, calls=%fused_computation.1 | custom fusion | bytes 1311360 | tf_op jit(solution)/shard_map/gather | solution.py:41
  21.2 3.3 %all-to-all-start.1 = ((bf16[32,5,16,128]{3,2,1,0:T(8,128)(2,1)}), bf16[32,5,16,128]{3,2,1,0:T(8,128)(2,1)}, u32[]{:S(2)}, u32[]{:S(2)}) async-start(bf16[32,5,16,128]{3,2,1,0:T(8,128)(2,1)} %bitcast.6), calls=%async_computation.1 | async-start | bytes 1310720 | tf_op jit(solution)/shard_map/all_to_all | solution.py:42
  25.0 22.3 %collective-permute-done = bf16[128,16,128]{2,1,0:T(8,128)(2,1)S(1)} collective-permute-done((bf16[128,16,128]{2,1,0:T(8,128)(2,1)S(1)}, bf16[128,16,128]{2,1,0:T(8,128)(2,1)S(1)}, u32[]{:S(2)}, u32[]{:S(2)}) %collective-permute-start) | collective-permute-done | bytes 524320 | tf_op jit(solution)/shard_map/ppermute | solution.py:10
  47.4 1.9 %gather_fusion = bf16[384,16,128]{2,1,0:T(8,128)(2,1)S(1)} fusion(bf16[256,16,128]{2,1,0:T(8,128)(2,1)S(1)} %pad_maximum_fusion, s32[1024]{0:T(1024)S(1)} %pad_clamp_fusion.2), kind=kCustom, calls=%fused_computation | custom fusion | bytes 3147264 | tf_op jit(solution)/shard_map/gather | solution.py:24
  49.3 1.8 %gather_fusion.2 = bf16[128,16,128]{2,1,0:T(8,128)(2,1)S(1)} fusion(bf16[160,16,128]{2,1,0:T(8,128)(2,1)} %bitcast.7, s32[1024]{0:T(1024)S(1)} %pad_clamp_fusion), kind=kCustom, calls=%fused_computation.2 | custom fusion | bytes 1049088 | tf_op jit(solution)/shard_map/gather | solution.py:43
  51.1 10.6 %convolution_convert_fusion = bf16[128,16,128]{2,1,0:T(8,128)(2,1)S(1)} fusion(bf16[128,128,128]{2,1,0:T(8,128)(2,1)} %param.6, bf16[128,4,128,128]{3,2,1,0:T(8,128)(2,1)} %param.5, bf16[128,1,16,128]{3,2,1,0:T(8,128)(2,1)S(1)} %bitcast.53, bf16[128,3,16,128]{3,2,1,0:T(8,128)(2,1)S(1)} %bitcast.52, bf16[128,16,128]{2,1,0:T(8,128)(2,1)S(1)} %copy-done), kind=kOutput, calls=%fused_computation.15 | convolution fusion | flops 337641472 | bytes 24117248 | tf_op jit(solution)/shard_map/bpm,bmn->bpn/dot_general | solution.py:47
  61.7 12.4 %convolution_bitcast_fusion = f32[128,4,16,128]{3,2,1,0:T(8,128)} fusion(bf16[128,4,128,128]{3,2,1,0:T(8,128)(2,1)} %param.5, bf16[128,16,128]{2,1,0:T(8,128)(2,1)S(1)} %convolution_convert_fusion), kind=kOutput, calls=%fused_computation.7 | convolution fusion | flops 268435456 | bytes 21495808 | tf_op jit(solution)/shard_map/bpn,bkmn->bkpm/dot_general | solution.py:50
  74.1 1.3 fusion.16
  75.4 0.9 broadcast_in_dim.33
  76.3 12.4 %scatter_fusion.1 = bf16[160,16,128]{2,1,0:T(8,128)(2,1)} fusion(bf16[160,16,128]{2,1,0:T(8,128)(2,1)} %broadcast_in_dim.33, s32[128]{0:T(128)S(1)} %fusion.22, bf16[128,16,128]{2,1,0:T(8,128)(2,1)S(1)} %fusion.16), kind=kCustom, calls=%fused_computation.5 | custom fusion | bytes 1573376 | tf_op jit(solution)/shard_map/scatter | solution.py:58
  88.7 3.2 %all-to-all-start.2 = ((bf16[32,5,16,128]{3,2,1,0:T(8,128)(2,1)}), bf16[32,5,16,128]{3,2,1,0:T(8,128)(2,1)S(1)}, u32[]{:S(2)}, u32[]{:S(2)}) async-start(bf16[32,5,16,128]{3,2,1,0:T(8,128)(2,1)} %bitcast.16), calls=%async_computation.2 | async-start | bytes 1310720 | tf_op jit(solution)/shard_map/all_to_all | solution.py:60
  92.2 3.8 %slice.35 = f32[128,3,16,128]{3,2,1,0:T(8,128)} slice(f32[128,4,16,128]{3,2,1,0:T(8,128)} %convolution_bitcast_fusion), slice={[0:128], [0:3], [0:16], [0:128]} | slice | bytes 6291456 | tf_op jit(solution)/shard_map/slice | solution.py:52
  96.1 30.7 %scatter_fusion = f32[256,16,128]{2,1,0:T(8,128)S(1)} fusion(f32[256,16,128]{2,1,0:T(8,128)S(1)} %broadcast_in_dim.31, s32[384]{0:T(512)S(1)} %reshape.129, f32[384,16,128]{2,1,0:T(8,128)} %bitcast.51), kind=kCustom, calls=%fused_computation.4 | custom fusion | flops 786432 | bytes 9438720 | tf_op jit(solution)/shard_map/scatter-add | solution.py:51
  126.9 1.0 slice.37
  127.9 5.2 %collective-permute-start.1 = (f32[128,16,128]{2,1,0:T(8,128)}, f32[128,16,128]{2,1,0:T(8,128)}, u32[]{:S(2)}, u32[]{:S(2)}) collective-permute-start(f32[128,16,128]{2,1,0:T(8,128)} %slice.37), channel_id=1, source_target_pairs={{1,0},{2,1},{3,2},{4,3},{5,4},{6,5},{7,6},{8,7},{9,8},{10,9},{11,1... | collective-permute-start | bytes 3145736 | tf_op jit(solution)/shard_map/ppermute | solution.py:10
  133.2 1.2 bitcast_convert_fusion
  134.5 13.0 %scatter_fusion.2 = f32[129,16,128]{2,1,0:T(8,128)S(1)} fusion(f32[129,16,128]{2,1,0:T(8,128)S(1)} %broadcast_in_dim.32, s32[160]{0:T(256)S(1)} %reshape.145, f32[160,16,128]{2,1,0:T(8,128)} %bitcast_convert_fusion), kind=kCustom, calls=%fused_computation.6 | custom fusion | flops 327680 | bytes 3932800 | tf_op jit(solution)/shard_map/scatter-add | solution.py:62
  147.6 2.6 %slice_subtract_fusion = f32[128,16,128]{2,1,0:T(8,128)} fusion(f32[129,16,128]{2,1,0:T(8,128)S(1)} %scatter_fusion.2, f32[128,16,128]{2,1,0:T(8,128)} %collective-permute-done.1, f32[256,16,128]{2,1,0:T(8,128)S(1)} %scatter_fusion, bf16[128,16,128]{2,1,0:T(8,128)(2,1)} %copy-done.1), kind=kLoop, calls=%fused_computation.16 | loop fusion | flops 1048576 | bytes 4718592 | tf_op jit(solution)/shard_map/sub | solution.py:65
  (26 shorter events, 1.7 us)
Async XLA Ops:
  0.0 24.6 %copy-start.2 = (s32[128,4]{0,1:T(4,128)S(1)}, s32[128,4]{0,1:T(4,128)}, u32[]{:S(2)}) copy-start(s32[128,4]{0,1:T(4,128)} %param.7) | copy-start | bytes 6148
  0.0 24.5 %copy-start = (bf16[128,16,128]{2,1,0:T(8,128)(2,1)S(1)}, bf16[128,16,128]{2,1,0:T(8,128)(2,1)}, u32[]{:S(2)}) copy-start(bf16[128,16,128]{2,1,0:T(8,128)(2,1)} %param.4) | copy-start | bytes 1572868
  21.2 28.1 %all-to-all-start.1 = ((bf16[32,5,16,128]{3,2,1,0:T(8,128)(2,1)}), bf16[32,5,16,128]{3,2,1,0:T(8,128)(2,1)}, u32[]{:S(2)}, u32[]{:S(2)}) async-start(bf16[32,5,16,128]{3,2,1,0:T(8,128)(2,1)} %bitcast.6), calls=%async_computation.1 | async-start | bytes 1310720 | tf_op jit(solution)/shard_map/all_to_all | solution.py:42
  24.5 22.7 %collective-permute-start = (bf16[128,16,128]{2,1,0:T(8,128)(2,1)S(1)}, bf16[128,16,128]{2,1,0:T(8,128)(2,1)S(1)}, u32[]{:S(2)}, u32[]{:S(2)}) collective-permute-start(bf16[128,16,128]{2,1,0:T(8,128)(2,1)S(1)} %copy-done), channel_id=1, source_target_pairs={{31,0},{0,1},{1,2},{2,3},{3,4},{4,5},{5,6},{6,7},{7,8},{8,9},{9,10... | collective-permute-start | bytes 1572872 | tf_op jit(solution)/shard_map/ppermute | solution.py:10
  61.7 12.4 %copy-start.1 = (bf16[128,16,128]{2,1,0:T(8,128)(2,1)}, bf16[128,16,128]{2,1,0:T(8,128)(2,1)S(1)}, u32[]{:S(2)}) copy-start(bf16[128,16,128]{2,1,0:T(8,128)(2,1)S(1)} %convolution_convert_fusion) | copy-start | bytes 1572868
  88.7 44.5 %all-to-all-start.2 = ((bf16[32,5,16,128]{3,2,1,0:T(8,128)(2,1)}), bf16[32,5,16,128]{3,2,1,0:T(8,128)(2,1)S(1)}, u32[]{:S(2)}, u32[]{:S(2)}) async-start(bf16[32,5,16,128]{3,2,1,0:T(8,128)(2,1)} %bitcast.16), calls=%async_computation.2 | async-start | bytes 1310720 | tf_op jit(solution)/shard_map/all_to_all | solution.py:60
  127.9 19.6 %collective-permute-start.1 = (f32[128,16,128]{2,1,0:T(8,128)}, f32[128,16,128]{2,1,0:T(8,128)}, u32[]{:S(2)}, u32[]{:S(2)}) collective-permute-start(f32[128,16,128]{2,1,0:T(8,128)} %slice.37), channel_id=1, source_target_pairs={{1,0},{2,1},{3,2},{4,3},{5,4},{6,5},{7,6},{8,7},{9,8},{10,9},{11,1... | collective-permute-start | bytes 3145736 | tf_op jit(solution)/shard_map/ppermute | solution.py:10
where the time goes:
time: 152 us; the launch traced here: 150 us
  other arithmetic  50.8 us (33%)
  local copies, waits for them, and re-layouts  27.9 us (18%)
  matrix products  23 us (15%)
  waiting for transfers between devices  22.3 us (15%)
  blocking collectives  14.3 us (9%)
  starting transfers between devices  11.8 us (8%)
    scatter-add x1, other arithmetic, per_device(): jax.ops.segment_sum(back_terms[:, :3].reshape(-1, probes, points), ext_po...  30.7 us
    ppermute x2, waiting for transfers between devices, passed_along(): return lax.ppermute(block, axis, route)  22.3 us
    all_to_all x1, blocking collectives, per_device(): lax.all_to_all(wanted, 'blk', split_axis=0, concat_axis=0, tiled=True)  14.3 us
    scatter-add x1, other arithmetic, per_device(): jax.ops.segment_sum(returned.reshape(-1, probes, points).astype(jnp.float...  13 us
    dot_general x1, matrix products, per_device(): jnp.einsum('bpn,bkmn->bkpm', scaled, coeffs, preferred_element_type=jnp.f...  12.4 us
    scatter x1, local copies, waits for them, and re-layouts, per_device(): jnp.zeros((groups * capacity, probes, points), jnp.bfloat16).at[slot_pos]  12.4 us
    dot_general x1, matrix products, per_device(): jnp.einsum('bpm,bmn->bpn', whitened, cond_prec, preferred_element_type=jn...  10.6 us
    ppermute x2, starting transfers between devices, passed_along(): return lax.ppermute(block, axis, route)  5.32 us
  transfers between devices with their start and end apart: 4, of which 1 were waited for; matrix products, arithmetic and copies ran while one was open for 35% of the time, Pallas kernels for 0%

commit v1 on v0

v1 whole, which is shorter than its diff:
```python
import functools

import jax
import jax.numpy as jnp
from jax import lax
from jax.experimental import pallas as pl
from jax.experimental.pallas import tpu as pltpu
from jax.sharding import PartitionSpec as P

REACH = 16
CHUNK = 16
VMEM = pl.BlockSpec(memory_space=pltpu.VMEM)
SMEM = pl.BlockSpec(memory_space=pltpu.SMEM)
HBM = pl.BlockSpec(memory_space=pl.ANY)
NT = (((1,), (1,)), ((), ()))


def params(mib):
    return pltpu.CompilerParams(vmem_limit_bytes=mib * 2**20)


def passed_along(block, axis, distance):
    size = lax.axis_size(axis)
    return lax.ppermute(block, axis, [((i - distance) % size, i) for i in range(size)])


def earlier_matrix(blocks):
    row = lax.broadcasted_iota(jnp.int32, (blocks, blocks), 0)
    col = lax.broadcasted_iota(jnp.int32, (blocks, blocks), 1)
    return (row < col).astype(jnp.float32).astype(jnp.bfloat16)


def ranks_in(mask, blocks):
    chosen = mask.astype(jnp.float32).astype(jnp.bfloat16)
    return jnp.dot(chosen, earlier_matrix(blocks), preferred_element_type=jnp.float32).astype(jnp.int32)


def pick_kernel(capacity, ids_ref, probe_ref, out_ref, picks_ref, picks_smem, sem):
    groups, blocks = ids_ref.shape
    me = lax.axis_index("blk")
    local = ids_ref[...] - me * blocks
    mask = (local >= 0) & (local < blocks)
    rank = ranks_in(mask, blocks)
    lane = lax.broadcasted_iota(jnp.int32, (groups, blocks), 1)
    picks = jnp.zeros((groups, blocks), jnp.int32)
    for r in range(capacity):
        found = jnp.sum(jnp.where(mask & (rank == r), local + 1, 0), axis=1, keepdims=True)
        picks = jnp.where(lane == r, found, picks)
    picks_ref[...] = picks
    copy = pltpu.make_async_copy(picks_ref, picks_smem, sem)
    copy.start()
    copy.wait()

    @pl.loop(0, groups, unroll=8)
    def _(g):
        for r in range(capacity):
            out_ref[g * capacity + r] = probe_ref[jnp.maximum(picks_smem[g, r] - 1, 0)]


def near_place(ids_ref, k, i, first, count):
    place = ids_ref[k, i] - first + REACH
    return jnp.where(place >= count, place - count, place)


def near_forward_kernel(
    groups, capacity, ids_ref, far_ref, halo_ref, probe_ref, coeffs_ref, out_ref, slot_ref, ext, coeffs, sems
):
    blocks = probe_ref.shape[0]
    chunks = blocks // CHUNK

    def load(c):
        own = pl.ds(c * CHUNK, CHUNK)
        return pltpu.make_async_copy(coeffs_ref.at[own, pl.ds(0, 3)], coeffs.at[own], sems.at[c])

    for c in range(chunks):
        load(c).start()
    ext[pl.ds(0, REACH)] = halo_ref[...]
    ext[pl.ds(REACH, blocks)] = probe_ref[...]
    owner = far_ref[...] // blocks
    mask = lax.broadcasted_iota(jnp.int32, (groups, blocks), 0) == owner
    rank = jnp.sum(jnp.where(mask, ranks_in(mask, blocks), 0), axis=0, keepdims=True)
    slot_ref[...] = owner * capacity + rank
    first = lax.axis_index("blk") * blocks

    @pl.loop(0, chunks)
    def _(c):
        load(c).wait()
        for b in range(CHUNK):
            i = c * CHUNK + b
            tiles = [ext[near_place(ids_ref, k, i, first, groups * blocks)] for k in range(3)]
            mat = coeffs[i].reshape(3 * coeffs.shape[2], coeffs.shape[3])
            mixed = jnp.dot(jnp.concatenate(tiles, axis=1), mat, preferred_element_type=jnp.float32)
            out_ref[i] = probe_ref[i].astype(jnp.float32) - mixed


def far_kernel(slot_ref, part_ref, far_ref, coeffs_ref, prec_ref, scaled_ref, parcel_ref, coeffs, prec, sems):
    blocks = part_ref.shape[0]
    chunks = blocks // CHUNK

    def loads(c):
        own = pl.ds(c * CHUNK, CHUNK)
        return (
            pltpu.make_async_copy(coeffs_ref.at[own, 3], coeffs.at[own], sems.at[0, c]),
            pltpu.make_async_copy(prec_ref.at[own], prec.at[own], sems.at[1, c]),
        )

    for c in range(chunks):
        for load in loads(c):
            load.start()
    parcel_ref[...] = jnp.zeros_like(parcel_ref)

    @pl.loop(0, chunks)
    def _(c):
        for load in loads(c):
            load.wait()
        white = []
        for b in range(CHUNK):
            i = c * CHUNK + b
            mixed = jnp.dot(far_ref[slot_ref[0, i]], coeffs[i], preferred_element_type=jnp.float32)
            white.append((part_ref[i] - mixed).astype(jnp.bfloat16))
        scaled = []
        for b in range(CHUNK):
            i = c * CHUNK + b
            scaled.append(jnp.dot(white[b], prec[i], preferred_element_type=jnp.float32).astype(jnp.bfloat16))
            scaled_ref[i] = scaled[b]
        for b in range(CHUNK):
            i = c * CHUNK + b
            term = lax.dot_general(scaled[b], coeffs[i], NT, preferred_element_type=jnp.float32)
            parcel_ref[slot_ref[0, i]] = term.astype(jnp.bfloat16)


def near_back_kernel(groups, ids_ref, scaled_ref, coeffs_ref, base_ref, halo_ref, total, coeffs, sems):
    blocks = scaled_ref.shape[0]
    points = scaled_ref.shape[2]
    chunks = blocks // CHUNK

    def load(c):
        own = pl.ds(c * CHUNK, CHUNK)
        return pltpu.make_async_copy(coeffs_ref.at[own, pl.ds(0, 3)], coeffs.at[own], sems.at[c])

    for c in range(chunks):
        load(c).start()
    total[pl.ds(0, REACH)] = jnp.zeros((REACH,) + total.shape[1:], jnp.float32)
    total[pl.ds(REACH, blocks)] = scaled_ref[...].astype(jnp.float32)
    first = lax.axis_index("blk") * blocks

    @pl.loop(0, chunks)
    def _(c):
        load(c).wait()
        terms = []
        for b in range(CHUNK):
            i = c * CHUNK + b
            mat = coeffs[i].reshape(3 * coeffs.shape[2], coeffs.shape[3])
            terms.append(lax.dot_general(scaled_ref[i], mat, NT, preferred_element_type=jnp.float32))
        for b in range(CHUNK):
            i = c * CHUNK + b
            for k in range(3):
                place = near_place(ids_ref, k, i, first, groups * blocks)
                total[place] = total[place] - terms[b][:, k * points : (k + 1) * points]

    halo_ref[...] = total[pl.ds(0, REACH)]
    base_ref[...] = total[pl.ds(REACH, blocks)]


def sum_kernel(capacity, picks_ref, base_ref, halo_ref, back_ref, out_ref, total):
    groups = picks_ref.shape[0]
    blocks = base_ref.shape[0]
    total[pl.ds(0, blocks)] = base_ref[...]
    last = pl.ds(blocks - REACH, REACH)
    total[last] = total[last] + halo_ref[...]

    @pl.loop(0, groups, unroll=8)
    def _(g):
        for r in range(capacity):
            pick = picks_ref[g, r]
            place = jnp.where(pick > 0, pick - 1, blocks)
            total[place] = total[place] - back_ref[g * capacity + r].astype(jnp.float32)

    out_ref[...] = total[pl.ds(0, blocks)]


def per_device(probe_vecs, coeffs, cond_prec, neighbours):
    blocks, probes, points = probe_vecs.shape
    groups = lax.axis_size("blk")
    capacity = max(2, blocks // (groups - 1) + 1)
    slots = groups * capacity
    chunks = blocks // CHUNK
    bf16, f32 = jnp.bfloat16, jnp.float32
    tile = (probes, points)
    flops = 2 * blocks * probes * points * points

    def exchange(x):
        return lax.all_to_all(x, "blk", split_axis=0, concat_axis=0, tiled=True)

    ids = neighbours.T
    far_ids = ids[3:]
    halo = passed_along(probe_vecs[blocks - REACH :], "blk", 1)
    all_ids = exchange(jnp.broadcast_to(far_ids, (groups, blocks)))
    outgoing, picks = pl.pallas_call(
        functools.partial(pick_kernel, capacity),
        name="pick_tiles",
        out_shape=(
            jax.ShapeDtypeStruct((slots,) + tile, bf16),
            jax.ShapeDtypeStruct((groups, blocks), jnp.int32),
        ),
        in_specs=[VMEM, VMEM],
        out_specs=(VMEM, VMEM),
        scratch_shapes=[pltpu.SMEM((groups, blocks), jnp.int32), pltpu.SemaphoreType.DMA],
        cost_estimate=pl.CostEstimate(flops=0, bytes_accessed=2 * slots * 4096, transcendentals=0),
    )(all_ids, probe_vecs)
    arrived = exchange(outgoing.reshape((groups, capacity) + tile)).reshape((slots,) + tile)
    part, slot_of = pl.pallas_call(
        functools.partial(near_forward_kernel, groups, capacity),
        name="near_forward",
        out_shape=(
            jax.ShapeDtypeStruct((blocks,) + tile, f32),
            jax.ShapeDtypeStruct((1, blocks), jnp.int32),
        ),
        in_specs=[SMEM, VMEM, VMEM, VMEM, HBM],
        out_specs=(VMEM, VMEM),
        scratch_shapes=[
            pltpu.VMEM((REACH + blocks,) + tile, bf16),
            pltpu.VMEM((blocks, 3, points, points), bf16),
            pltpu.SemaphoreType.DMA((chunks,)),
        ],
        compiler_params=params(24),
        cost_estimate=pl.CostEstimate(flops=3 * flops, bytes_accessed=14 * 2**20, transcendentals=0),
    )(ids, far_ids, halo, probe_vecs, coeffs)
    scaled, parcel = pl.pallas_call(
        far_kernel,
        name="far_and_scale",
        out_shape=(
            jax.ShapeDtypeStruct((blocks,) + tile, bf16),
            jax.ShapeDtypeStruct((slots,) + tile, bf16),
        ),
        in_specs=[SMEM, VMEM, VMEM, HBM, HBM],
        out_specs=(VMEM, VMEM),
        scratch_shapes=[
            pltpu.VMEM((blocks, points, points), bf16),
            pltpu.VMEM((blocks, points, points), bf16),
            pltpu.SemaphoreType.DMA((2, chunks)),
        ],
        compiler_params=params(24),
        cost_estimate=pl.CostEstimate(flops=3 * flops, bytes_accessed=11 * 2**20, transcendentals=0),
    )(slot_of, part, arrived, coeffs, cond_prec)
    returned = exchange(parcel.reshape((groups, capacity) + tile)).reshape((slots,) + tile)
    base, halo_back = pl.pallas_call(
        functools.partial(near_back_kernel, groups),
        name="near_back",
        out_shape=(
            jax.ShapeDtypeStruct((blocks,) + tile, f32),
            jax.ShapeDtypeStruct((REACH,) + tile, f32),
        ),
        in_specs=[SMEM, VMEM, HBM],
        out_specs=(VMEM, VMEM),
        scratch_shapes=[
            pltpu.VMEM((REACH + blocks,) + tile, f32),
            pltpu.VMEM((blocks, 3, points, points), bf16),
            pltpu.SemaphoreType.DMA((chunks,)),
        ],
        compiler_params=params(24),
        cost_estimate=pl.CostEstimate(flops=3 * flops, bytes_accessed=14 * 2**20, transcendentals=0),
    )(ids, scaled, coeffs)
    halo_sum = passed_along(halo_back, "blk", -1)
    return pl.pallas_call(
        functools.partial(sum_kernel, capacity),
        name="final_sum",
        out_shape=jax.ShapeDtypeStruct((blocks,) + tile, f32),
        in_specs=[SMEM, VMEM, VMEM, VMEM],
        out_specs=VMEM,
        scratch_shapes=[pltpu.VMEM((blocks + 1,) + tile, f32)],
        cost_estimate=pl.CostEstimate(flops=0, bytes_accessed=3 * 2**20, transcendentals=0),
    )(picks, base, halo_sum, returned)


def solution(mesh):
    in_specs = (
        P("blk", None, None),
        P("blk", None, None, None),
        P("blk", None, None),
        P("blk", None),
    )
    return jax.shard_map(
        per_device, mesh=mesh, in_specs=in_specs, out_specs=P("blk", None, None), check_vma=False
    )
```

time: 152 us -> 96.2 us (0.63)
  other arithmetic: 50.8 us -> 0 us
  Pallas kernels: 0 us -> 25.8 us
  matrix products: 23 us -> 0 us
  local copies, waits for them, and re-layouts: 27.9 us -> 24.6 us
  waiting for transfers between devices: 22.3 us -> 19.5 us
    scatter-add x2 -> x0, other arithmetic: 43.8 us -> none  [the longest x1 30.7 us: per_device(): jax.ops.segment_sum(back_terms[:, :3].reshape(-1, probes, points), ext_po...]
    pallas_call x0 -> x5, Pallas kernels: none -> 25.8 us  [the longest x1 7.54 us: per_device(): pl.pallas_call(far_kernel, name='far_and_scale', out_shape=(jax.ShapeDtyp...]
    unnamed x6 -> x20, local copies, waits for them, and re-layouts: 0.01 us -> 23.1 us
    dot_general x2 -> x0, matrix products: 23 us -> none  [the longest x1 12.4 us: per_device(): jnp.einsum('bpn,bkmn->bkpm', scaled, coeffs, preferred_element_type=jnp.f...]
    scatter x2 -> x0, local copies, waits for them, and re-layouts: 13.3 us -> none  [the longest x1 12.4 us: per_device(): jnp.zeros((groups * capacity, probes, points), jnp.bfloat16).at[slot_pos]]
    gather x3 -> x0, local copies, waits for them, and re-layouts: 6.32 us -> none  [the longest x1 2.61 us: per_device(): outgoing = probe_vecs[picked]]
    slice x2, local copies, waits for them, and re-layouts: 4.83 us -> 1.53 us  [the longest x1 0.85 us: per_device(): halo = passed_along(probe_vecs[blocks - REACH:], 'blk', 1)]
    ppermute x2, waiting for transfers between devices: 22.3 us -> 19.5 us  [passed_along(): lax.ppermute(block, axis, [((i - distance) % size, i) for i in range(size)])]
  transfers between devices with their start and end apart: 4 -> 4, of which waited for: 1 -> 2; matrix products, arithmetic and copies ran while one was open for 35% -> 1% of each run, Pallas kernels for 0% -> 12%
where the time goes in v1:
time: 96.2 us; the launch traced here: 95.6 us
  Pallas kernels  25.8 us (27%)
  local copies, waits for them, and re-layouts  24.6 us (26%)
  waiting for transfers between devices  19.5 us (20%)
  blocking collectives  14.4 us (15%)
  starting transfers between devices  11.2 us (12%)
    unnamed x20, local copies, waits for them, and re-layouts  23.1 us
    ppermute x2, waiting for transfers between devices, passed_along(): lax.ppermute(block, axis, [((i - distance) % size, i) for i in range(size)])  19.5 us
    all_to_all x1, blocking collectives, exchange(): return lax.all_to_all(x, 'blk', split_axis=0, concat_axis=0, tiled=True)  14.4 us
    pallas_call x1, Pallas kernels, per_device(): pl.pallas_call(far_kernel, name='far_and_scale', out_shape=(jax.ShapeDtyp...  7.54 us
    pallas_call x1, Pallas kernels, per_device(): pl.pallas_call(functools.partial(near_back_kernel, groups), name='near_ba...  7 us
    all_to_all x2, starting transfers between devices, exchange(): return lax.all_to_all(x, 'blk', split_axis=0, concat_axis=0, tiled=True)  5.86 us
    ppermute x2, starting transfers between devices, passed_along(): lax.ppermute(block, axis, [((i - distance) % size, i) for i in range(size)])  5.33 us
    pallas_call x1, Pallas kernels, per_device(): pl.pallas_call(functools.partial(near_forward_kernel, groups, capacity),...  4.84 us
  transfers between devices with their start and end apart: 4, of which 2 were waited for; matrix products, arithmetic and copies ran while one was open for 1% of the time, Pallas kernels for 12%

profile of v1, /device:TPU:0, one launch (start us, length us, event | category | flops | bytes accessed | tf_op | source)
XLA Modules:
  0.0 95.6 jit_solution(5122660010148368878)
XLA Ops:
  0.0 0.7 fusion
  0.7 14.4 %all_to_all.18 = s32[32,1,128]{2,1,0:T(1,128)} all-to-all(s32[32,1,128]{2,1,0:T(1,128)S(1)} %broadcast_in_dim.2), channel_id=1, replica_groups=mesh['blk'=32] {'blk'}, dimensions={0} | all-to-all | bytes 32768 | tf_op jit(solution)/shard_map/all_to_all | solution.py:193
  15.1 3.3 %pick_tiles.1 = (bf16[160,16,128]{2,1,0:T(8,128)(2,1)}, s32[32,128]{1,0:T(8,128)}) custom-call(s32[32,128]{1,0:T(8,128)} %bitcast.14, bf16[128,16,128]{2,1,0:T(8,128)(2,1)} %probe_ref.3), custom_call_target="tpu_custom_call" | custom-call | bytes 1310720 | tf_op jit(solution)/shard_map/pick_tiles/pallas_call | solution.py:199
  18.3 2.6 %all-to-all-start.1 = ((bf16[32,5,16,128]{3,2,1,0:T(8,128)(2,1)}), bf16[32,5,16,128]{3,2,1,0:T(8,128)(2,1)S(1)}, u32[]{:S(2)}, u32[]{:S(2)}) async-start(bf16[32,5,16,128]{3,2,1,0:T(8,128)(2,1)} %bitcast.13), calls=%async_computation.1 | async-start | bytes 1310720 | tf_op jit(solution)/shard_map/all_to_all | solution.py:193
  21.0 0.8 slice.10
  21.8 0.1 collective-permute-start
  21.9 16.9 %collective-permute-done.halo_ref = bf16[16,16,128]{2,1,0:T(8,128)(2,1)S(1)} collective-permute-done((bf16[16,16,128]{2,1,0:T(8,128)(2,1)S(1)}, bf16[16,16,128]{2,1,0:T(8,128)(2,1)S(1)}, u32[]{:S(2)}, u32[]{:S(2)}) %collective-permute-start) | collective-permute-done | bytes 65568 | tf_op jit(solution)/shard_map/ppermute | solution.py:24
  38.9 5.8 %copy-done = bf16[128,4,128,128]{3,2,1,0:T(8,128)(2,1)S(1)} copy-done((bf16[128,4,128,128]{3,2,1,0:T(8,128)(2,1)S(1)}, bf16[128,4,128,128]{3,2,1,0:T(8,128)(2,1)}, u32[]{:S(2)}) %copy-start) | copy-done | bytes 16777240
  44.7 1.0 %copy-done.4 = bf16[128,16,128]{2,1,0:T(8,128)(2,1)S(1)} copy-done((bf16[128,16,128]{2,1,0:T(8,128)(2,1)S(1)}, bf16[128,16,128]{2,1,0:T(8,128)(2,1)}, u32[]{:S(2)}) %copy-start.4) | copy-done | bytes 524312
  45.7 0.7 copy-done.6
  46.4 4.8 %near_forward.1 = (f32[128,16,128]{2,1,0:T(8,128)S(1)}, s32[1,128]{1,0:T(1,128)S(1)}) custom-call(s32[4,128]{1,0:T(4,128)S(1)} %bitcast.10, s32[1,128]{1,0:T(1,128)S(1)} %get-tuple-element.21.far_ref, bf16[16,16,128]{2,1,0:T(8,128)(2,1)S(1)} %collective-permute-done.halo_ref, bf16[128,16,128]{2,1,0:T(8,128)(2,1)S(1)} %copy-done.4, ...), custom_call_target="tpu_custom_call" | custom-call | flops 201326592 | bytes 14680064 | tf_op jit(solution)/shard_map/near_forward/pallas_call | solution.py:212
  51.2 0.0 copy-start.1
  51.3 5.8 %copy-done.1 = bf16[128,4,128,128]{3,2,1,0:T(8,128)(2,1)S(1)} copy-done((bf16[128,4,128,128]{3,2,1,0:T(8,128)(2,1)S(1)}, bf16[128,4,128,128]{3,2,1,0:T(8,128)(2,1)}, u32[]{:S(2)}) %copy-start.1) | copy-done | bytes 16777240
  57.0 2.2 %copy-done.3 = bf16[128,128,128]{2,1,0:T(8,128)(2,1)S(1)} copy-done((bf16[128,128,128]{2,1,0:T(8,128)(2,1)S(1)}, bf16[128,128,128]{2,1,0:T(8,128)(2,1)}, u32[]{:S(2)}) %copy-start.3) | copy-done | bytes 4194328
  59.2 7.5 %far_and_scale.1 = (bf16[128,16,128]{2,1,0:T(8,128)(2,1)S(1)}, bf16[160,16,128]{2,1,0:T(8,128)(2,1)}) custom-call(s32[1,128]{1,0:T(1,128)S(1)} %get-tuple-element.14.slot_ref, f32[128,16,128]{2,1,0:T(8,128)S(1)} %get-tuple-element.15.part_ref, bf16[160,16,128]{2,1,0:T(8,128)(2,1)S(1)} %bitcast.8, bf16[128,4,128,128]{3,2,1,0:T(8,128)(2,1)S(1)} %copy-done.1, ...), custom_call_target="tpu_custom_call" | custom-call | flops 201326592 | bytes 11534336 | tf_op jit(solution)/shard_map/far_and_scale/pallas_call | solution.py:229
  66.8 3.2 %all-to-all-start.2 = ((bf16[32,5,16,128]{3,2,1,0:T(8,128)(2,1)}), bf16[32,5,16,128]{3,2,1,0:T(8,128)(2,1)S(1)}, u32[]{:S(2)}, u32[]{:S(2)}) async-start(bf16[32,5,16,128]{3,2,1,0:T(8,128)(2,1)} %bitcast.5), calls=%async_computation.2 | async-start | bytes 1310720 | tf_op jit(solution)/shard_map/all_to_all | solution.py:193
  70.0 5.8 %copy-done.2 = bf16[128,4,128,128]{3,2,1,0:T(8,128)(2,1)S(1)} copy-done((bf16[128,4,128,128]{3,2,1,0:T(8,128)(2,1)S(1)}, bf16[128,4,128,128]{3,2,1,0:T(8,128)(2,1)}, u32[]{:S(2)}) %copy-start.2) | copy-done | bytes 16777240
  75.8 7.0 %near_back.1 = (f32[128,16,128]{2,1,0:T(8,128)S(1)}, f32[16,16,128]{2,1,0:T(8,128)S(1)}) custom-call(s32[4,128]{1,0:T(4,128)S(1)} %bitcast.11, bf16[128,16,128]{2,1,0:T(8,128)(2,1)S(1)} %get-tuple-element.17.scaled_ref, bf16[128,4,128,128]{3,2,1,0:T(8,128)(2,1)S(1)} %copy-done.2), custom_call_target="tpu_custom_call" | custom-call | flops 201326592 | bytes 14680064 | tf_op jit(solution)/shard_map/near_back/pallas_call | solution.py:247
  82.8 1.0 %copy-done.5 = f32[128,16,128]{2,1,0:T(8,128)} copy-done((f32[128,16,128]{2,1,0:T(8,128)}, f32[128,16,128]{2,1,0:T(8,128)S(1)}, u32[]{:S(2)}) %copy-start.5) | copy-done | bytes 1048600
  83.8 5.2 %collective-permute-start.1 = (f32[16,16,128]{2,1,0:T(8,128)S(1)}, f32[16,16,128]{2,1,0:T(8,128)S(1)}, u32[]{:S(2)}, u32[]{:S(2)}) collective-permute-start(f32[16,16,128]{2,1,0:T(8,128)S(1)} %get-tuple-element.19), channel_id=1, source_target_pairs={{1,0},{2,1},{3,2},{4,3},{5,4},{6,5},{7,6},{8,7},{9,8},{10,9},{11,1... | collective-permute-start | bytes 393224 | tf_op jit(solution)/shard_map/ppermute | solution.py:24
  89.0 2.5 %collective-permute-done.1.halo_ref = f32[16,16,128]{2,1,0:T(8,128)S(1)} collective-permute-done((f32[16,16,128]{2,1,0:T(8,128)S(1)}, f32[16,16,128]{2,1,0:T(8,128)S(1)}, u32[]{:S(2)}, u32[]{:S(2)}) %collective-permute-start.1) | collective-permute-done | bytes 131104 | tf_op jit(solution)/shard_map/ppermute | solution.py:24
  91.5 0.7 copy-done.9
  92.2 0.2 copy-done.8
  92.4 3.2 %final_sum.1 = f32[128,16,128]{2,1,0:T(8,128)} custom-call(s32[32,128]{1,0:T(8,128)} %get-tuple-element.13.picks_ref, f32[128,16,128]{2,1,0:T(8,128)} %copy-done.5, f32[16,16,128]{2,1,0:T(8,128)} %copy-done.9, bf16[160,16,128]{2,1,0:T(8,128)(2,1)} %bitcast.12), custom_call_target="tpu_custom_call" | custom-call | bytes 3145728 | tf_op jit(solution)/shard_map/final_sum/pallas_call | solution.py:265
  (13 shorter events, 0.0 us)
Async XLA Ops:
  18.3 32.9 %all-to-all-start.1 = ((bf16[32,5,16,128]{3,2,1,0:T(8,128)(2,1)}), bf16[32,5,16,128]{3,2,1,0:T(8,128)(2,1)S(1)}, u32[]{:S(2)}, u32[]{:S(2)}) async-start(bf16[32,5,16,128]{3,2,1,0:T(8,128)(2,1)} %bitcast.13), calls=%async_computation.1 | async-start | bytes 1310720 | tf_op jit(solution)/shard_map/all_to_all | solution.py:193
  21.8 17.1 %collective-permute-start = (bf16[16,16,128]{2,1,0:T(8,128)(2,1)S(1)}, bf16[16,16,128]{2,1,0:T(8,128)(2,1)S(1)}, u32[]{:S(2)}, u32[]{:S(2)}) collective-permute-start(bf16[16,16,128]{2,1,0:T(8,128)(2,1)S(1)} %slice.10), channel_id=1, source_target_pairs={{31,0},{0,1},{1,2},{2,3},{3,4},{4,5},{5,6},{6,7},{7,8},{8,9},{9,10... | collective-permute-start | bytes 196616 | tf_op jit(solution)/shard_map/ppermute | solution.py:24
  38.9 5.8 %copy-start = (bf16[128,4,128,128]{3,2,1,0:T(8,128)(2,1)S(1)}, bf16[128,4,128,128]{3,2,1,0:T(8,128)(2,1)}, u32[]{:S(2)}) copy-start(bf16[128,4,128,128]{3,2,1,0:T(8,128)(2,1)} %coeffs_ref.5) | copy-start | bytes 50331652
  44.7 1.0 %copy-start.4 = (bf16[128,16,128]{2,1,0:T(8,128)(2,1)S(1)}, bf16[128,16,128]{2,1,0:T(8,128)(2,1)}, u32[]{:S(2)}) copy-start(bf16[128,16,128]{2,1,0:T(8,128)(2,1)} %probe_ref.3) | copy-start | bytes 1572868
  45.7 0.7 copy-start.6
  46.4 23.6 %copy-start.7 = (s32[128,4]{0,1:T(4,128)S(1)}, s32[128,4]{0,1:T(4,128)}, u32[]{:S(2)}) copy-start(s32[128,4]{0,1:T(4,128)} %param.7) | copy-start | bytes 6148
  51.2 5.8 %copy-start.1 = (bf16[128,4,128,128]{3,2,1,0:T(8,128)(2,1)S(1)}, bf16[128,4,128,128]{3,2,1,0:T(8,128)(2,1)}, u32[]{:S(2)}) copy-start(bf16[128,4,128,128]{3,2,1,0:T(8,128)(2,1)} %coeffs_ref.5) | copy-start | bytes 50331652
  57.0 2.2 %copy-start.3 = (bf16[128,128,128]{2,1,0:T(8,128)(2,1)S(1)}, bf16[128,128,128]{2,1,0:T(8,128)(2,1)}, u32[]{:S(2)}) copy-start(bf16[128,128,128]{2,1,0:T(8,128)(2,1)} %prec_ref.1) | copy-start | bytes 12582916
  66.8 24.8 %all-to-all-start.2 = ((bf16[32,5,16,128]{3,2,1,0:T(8,128)(2,1)}), bf16[32,5,16,128]{3,2,1,0:T(8,128)(2,1)S(1)}, u32[]{:S(2)}, u32[]{:S(2)}) async-start(bf16[32,5,16,128]{3,2,1,0:T(8,128)(2,1)} %bitcast.5), calls=%async_computation.2 | async-start | bytes 1310720 | tf_op jit(solution)/shard_map/all_to_all | solution.py:193
  70.0 5.8 %copy-start.2 = (bf16[128,4,128,128]{3,2,1,0:T(8,128)(2,1)S(1)}, bf16[128,4,128,128]{3,2,1,0:T(8,128)(2,1)}, u32[]{:S(2)}) copy-start(bf16[128,4,128,128]{3,2,1,0:T(8,128)(2,1)} %coeffs_ref.5) | copy-start | bytes 50331652
  82.8 1.0 %copy-start.5 = (f32[128,16,128]{2,1,0:T(8,128)}, f32[128,16,128]{2,1,0:T(8,128)S(1)}, u32[]{:S(2)}) copy-start(f32[128,16,128]{2,1,0:T(8,128)S(1)} %get-tuple-element.18.base_ref) | copy-start | bytes 3145732
  83.8 7.7 %collective-permute-start.1 = (f32[16,16,128]{2,1,0:T(8,128)S(1)}, f32[16,16,128]{2,1,0:T(8,128)S(1)}, u32[]{:S(2)}, u32[]{:S(2)}) collective-permute-start(f32[16,16,128]{2,1,0:T(8,128)S(1)} %get-tuple-element.19), channel_id=1, source_target_pairs={{1,0},{2,1},{3,2},{4,3},{5,4},{6,5},{7,6},{8,7},{9,8},{10,9},{11,1... | collective-permute-start | bytes 393224 | tf_op jit(solution)/shard_map/ppermute | solution.py:24
  91.5 0.7 copy-start.9
  91.5 0.9 copy-start.8

commit v2 on v1

--- a/solution.py
+++ b/solution.py
@@ -154,9 +154,10 @@
             terms.append(lax.dot_general(scaled_ref[i], mat, NT, preferred_element_type=jnp.float32))
         for b in range(CHUNK):
             i = c * CHUNK + b
+            places = [near_place(ids_ref, k, i, first, groups * blocks) for k in range(3)]
+            olds = [total[place] for place in places]
             for k in range(3):
-                place = near_place(ids_ref, k, i, first, groups * blocks)
-                total[place] = total[place] - terms[b][:, k * points : (k + 1) * points]
+                total[places[k]] = olds[k] - terms[b][:, k * points : (k + 1) * points]
 
     halo_ref[...] = total[pl.ds(0, REACH)]
     base_ref[...] = total[pl.ds(REACH, blocks)]
@@ -171,10 +172,11 @@
 
     @pl.loop(0, groups, unroll=8)
     def _(g):
+        picks = [picks_ref[g, r] for r in range(capacity)]
+        places = [jnp.where(pick > 0, pick - 1, blocks) for pick in picks]
+        olds = [total[place] for place in places]
         for r in range(capacity):
-            pick = picks_ref[g, r]
-            place = jnp.where(pick > 0, pick - 1, blocks)
-            total[place] = total[place] - back_ref[g * capacity + r].astype(jnp.float32)
+            total[places[r]] = olds[r] - back_ref[g * capacity + r].astype(jnp.float32)
 
     out_ref[...] = total[pl.ds(0, blocks)]
 
@@ -195,7 +197,8 @@
     ids = neighbours.T
     far_ids = ids[3:]
     halo = passed_along(probe_vecs[blocks - REACH :], "blk", 1)
-    all_ids = exchange(jnp.broadcast_to(far_ids, (groups, blocks)))
+    all_ids = lax.all_gather(far_ids, "blk", axis=0, tiled=True)
+    all_ids, halo = lax.optimization_barrier((all_ids, halo))
     outgoing, picks = pl.pallas_call(
         functools.partial(pick_kernel, capacity),
         name="pick_tiles",
@@ -206,6 +209,7 @@
         in_specs=[VMEM, VMEM],
         out_specs=(VMEM, VMEM),
         scratch_shapes=[pltpu.SMEM((groups, blocks), jnp.int32), pltpu.SemaphoreType.DMA],
+        compiler_params=params(8),
         cost_estimate=pl.CostEstimate(flops=0, bytes_accessed=2 * slots * 4096, transcendentals=0),
     )(all_ids, probe_vecs)
     arrived = exchange(outgoing.reshape((groups, capacity) + tile)).reshape((slots,) + tile)
@@ -223,7 +227,7 @@
             pltpu.VMEM((blocks, 3, points, points), bf16),
             pltpu.SemaphoreType.DMA((chunks,)),
         ],
-        compiler_params=params(24),
+        compiler_params=params(60),
         cost_estimate=pl.CostEstimate(flops=3 * flops, bytes_accessed=14 * 2**20, transcendentals=0),
     )(ids, far_ids, halo, probe_vecs, coeffs)
     scaled, parcel = pl.pallas_call(
@@ -240,7 +244,7 @@
             pltpu.VMEM((blocks, points, points), bf16),
             pltpu.SemaphoreType.DMA((2, chunks)),
         ],
-        compiler_params=params(24),
+        compiler_params=params(60),
         cost_estimate=pl.CostEstimate(flops=3 * flops, bytes_accessed=11 * 2**20, transcendentals=0),
     )(slot_of, part, arrived, coeffs, cond_prec)
     returned = exchange(parcel.reshape((groups, capacity) + tile)).reshape((slots,) + tile)
@@ -258,7 +262,7 @@
             pltpu.VMEM((blocks, 3, points, points), bf16),
             pltpu.SemaphoreType.DMA((chunks,)),
         ],
-        compiler_params=params(24),
+        compiler_params=params(60),
         cost_estimate=pl.CostEstimate(flops=3 * flops, bytes_accessed=14 * 2**20, transcendentals=0),
     )(ids, scaled, coeffs)
     halo_sum = passed_along(halo_back, "blk", -1)
@@ -269,6 +273,7 @@
         in_specs=[SMEM, VMEM, VMEM, VMEM],
         out_specs=VMEM,
         scratch_shapes=[pltpu.VMEM((blocks + 1,) + tile, f32)],
+        compiler_params=params(8),
         cost_estimate=pl.CostEstimate(flops=0, bytes_accessed=3 * 2**20, transcendentals=0),
     )(picks, base, halo_sum, returned)
 

time: 96.2 us -> 104 us (1.081)
  blocking collectives: 14.4 us -> 42.6 us
  local copies, waits for them, and re-layouts: 24.6 us -> 5.21 us
  waiting for transfers between devices: 19.5 us -> 14.4 us
  Pallas kernels: 25.8 us -> 29.5 us
    all_gather x0 -> x1, blocking collectives: none -> 42.6 us  [per_device(): all_ids = lax.all_gather(far_ids, 'blk', axis=0, tiled=True)]
    unnamed x20 -> x8, local copies, waits for them, and re-layouts: 23.1 us -> 3.15 us
    ppermute x2, waiting for transfers between devices: 19.5 us -> 2.84 us  [passed_along(): lax.ppermute(block, axis, [((i - distance) % size, i) for i in range(size)])]
    all_to_all x1 -> x0, blocking collectives: 14.4 us -> none  [exchange(): return lax.all_to_all(x, 'blk', split_axis=0, concat_axis=0, tiled=True)]
    all_to_all x2, waiting for transfers between devices: 0.01 us -> 11.6 us  [exchange(): return lax.all_to_all(x, 'blk', split_axis=0, concat_axis=0, tiled=True)]
    pallas_call x1, Pallas kernels: 4.84 us -> 7.16 us  [per_device(): pl.pallas_call(functools.partial(near_forward_kernel, groups, capacity),...]
    pallas_call x1, Pallas kernels: 7 us -> 8.93 us  [per_device(): pl.pallas_call(functools.partial(near_back_kernel, groups), name='near_ba...]
    pallas_call x1, Pallas kernels: 7.54 us -> 8.98 us  [per_device(): pl.pallas_call(far_kernel, name='far_and_scale', out_shape=(jax.ShapeDtyp...]
  transfers between devices with their start and end apart: 4 -> 4, of which waited for: 2 -> 3; matrix products, arithmetic and copies ran while one was open for 1% -> 1% of each run, Pallas kernels for 12% -> 16%
where the time goes in v2:
time: 104 us
  blocking collectives  42.6 us (41%)
  Pallas kernels  29.5 us (28%)
  waiting for transfers between devices  14.4 us (14%)
  starting transfers between devices  11.8 us (11%)
  local copies, waits for them, and re-layouts  5.21 us (5%)
    all_gather x1, blocking collectives, per_device(): all_ids = lax.all_gather(far_ids, 'blk', axis=0, tiled=True)  42.6 us
    all_to_all x2, waiting for transfers between devices, exchange(): return lax.all_to_all(x, 'blk', split_axis=0, concat_axis=0, tiled=True)  11.6 us
    pallas_call x1, Pallas kernels, per_device(): pl.pallas_call(far_kernel, name='far_and_scale', out_shape=(jax.ShapeDtyp...  8.98 us
    pallas_call x1, Pallas kernels, per_device(): pl.pallas_call(functools.partial(near_back_kernel, groups), name='near_ba...  8.93 us
    pallas_call x1, Pallas kernels, per_device(): pl.pallas_call(functools.partial(near_forward_kernel, groups, capacity),...  7.16 us
    all_to_all x2, starting transfers between devices, exchange(): return lax.all_to_all(x, 'blk', split_axis=0, concat_axis=0, tiled=True)  6.06 us
    ppermute x2, starting transfers between devices, passed_along(): lax.ppermute(block, axis, [((i - distance) % size, i) for i in range(size)])  5.72 us
    unnamed x8, local copies, waits for them, and re-layouts  3.15 us
  transfers between devices with their start and end apart: 4, of which 3 were waited for; matrix products, arithmetic and copies ran while one was open for 1% of the time, Pallas kernels for 16%

profile of v2, /device:TPU:0, one launch (start us, length us, event | category | flops | bytes accessed | tf_op | source)
XLA Modules:
  0.0 103.6 jit_solution(14114293149424547091)
XLA Ops:
  0.0 0.8 slice.7
  0.8 0.5 collective-permute-start
  1.3 1.2 %fusion = (s32[1,128]{1,0:T(1,128)}, s32[1,1,128]{2,1,0:T(1,128)S(1)}) fusion(s32[4,128]{1,0:T(4,128)} %bitcast.12), kind=kLoop, calls=%fused_computation.1 | loop fusion | bytes 1536 | tf_op jit(solution)/shard_map/slice | solution.py:198
  2.5 42.6 %all-gather = s32[32,1,128]{2,1,0:T(1,128)S(1)} all-gather(s32[1,1,128]{2,1,0:T(1,128)S(1)} %get-tuple-element.26), channel_id=1, replica_groups=mesh['blk'=32] {'blk'}, dimensions={0}, use_global_device_ids=true | all-gather | bytes 16896 | tf_op jit(solution)/shard_map/all_gather | solution.py:200
  45.1 0.0 collective-permute-done.halo_ref
  45.1 0.0 copy-start.3
  45.1 0.0 copy-start
  45.1 1.1 %copy-done = bf16[128,16,128]{2,1,0:T(8,128)(2,1)S(1)} copy-done((bf16[128,16,128]{2,1,0:T(8,128)(2,1)S(1)}, bf16[128,16,128]{2,1,0:T(8,128)(2,1)}, u32[]{:S(2)}) %copy-start) | copy-done | bytes 524312
  46.2 2.2 %pick_tiles.1 = (bf16[160,16,128]{2,1,0:T(8,128)(2,1)}, s32[32,128]{1,0:T(8,128)S(1)}) custom-call(s32[32,128]{1,0:T(8,128)S(1)} %bitcast.9, bf16[128,16,128]{2,1,0:T(8,128)(2,1)S(1)} %copy-done), custom_call_target="tpu_custom_call" | custom-call | bytes 1310720 | tf_op jit(solution)/shard_map/pick_tiles/pallas_call | solution.py:202
  48.4 2.6 %all-to-all-start = ((bf16[32,5,16,128]{3,2,1,0:T(8,128)(2,1)}), bf16[32,5,16,128]{3,2,1,0:T(8,128)(2,1)S(1)}, u32[]{:S(2)}, u32[]{:S(2)}) async-start(bf16[32,5,16,128]{3,2,1,0:T(8,128)(2,1)} %bitcast.3), calls=%async_computation | async-start | bytes 1310720 | tf_op jit(solution)/shard_map/all_to_all | solution.py:195
  51.0 0.0 copy-done.3
  51.0 7.2 %near_forward.1 = (f32[128,16,128]{2,1,0:T(8,128)}, s32[1,128]{1,0:T(1,128)}) custom-call(s32[4,128]{1,0:T(4,128)} %bitcast.13, s32[1,128]{1,0:T(1,128)} %get-tuple-element.25.far_ref, bf16[16,16,128]{2,1,0:T(8,128)(2,1)} %copy-done.3, bf16[128,16,128]{2,1,0:T(8,128)(2,1)} %probe_ref.3, bf16[128,4,128,128]{3,2,1,0:T(8,128)(2,1)} %coeffs_ref.5), custom_call_target="tpu_custom_call" | custom-call | flops 201326592 | bytes 14680064 | tf_op jit(solution)/shard_map/near_forward/pallas_call | solution.py:216
  58.2 10.7 %all-to-all-done = bf16[32,5,16,128]{3,2,1,0:T(8,128)(2,1)S(1)} async-done(((bf16[32,5,16,128]{3,2,1,0:T(8,128)(2,1)}), bf16[32,5,16,128]{3,2,1,0:T(8,128)(2,1)S(1)}, u32[]{:S(2)}, u32[]{:S(2)}) %all-to-all-start) | async-done | bytes 655392 | tf_op jit(solution)/shard_map/all_to_all | solution.py:195
  68.9 0.0 copy-start.2
  68.9 0.9 copy-done.2
  69.8 9.0 %far_and_scale.1 = (bf16[128,16,128]{2,1,0:T(8,128)(2,1)}, bf16[160,16,128]{2,1,0:T(8,128)(2,1)}) custom-call(s32[1,128]{1,0:T(1,128)} %get-tuple-element.18.slot_ref, f32[128,16,128]{2,1,0:T(8,128)} %get-tuple-element.19.part_ref, bf16[160,16,128]{2,1,0:T(8,128)(2,1)} %bitcast.10, bf16[128,4,128,128]{3,2,1,0:T(8,128)(2,1)} %coeffs_ref.5, ...), custom_call_target="tpu_custom_call" | custom-call | flops 201326592 | bytes 11534336 | tf_op jit(solution)/shard_map/far_and_scale/pallas_call | solution.py:233
  78.8 3.4 %all-to-all-start.1 = ((bf16[32,5,16,128]{3,2,1,0:T(8,128)(2,1)}), bf16[32,5,16,128]{3,2,1,0:T(8,128)(2,1)S(1)}, u32[]{:S(2)}, u32[]{:S(2)}) async-start(bf16[32,5,16,128]{3,2,1,0:T(8,128)(2,1)} %bitcast.11), calls=%async_computation.1 | async-start | bytes 1310720 | tf_op jit(solution)/shard_map/all_to_all | solution.py:195
  82.2 8.9 %near_back.1 = (f32[128,16,128]{2,1,0:T(8,128)}, f32[16,16,128]{2,1,0:T(8,128)}) custom-call(s32[4,128]{1,0:T(4,128)} %bitcast.14, bf16[128,16,128]{2,1,0:T(8,128)(2,1)} %get-tuple-element.21.scaled_ref, bf16[128,4,128,128]{3,2,1,0:T(8,128)(2,1)} %coeffs_ref.5), custom_call_target="tpu_custom_call" | custom-call | flops 201326592 | bytes 14680064 | tf_op jit(solution)/shard_map/near_back/pallas_call | solution.py:251
  91.1 5.3 %collective-permute-start.1 = (f32[16,16,128]{2,1,0:T(8,128)}, f32[16,16,128]{2,1,0:T(8,128)S(1)}, u32[]{:S(2)}, u32[]{:S(2)}) collective-permute-start(f32[16,16,128]{2,1,0:T(8,128)} %get-tuple-element.23), channel_id=1, source_target_pairs={{1,0},{2,1},{3,2},{4,3},{5,4},{6,5},{7,6},{8,7},{9,8},{10,9},{11,1... | collective-permute-start | bytes 393224 | tf_op jit(solution)/shard_map/ppermute | solution.py:24
  96.4 2.8 %collective-permute-done.1.halo_ref = f32[16,16,128]{2,1,0:T(8,128)S(1)} collective-permute-done((f32[16,16,128]{2,1,0:T(8,128)}, f32[16,16,128]{2,1,0:T(8,128)S(1)}, u32[]{:S(2)}, u32[]{:S(2)}) %collective-permute-start.1) | collective-permute-done | bytes 131104 | tf_op jit(solution)/shard_map/ppermute | solution.py:24
  99.3 0.9 all-to-all-done.1
  100.1 0.0 copy-start.1
  100.1 1.2 %copy-done.1 = f32[128,16,128]{2,1,0:T(8,128)S(1)} copy-done((f32[128,16,128]{2,1,0:T(8,128)S(1)}, f32[128,16,128]{2,1,0:T(8,128)}, u32[]{:S(2)}) %copy-start.1) | copy-done | bytes 1048600
  101.4 2.2 %final_sum.1 = f32[128,16,128]{2,1,0:T(8,128)} custom-call(s32[32,128]{1,0:T(8,128)S(1)} %get-tuple-element.16.picks_ref, f32[128,16,128]{2,1,0:T(8,128)S(1)} %copy-done.1, f32[16,16,128]{2,1,0:T(8,128)S(1)} %collective-permute-done.1.halo_ref, bf16[160,16,128]{2,1,0:T(8,128)(2,1)S(1)} %bitcast.8), custom_call_target="tpu_custom_call" | custom-call | bytes 3145728 | tf_op jit(solution)/shard_map/final_sum/pallas_call | solution.py:269
Async XLA Ops:
  0.8 44.2 %collective-permute-start = (bf16[16,16,128]{2,1,0:T(8,128)(2,1)S(1)}, bf16[16,16,128]{2,1,0:T(8,128)(2,1)S(1)}, u32[]{:S(2)}, u32[]{:S(2)}) collective-permute-start(bf16[16,16,128]{2,1,0:T(8,128)(2,1)S(1)} %slice.7), channel_id=1, source_target_pairs={{31,0},{0,1},{1,2},{2,3},{3,4},{4,5},{5,6},{6,7},{7,8},{8,9},{9,10... | collective-permute-start | bytes 196616 | tf_op jit(solution)/shard_map/ppermute | solution.py:24
  45.1 5.9 %copy-start.3 = (bf16[16,16,128]{2,1,0:T(8,128)(2,1)}, bf16[16,16,128]{2,1,0:T(8,128)(2,1)S(1)}, u32[]{:S(2)}) copy-start(bf16[16,16,128]{2,1,0:T(8,128)(2,1)S(1)} %collective-permute-done.halo_ref) | copy-start | bytes 196612
  45.1 1.1 %copy-start = (bf16[128,16,128]{2,1,0:T(8,128)(2,1)S(1)}, bf16[128,16,128]{2,1,0:T(8,128)(2,1)}, u32[]{:S(2)}) copy-start(bf16[128,16,128]{2,1,0:T(8,128)(2,1)} %probe_ref.3) | copy-start | bytes 1572868
  48.4 20.6 %all-to-all-start = ((bf16[32,5,16,128]{3,2,1,0:T(8,128)(2,1)}), bf16[32,5,16,128]{3,2,1,0:T(8,128)(2,1)S(1)}, u32[]{:S(2)}, u32[]{:S(2)}) async-start(bf16[32,5,16,128]{3,2,1,0:T(8,128)(2,1)} %bitcast.3), calls=%async_computation | async-start | bytes 1310720 | tf_op jit(solution)/shard_map/all_to_all | solution.py:195
  68.9 0.9 copy-start.2
  78.8 21.3 %all-to-all-start.1 = ((bf16[32,5,16,128]{3,2,1,0:T(8,128)(2,1)}), bf16[32,5,16,128]{3,2,1,0:T(8,128)(2,1)S(1)}, u32[]{:S(2)}, u32[]{:S(2)}) async-start(bf16[32,5,16,128]{3,2,1,0:T(8,128)(2,1)} %bitcast.11), calls=%async_computation.1 | async-start | bytes 1310720 | tf_op jit(solution)/shard_map/all_to_all | solution.py:195
  91.1 8.1 %collective-permute-start.1 = (f32[16,16,128]{2,1,0:T(8,128)}, f32[16,16,128]{2,1,0:T(8,128)S(1)}, u32[]{:S(2)}, u32[]{:S(2)}) collective-permute-start(f32[16,16,128]{2,1,0:T(8,128)} %get-tuple-element.23), channel_id=1, source_target_pairs={{1,0},{2,1},{3,2},{4,3},{5,4},{6,5},{7,6},{8,7},{9,8},{10,9},{11,1... | collective-permute-start | bytes 393224 | tf_op jit(solution)/shard_map/ppermute | solution.py:24
  100.1 1.2 %copy-start.1 = (f32[128,16,128]{2,1,0:T(8,128)S(1)}, f32[128,16,128]{2,1,0:T(8,128)}, u32[]{:S(2)}) copy-start(f32[128,16,128]{2,1,0:T(8,128)} %get-tuple-element.22.base_ref) | copy-start | bytes 3145732

commit v3 on v2

--- a/solution.py
+++ b/solution.py
@@ -9,6 +9,8 @@
 
 REACH = 16
 CHUNK = 16
+AHEAD = 4
+STORES = 4
 VMEM = pl.BlockSpec(memory_space=pltpu.VMEM)
 SMEM = pl.BlockSpec(memory_space=pltpu.SMEM)
 HBM = pl.BlockSpec(memory_space=pl.ANY)
@@ -19,6 +21,10 @@
     return pltpu.CompilerParams(vmem_limit_bytes=mib * 2**20)
 
 
+def in_hbm(x):
+    return pltpu.with_memory_space_constraint(x, pltpu.HBM)
+
+
 def passed_along(block, axis, distance):
     size = lax.axis_size(axis)
     return lax.ppermute(block, axis, [((i - distance) % size, i) for i in range(size)])
@@ -35,8 +41,10 @@
     return jnp.dot(chosen, earlier_matrix(blocks), preferred_element_type=jnp.float32).astype(jnp.int32)
 
 
-def pick_kernel(capacity, ids_ref, probe_ref, out_ref, picks_ref, picks_smem, sem):
+def pick_kernel(capacity, ids_ref, probe_ref, out_ref, picks_ref, probe, out, picks_smem, sems):
     groups, blocks = ids_ref.shape
+    load = pltpu.make_async_copy(probe_ref, probe, sems.at[0])
+    load.start()
     me = lax.axis_index("blk")
     local = ids_ref[...] - me * blocks
     mask = (local >= 0) & (local < blocks)
@@ -47,14 +55,26 @@
         found = jnp.sum(jnp.where(mask & (rank == r), local + 1, 0), axis=1, keepdims=True)
         picks = jnp.where(lane == r, found, picks)
     picks_ref[...] = picks
-    copy = pltpu.make_async_copy(picks_ref, picks_smem, sem)
+    copy = pltpu.make_async_copy(picks_ref, picks_smem, sems.at[1])
     copy.start()
     copy.wait()
-
-    @pl.loop(0, groups, unroll=8)
-    def _(g):
-        for r in range(capacity):
-            out_ref[g * capacity + r] = probe_ref[jnp.maximum(picks_smem[g, r] - 1, 0)]
+    load.wait()
+    part = groups // STORES
+
+    def store(p):
+        rows = pl.ds(p * part * capacity, part * capacity)
+        return pltpu.make_async_copy(out.at[rows], out_ref.at[rows], sems.at[2 + p])
+
+    for p in range(STORES):
+
+        @pl.loop(p * part, (p + 1) * part, unroll=8)
+        def _(g):
+            for r in range(capacity):
+                out[g * capacity + r] = probe[jnp.maximum(picks_smem[g, r] - 1, 0)]
+
+        store(p).start()
+    for p in range(STORES):
+        store(p).wait()
 
 
 def near_place(ids_ref, k, i, first, count):
@@ -93,7 +113,7 @@
             out_ref[i] = probe_ref[i].astype(jnp.float32) - mixed
 
 
-def far_kernel(slot_ref, part_ref, far_ref, coeffs_ref, prec_ref, scaled_ref, parcel_ref, coeffs, prec, sems):
+def far_kernel(slot_ref, part_ref, far_ref, coeffs_ref, prec_ref, scaled_ref, parcel_ref, coeffs, prec, white, sems):
     blocks = part_ref.shape[0]
     chunks = blocks // CHUNK
 
@@ -109,24 +129,43 @@
             load.start()
     parcel_ref[...] = jnp.zeros_like(parcel_ref)
 
-    @pl.loop(0, chunks)
-    def _(c):
-        for load in loads(c):
-            load.wait()
-        white = []
+    def mix(c):
         for b in range(CHUNK):
             i = c * CHUNK + b
             mixed = jnp.dot(far_ref[slot_ref[0, i]], coeffs[i], preferred_element_type=jnp.float32)
-            white.append((part_ref[i] - mixed).astype(jnp.bfloat16))
-        scaled = []
+            white[i] = (part_ref[i] - mixed).astype(jnp.bfloat16)
+
+    def scale(c):
         for b in range(CHUNK):
             i = c * CHUNK + b
-            scaled.append(jnp.dot(white[b], prec[i], preferred_element_type=jnp.float32).astype(jnp.bfloat16))
-            scaled_ref[i] = scaled[b]
+            scaled_ref[i] = jnp.dot(white[i], prec[i], preferred_element_type=jnp.float32).astype(jnp.bfloat16)
+
+    def back(c):
         for b in range(CHUNK):
             i = c * CHUNK + b
-            term = lax.dot_general(scaled[b], coeffs[i], NT, preferred_element_type=jnp.float32)
+            term = lax.dot_general(scaled_ref[i], coeffs[i], NT, preferred_element_type=jnp.float32)
             parcel_ref[slot_ref[0, i]] = term.astype(jnp.bfloat16)
+
+    def ready(c):
+        for load in loads(c):
+            load.wait()
+
+    ready(0)
+    mix(0)
+    ready(1)
+    scale(0)
+    mix(1)
+
+    @pl.loop(2, chunks)
+    def _(c):
+        ready(c)
+        back(c - 2)
+        scale(c - 1)
+        mix(c)
+
+    back(chunks - 2)
+    scale(chunks - 1)
+    back(chunks - 1)
 
 
 def near_back_kernel(groups, ids_ref, scaled_ref, coeffs_ref, base_ref, halo_ref, total, coeffs, sems):
@@ -148,27 +187,28 @@
     def _(c):
         load(c).wait()
         terms = []
-        for b in range(CHUNK):
-            i = c * CHUNK + b
-            mat = coeffs[i].reshape(3 * coeffs.shape[2], coeffs.shape[3])
-            terms.append(lax.dot_general(scaled_ref[i], mat, NT, preferred_element_type=jnp.float32))
-        for b in range(CHUNK):
-            i = c * CHUNK + b
-            places = [near_place(ids_ref, k, i, first, groups * blocks) for k in range(3)]
-            olds = [total[place] for place in places]
-            for k in range(3):
-                total[places[k]] = olds[k] - terms[b][:, k * points : (k + 1) * points]
-
-    halo_ref[...] = total[pl.ds(0, REACH)]
+        for b in range(CHUNK + AHEAD):
+            if b < CHUNK:
+                i = c * CHUNK + b
+                mat = coeffs[i].reshape(3 * coeffs.shape[2], coeffs.shape[3])
+                terms.append(lax.dot_general(scaled_ref[i], mat, NT, preferred_element_type=jnp.float32))
+            if b >= AHEAD:
+                i = c * CHUNK + b - AHEAD
+                places = [near_place(ids_ref, k, i, first, groups * blocks) for k in range(3)]
+                olds = [total[place] for place in places]
+                for k in range(3):
+                    total[places[k]] = olds[k] - terms[b - AHEAD][:, k * points : (k + 1) * points]
+
+    halo_ref[...] = total[pl.ds(0, REACH)].astype(halo_ref.dtype)
     base_ref[...] = total[pl.ds(REACH, blocks)]
 
 
-def sum_kernel(capacity, picks_ref, base_ref, halo_ref, back_ref, out_ref, total):
+def sum_kernel(capacity, picks_ref, base_ref, halo_ref, back_ref, out_ref, total, sem):
     groups = picks_ref.shape[0]
     blocks = base_ref.shape[0]
     total[pl.ds(0, blocks)] = base_ref[...]
     last = pl.ds(blocks - REACH, REACH)
-    total[last] = total[last] + halo_ref[...]
+    total[last] = total[last] + halo_ref[...].astype(jnp.float32)
 
     @pl.loop(0, groups, unroll=8)
     def _(g):
@@ -178,7 +218,9 @@
         for r in range(capacity):
             total[places[r]] = olds[r] - back_ref[g * capacity + r].astype(jnp.float32)
 
-    out_ref[...] = total[pl.ds(0, blocks)]
+    store = pltpu.make_async_copy(total.at[pl.ds(0, blocks)], out_ref, sem)
+    store.start()
+    store.wait()
 
 
 def per_device(probe_vecs, coeffs, cond_prec, neighbours):
@@ -197,7 +239,7 @@
     ids = neighbours.T
     far_ids = ids[3:]
     halo = passed_along(probe_vecs[blocks - REACH :], "blk", 1)
-    all_ids = lax.all_gather(far_ids, "blk", axis=0, tiled=True)
+    all_ids = exchange(jnp.broadcast_to(far_ids, (groups, blocks)))
     all_ids, halo = lax.optimization_barrier((all_ids, halo))
     outgoing, picks = pl.pallas_call(
         functools.partial(pick_kernel, capacity),
@@ -206,12 +248,17 @@
             jax.ShapeDtypeStruct((slots,) + tile, bf16),
             jax.ShapeDtypeStruct((groups, blocks), jnp.int32),
         ),
-        in_specs=[VMEM, VMEM],
-        out_specs=(VMEM, VMEM),
-        scratch_shapes=[pltpu.SMEM((groups, blocks), jnp.int32), pltpu.SemaphoreType.DMA],
+        in_specs=[VMEM, HBM],
+        out_specs=(HBM, VMEM),
+        scratch_shapes=[
+            pltpu.VMEM((blocks,) + tile, bf16),
+            pltpu.VMEM((slots,) + tile, bf16),
+            pltpu.SMEM((groups, blocks), jnp.int32),
+            pltpu.SemaphoreType.DMA((2 + STORES,)),
+        ],
         compiler_params=params(8),
         cost_estimate=pl.CostEstimate(flops=0, bytes_accessed=2 * slots * 4096, transcendentals=0),
-    )(all_ids, probe_vecs)
+    )(all_ids, in_hbm(probe_vecs))
     arrived = exchange(outgoing.reshape((groups, capacity) + tile)).reshape((slots,) + tile)
     part, slot_of = pl.pallas_call(
         functools.partial(near_forward_kernel, groups, capacity),
@@ -227,9 +274,9 @@
             pltpu.VMEM((blocks, 3, points, points), bf16),
             pltpu.SemaphoreType.DMA((chunks,)),
         ],
-        compiler_params=params(60),
+        compiler_params=params(24),
         cost_estimate=pl.CostEstimate(flops=3 * flops, bytes_accessed=14 * 2**20, transcendentals=0),
-    )(ids, far_ids, halo, probe_vecs, coeffs)
+    )(ids, far_ids, halo, probe_vecs, in_hbm(coeffs))
     scaled, parcel = pl.pallas_call(
         far_kernel,
         name="far_and_scale",
@@ -242,18 +289,19 @@
         scratch_shapes=[
             pltpu.VMEM((blocks, points, points), bf16),
             pltpu.VMEM((blocks, points, points), bf16),
+            pltpu.VMEM((blocks,) + tile, bf16),
             pltpu.SemaphoreType.DMA((2, chunks)),
         ],
-        compiler_params=params(60),
+        compiler_params=params(24),
         cost_estimate=pl.CostEstimate(flops=3 * flops, bytes_accessed=11 * 2**20, transcendentals=0),
-    )(slot_of, part, arrived, coeffs, cond_prec)
+    )(slot_of, part, arrived, in_hbm(coeffs), in_hbm(cond_prec))
     returned = exchange(parcel.reshape((groups, capacity) + tile)).reshape((slots,) + tile)
     base, halo_back = pl.pallas_call(
         functools.partial(near_back_kernel, groups),
         name="near_back",
         out_shape=(
             jax.ShapeDtypeStruct((blocks,) + tile, f32),
-            jax.ShapeDtypeStruct((REACH,) + tile, f32),
+            jax.ShapeDtypeStruct((REACH,) + tile, bf16),
         ),
         in_specs=[SMEM, VMEM, HBM],
         out_specs=(VMEM, VMEM),
@@ -262,17 +310,17 @@
             pltpu.VMEM((blocks, 3, points, points), bf16),
             pltpu.SemaphoreType.DMA((chunks,)),
         ],
-        compiler_params=params(60),
+        compiler_params=params(24),
         cost_estimate=pl.CostEstimate(flops=3 * flops, bytes_accessed=14 * 2**20, transcendentals=0),
-    )(ids, scaled, coeffs)
+    )(ids, scaled, in_hbm(coeffs))
     halo_sum = passed_along(halo_back, "blk", -1)
     return pl.pallas_call(
         functools.partial(sum_kernel, capacity),
         name="final_sum",
         out_shape=jax.ShapeDtypeStruct((blocks,) + tile, f32),
         in_specs=[SMEM, VMEM, VMEM, VMEM],
-        out_specs=VMEM,
-        scratch_shapes=[pltpu.VMEM((blocks + 1,) + tile, f32)],
+        out_specs=HBM,
+        scratch_shapes=[pltpu.VMEM((blocks + 1,) + tile, f32), pltpu.SemaphoreType.DMA],
         compiler_params=params(8),
         cost_estimate=pl.CostEstimate(flops=0, bytes_accessed=3 * 2**20, transcendentals=0),
     )(picks, base, halo_sum, returned)

time: 104 us -> 70.8 us (0.68)
  blocking collectives: 42.6 us -> 14.1 us
  Pallas kernels: 29.5 us -> 25.5 us
  local copies, waits for them, and re-layouts: 5.21 us -> 3.26 us
  waiting for transfers between devices: 14.4 us -> 15.6 us
    all_gather x1 -> x0, blocking collectives: 42.6 us -> none  [per_device(): all_ids = lax.all_gather(far_ids, 'blk', axis=0, tiled=True)]
    all_to_all x0 -> x1, blocking collectives: none -> 14.1 us  [exchange(): return lax.all_to_all(x, 'blk', split_axis=0, concat_axis=0, tiled=True)]
    all_to_all x2, waiting for transfers between devices: 11.6 us -> 13.7 us  [exchange(): return lax.all_to_all(x, 'blk', split_axis=0, concat_axis=0, tiled=True)]
    pallas_call x1, Pallas kernels: 8.93 us -> 7.46 us  [per_device(): pl.pallas_call(functools.partial(near_back_kernel, groups), name='near_ba...]
    pallas_call x1, Pallas kernels: 7.16 us -> 5.7 us  [per_device(): pl.pallas_call(functools.partial(near_forward_kernel, groups, capacity),...]
    unnamed x8 -> x6, local copies, waits for them, and re-layouts: 3.15 us -> 1.72 us
  transfers between devices with their start and end apart: 4 -> 4, of which waited for: 3 -> 3; matrix products, arithmetic and copies ran while one was open for 1% -> 1% of each run, Pallas kernels for 16% -> 19%
where the time goes in v3:
time: 70.8 us; the launch traced here: 70.4 us
  Pallas kernels  25.5 us (36%)
  waiting for transfers between devices  15.6 us (22%)
  blocking collectives  14.1 us (20%)
  starting transfers between devices  11.8 us (17%)
  local copies, waits for them, and re-layouts  3.26 us (5%)
    all_to_all x1, blocking collectives, exchange(): return lax.all_to_all(x, 'blk', split_axis=0, concat_axis=0, tiled=True)  14.1 us
    all_to_all x2, waiting for transfers between devices, exchange(): return lax.all_to_all(x, 'blk', split_axis=0, concat_axis=0, tiled=True)  13.7 us
    pallas_call x1, Pallas kernels, per_device(): pl.pallas_call(far_kernel, name='far_and_scale', out_shape=(jax.ShapeDtyp...  8.17 us
    pallas_call x1, Pallas kernels, per_device(): pl.pallas_call(functools.partial(near_back_kernel, groups), name='near_ba...  7.46 us
    all_to_all x2, starting transfers between devices, exchange(): return lax.all_to_all(x, 'blk', split_axis=0, concat_axis=0, tiled=True)  6.05 us
    ppermute x2, starting transfers between devices, passed_along(): lax.ppermute(block, axis, [((i - distance) % size, i) for i in range(size)])  5.73 us
    pallas_call x1, Pallas kernels, per_device(): pl.pallas_call(functools.partial(near_forward_kernel, groups, capacity),...  5.7 us
    pallas_call x1, Pallas kernels, per_device(): pl.pallas_call(functools.partial(sum_kernel, capacity), name='final_sum',...  2.16 us
  transfers between devices with their start and end apart: 4, of which 3 were waited for; matrix products, arithmetic and copies ran while one was open for 1% of the time, Pallas kernels for 19%

profile of v3, /device:TPU:0, one launch (start us, length us, event | category | flops | bytes accessed | tf_op | source)
XLA Modules:
  0.0 70.4 jit_solution(4977770906771366837)
XLA Ops:
  0.0 0.8 %slice.10 = bf16[16,16,128]{2,1,0:T(8,128)(2,1)S(1)} slice(bf16[128,16,128]{2,1,0:T(8,128)(2,1)} %probe_ref.3), slice={[112:128], [0:16], [0:128]} | slice | bytes 131072 | tf_op jit(solution)/shard_map/slice | solution.py:241
  0.8 0.5 collective-permute-start
  1.3 0.7 fusion
  2.0 14.1 %all_to_all.19 = s32[32,1,128]{2,1,0:T(1,128)S(1)} all-to-all(s32[32,1,128]{2,1,0:T(1,128)S(1)} %broadcast_in_dim.2), channel_id=1, replica_groups=mesh['blk'=32] {'blk'}, dimensions={0} | all-to-all | bytes 32768 | tf_op jit(solution)/shard_map/all_to_all | solution.py:237
  16.1 0.0 collective-permute-done.halo_ref
  16.1 2.0 %pick_tiles.1 = (bf16[160,16,128]{2,1,0:T(8,128)(2,1)}, s32[32,128]{1,0:T(8,128)S(1)}) custom-call(s32[32,128]{1,0:T(8,128)S(1)} %bitcast.10, bf16[128,16,128]{2,1,0:T(8,128)(2,1)} %probe_ref.3), custom_call_target="tpu_custom_call" | custom-call | bytes 1310720 | tf_op jit(solution)/shard_map/pick_tiles/pallas_call | solution.py:244
  18.1 2.6 %all-to-all-start.1 = ((bf16[32,5,16,128]{3,2,1,0:T(8,128)(2,1)}), bf16[32,5,16,128]{3,2,1,0:T(8,128)(2,1)S(1)}, u32[]{:S(2)}, u32[]{:S(2)}) async-start(bf16[32,5,16,128]{3,2,1,0:T(8,128)(2,1)} %bitcast.3), calls=%async_computation.1 | async-start | bytes 1310720 | tf_op jit(solution)/shard_map/all_to_all | solution.py:237
  20.8 0.0 copy-start
  20.8 1.0 %copy-done = bf16[128,16,128]{2,1,0:T(8,128)(2,1)S(1)} copy-done((bf16[128,16,128]{2,1,0:T(8,128)(2,1)S(1)}, bf16[128,16,128]{2,1,0:T(8,128)(2,1)}, u32[]{:S(2)}) %copy-start) | copy-done | bytes 524312
  21.8 0.0 copy-start.1
  21.8 0.7 copy-done.1
  22.5 0.0 copy-start.2
  22.5 5.7 %near_forward.1 = (f32[128,16,128]{2,1,0:T(8,128)S(1)}, s32[1,128]{1,0:T(1,128)S(1)}) custom-call(s32[4,128]{1,0:T(4,128)S(1)} %bitcast.12, s32[1,128]{1,0:T(1,128)S(1)} %get-tuple-element.25.far_ref, bf16[16,16,128]{2,1,0:T(8,128)(2,1)S(1)} %collective-permute-done.halo_ref, bf16[128,16,128]{2,1,0:T(8,128)(2,1)S(1)} %copy-done, ...), custom_call_target="tpu_custom_call" | custom-call | flops 201326592 | bytes 14680064 | tf_op jit(solution)/shard_map/near_forward/pallas_call | solution.py:263
  28.2 10.5 %all-to-all-done.1 = bf16[32,5,16,128]{3,2,1,0:T(8,128)(2,1)S(1)} async-done(((bf16[32,5,16,128]{3,2,1,0:T(8,128)(2,1)}), bf16[32,5,16,128]{3,2,1,0:T(8,128)(2,1)S(1)}, u32[]{:S(2)}, u32[]{:S(2)}) %all-to-all-start.1) | async-done | bytes 655392 | tf_op jit(solution)/shard_map/all_to_all | solution.py:237
  38.7 8.2 %far_and_scale.1 = (bf16[128,16,128]{2,1,0:T(8,128)(2,1)S(1)}, bf16[160,16,128]{2,1,0:T(8,128)(2,1)}) custom-call(s32[1,128]{1,0:T(1,128)S(1)} %get-tuple-element.18.slot_ref, f32[128,16,128]{2,1,0:T(8,128)S(1)} %get-tuple-element.19.part_ref, bf16[160,16,128]{2,1,0:T(8,128)(2,1)S(1)} %bitcast.8, bf16[128,4,128,128]{3,2,1,0:T(8,128)(2,1)} %coeffs_ref.5, ...), custom_call_target="tpu_custom_call" | custom-call | flops 201326592 | bytes 11534336 | tf_op jit(solution)/shard_map/far_and_scale/pallas_call | solution.py:280
  46.9 3.4 %all-to-all-start.2 = ((bf16[32,5,16,128]{3,2,1,0:T(8,128)(2,1)}), bf16[32,5,16,128]{3,2,1,0:T(8,128)(2,1)S(1)}, u32[]{:S(2)}, u32[]{:S(2)}) async-start(bf16[32,5,16,128]{3,2,1,0:T(8,128)(2,1)} %bitcast.5), calls=%async_computation.2 | async-start | bytes 1310720 | tf_op jit(solution)/shard_map/all_to_all | solution.py:237
  50.3 0.0 copy-done.2
  50.3 7.5 %near_back.1 = (f32[128,16,128]{2,1,0:T(8,128)S(1)}, bf16[16,16,128]{2,1,0:T(8,128)(2,1)S(1)}) custom-call(s32[4,128]{1,0:T(4,128)S(1)} %bitcast.13, bf16[128,16,128]{2,1,0:T(8,128)(2,1)S(1)} %get-tuple-element.21.scaled_ref, bf16[128,4,128,128]{3,2,1,0:T(8,128)(2,1)} %coeffs_ref.5), custom_call_target="tpu_custom_call" | custom-call | flops 201326592 | bytes 14680064 | tf_op jit(solution)/shard_map/near_back/pallas_call | solution.py:299
  57.8 5.3 %collective-permute-start.1 = (bf16[16,16,128]{2,1,0:T(8,128)(2,1)S(1)}, bf16[16,16,128]{2,1,0:T(8,128)(2,1)S(1)}, u32[]{:S(2)}, u32[]{:S(2)}) collective-permute-start(bf16[16,16,128]{2,1,0:T(8,128)(2,1)S(1)} %get-tuple-element.23), channel_id=1, source_target_pairs={{1,0},{2,1},{3,2},{4,3},{5,4},{6,5},{7,6},{8,7},{9,8},{10,9},{11,1... | collective-permute-start | bytes 196616 | tf_op jit(solution)/shard_map/ppermute | solution.py:30
  63.1 1.9 %collective-permute-done.1.halo_ref = bf16[16,16,128]{2,1,0:T(8,128)(2,1)S(1)} collective-permute-done((bf16[16,16,128]{2,1,0:T(8,128)(2,1)S(1)}, bf16[16,16,128]{2,1,0:T(8,128)(2,1)S(1)}, u32[]{:S(2)}, u32[]{:S(2)}) %collective-permute-start.1) | collective-permute-done | bytes 65568 | tf_op jit(solution)/shard_map/ppermute | solution.py:30
  65.0 3.2 %all-to-all-done.2 = bf16[32,5,16,128]{3,2,1,0:T(8,128)(2,1)S(1)} async-done(((bf16[32,5,16,128]{3,2,1,0:T(8,128)(2,1)}), bf16[32,5,16,128]{3,2,1,0:T(8,128)(2,1)S(1)}, u32[]{:S(2)}, u32[]{:S(2)}) %all-to-all-start.2) | async-done | bytes 655392 | tf_op jit(solution)/shard_map/all_to_all | solution.py:237
  68.2 2.2 %final_sum.1 = f32[128,16,128]{2,1,0:T(8,128)} custom-call(s32[32,128]{1,0:T(8,128)S(1)} %get-tuple-element.16.picks_ref, f32[128,16,128]{2,1,0:T(8,128)S(1)} %get-tuple-element.22.base_ref, bf16[16,16,128]{2,1,0:T(8,128)(2,1)S(1)} %collective-permute-done.1.halo_ref, bf16[160,16,128]{2,1,0:T(8,128)(2,1)S(1)} %bitcast.9), custom_call_target="tpu_custom_call" | custom-call | bytes 3145728 | tf_op jit(solution)/shard_map/final_sum/pallas_call | solution.py:317
  (1 shorter events, 0.0 us)
Async XLA Ops:
  0.8 15.2 %collective-permute-start = (bf16[16,16,128]{2,1,0:T(8,128)(2,1)S(1)}, bf16[16,16,128]{2,1,0:T(8,128)(2,1)S(1)}, u32[]{:S(2)}, u32[]{:S(2)}) collective-permute-start(bf16[16,16,128]{2,1,0:T(8,128)(2,1)S(1)} %slice.10), channel_id=1, source_target_pairs={{31,0},{0,1},{1,2},{2,3},{3,4},{4,5},{5,6},{6,7},{7,8},{8,9},{9,10... | collective-permute-start | bytes 196616 | tf_op jit(solution)/shard_map/ppermute | solution.py:30
  18.1 20.6 %all-to-all-start.1 = ((bf16[32,5,16,128]{3,2,1,0:T(8,128)(2,1)}), bf16[32,5,16,128]{3,2,1,0:T(8,128)(2,1)S(1)}, u32[]{:S(2)}, u32[]{:S(2)}) async-start(bf16[32,5,16,128]{3,2,1,0:T(8,128)(2,1)} %bitcast.3), calls=%async_computation.1 | async-start | bytes 1310720 | tf_op jit(solution)/shard_map/all_to_all | solution.py:237
  20.8 1.0 %copy-start = (bf16[128,16,128]{2,1,0:T(8,128)(2,1)S(1)}, bf16[128,16,128]{2,1,0:T(8,128)(2,1)}, u32[]{:S(2)}) copy-start(bf16[128,16,128]{2,1,0:T(8,128)(2,1)} %probe_ref.3) | copy-start | bytes 1572868
  21.8 0.7 copy-start.1
  22.5 27.8 %copy-start.2 = (s32[128,4]{0,1:T(4,128)S(1)}, s32[128,4]{0,1:T(4,128)}, u32[]{:S(2)}) copy-start(s32[128,4]{0,1:T(4,128)} %param.7) | copy-start | bytes 6148
  46.9 21.3 %all-to-all-start.2 = ((bf16[32,5,16,128]{3,2,1,0:T(8,128)(2,1)}), bf16[32,5,16,128]{3,2,1,0:T(8,128)(2,1)S(1)}, u32[]{:S(2)}, u32[]{:S(2)}) async-start(bf16[32,5,16,128]{3,2,1,0:T(8,128)(2,1)} %bitcast.5), calls=%async_computation.2 | async-start | bytes 1310720 | tf_op jit(solution)/shard_map/all_to_all | solution.py:237
  57.8 7.2 %collective-permute-start.1 = (bf16[16,16,128]{2,1,0:T(8,128)(2,1)S(1)}, bf16[16,16,128]{2,1,0:T(8,128)(2,1)S(1)}, u32[]{:S(2)}, u32[]{:S(2)}) collective-permute-start(bf16[16,16,128]{2,1,0:T(8,128)(2,1)S(1)} %get-tuple-element.23), channel_id=1, source_target_pairs={{1,0},{2,1},{3,2},{4,3},{5,4},{6,5},{7,6},{8,7},{9,8},{10,9},{11,1... | collective-permute-start | bytes 196616 | tf_op jit(solution)/shard_map/ppermute | solution.py:30

commit v4 on v3

--- a/solution.py
+++ b/solution.py
@@ -77,6 +77,25 @@
         store(p).wait()
 
 
+def stacked(mats):
+    return mats.reshape(-1, mats.shape[-1])
+
+
+def apart(left0, left1, mats):
+    zero = jnp.zeros_like(left0)
+    left = jnp.concatenate(
+        [jnp.concatenate([left0, zero], axis=1), jnp.concatenate([zero, left1], axis=1)], axis=0
+    )
+    out = jnp.dot(left, mats, preferred_element_type=jnp.float32)
+    return out.reshape((2,) + (left0.shape[0], mats.shape[1]))
+
+
+def apart_back(lefts, mats):
+    rows, half = lefts.shape[1], mats.shape[0] // 2
+    out = lax.dot_general(lefts.reshape(2 * rows, lefts.shape[2]), mats, NT, preferred_element_type=jnp.float32)
+    return out[:rows, :half], out[rows:, half:]
+
+
 def near_place(ids_ref, k, i, first, count):
     place = ids_ref[k, i] - first + REACH
     return jnp.where(place >= count, place - count, place)
@@ -105,12 +124,14 @@
     @pl.loop(0, chunks)
     def _(c):
         load(c).wait()
-        for b in range(CHUNK):
+        for b in range(0, CHUNK, 2):
             i = c * CHUNK + b
-            tiles = [ext[near_place(ids_ref, k, i, first, groups * blocks)] for k in range(3)]
-            mat = coeffs[i].reshape(3 * coeffs.shape[2], coeffs.shape[3])
-            mixed = jnp.dot(jnp.concatenate(tiles, axis=1), mat, preferred_element_type=jnp.float32)
-            out_ref[i] = probe_ref[i].astype(jnp.float32) - mixed
+            rows = []
+            for j in range(2):
+                tiles = [ext[near_place(ids_ref, k, i + j, first, groups * blocks)] for k in range(3)]
+                rows.append(jnp.concatenate(tiles, axis=1))
+            mixed = apart(rows[0], rows[1], stacked(coeffs[pl.ds(i, 2)]))
+            out_ref[pl.ds(i, 2)] = probe_ref[pl.ds(i, 2)].astype(jnp.float32) - mixed
 
 
 def far_kernel(slot_ref, part_ref, far_ref, coeffs_ref, prec_ref, scaled_ref, parcel_ref, coeffs, prec, white, sems):
@@ -130,21 +151,22 @@
     parcel_ref[...] = jnp.zeros_like(parcel_ref)
 
     def mix(c):
-        for b in range(CHUNK):
+        for b in range(0, CHUNK, 2):
             i = c * CHUNK + b
-            mixed = jnp.dot(far_ref[slot_ref[0, i]], coeffs[i], preferred_element_type=jnp.float32)
-            white[i] = (part_ref[i] - mixed).astype(jnp.bfloat16)
+            mixed = apart(far_ref[slot_ref[0, i]], far_ref[slot_ref[0, i + 1]], stacked(coeffs[pl.ds(i, 2)]))
+            white[pl.ds(i, 2)] = (part_ref[pl.ds(i, 2)] - mixed).astype(jnp.bfloat16)
 
     def scale(c):
-        for b in range(CHUNK):
+        for b in range(0, CHUNK, 2):
             i = c * CHUNK + b
-            scaled_ref[i] = jnp.dot(white[i], prec[i], preferred_element_type=jnp.float32).astype(jnp.bfloat16)
+            scaled_ref[pl.ds(i, 2)] = apart(white[i], white[i + 1], stacked(prec[pl.ds(i, 2)])).astype(jnp.bfloat16)
 
     def back(c):
-        for b in range(CHUNK):
+        for b in range(0, CHUNK, 2):
             i = c * CHUNK + b
-            term = lax.dot_general(scaled_ref[i], coeffs[i], NT, preferred_element_type=jnp.float32)
-            parcel_ref[slot_ref[0, i]] = term.astype(jnp.bfloat16)
+            terms = apart_back(scaled_ref[pl.ds(i, 2)], stacked(coeffs[pl.ds(i, 2)]))
+            for j in range(2):
+                parcel_ref[slot_ref[0, i + j]] = terms[j].astype(jnp.bfloat16)
 
     def ready(c):
         for load in loads(c):
@@ -188,10 +210,9 @@
         load(c).wait()
         terms = []
         for b in range(CHUNK + AHEAD):
-            if b < CHUNK:
+            if b < CHUNK and b % 2 == 0:
                 i = c * CHUNK + b
-                mat = coeffs[i].reshape(3 * coeffs.shape[2], coeffs.shape[3])
-                terms.append(lax.dot_general(scaled_ref[i], mat, NT, preferred_element_type=jnp.float32))
+                terms.extend(apart_back(scaled_ref[pl.ds(i, 2)], stacked(coeffs[pl.ds(i, 2)])))
             if b >= AHEAD:
                 i = c * CHUNK + b - AHEAD
                 places = [near_place(ids_ref, k, i, first, groups * blocks) for k in range(3)]

time: 70.8 us -> 69.2 us (0.977)
  Pallas kernels: 25.5 us -> 23.7 us
    pallas_call x1, Pallas kernels: 8.17 us -> 6.52 us  [per_device(): pl.pallas_call(far_kernel, name='far_and_scale', out_shape=(jax.ShapeDtyp...]
where the time goes in v4:
time: 69.2 us; the launch traced here: 68.7 us
  Pallas kernels  23.7 us (34%)
  waiting for transfers between devices  15.8 us (23%)
  blocking collectives  14.1 us (20%)
  starting transfers between devices  11.8 us (17%)
  local copies, waits for them, and re-layouts  3.26 us (5%)
    all_to_all x1, blocking collectives, exchange(): return lax.all_to_all(x, 'blk', split_axis=0, concat_axis=0, tiled=True)  14.1 us
    all_to_all x2, waiting for transfers between devices, exchange(): return lax.all_to_all(x, 'blk', split_axis=0, concat_axis=0, tiled=True)  13.9 us
    pallas_call x1, Pallas kernels, per_device(): pl.pallas_call(functools.partial(near_back_kernel, groups), name='near_ba...  7.31 us
    pallas_call x1, Pallas kernels, per_device(): pl.pallas_call(far_kernel, name='far_and_scale', out_shape=(jax.ShapeDtyp...  6.52 us
    all_to_all x2, starting transfers between devices, exchange(): return lax.all_to_all(x, 'blk', split_axis=0, concat_axis=0, tiled=True)  6.05 us
    ppermute x2, starting transfers between devices, passed_along(): lax.ppermute(block, axis, [((i - distance) % size, i) for i in range(size)])  5.72 us
    pallas_call x1, Pallas kernels, per_device(): pl.pallas_call(functools.partial(near_forward_kernel, groups, capacity),...  5.67 us
    pallas_call x1, Pallas kernels, per_device(): pl.pallas_call(functools.partial(sum_kernel, capacity), name='final_sum',...  2.16 us
  transfers between devices with their start and end apart: 4, of which 3 were waited for; matrix products, arithmetic and copies ran while one was open for 1% of the time, Pallas kernels for 19%

profile of v4, /device:TPU:0, one launch (start us, length us, event | category | flops | bytes accessed | tf_op | source)
XLA Modules:
  0.0 68.7 jit_solution(15456183388271635146)
XLA Ops:
  0.0 0.8 %slice.10 = bf16[16,16,128]{2,1,0:T(8,128)(2,1)S(1)} slice(bf16[128,16,128]{2,1,0:T(8,128)(2,1)} %probe_ref.3), slice={[112:128], [0:16], [0:128]} | slice | bytes 131072 | tf_op jit(solution)/shard_map/slice | solution.py:262
  0.8 0.5 collective-permute-start
  1.3 0.7 fusion
  2.0 14.1 %all_to_all.19 = s32[32,1,128]{2,1,0:T(1,128)S(1)} all-to-all(s32[32,1,128]{2,1,0:T(1,128)S(1)} %broadcast_in_dim.2), channel_id=1, replica_groups=mesh['blk'=32] {'blk'}, dimensions={0} | all-to-all | bytes 32768 | tf_op jit(solution)/shard_map/all_to_all | solution.py:258
  16.1 0.0 collective-permute-done.halo_ref
  16.1 2.0 %pick_tiles.1 = (bf16[160,16,128]{2,1,0:T(8,128)(2,1)}, s32[32,128]{1,0:T(8,128)S(1)}) custom-call(s32[32,128]{1,0:T(8,128)S(1)} %bitcast.10, bf16[128,16,128]{2,1,0:T(8,128)(2,1)} %probe_ref.3), custom_call_target="tpu_custom_call" | custom-call | bytes 1310720 | tf_op jit(solution)/shard_map/pick_tiles/pallas_call | solution.py:265
  18.1 2.6 %all-to-all-start.1 = ((bf16[32,5,16,128]{3,2,1,0:T(8,128)(2,1)}), bf16[32,5,16,128]{3,2,1,0:T(8,128)(2,1)S(1)}, u32[]{:S(2)}, u32[]{:S(2)}) async-start(bf16[32,5,16,128]{3,2,1,0:T(8,128)(2,1)} %bitcast.3), calls=%async_computation.1 | async-start | bytes 1310720 | tf_op jit(solution)/shard_map/all_to_all | solution.py:258
  20.8 0.0 copy-start
  20.8 1.0 %copy-done = bf16[128,16,128]{2,1,0:T(8,128)(2,1)S(1)} copy-done((bf16[128,16,128]{2,1,0:T(8,128)(2,1)S(1)}, bf16[128,16,128]{2,1,0:T(8,128)(2,1)}, u32[]{:S(2)}) %copy-start) | copy-done | bytes 524312
  21.8 0.0 copy-start.1
  21.8 0.7 copy-done.1
  22.5 0.0 copy-start.2
  22.5 5.7 %near_forward.1 = (f32[128,16,128]{2,1,0:T(8,128)S(1)}, s32[1,128]{1,0:T(1,128)S(1)}) custom-call(s32[4,128]{1,0:T(4,128)S(1)} %bitcast.12, s32[1,128]{1,0:T(1,128)S(1)} %get-tuple-element.25.far_ref, bf16[16,16,128]{2,1,0:T(8,128)(2,1)S(1)} %collective-permute-done.halo_ref, bf16[128,16,128]{2,1,0:T(8,128)(2,1)S(1)} %copy-done, ...), custom_call_target="tpu_custom_call" | custom-call | flops 201326592 | bytes 14680064 | tf_op jit(solution)/shard_map/near_forward/pallas_call | solution.py:284
  28.2 10.5 %all-to-all-done.1 = bf16[32,5,16,128]{3,2,1,0:T(8,128)(2,1)S(1)} async-done(((bf16[32,5,16,128]{3,2,1,0:T(8,128)(2,1)}), bf16[32,5,16,128]{3,2,1,0:T(8,128)(2,1)S(1)}, u32[]{:S(2)}, u32[]{:S(2)}) %all-to-all-start.1) | async-done | bytes 655392 | tf_op jit(solution)/shard_map/all_to_all | solution.py:258
  38.7 6.5 %far_and_scale.1 = (bf16[128,16,128]{2,1,0:T(8,128)(2,1)S(1)}, bf16[160,16,128]{2,1,0:T(8,128)(2,1)}) custom-call(s32[1,128]{1,0:T(1,128)S(1)} %get-tuple-element.18.slot_ref, f32[128,16,128]{2,1,0:T(8,128)S(1)} %get-tuple-element.19.part_ref, bf16[160,16,128]{2,1,0:T(8,128)(2,1)S(1)} %bitcast.8, bf16[128,4,128,128]{3,2,1,0:T(8,128)(2,1)} %coeffs_ref.5, ...), custom_call_target="tpu_custom_call" | custom-call | flops 201326592 | bytes 11534336 | tf_op jit(solution)/shard_map/far_and_scale/pallas_call | solution.py:301
  45.2 3.4 %all-to-all-start.2 = ((bf16[32,5,16,128]{3,2,1,0:T(8,128)(2,1)}), bf16[32,5,16,128]{3,2,1,0:T(8,128)(2,1)S(1)}, u32[]{:S(2)}, u32[]{:S(2)}) async-start(bf16[32,5,16,128]{3,2,1,0:T(8,128)(2,1)} %bitcast.5), calls=%async_computation.2 | async-start | bytes 1310720 | tf_op jit(solution)/shard_map/all_to_all | solution.py:258
  48.6 0.0 copy-done.2
  48.7 7.3 %near_back.1 = (f32[128,16,128]{2,1,0:T(8,128)S(1)}, bf16[16,16,128]{2,1,0:T(8,128)(2,1)S(1)}) custom-call(s32[4,128]{1,0:T(4,128)S(1)} %bitcast.13, bf16[128,16,128]{2,1,0:T(8,128)(2,1)S(1)} %get-tuple-element.21.scaled_ref, bf16[128,4,128,128]{3,2,1,0:T(8,128)(2,1)} %coeffs_ref.5), custom_call_target="tpu_custom_call" | custom-call | flops 201326592 | bytes 14680064 | tf_op jit(solution)/shard_map/near_back/pallas_call | solution.py:320
  56.0 5.3 %collective-permute-start.1 = (bf16[16,16,128]{2,1,0:T(8,128)(2,1)S(1)}, bf16[16,16,128]{2,1,0:T(8,128)(2,1)S(1)}, u32[]{:S(2)}, u32[]{:S(2)}) collective-permute-start(bf16[16,16,128]{2,1,0:T(8,128)(2,1)S(1)} %get-tuple-element.23), channel_id=1, source_target_pairs={{1,0},{2,1},{3,2},{4,3},{5,4},{6,5},{7,6},{8,7},{9,8},{10,9},{11,1... | collective-permute-start | bytes 196616 | tf_op jit(solution)/shard_map/ppermute | solution.py:30
  61.2 1.9 %collective-permute-done.1.halo_ref = bf16[16,16,128]{2,1,0:T(8,128)(2,1)S(1)} collective-permute-done((bf16[16,16,128]{2,1,0:T(8,128)(2,1)S(1)}, bf16[16,16,128]{2,1,0:T(8,128)(2,1)S(1)}, u32[]{:S(2)}, u32[]{:S(2)}) %collective-permute-start.1) | collective-permute-done | bytes 65568 | tf_op jit(solution)/shard_map/ppermute | solution.py:30
  63.1 3.4 %all-to-all-done.2 = bf16[32,5,16,128]{3,2,1,0:T(8,128)(2,1)S(1)} async-done(((bf16[32,5,16,128]{3,2,1,0:T(8,128)(2,1)}), bf16[32,5,16,128]{3,2,1,0:T(8,128)(2,1)S(1)}, u32[]{:S(2)}, u32[]{:S(2)}) %all-to-all-start.2) | async-done | bytes 655392 | tf_op jit(solution)/shard_map/all_to_all | solution.py:258
  66.6 2.2 %final_sum.1 = f32[128,16,128]{2,1,0:T(8,128)} custom-call(s32[32,128]{1,0:T(8,128)S(1)} %get-tuple-element.16.picks_ref, f32[128,16,128]{2,1,0:T(8,128)S(1)} %get-tuple-element.22.base_ref, bf16[16,16,128]{2,1,0:T(8,128)(2,1)S(1)} %collective-permute-done.1.halo_ref, bf16[160,16,128]{2,1,0:T(8,128)(2,1)S(1)} %bitcast.9), custom_call_target="tpu_custom_call" | custom-call | bytes 3145728 | tf_op jit(solution)/shard_map/final_sum/pallas_call | solution.py:338
  (1 shorter events, 0.0 us)
Async XLA Ops:
  0.8 15.2 %collective-permute-start = (bf16[16,16,128]{2,1,0:T(8,128)(2,1)S(1)}, bf16[16,16,128]{2,1,0:T(8,128)(2,1)S(1)}, u32[]{:S(2)}, u32[]{:S(2)}) collective-permute-start(bf16[16,16,128]{2,1,0:T(8,128)(2,1)S(1)} %slice.10), channel_id=1, source_target_pairs={{31,0},{0,1},{1,2},{2,3},{3,4},{4,5},{5,6},{6,7},{7,8},{8,9},{9,10... | collective-permute-start | bytes 196616 | tf_op jit(solution)/shard_map/ppermute | solution.py:30
  18.1 20.6 %all-to-all-start.1 = ((bf16[32,5,16,128]{3,2,1,0:T(8,128)(2,1)}), bf16[32,5,16,128]{3,2,1,0:T(8,128)(2,1)S(1)}, u32[]{:S(2)}, u32[]{:S(2)}) async-start(bf16[32,5,16,128]{3,2,1,0:T(8,128)(2,1)} %bitcast.3), calls=%async_computation.1 | async-start | bytes 1310720 | tf_op jit(solution)/shard_map/all_to_all | solution.py:258
  20.8 1.0 %copy-start = (bf16[128,16,128]{2,1,0:T(8,128)(2,1)S(1)}, bf16[128,16,128]{2,1,0:T(8,128)(2,1)}, u32[]{:S(2)}) copy-start(bf16[128,16,128]{2,1,0:T(8,128)(2,1)} %probe_ref.3) | copy-start | bytes 1572868
  21.8 0.7 copy-start.1
  22.5 26.1 %copy-start.2 = (s32[128,4]{0,1:T(4,128)S(1)}, s32[128,4]{0,1:T(4,128)}, u32[]{:S(2)}) copy-start(s32[128,4]{0,1:T(4,128)} %param.7) | copy-start | bytes 6148
  45.2 21.3 %all-to-all-start.2 = ((bf16[32,5,16,128]{3,2,1,0:T(8,128)(2,1)}), bf16[32,5,16,128]{3,2,1,0:T(8,128)(2,1)S(1)}, u32[]{:S(2)}, u32[]{:S(2)}) async-start(bf16[32,5,16,128]{3,2,1,0:T(8,128)(2,1)} %bitcast.5), calls=%async_computation.2 | async-start | bytes 1310720 | tf_op jit(solution)/shard_map/all_to_all | solution.py:258
  56.0 7.2 %collective-permute-start.1 = (bf16[16,16,128]{2,1,0:T(8,128)(2,1)S(1)}, bf16[16,16,128]{2,1,0:T(8,128)(2,1)S(1)}, u32[]{:S(2)}, u32[]{:S(2)}) collective-permute-start(bf16[16,16,128]{2,1,0:T(8,128)(2,1)S(1)} %get-tuple-element.23), channel_id=1, source_target_pairs={{1,0},{2,1},{3,2},{4,3},{5,4},{6,5},{7,6},{8,7},{9,8},{10,9},{11,1... | collective-permute-start | bytes 196616 | tf_op jit(solution)/shard_map/ppermute | solution.py:30

commit v5 on v4

v5 whole, which is shorter than its diff:
```python
import functools

import jax
import jax.numpy as jnp
from jax import lax
from jax.experimental import pallas as pl
from jax.experimental.pallas import tpu as pltpu
from jax.sharding import PartitionSpec as P

REACH = 16
CHUNK = 16
AHEAD = 4
VMEM = pl.BlockSpec(memory_space=pltpu.VMEM)
SMEM = pl.BlockSpec(memory_space=pltpu.SMEM)
HBM = pl.BlockSpec(memory_space=pl.ANY)
NT = (((1,), (1,)), ((), ()))


def params(mib):
    return pltpu.CompilerParams(vmem_limit_bytes=mib * 2**20)


def in_hbm(x):
    return pltpu.with_memory_space_constraint(x, pltpu.HBM)


def passed_along(block, axis, distance):
    size = lax.axis_size(axis)
    return lax.ppermute(block, axis, [((i - distance) % size, i) for i in range(size)])


def earlier_matrix(blocks):
    row = lax.broadcasted_iota(jnp.int32, (blocks, blocks), 0)
    col = lax.broadcasted_iota(jnp.int32, (blocks, blocks), 1)
    return (row < col).astype(jnp.float32).astype(jnp.bfloat16)


def ranks_in(mask, blocks):
    chosen = mask.astype(jnp.float32).astype(jnp.bfloat16)
    return jnp.dot(chosen, earlier_matrix(blocks), preferred_element_type=jnp.float32).astype(jnp.int32)


def pick_kernel(shares, ids_ref, probe_ref, *refs):
    out_refs, picks_ref, probe, outs = refs[:2], refs[2], refs[3], refs[4:6]
    picks_smem, sems = refs[6:]
    groups, blocks = ids_ref.shape
    load = pltpu.make_async_copy(probe_ref, probe, sems.at[0])
    load.start()
    me = lax.axis_index("blk")
    local = ids_ref[...] - me * blocks
    mask = (local >= 0) & (local < blocks)
    rank = ranks_in(mask, blocks)
    lane = lax.broadcasted_iota(jnp.int32, (groups, blocks), 1)
    picks = jnp.zeros((groups, blocks), jnp.int32)
    for r in range(sum(shares)):
        found = jnp.sum(jnp.where(mask & (rank == r), local + 1, 0), axis=1, keepdims=True)
        picks = jnp.where(lane == r, found, picks)
    picks_ref[...] = picks
    copy = pltpu.make_async_copy(picks_ref, picks_smem, sems.at[1])
    copy.start()
    copy.wait()
    load.wait()

    def store(p):
        return pltpu.make_async_copy(outs[p], out_refs[p], sems.at[2 + p])

    for p, share in enumerate(shares):

        @pl.loop(0, groups, unroll=8)
        def _(g):
            for r in range(share):
                pick = picks_smem[g, sum(shares[:p]) + r]
                outs[p][g * share + r] = probe[jnp.maximum(pick - 1, 0)]

        store(p).start()
    for p in range(2):
        store(p).wait()


def stacked(mats):
    return mats.reshape(-1, mats.shape[-1])


def apart(left0, left1, mats):
    zero = jnp.zeros_like(left0)
    left = jnp.concatenate(
        [jnp.concatenate([left0, zero], axis=1), jnp.concatenate([zero, left1], axis=1)], axis=0
    )
    out = jnp.dot(left, mats, preferred_element_type=jnp.float32)
    return out.reshape((2,) + (left0.shape[0], mats.shape[1]))


def apart_back(lefts, mats):
    rows, half = lefts.shape[1], mats.shape[0] // 2
    out = lax.dot_general(lefts.reshape(2 * rows, lefts.shape[2]), mats, NT, preferred_element_type=jnp.float32)
    return out[:rows, :half], out[rows:, half:]


def near_place(ids_ref, k, i, first, count):
    place = ids_ref[k, i] - first + REACH
    return jnp.where(place >= count, place - count, place)


def near_forward_kernel(
    groups, shares, ids_ref, halo_ref, probe_ref, coeffs_ref, out_ref, slot_ref, block_ref, counts, ext, coeffs, sems
):
    blocks = probe_ref.shape[0]
    chunks = blocks // CHUNK

    def load(c):
        own = pl.ds(c * CHUNK, CHUNK)
        return pltpu.make_async_copy(coeffs_ref.at[own, pl.ds(0, 3)], coeffs.at[own], sems.at[c])

    for c in range(chunks):
        load(c).start()
    ext[pl.ds(0, REACH)] = halo_ref[...]
    ext[pl.ds(REACH, blocks)] = probe_ref[...]

    @pl.loop(0, groups, unroll=8)
    def _(g):
        counts[g] = 0

    @pl.loop(0, groups * sum(shares), unroll=8)
    def _(s):
        block_ref[0, s] = 0

    @pl.loop(0, blocks, unroll=4)
    def _(i):
        owner = lax.div(ids_ref[3, i], blocks)
        rank = counts[owner]
        counts[owner] = rank + 1
        late = groups * shares[0] + owner * shares[1] + rank - shares[0]
        slot = jnp.where(rank < shares[0], owner * shares[0] + rank, late)
        slot_ref[0, i] = slot
        block_ref[0, slot] = i

    first = lax.axis_index("blk") * blocks

    @pl.loop(0, chunks)
    def _(c):
        load(c).wait()
        for b in range(0, CHUNK, 2):
            i = c * CHUNK + b
            rows = []
            for j in range(2):
                tiles = [ext[near_place(ids_ref, k, i + j, first, groups * blocks)] for k in range(3)]
                rows.append(jnp.concatenate(tiles, axis=1))
            mixed = apart(rows[0], rows[1], stacked(coeffs[pl.ds(i, 2)]))
            out_ref[pl.ds(i, 2)] = probe_ref[pl.ds(i, 2)].astype(jnp.float32) - mixed


def far_kernel(start, block_ref, part_ref, far_ref, coeffs_ref, prec_ref, scaled_ref, parcel_ref, coeffs, prec, white, sems):
    chunks = far_ref.shape[0] // CHUNK

    def fetch(c):
        for b in range(CHUNK):
            s = c * CHUNK + b
            i = block_ref[0, start + s]
            pltpu.make_async_copy(coeffs_ref.at[i, 3], coeffs.at[s], sems.at[0, c]).start()
            pltpu.make_async_copy(prec_ref.at[i], prec.at[s], sems.at[1, c]).start()

    def ready(c):
        own = pl.ds(c * CHUNK, CHUNK)
        pltpu.make_async_copy(prec_ref.at[pl.ds(0, CHUNK)], coeffs.at[own], sems.at[0, c]).wait()
        pltpu.make_async_copy(prec_ref.at[pl.ds(0, CHUNK)], prec.at[own], sems.at[1, c]).wait()

    def mix(c):
        for b in range(0, CHUNK, 2):
            s = c * CHUNK + b
            mixed = apart(far_ref[s], far_ref[s + 1], stacked(coeffs[pl.ds(s, 2)]))
            for j in range(2):
                white[s + j] = (part_ref[block_ref[0, start + s + j]] - mixed[j]).astype(jnp.bfloat16)

    def scale(c):
        for b in range(0, CHUNK, 2):
            s = c * CHUNK + b
            scaled_ref[pl.ds(s, 2)] = apart(white[s], white[s + 1], stacked(prec[pl.ds(s, 2)])).astype(jnp.bfloat16)

    def back(c):
        for b in range(0, CHUNK, 2):
            s = c * CHUNK + b
            terms = apart_back(scaled_ref[pl.ds(s, 2)], stacked(coeffs[pl.ds(s, 2)]))
            for j in range(2):
                parcel_ref[s + j] = terms[j].astype(jnp.bfloat16)

    @pl.loop(0, min(3, chunks))
    def _(c):
        fetch(c)

    ready(0)
    mix(0)
    ready(1)
    scale(0)
    mix(1)

    @pl.loop(2, chunks)
    def _(c):
        @pl.when(c + 1 < chunks)
        def _():
            fetch(c + 1)

        ready(c)
        back(c - 2)
        scale(c - 1)
        mix(c)

    back(chunks - 2)
    scale(chunks - 1)
    back(chunks - 1)


def near_back_kernel(
    groups, ids_ref, slot_ref, early_ref, late_ref, coeffs_ref, base_ref, halo_ref, total, scaled, coeffs, sems
):
    blocks = base_ref.shape[0]
    points = base_ref.shape[2]
    early = early_ref.shape[0]
    chunks = blocks // CHUNK

    def load(c):
        own = pl.ds(c * CHUNK, CHUNK)
        return pltpu.make_async_copy(coeffs_ref.at[own, pl.ds(0, 3)], coeffs.at[own], sems.at[c])

    for c in range(chunks):
        load(c).start()
    scaled[pl.ds(0, early)] = early_ref[...]
    scaled[pl.ds(early, late_ref.shape[0])] = late_ref[...]
    total[pl.ds(0, REACH)] = jnp.zeros((REACH,) + total.shape[1:], jnp.float32)

    @pl.loop(0, blocks, unroll=8)
    def _(i):
        total[REACH + i] = scaled[slot_ref[0, i]].astype(jnp.float32)

    first = lax.axis_index("blk") * blocks

    @pl.loop(0, chunks)
    def _(c):
        load(c).wait()
        terms = []
        for b in range(CHUNK + AHEAD):
            if b < CHUNK and b % 2 == 0:
                i = c * CHUNK + b
                pair = jnp.concatenate([scaled[slot_ref[0, i]][None], scaled[slot_ref[0, i + 1]][None]], axis=0)
                terms.extend(apart_back(pair, stacked(coeffs[pl.ds(i, 2)])))
            if b >= AHEAD:
                i = c * CHUNK + b - AHEAD
                places = [near_place(ids_ref, k, i, first, groups * blocks) for k in range(3)]
                olds = [total[place] for place in places]
                for k in range(3):
                    total[places[k]] = olds[k] - terms[b - AHEAD][:, k * points : (k + 1) * points]

    halo_ref[...] = total[pl.ds(0, REACH)].astype(halo_ref.dtype)
    base_ref[...] = total[pl.ds(REACH, blocks)]


def subtract_far(column, share, picks_ref, back_ref, total):
    groups = picks_ref.shape[0]
    empty = total.shape[0] - 1

    @pl.loop(0, groups, unroll=8)
    def _(g):
        picks = [picks_ref[g, column + r] for r in range(share)]
        places = [jnp.where(pick > 0, pick - 1, empty) for pick in picks]
        olds = [total[place] for place in places]
        for r in range(share):
            total[places[r]] = olds[r] - back_ref[g * share + r].astype(jnp.float32)


def early_sum_kernel(shares, picks_ref, base_ref, halo_ref, back_ref, out_ref, total):
    blocks = base_ref.shape[0]
    total[pl.ds(0, blocks)] = base_ref[...]
    last = pl.ds(blocks - REACH, REACH)
    total[last] = total[last] + halo_ref[...].astype(jnp.float32)
    subtract_far(0, shares[0], picks_ref, back_ref, total)
    out_ref[...] = total[pl.ds(0, blocks)]


def late_sum_kernel(shares, picks_ref, base_ref, back_ref, out_ref, total, sem):
    blocks = base_ref.shape[0]
    total[pl.ds(0, blocks)] = base_ref[...]
    subtract_far(shares[0], shares[1], picks_ref, back_ref, total)
    store = pltpu.make_async_copy(total.at[pl.ds(0, blocks)], out_ref, sem)
    store.start()
    store.wait()


def per_device(probe_vecs, coeffs, cond_prec, neighbours):
    blocks, probes, points = probe_vecs.shape
    groups = lax.axis_size("blk")
    capacity = max(2, blocks // (groups - 1) + 1)
    shares = ((capacity + 1) // 2, capacity // 2)
    slots = groups * capacity
    chunks = blocks // CHUNK
    bf16, f32, i32 = jnp.bfloat16, jnp.float32, jnp.int32
    tile = (probes, points)
    flops = 2 * blocks * probes * points * points

    def array(rows, kind):
        return jax.ShapeDtypeStruct((rows,) + tile, kind)

    def cost(flops, mib):
        return pl.CostEstimate(flops=flops, bytes_accessed=mib * 2**20, transcendentals=0)

    def exchange(x):
        return lax.all_to_all(x, "blk", split_axis=0, concat_axis=0, tiled=True)

    def exchange_tiles(x):
        return exchange(x.reshape((groups, -1) + tile)).reshape((-1,) + tile)

    ids = neighbours.T
    halo = passed_along(probe_vecs[blocks - REACH :], "blk", 1)
    all_ids = exchange(jnp.broadcast_to(ids[3:], (groups, blocks)))
    all_ids, halo = lax.optimization_barrier((all_ids, halo))
    *outgoing, picks = pl.pallas_call(
        functools.partial(pick_kernel, shares),
        name="pick_tiles",
        out_shape=[array(groups * share, bf16) for share in shares] + [jax.ShapeDtypeStruct((groups, blocks), i32)],
        in_specs=[VMEM, HBM],
        out_specs=[HBM, HBM, VMEM],
        scratch_shapes=[
            pltpu.VMEM((blocks,) + tile, bf16),
            pltpu.VMEM((groups * shares[0],) + tile, bf16),
            pltpu.VMEM((groups * shares[1],) + tile, bf16),
            pltpu.SMEM((groups, blocks), i32),
            pltpu.SemaphoreType.DMA((4,)),
        ],
        compiler_params=params(8),
        cost_estimate=cost(0, 1),
    )(all_ids, in_hbm(probe_vecs))
    arrived = [exchange_tiles(x) for x in outgoing]
    part, slot_of, block_of = pl.pallas_call(
        functools.partial(near_forward_kernel, groups, shares),
        name="near_forward",
        out_shape=(
            array(blocks, f32),
            jax.ShapeDtypeStruct((1, blocks), i32),
            jax.ShapeDtypeStruct((1, slots), i32),
        ),
        in_specs=[SMEM, VMEM, VMEM, HBM],
        out_specs=(VMEM, SMEM, SMEM),
        scratch_shapes=[
            pltpu.SMEM((groups,), i32),
            pltpu.VMEM((REACH + blocks,) + tile, bf16),
            pltpu.VMEM((blocks, 3, points, points), bf16),
            pltpu.SemaphoreType.DMA((chunks,)),
        ],
        compiler_params=params(24),
        cost_estimate=cost(3 * flops, 14),
    )(ids, halo, probe_vecs, in_hbm(coeffs))

    scaled, returned = [], []
    for p, share in enumerate(shares):
        count = groups * share
        mats = pltpu.VMEM((count, points, points), bf16)
        if scaled:
            arrived[p], scaled[0] = lax.optimization_barrier((arrived[p], scaled[0]))
        scaled_part, parcel = pl.pallas_call(
            functools.partial(far_kernel, p * groups * shares[0]),
            name=("far_early", "far_late")[p],
            out_shape=(array(count, bf16), array(count, bf16)),
            in_specs=[SMEM, VMEM, VMEM, HBM, HBM],
            out_specs=(VMEM, VMEM),
            scratch_shapes=[
                mats,
                mats,
                pltpu.VMEM((count,) + tile, bf16),
                pltpu.SemaphoreType.DMA((2, count // CHUNK)),
            ],
            compiler_params=params(24),
            cost_estimate=cost(2 * flops, 6),
        )(block_of, part, arrived[p], in_hbm(coeffs), in_hbm(cond_prec))
        scaled.append(scaled_part)
        returned.append(exchange_tiles(parcel))
    base, halo_back = pl.pallas_call(
        functools.partial(near_back_kernel, groups),
        name="near_back",
        out_shape=(array(blocks, f32), array(REACH, bf16)),
        in_specs=[SMEM, SMEM, VMEM, VMEM, HBM],
        out_specs=(VMEM, VMEM),
        scratch_shapes=[
            pltpu.VMEM((REACH + blocks,) + tile, f32),
            pltpu.VMEM((slots,) + tile, bf16),
            pltpu.VMEM((blocks, 3, points, points), bf16),
            pltpu.SemaphoreType.DMA((chunks,)),
        ],
        compiler_params=params(24),
        cost_estimate=cost(3 * flops, 14),
    )(ids, slot_of, *scaled, in_hbm(coeffs))
    halo_sum = passed_along(halo_back, "blk", -1)
    base = pl.pallas_call(
        functools.partial(early_sum_kernel, shares),
        name="early_sum",
        out_shape=array(blocks, f32),
        in_specs=[SMEM, VMEM, VMEM, VMEM],
        out_specs=VMEM,
        scratch_shapes=[pltpu.VMEM((blocks + 1,) + tile, f32)],
        compiler_params=params(8),
        cost_estimate=cost(0, 2),
    )(picks, base, halo_sum, returned[0])
    return pl.pallas_call(
        functools.partial(late_sum_kernel, shares),
        name="late_sum",
        out_shape=array(blocks, f32),
        in_specs=[SMEM, VMEM, VMEM],
        out_specs=HBM,
        scratch_shapes=[pltpu.VMEM((blocks + 1,) + tile, f32), pltpu.SemaphoreType.DMA],
        compiler_params=params(8),
        cost_estimate=cost(0, 2),
    )(picks, base, returned[1])


def solution(mesh):
    in_specs = (
        P("blk", None, None),
        P("blk", None, None, None),
        P("blk", None, None),
        P("blk", None),
    )
    return jax.shard_map(
        per_device, mesh=mesh, in_specs=in_specs, out_specs=P("blk", None, None), check_vma=False
    )
```

time: 69.2 us -> 91.1 us (1.32)
  blocking collectives: 14.1 us -> 29 us
  Pallas kernels: 23.7 us -> 32.1 us
  waiting for transfers between devices: 15.8 us -> 8.74 us
  starting transfers between devices: 11.8 us -> 16.8 us
    all_to_all x1 -> x2, blocking collectives: 14.1 us -> 29 us  [exchange(): return lax.all_to_all(x, 'blk', split_axis=0, concat_axis=0, tiled=True)]
    pallas_call x4 -> x6, Pallas kernels: 16.4 us -> 24.8 us  [the longest x2 13.2 us: per_device(): pl.pallas_call(functools.partial(far_kernel, p * groups * shares[0]), nam...]
    all_to_all x2 -> x3, waiting for transfers between devices: 13.9 us -> 6.83 us  [exchange(): return lax.all_to_all(x, 'blk', split_axis=0, concat_axis=0, tiled=True)]
    all_to_all x2 -> x3, starting transfers between devices: 6.05 us -> 11.1 us  [exchange(): return lax.all_to_all(x, 'blk', split_axis=0, concat_axis=0, tiled=True)]
  transfers between devices with their start and end apart: 4 -> 5, of which waited for: 3 -> 2; matrix products, arithmetic and copies ran while one was open for 1% -> 1% of each run, Pallas kernels for 19% -> 31%
where the time goes in v5:
time: 91.1 us; the launch traced here: 90 us
  Pallas kernels  32.1 us (35%)
  blocking collectives  29 us (32%)
  starting transfers between devices  16.8 us (18%)
  waiting for transfers between devices  8.74 us (10%)
  local copies, waits for them, and re-layouts  3.26 us (4%)
    all_to_all x2, blocking collectives, exchange(): return lax.all_to_all(x, 'blk', split_axis=0, concat_axis=0, tiled=True)  29 us
    pallas_call x2, Pallas kernels, per_device(): pl.pallas_call(functools.partial(far_kernel, p * groups * shares[0]), nam...  13.2 us
    all_to_all x3, starting transfers between devices, exchange(): return lax.all_to_all(x, 'blk', split_axis=0, concat_axis=0, tiled=True)  11.1 us
    pallas_call x1, Pallas kernels, per_device(): pl.pallas_call(functools.partial(near_back_kernel, groups), name='near_ba...  7.3 us
    all_to_all x3, waiting for transfers between devices, exchange(): return lax.all_to_all(x, 'blk', split_axis=0, concat_axis=0, tiled=True)  6.83 us
    pallas_call x1, Pallas kernels, per_device(): pl.pallas_call(functools.partial(near_forward_kernel, groups, shares), na...  6.09 us
    ppermute x2, starting transfers between devices, passed_along(): lax.ppermute(block, axis, [((i - distance) % size, i) for i in range(size)])  5.73 us
    pallas_call x1, Pallas kernels, per_device(): pl.pallas_call(functools.partial(pick_kernel, shares), name='pick_tiles',...  2.32 us
  transfers between devices with their start and end apart: 5, of which 2 were waited for; matrix products, arithmetic and copies ran while one was open for 1% of the time, Pallas kernels for 31%

profile of v5, /device:TPU:0, one launch (start us, length us, event | category | flops | bytes accessed | tf_op | source)
XLA Modules:
  0.0 90.0 jit_solution(7047150655136115940)
XLA Ops:
  0.0 0.8 slice.10
  0.8 0.5 collective-permute-start
  1.3 0.7 slice_bitcast_fusion
  2.0 14.1 %all_to_all.29 = s32[32,1,128]{2,1,0:T(1,128)S(1)} all-to-all(s32[32,1,128]{2,1,0:T(1,128)S(1)} %broadcast_in_dim.2), channel_id=1, replica_groups=mesh['blk'=32] {'blk'}, dimensions={0} | all-to-all | bytes 32768 | tf_op jit(solution)/shard_map/all_to_all | solution.py:305
  16.1 0.0 collective-permute-done.halo_ref
  16.1 2.3 %pick_tiles.1 = (bf16[96,16,128]{2,1,0:T(8,128)(2,1)S(1)}, bf16[64,16,128]{2,1,0:T(8,128)(2,1)}, s32[32,128]{1,0:T(8,128)S(1)}) custom-call(s32[32,128]{1,0:T(8,128)S(1)} %bitcast.17, bf16[128,16,128]{2,1,0:T(8,128)(2,1)} %probe_ref.3), custom_call_target="tpu_custom_call" | custom-call | bytes 1048576 | tf_op jit(solution)/shard_map/pick_tiles/pallas_call | solution.py:314
  18.4 14.9 %all_to_all.30 = bf16[32,3,16,128]{3,2,1,0:T(8,128)(2,1)S(1)} all-to-all(bf16[32,3,16,128]{3,2,1,0:T(8,128)(2,1)S(1)} %bitcast.16), channel_id=1, replica_groups=mesh['blk'=32] {'blk'}, dimensions={0} | all-to-all | bytes 786432 | tf_op jit(solution)/shard_map/all_to_all | solution.py:305
  33.3 2.6 %all-to-all-start.1 = ((bf16[32,2,16,128]{3,2,1,0:T(8,128)(2,1)}), bf16[32,2,16,128]{3,2,1,0:T(8,128)(2,1)S(1)}, u32[]{:S(2)}, u32[]{:S(2)}) async-start(bf16[32,2,16,128]{3,2,1,0:T(8,128)(2,1)} %bitcast.3), calls=%async_computation.1 | async-start | bytes 524288 | tf_op jit(solution)/shard_map/all_to_all | solution.py:305
  35.9 0.0 copy-start
  35.9 1.0 %copy-done = bf16[128,16,128]{2,1,0:T(8,128)(2,1)S(1)} copy-done((bf16[128,16,128]{2,1,0:T(8,128)(2,1)S(1)}, bf16[128,16,128]{2,1,0:T(8,128)(2,1)}, u32[]{:S(2)}) %copy-start) | copy-done | bytes 524312
  36.9 0.7 copy-done.1
  37.6 6.1 %near_forward.1 = (f32[128,16,128]{2,1,0:T(8,128)S(1)}, s32[1,128]{1,0:T(1,128)S(1)}, s32[1,160]{1,0:T(1,128)S(1)}) custom-call(s32[4,128]{1,0:T(4,128)S(1)} %bitcast.19, bf16[16,16,128]{2,1,0:T(8,128)(2,1)S(1)} %collective-permute-done.halo_ref, bf16[128,16,128]{2,1,0:T(8,128)(2,1)S(1)} %copy-done, bf16[128,4,128,128]{3,2,1,0:T(8,128)(2,1)} %coeffs_ref.7), custom_call_target="tpu_custom_call" | custom-call | flops 201326592 | bytes 14680064 | tf_op jit(solution)/shard_map/near_forward/pallas_call | solution.py:331
  43.7 6.9 %far_early.1 = (bf16[96,16,128]{2,1,0:T(8,128)(2,1)S(1)}, bf16[96,16,128]{2,1,0:T(8,128)(2,1)}) custom-call(s32[1,160]{1,0:T(1,128)S(1)} %get-tuple-element.26.block_ref, f32[128,16,128]{2,1,0:T(8,128)S(1)} %get-tuple-element.27.part_ref, bf16[96,16,128]{2,1,0:T(8,128)(2,1)S(1)} %bitcast.13, bf16[128,4,128,128]{3,2,1,0:T(8,128)(2,1)} %coeffs_ref.7, ...), custom_call_target="tpu_custom_call" | custom-call | flops 134217728 | bytes 6291456 | tf_op jit(solution)/shard_map/far_early/pallas_call | solution.py:357
  50.6 0.0 copy-start.2
  50.6 0.0 all-to-all-done.1
  50.6 5.8 %all-to-all-start.3 = ((bf16[32,3,16,128]{3,2,1,0:T(8,128)(2,1)}), bf16[32,3,16,128]{3,2,1,0:T(8,128)(2,1)S(1)}, u32[]{:S(2)}, u32[]{:S(2)}) async-start(bf16[32,3,16,128]{3,2,1,0:T(8,128)(2,1)} %bitcast.7), calls=%async_computation.3 | async-start | bytes 786432 | tf_op jit(solution)/shard_map/all_to_all | solution.py:305
  56.5 6.3 %far_late.1 = (bf16[64,16,128]{2,1,0:T(8,128)(2,1)S(1)}, bf16[64,16,128]{2,1,0:T(8,128)(2,1)}) custom-call(s32[1,160]{1,0:T(1,128)S(1)} %get-tuple-element.26.block_ref, f32[128,16,128]{2,1,0:T(8,128)S(1)} %get-tuple-element.27.part_ref, bf16[64,16,128]{2,1,0:T(8,128)(2,1)S(1)} %bitcast.14, bf16[128,4,128,128]{3,2,1,0:T(8,128)(2,1)} %coeffs_ref.7, ...), custom_call_target="tpu_custom_call" | custom-call | flops 134217728 | bytes 6291456 | tf_op jit(solution)/shard_map/far_late/pallas_call | solution.py:357
  62.8 6.8 %all-to-all-done.3 = bf16[32,3,16,128]{3,2,1,0:T(8,128)(2,1)S(1)} async-done(((bf16[32,3,16,128]{3,2,1,0:T(8,128)(2,1)}), bf16[32,3,16,128]{3,2,1,0:T(8,128)(2,1)S(1)}, u32[]{:S(2)}, u32[]{:S(2)}) %all-to-all-start.3) | async-done | bytes 393248 | tf_op jit(solution)/shard_map/all_to_all | solution.py:305
  69.7 2.6 %all-to-all-start.4 = ((bf16[32,2,16,128]{3,2,1,0:T(8,128)(2,1)}), bf16[32,2,16,128]{3,2,1,0:T(8,128)(2,1)S(1)}, u32[]{:S(2)}, u32[]{:S(2)}) async-start(bf16[32,2,16,128]{3,2,1,0:T(8,128)(2,1)} %bitcast.9), calls=%async_computation.4 | async-start | bytes 524288 | tf_op jit(solution)/shard_map/all_to_all | solution.py:305
  72.3 7.3 %near_back.1 = (f32[128,16,128]{2,1,0:T(8,128)S(1)}, bf16[16,16,128]{2,1,0:T(8,128)(2,1)S(1)}) custom-call(s32[4,128]{1,0:T(4,128)S(1)} %bitcast.20, s32[1,128]{1,0:T(1,128)S(1)} %get-tuple-element.24.slot_ref, bf16[96,16,128]{2,1,0:T(8,128)(2,1)S(1)} %get-tuple-element.30.early_ref, bf16[64,16,128]{2,1,0:T(8,128)(2,1)S(1)} %get-tuple-element.32.late_ref, ...), custom_call_target="tpu_custom_call" | custom-call | flops 201326592 | bytes 14680064 | tf_op jit(solution)/shard_map/near_back/pallas_call | solution.py:374
  79.6 5.3 %collective-permute-start.1 = (bf16[16,16,128]{2,1,0:T(8,128)(2,1)S(1)}, bf16[16,16,128]{2,1,0:T(8,128)(2,1)S(1)}, u32[]{:S(2)}, u32[]{:S(2)}) collective-permute-start(bf16[16,16,128]{2,1,0:T(8,128)(2,1)S(1)} %get-tuple-element.34), channel_id=1, source_target_pairs={{1,0},{2,1},{3,2},{4,3},{5,4},{6,5},{7,6},{8,7},{9,8},{10,9},{11,1... | collective-permute-start | bytes 196616 | tf_op jit(solution)/shard_map/ppermute | solution.py:29
  84.9 1.9 %collective-permute-done.1.halo_ref = bf16[16,16,128]{2,1,0:T(8,128)(2,1)S(1)} collective-permute-done((bf16[16,16,128]{2,1,0:T(8,128)(2,1)S(1)}, bf16[16,16,128]{2,1,0:T(8,128)(2,1)S(1)}, u32[]{:S(2)}, u32[]{:S(2)}) %collective-permute-start.1) | collective-permute-done | bytes 65568 | tf_op jit(solution)/shard_map/ppermute | solution.py:29
  86.8 1.2 %early_sum.1.base_ref = f32[128,16,128]{2,1,0:T(8,128)S(1)} custom-call(s32[32,128]{1,0:T(8,128)S(1)} %get-tuple-element.22.picks_ref, f32[128,16,128]{2,1,0:T(8,128)S(1)} %get-tuple-element.33.base_ref, bf16[16,16,128]{2,1,0:T(8,128)(2,1)S(1)} %collective-permute-done.1.halo_ref, bf16[96,16,128]{2,1,0:T(8,128)(2,1)S(1)} %bitcast.12), custom_call_target="tpu_custom_call" | custom-call | bytes 2097152 | tf_op jit(solution)/shard_map/early_sum/pallas_call | solution.py:390
  88.0 2.0 %late_sum.1 = f32[128,16,128]{2,1,0:T(8,128)} custom-call(s32[32,128]{1,0:T(8,128)S(1)} %get-tuple-element.22.picks_ref, f32[128,16,128]{2,1,0:T(8,128)S(1)} %early_sum.1.base_ref, bf16[64,16,128]{2,1,0:T(8,128)(2,1)S(1)} %bitcast.15), custom_call_target="tpu_custom_call" | custom-call | bytes 2097152 | tf_op jit(solution)/shard_map/late_sum/pallas_call | solution.py:400
  (4 shorter events, 0.0 us)
Async XLA Ops:
  0.8 15.2 %collective-permute-start = (bf16[16,16,128]{2,1,0:T(8,128)(2,1)S(1)}, bf16[16,16,128]{2,1,0:T(8,128)(2,1)S(1)}, u32[]{:S(2)}, u32[]{:S(2)}) collective-permute-start(bf16[16,16,128]{2,1,0:T(8,128)(2,1)S(1)} %slice.10), channel_id=1, source_target_pairs={{31,0},{0,1},{1,2},{2,3},{3,4},{4,5},{5,6},{6,7},{7,8},{8,9},{9,10... | collective-permute-start | bytes 196616 | tf_op jit(solution)/shard_map/ppermute | solution.py:29
  33.3 17.3 %all-to-all-start.1 = ((bf16[32,2,16,128]{3,2,1,0:T(8,128)(2,1)}), bf16[32,2,16,128]{3,2,1,0:T(8,128)(2,1)S(1)}, u32[]{:S(2)}, u32[]{:S(2)}) async-start(bf16[32,2,16,128]{3,2,1,0:T(8,128)(2,1)} %bitcast.3), calls=%async_computation.1 | async-start | bytes 524288 | tf_op jit(solution)/shard_map/all_to_all | solution.py:305
  35.9 1.0 %copy-start = (bf16[128,16,128]{2,1,0:T(8,128)(2,1)S(1)}, bf16[128,16,128]{2,1,0:T(8,128)(2,1)}, u32[]{:S(2)}) copy-start(bf16[128,16,128]{2,1,0:T(8,128)(2,1)} %probe_ref.3) | copy-start | bytes 1572868
  36.9 0.7 copy-start.1
  50.6 21.7 %copy-start.2 = (s32[128,4]{0,1:T(4,128)S(1)}, s32[128,4]{0,1:T(4,128)}, u32[]{:S(2)}) copy-start(s32[128,4]{0,1:T(4,128)} %param.7) | copy-start | bytes 6148
  50.6 19.0 %all-to-all-start.3 = ((bf16[32,3,16,128]{3,2,1,0:T(8,128)(2,1)}), bf16[32,3,16,128]{3,2,1,0:T(8,128)(2,1)S(1)}, u32[]{:S(2)}, u32[]{:S(2)}) async-start(bf16[32,3,16,128]{3,2,1,0:T(8,128)(2,1)} %bitcast.7), calls=%async_computation.3 | async-start | bytes 786432 | tf_op jit(solution)/shard_map/all_to_all | solution.py:305
  69.7 18.3 %all-to-all-start.4 = ((bf16[32,2,16,128]{3,2,1,0:T(8,128)(2,1)}), bf16[32,2,16,128]{3,2,1,0:T(8,128)(2,1)S(1)}, u32[]{:S(2)}, u32[]{:S(2)}) async-start(bf16[32,2,16,128]{3,2,1,0:T(8,128)(2,1)} %bitcast.9), calls=%async_computation.4 | async-start | bytes 524288 | tf_op jit(solution)/shard_map/all_to_all | solution.py:305
  79.6 7.2 %collective-permute-start.1 = (bf16[16,16,128]{2,1,0:T(8,128)(2,1)S(1)}, bf16[16,16,128]{2,1,0:T(8,128)(2,1)S(1)}, u32[]{:S(2)}, u32[]{:S(2)}) collective-permute-start(bf16[16,16,128]{2,1,0:T(8,128)(2,1)S(1)} %get-tuple-element.34), channel_id=1, source_target_pairs={{1,0},{2,1},{3,2},{4,3},{5,4},{6,5},{7,6},{8,7},{9,8},{10,9},{11,1... | collective-permute-start | bytes 196616 | tf_op jit(solution)/shard_map/ppermute | solution.py:29

commit v6 on v4

--- a/solution.py
+++ b/solution.py
@@ -30,6 +30,16 @@
     return lax.ppermute(block, axis, [((i - distance) % size, i) for i in range(size)])
 
 
+def turned(device, groups):
+    bits = groups.bit_length() - 1
+    if groups != 1 << bits:
+        return device
+    place = device * 0
+    for bit in range(bits):
+        place = place + ((device >> bit) & 1) * (1 << (bits - 1 - bit))
+    return place
+
+
 def earlier_matrix(blocks):
     row = lax.broadcasted_iota(jnp.int32, (blocks, blocks), 0)
     col = lax.broadcasted_iota(jnp.int32, (blocks, blocks), 1)
@@ -41,7 +51,7 @@
     return jnp.dot(chosen, earlier_matrix(blocks), preferred_element_type=jnp.float32).astype(jnp.int32)
 
 
-def pick_kernel(capacity, ids_ref, probe_ref, out_ref, picks_ref, probe, out, picks_smem, sems):
+def pick_kernel(capacity, ids_ref, probe_ref, out_ref, picks_ref, tail_ref, probe, out, picks_smem, sems):
     groups, blocks = ids_ref.shape
     load = pltpu.make_async_copy(probe_ref, probe, sems.at[0])
     load.start()
@@ -73,6 +83,7 @@
                 out[g * capacity + r] = probe[jnp.maximum(picks_smem[g, r] - 1, 0)]
 
         store(p).start()
+    tail_ref[...] = probe[pl.ds(blocks - REACH, REACH)]
     for p in range(STORES):
         store(p).wait()
 
@@ -101,8 +112,16 @@
     return jnp.where(place >= count, place - count, place)
 
 
+def near_mix(ids_ref, tiles, coeffs, i, at, first, count, shift):
+    rows = []
+    for j in range(2):
+        places = [near_place(ids_ref, k, i + j, first, count) - shift for k in range(3)]
+        rows.append(jnp.concatenate([tiles[place] for place in places], axis=1))
+    return apart(rows[0], rows[1], stacked(coeffs[pl.ds(at, 2)]))
+
+
 def near_forward_kernel(
-    groups, capacity, ids_ref, far_ref, halo_ref, probe_ref, coeffs_ref, out_ref, slot_ref, ext, coeffs, sems
+    groups, capacity, ids_ref, far_ref, probe_ref, coeffs_ref, out_ref, slot_ref, coeffs, sems
 ):
     blocks = probe_ref.shape[0]
     chunks = blocks // CHUNK
@@ -111,32 +130,31 @@
         own = pl.ds(c * CHUNK, CHUNK)
         return pltpu.make_async_copy(coeffs_ref.at[own, pl.ds(0, 3)], coeffs.at[own], sems.at[c])
 
-    for c in range(chunks):
+    for c in range(1, chunks):
         load(c).start()
-    ext[pl.ds(0, REACH)] = halo_ref[...]
-    ext[pl.ds(REACH, blocks)] = probe_ref[...]
     owner = far_ref[...] // blocks
     mask = lax.broadcasted_iota(jnp.int32, (groups, blocks), 0) == owner
     rank = jnp.sum(jnp.where(mask, ranks_in(mask, blocks), 0), axis=0, keepdims=True)
-    slot_ref[...] = owner * capacity + rank
+    slot_ref[...] = turned(owner, groups) * capacity + rank
     first = lax.axis_index("blk") * blocks
-
-    @pl.loop(0, chunks)
+    out_ref[pl.ds(0, REACH)] = probe_ref[pl.ds(0, REACH)].astype(jnp.float32)
+
+    @pl.loop(1, chunks)
     def _(c):
         load(c).wait()
         for b in range(0, CHUNK, 2):
             i = c * CHUNK + b
-            rows = []
-            for j in range(2):
-                tiles = [ext[near_place(ids_ref, k, i + j, first, groups * blocks)] for k in range(3)]
-                rows.append(jnp.concatenate(tiles, axis=1))
-            mixed = apart(rows[0], rows[1], stacked(coeffs[pl.ds(i, 2)]))
+            mixed = near_mix(ids_ref, probe_ref, coeffs, i, i, first, groups * blocks, REACH)
             out_ref[pl.ds(i, 2)] = probe_ref[pl.ds(i, 2)].astype(jnp.float32) - mixed
 
 
-def far_kernel(slot_ref, part_ref, far_ref, coeffs_ref, prec_ref, scaled_ref, parcel_ref, coeffs, prec, white, sems):
+def far_kernel(
+    groups, ids_ref, slot_ref, part_ref, far_ref, halo_ref, probe_ref, coeffs_ref, prec_ref,
+    scaled_ref, parcel_ref, coeffs, prec, white, near, head, sems
+):
     blocks = part_ref.shape[0]
     chunks = blocks // CHUNK
+    order = list(range(1, chunks)) + [0]
 
     def loads(c):
         own = pl.ds(c * CHUNK, CHUNK)
@@ -145,15 +163,23 @@
             pltpu.make_async_copy(prec_ref.at[own], prec.at[own], sems.at[1, c]),
         )
 
-    for c in range(chunks):
+    own_head = pltpu.make_async_copy(probe_ref.at[pl.ds(0, REACH)], head.at[pl.ds(REACH, REACH)], sems.at[2, 0])
+    near_load = pltpu.make_async_copy(coeffs_ref.at[pl.ds(0, REACH), pl.ds(0, 3)], near, sems.at[2, 1])
+    for c in order:
         for load in loads(c):
             load.start()
+    own_head.start()
+    near_load.start()
+    head[pl.ds(0, REACH)] = halo_ref[...]
     parcel_ref[...] = jnp.zeros_like(parcel_ref)
 
-    def mix(c):
+    def mix(c, first_chunk=False):
         for b in range(0, CHUNK, 2):
             i = c * CHUNK + b
             mixed = apart(far_ref[slot_ref[0, i]], far_ref[slot_ref[0, i + 1]], stacked(coeffs[pl.ds(i, 2)]))
+            if first_chunk:
+                first = lax.axis_index("blk") * blocks
+                mixed = mixed + near_mix(ids_ref, head, near, i, i, first, groups * blocks, 0)
             white[pl.ds(i, 2)] = (part_ref[pl.ds(i, 2)] - mixed).astype(jnp.bfloat16)
 
     def scale(c):
@@ -172,22 +198,28 @@
         for load in loads(c):
             load.wait()
 
-    ready(0)
-    mix(0)
     ready(1)
-    scale(0)
     mix(1)
-
-    @pl.loop(2, chunks)
+    ready(2)
+    scale(1)
+    mix(2)
+
+    @pl.loop(3, chunks)
     def _(c):
         ready(c)
         back(c - 2)
         scale(c - 1)
         mix(c)
 
+    ready(0)
+    own_head.wait()
+    near_load.wait()
     back(chunks - 2)
     scale(chunks - 1)
+    mix(0, True)
     back(chunks - 1)
+    scale(0)
+    back(0)
 
 
 def near_back_kernel(groups, ids_ref, scaled_ref, coeffs_ref, base_ref, halo_ref, total, coeffs, sems):
@@ -255,22 +287,22 @@
     flops = 2 * blocks * probes * points * points
 
     def exchange(x):
-        return lax.all_to_all(x, "blk", split_axis=0, concat_axis=0, tiled=True)
+        order = [turned(place, groups) for place in range(groups)]
+        return lax.all_to_all(x, "blk", split_axis=0, concat_axis=0, tiled=True, axis_index_groups=[order])
 
     ids = neighbours.T
     far_ids = ids[3:]
-    halo = passed_along(probe_vecs[blocks - REACH :], "blk", 1)
     all_ids = exchange(jnp.broadcast_to(far_ids, (groups, blocks)))
-    all_ids, halo = lax.optimization_barrier((all_ids, halo))
-    outgoing, picks = pl.pallas_call(
+    outgoing, picks, tail = pl.pallas_call(
         functools.partial(pick_kernel, capacity),
         name="pick_tiles",
         out_shape=(
             jax.ShapeDtypeStruct((slots,) + tile, bf16),
             jax.ShapeDtypeStruct((groups, blocks), jnp.int32),
+            jax.ShapeDtypeStruct((REACH,) + tile, bf16),
         ),
         in_specs=[VMEM, HBM],
-        out_specs=(HBM, VMEM),
+        out_specs=(HBM, VMEM, VMEM),
         scratch_shapes=[
             pltpu.VMEM((blocks,) + tile, bf16),
             pltpu.VMEM((slots,) + tile, bf16),
@@ -281,6 +313,7 @@
         cost_estimate=pl.CostEstimate(flops=0, bytes_accessed=2 * slots * 4096, transcendentals=0),
     )(all_ids, in_hbm(probe_vecs))
     arrived = exchange(outgoing.reshape((groups, capacity) + tile)).reshape((slots,) + tile)
+    halo = passed_along(tail, "blk", 1)
     part, slot_of = pl.pallas_call(
         functools.partial(near_forward_kernel, groups, capacity),
         name="near_forward",
@@ -288,34 +321,35 @@
             jax.ShapeDtypeStruct((blocks,) + tile, f32),
             jax.ShapeDtypeStruct((1, blocks), jnp.int32),
         ),
-        in_specs=[SMEM, VMEM, VMEM, VMEM, HBM],
+        in_specs=[SMEM, VMEM, VMEM, HBM],
         out_specs=(VMEM, VMEM),
         scratch_shapes=[
-            pltpu.VMEM((REACH + blocks,) + tile, bf16),
             pltpu.VMEM((blocks, 3, points, points), bf16),
             pltpu.SemaphoreType.DMA((chunks,)),
         ],
         compiler_params=params(24),
         cost_estimate=pl.CostEstimate(flops=3 * flops, bytes_accessed=14 * 2**20, transcendentals=0),
-    )(ids, far_ids, halo, probe_vecs, in_hbm(coeffs))
+    )(ids, far_ids, probe_vecs, in_hbm(coeffs))
     scaled, parcel = pl.pallas_call(
-        far_kernel,
+        functools.partial(far_kernel, groups),
         name="far_and_scale",
         out_shape=(
             jax.ShapeDtypeStruct((blocks,) + tile, bf16),
             jax.ShapeDtypeStruct((slots,) + tile, bf16),
         ),
-        in_specs=[SMEM, VMEM, VMEM, HBM, HBM],
+        in_specs=[SMEM, SMEM, VMEM, VMEM, VMEM, HBM, HBM, HBM],
         out_specs=(VMEM, VMEM),
         scratch_shapes=[
             pltpu.VMEM((blocks, points, points), bf16),
             pltpu.VMEM((blocks, points, points), bf16),
             pltpu.VMEM((blocks,) + tile, bf16),
-            pltpu.SemaphoreType.DMA((2, chunks)),
+            pltpu.VMEM((REACH, 3, points, points), bf16),
+            pltpu.VMEM((2 * REACH,) + tile, bf16),
+            pltpu.SemaphoreType.DMA((3, chunks)),
         ],
         compiler_params=params(24),
         cost_estimate=pl.CostEstimate(flops=3 * flops, bytes_accessed=11 * 2**20, transcendentals=0),
-    )(slot_of, part, arrived, in_hbm(coeffs), in_hbm(cond_prec))
+    )(ids, slot_of, part, arrived, halo, in_hbm(probe_vecs), in_hbm(coeffs), in_hbm(cond_prec))
     returned = exchange(parcel.reshape((groups, capacity) + tile)).reshape((slots,) + tile)
     base, halo_back = pl.pallas_call(
         functools.partial(near_back_kernel, groups),

time: 69.2 us -> 70.7 us (1.022)
  waiting for transfers between devices: 15.8 us -> 19.4 us
  starting transfers between devices: 11.8 us -> 10.7 us
  local copies, waits for them, and re-layouts: 3.26 us -> 2.49 us
    ppermute x2, waiting for transfers between devices: 1.91 us -> 12.6 us  [passed_along(): lax.ppermute(block, axis, [((i - distance) % size, i) for i in range(size)])]
    all_to_all x2, waiting for transfers between devices: 13.9 us -> 6.74 us  [exchange(): lax.all_to_all(x, 'blk', split_axis=0, concat_axis=0, tiled=True, axis_in...]
    slice x1 -> x0, local copies, waits for them, and re-layouts: 0.84 us -> none  [per_device(): halo = passed_along(probe_vecs[blocks - REACH:], 'blk', 1)]
    all_to_all x2, starting transfers between devices: 6.05 us -> 5.27 us  [exchange(): lax.all_to_all(x, 'blk', split_axis=0, concat_axis=0, tiled=True, axis_in...]
  transfers between devices with their start and end apart: 4 -> 4, of which waited for: 3 -> 4; matrix products, arithmetic and copies ran while one was open for 1% -> 0% of each run, Pallas kernels for 19% -> 18%
where the time goes in v6:
time: 70.7 us; the launch traced here: 70.3 us
  Pallas kernels  23.4 us (33%)
  waiting for transfers between devices  19.4 us (27%)
  blocking collectives  14.2 us (20%)
  starting transfers between devices  10.7 us (15%)
  local copies, waits for them, and re-layouts  2.49 us (4%)
    all_to_all x1, blocking collectives, exchange(): lax.all_to_all(x, 'blk', split_axis=0, concat_axis=0, tiled=True, axis_in...  14.2 us
    ppermute x2, waiting for transfers between devices, passed_along(): lax.ppermute(block, axis, [((i - distance) % size, i) for i in range(size)])  12.6 us
    pallas_call x1, Pallas kernels, per_device(): pl.pallas_call(functools.partial(near_back_kernel, groups), name='near_ba...  7.3 us
    all_to_all x2, waiting for transfers between devices, exchange(): lax.all_to_all(x, 'blk', split_axis=0, concat_axis=0, tiled=True, axis_in...  6.74 us
    pallas_call x1, Pallas kernels, per_device(): pl.pallas_call(functools.partial(far_kernel, groups), name='far_and_scale...  6.72 us
    ppermute x2, starting transfers between devices, passed_along(): lax.ppermute(block, axis, [((i - distance) % size, i) for i in range(size)])  5.43 us
    all_to_all x2, starting transfers between devices, exchange(): lax.all_to_all(x, 'blk', split_axis=0, concat_axis=0, tiled=True, axis_in...  5.27 us
    pallas_call x1, Pallas kernels, per_device(): pl.pallas_call(functools.partial(near_forward_kernel, groups, capacity),...  5.18 us
  transfers between devices with their start and end apart: 4, of which 4 were waited for; matrix products, arithmetic and copies ran while one was open for 0% of the time, Pallas kernels for 18%

profile of v6, /device:TPU:0, one launch (start us, length us, event | category | flops | bytes accessed | tf_op | source)
XLA Modules:
  0.0 70.3 jit_solution(11986203905056085256)
XLA Ops:
  0.0 0.0 copy-start.2
  0.0 0.8 %fusion = (s32[1,128]{1,0:T(1,128)S(1)}, s32[128]{0:T(128)S(1)}) fusion(s32[4,128]{1,0:T(4,128)} %bitcast.11), kind=kLoop, calls=%fused_computation.1 | loop fusion | bytes 1536 | tf_op jit(solution)/shard_map/slice | solution.py:294
  0.8 14.2 %all_to_all.18 = s32[32,1,128]{2,1,0:T(1,128)S(1)} all-to-all(s32[32,1,128]{2,1,0:T(1,128)S(1)} %broadcast_in_dim.2), channel_id=1, replica_groups={{0,16,8,24,4,20,12,28,2,18,10,26,6,22,14,30,1,17,9,25,5,21,13,29,3,19,1..., dimensions={0} | all-to-all | bytes 32768 | tf_op jit(solution)/shard_map/all_to_all | solution.py:291
  15.0 2.0 %pick_tiles.1 = (bf16[160,16,128]{2,1,0:T(8,128)(2,1)}, s32[32,128]{1,0:T(8,128)S(1)}, bf16[16,16,128]{2,1,0:T(8,128)(2,1)S(1)}) custom-call(s32[32,128]{1,0:T(8,128)S(1)} %bitcast.10, bf16[128,16,128]{2,1,0:T(8,128)(2,1)} %probe_ref.5), custom_call_target="tpu_custom_call" | custom-call | bytes 1310720 | tf_op jit(solution)/shard_map/pick_tiles/pallas_call | solution.py:296
  17.0 2.6 %all-to-all-start.1 = ((bf16[32,5,16,128]{3,2,1,0:T(8,128)(2,1)}), bf16[32,5,16,128]{3,2,1,0:T(8,128)(2,1)S(1)}, u32[]{:S(2)}, u32[]{:S(2)}) async-start(bf16[32,5,16,128]{3,2,1,0:T(8,128)(2,1)} %bitcast.3), calls=%async_computation.1 | async-start | bytes 1310720 | tf_op jit(solution)/shard_map/all_to_all | solution.py:291
  19.7 0.2 collective-permute-start
  19.9 0.0 copy-start
  19.9 1.0 %copy-done = bf16[128,16,128]{2,1,0:T(8,128)(2,1)S(1)} copy-done((bf16[128,16,128]{2,1,0:T(8,128)(2,1)S(1)}, bf16[128,16,128]{2,1,0:T(8,128)(2,1)}, u32[]{:S(2)}) %copy-start) | copy-done | bytes 524312
  20.9 0.0 copy-start.1
  20.9 0.7 copy-done.1
  21.6 5.2 %near_forward.1 = (f32[128,16,128]{2,1,0:T(8,128)S(1)}, s32[1,128]{1,0:T(1,128)S(1)}) custom-call(s32[4,128]{1,0:T(4,128)S(1)} %bitcast.12, s32[1,128]{1,0:T(1,128)S(1)} %get-tuple-element.23.far_ref, bf16[128,16,128]{2,1,0:T(8,128)(2,1)S(1)} %copy-done, bf16[128,4,128,128]{3,2,1,0:T(8,128)(2,1)} %coeffs_ref.5), custom_call_target="tpu_custom_call" | custom-call | flops 201326592 | bytes 14680064 | tf_op jit(solution)/shard_map/near_forward/pallas_call | solution.py:317
  26.8 10.7 %collective-permute-done.halo_ref = bf16[16,16,128]{2,1,0:T(8,128)(2,1)S(1)} collective-permute-done((bf16[16,16,128]{2,1,0:T(8,128)(2,1)S(1)}, bf16[16,16,128]{2,1,0:T(8,128)(2,1)S(1)}, u32[]{:S(2)}, u32[]{:S(2)}) %collective-permute-start) | collective-permute-done | bytes 65568 | tf_op jit(solution)/shard_map/ppermute | solution.py:30
  37.5 2.1 %all-to-all-done.1 = bf16[32,5,16,128]{3,2,1,0:T(8,128)(2,1)S(1)} async-done(((bf16[32,5,16,128]{3,2,1,0:T(8,128)(2,1)}), bf16[32,5,16,128]{3,2,1,0:T(8,128)(2,1)S(1)}, u32[]{:S(2)}, u32[]{:S(2)}) %all-to-all-start.1) | async-done | bytes 655392 | tf_op jit(solution)/shard_map/all_to_all | solution.py:291
  39.6 0.0 copy-done.2
  39.6 6.7 %far_and_scale.1 = (bf16[128,16,128]{2,1,0:T(8,128)(2,1)S(1)}, bf16[160,16,128]{2,1,0:T(8,128)(2,1)}) custom-call(s32[4,128]{1,0:T(4,128)S(1)} %bitcast.13, s32[1,128]{1,0:T(1,128)S(1)} %get-tuple-element.15.slot_ref, f32[128,16,128]{2,1,0:T(8,128)S(1)} %get-tuple-element.16.part_ref, bf16[160,16,128]{2,1,0:T(8,128)(2,1)S(1)} %bitcast.9, ...), custom_call_target="tpu_custom_call" | custom-call | flops 201326592 | bytes 11534336 | tf_op jit(solution)/shard_map/far_and_scale/pallas_call | solution.py:333
  46.3 2.6 %all-to-all-start.2 = ((bf16[32,5,16,128]{3,2,1,0:T(8,128)(2,1)}), bf16[32,5,16,128]{3,2,1,0:T(8,128)(2,1)S(1)}, u32[]{:S(2)}, u32[]{:S(2)}) async-start(bf16[32,5,16,128]{3,2,1,0:T(8,128)(2,1)} %bitcast.5), calls=%async_computation.2 | async-start | bytes 1310720 | tf_op jit(solution)/shard_map/all_to_all | solution.py:291
  48.9 7.3 %near_back.1 = (f32[128,16,128]{2,1,0:T(8,128)S(1)}, bf16[16,16,128]{2,1,0:T(8,128)(2,1)S(1)}) custom-call(s32[4,128]{1,0:T(4,128)S(1)} %bitcast.14, bf16[128,16,128]{2,1,0:T(8,128)(2,1)S(1)} %get-tuple-element.19.scaled_ref, bf16[128,4,128,128]{3,2,1,0:T(8,128)(2,1)} %coeffs_ref.5), custom_call_target="tpu_custom_call" | custom-call | flops 201326592 | bytes 14680064 | tf_op jit(solution)/shard_map/near_back/pallas_call | solution.py:354
  56.2 5.3 %collective-permute-start.1 = (bf16[16,16,128]{2,1,0:T(8,128)(2,1)S(1)}, bf16[16,16,128]{2,1,0:T(8,128)(2,1)S(1)}, u32[]{:S(2)}, u32[]{:S(2)}) collective-permute-start(bf16[16,16,128]{2,1,0:T(8,128)(2,1)S(1)} %get-tuple-element.21), channel_id=1, source_target_pairs={{1,0},{2,1},{3,2},{4,3},{5,4},{6,5},{7,6},{8,7},{9,8},{10,9},{11,1... | collective-permute-start | bytes 196616 | tf_op jit(solution)/shard_map/ppermute | solution.py:30
  61.5 1.9 %collective-permute-done.1.halo_ref = bf16[16,16,128]{2,1,0:T(8,128)(2,1)S(1)} collective-permute-done((bf16[16,16,128]{2,1,0:T(8,128)(2,1)S(1)}, bf16[16,16,128]{2,1,0:T(8,128)(2,1)S(1)}, u32[]{:S(2)}, u32[]{:S(2)}) %collective-permute-start.1) | collective-permute-done | bytes 65568 | tf_op jit(solution)/shard_map/ppermute | solution.py:30
  63.4 4.7 %all-to-all-done.2 = bf16[32,5,16,128]{3,2,1,0:T(8,128)(2,1)S(1)} async-done(((bf16[32,5,16,128]{3,2,1,0:T(8,128)(2,1)}), bf16[32,5,16,128]{3,2,1,0:T(8,128)(2,1)S(1)}, u32[]{:S(2)}, u32[]{:S(2)}) %all-to-all-start.2) | async-done | bytes 655392 | tf_op jit(solution)/shard_map/all_to_all | solution.py:291
  68.1 2.2 %final_sum.1 = f32[128,16,128]{2,1,0:T(8,128)} custom-call(s32[32,128]{1,0:T(8,128)S(1)} %get-tuple-element.14.picks_ref, f32[128,16,128]{2,1,0:T(8,128)S(1)} %get-tuple-element.20.base_ref, bf16[16,16,128]{2,1,0:T(8,128)(2,1)S(1)} %collective-permute-done.1.halo_ref, bf16[160,16,128]{2,1,0:T(8,128)(2,1)S(1)} %bitcast.8), custom_call_target="tpu_custom_call" | custom-call | bytes 3145728 | tf_op jit(solution)/shard_map/final_sum/pallas_call | solution.py:372
  (1 shorter events, 0.0 us)
Async XLA Ops:
  0.0 39.6 %copy-start.2 = (s32[128,4]{0,1:T(4,128)S(1)}, s32[128,4]{0,1:T(4,128)}, u32[]{:S(2)}) copy-start(s32[128,4]{0,1:T(4,128)} %param.7) | copy-start | bytes 6148
  17.0 22.5 %all-to-all-start.1 = ((bf16[32,5,16,128]{3,2,1,0:T(8,128)(2,1)}), bf16[32,5,16,128]{3,2,1,0:T(8,128)(2,1)S(1)}, u32[]{:S(2)}, u32[]{:S(2)}) async-start(bf16[32,5,16,128]{3,2,1,0:T(8,128)(2,1)} %bitcast.3), calls=%async_computation.1 | async-start | bytes 1310720 | tf_op jit(solution)/shard_map/all_to_all | solution.py:291
  19.7 17.8 %collective-permute-start = (bf16[16,16,128]{2,1,0:T(8,128)(2,1)S(1)}, bf16[16,16,128]{2,1,0:T(8,128)(2,1)S(1)}, u32[]{:S(2)}, u32[]{:S(2)}) collective-permute-start(bf16[16,16,128]{2,1,0:T(8,128)(2,1)S(1)} %get-tuple-element.18), channel_id=1, source_target_pairs={{31,0},{0,1},{1,2},{2,3},{3,4},{4,5},{5,6},{6,7},{7,8},{8,9},{9,10... | collective-permute-start | bytes 196616 | tf_op jit(solution)/shard_map/ppermute | solution.py:30
  19.9 1.0 %copy-start = (bf16[128,16,128]{2,1,0:T(8,128)(2,1)S(1)}, bf16[128,16,128]{2,1,0:T(8,128)(2,1)}, u32[]{:S(2)}) copy-start(bf16[128,16,128]{2,1,0:T(8,128)(2,1)} %probe_ref.5) | copy-start | bytes 1572868
  20.9 0.7 copy-start.1
  46.3 21.8 %all-to-all-start.2 = ((bf16[32,5,16,128]{3,2,1,0:T(8,128)(2,1)}), bf16[32,5,16,128]{3,2,1,0:T(8,128)(2,1)S(1)}, u32[]{:S(2)}, u32[]{:S(2)}) async-start(bf16[32,5,16,128]{3,2,1,0:T(8,128)(2,1)} %bitcast.5), calls=%async_computation.2 | async-start | bytes 1310720 | tf_op jit(solution)/shard_map/all_to_all | solution.py:291
  56.2 7.2 %collective-permute-start.1 = (bf16[16,16,128]{2,1,0:T(8,128)(2,1)S(1)}, bf16[16,16,128]{2,1,0:T(8,128)(2,1)S(1)}, u32[]{:S(2)}, u32[]{:S(2)}) collective-permute-start(bf16[16,16,128]{2,1,0:T(8,128)(2,1)S(1)} %get-tuple-element.21), channel_id=1, source_target_pairs={{1,0},{2,1},{3,2},{4,3},{5,4},{6,5},{7,6},{8,7},{9,8},{10,9},{11,1... | collective-permute-start | bytes 196616 | tf_op jit(solution)/shard_map/ppermute | solution.py:30

commit v7 on v4

v7 whole, which is shorter than its diff:
```python
import functools

import jax
import jax.numpy as jnp
from jax import lax
from jax.experimental import pallas as pl
from jax.experimental.pallas import tpu as pltpu
from jax.sharding import PartitionSpec as P

REACH = 16
CHUNK = 16
AHEAD = 4
STORES = 4
VMEM = pl.BlockSpec(memory_space=pltpu.VMEM)
SMEM = pl.BlockSpec(memory_space=pltpu.SMEM)
HBM = pl.BlockSpec(memory_space=pl.ANY)
NT = (((1,), (1,)), ((), ()))


def params(mib):
    return pltpu.CompilerParams(vmem_limit_bytes=mib * 2**20)


def in_hbm(x):
    return pltpu.with_memory_space_constraint(x, pltpu.HBM)


def passed_along(block, axis, distance):
    size = lax.axis_size(axis)
    return lax.ppermute(block, axis, [((i - distance) % size, i) for i in range(size)])


def exchange_order(groups):
    return list(range(0, groups, 2)) + list(range(groups - 1, 0, -2))


def exchange_place(device, groups):
    return jnp.where(device % 2 == 0, device // 2, groups - 1 - device // 2)


def earlier_matrix(blocks):
    row = lax.broadcasted_iota(jnp.int32, (blocks, blocks), 0)
    col = lax.broadcasted_iota(jnp.int32, (blocks, blocks), 1)
    return (row < col).astype(jnp.float32).astype(jnp.bfloat16)


def ranks_in(mask, blocks):
    chosen = mask.astype(jnp.float32).astype(jnp.bfloat16)
    return jnp.dot(chosen, earlier_matrix(blocks), preferred_element_type=jnp.float32).astype(jnp.int32)


def prep_kernel(ids_ref, probe_ref, sent_ref, tail_ref, sem):
    blocks = probe_ref.shape[0]
    copy = pltpu.make_async_copy(probe_ref.at[pl.ds(blocks - REACH, REACH)], tail_ref, sem)
    copy.start()
    sent_ref[...] = jnp.broadcast_to(ids_ref[3:4, :], sent_ref.shape)
    copy.wait()


def pick_kernel(capacity, ids_ref, probe_ref, out_ref, picks_ref, probe, out, picks_smem, sems):
    groups, blocks = ids_ref.shape
    load = pltpu.make_async_copy(probe_ref, probe, sems.at[0])
    load.start()
    me = lax.axis_index("blk")
    local = ids_ref[...] - me * blocks
    mask = (local >= 0) & (local < blocks)
    rank = ranks_in(mask, blocks)
    lane = lax.broadcasted_iota(jnp.int32, (groups, blocks), 1)
    picks = jnp.zeros((groups, blocks), jnp.int32)
    for r in range(capacity):
        found = jnp.sum(jnp.where(mask & (rank == r), local + 1, 0), axis=1, keepdims=True)
        picks = jnp.where(lane == r, found, picks)
    picks_ref[...] = picks
    copy = pltpu.make_async_copy(picks_ref, picks_smem, sems.at[1])
    copy.start()
    copy.wait()
    load.wait()
    part = groups // STORES

    def store(p):
        rows = pl.ds(p * part * capacity, part * capacity)
        return pltpu.make_async_copy(out.at[rows], out_ref.at[rows], sems.at[2 + p])

    for p in range(STORES):

        @pl.loop(p * part, (p + 1) * part, unroll=8)
        def _(g):
            for r in range(capacity):
                out[g * capacity + r] = probe[jnp.maximum(picks_smem[g, r] - 1, 0)]

        store(p).start()
    for p in range(STORES):
        store(p).wait()


def stacked(mats):
    return mats.reshape(-1, mats.shape[-1])


def apart(left0, left1, mats):
    zero = jnp.zeros_like(left0)
    left = jnp.concatenate(
        [jnp.concatenate([left0, zero], axis=1), jnp.concatenate([zero, left1], axis=1)], axis=0
    )
    out = jnp.dot(left, mats, preferred_element_type=jnp.float32)
    return out.reshape((2,) + (left0.shape[0], mats.shape[1]))


def apart_back(lefts, mats):
    rows, half = lefts.shape[1], mats.shape[0] // 2
    out = lax.dot_general(lefts.reshape(2 * rows, lefts.shape[2]), mats, NT, preferred_element_type=jnp.float32)
    return out[:rows, :half], out[rows:, half:]


def near_place(ids_ref, k, i, first, count):
    place = ids_ref[k, i] - first + REACH
    return jnp.where(place >= count, place - count, place)


def near_forward_kernel(
    groups, capacity, ids_ref, ids_row_ref, halo_ref, probe_ref, coeffs_ref, prec_ref,
    out_ref, slot_ref, first_ref, back_ref, ext, coeffs, prec, back, sems
):
    blocks = probe_ref.shape[0]
    chunks = blocks // CHUNK

    def loads(c):
        own = pl.ds(c * CHUNK, CHUNK)
        return (
            pltpu.make_async_copy(coeffs_ref.at[own], coeffs.at[own], sems.at[0, c]),
            pltpu.make_async_copy(prec_ref.at[own], prec.at[own], sems.at[1, c]),
        )

    def store(c):
        own = pl.ds(c * CHUNK, CHUNK)
        return pltpu.make_async_copy(back.at[own], back_ref.at[own], sems.at[2, c])

    for c in range(chunks):
        for load in loads(c):
            load.start()
    ext[pl.ds(0, REACH)] = halo_ref[...]
    ext[pl.ds(REACH, blocks)] = probe_ref[...]
    owner = ids_row_ref[3:4, :] // blocks
    mask = lax.broadcasted_iota(jnp.int32, (groups, blocks), 0) == owner
    rank = jnp.sum(jnp.where(mask, ranks_in(mask, blocks), 0), axis=0, keepdims=True)
    slot_ref[...] = exchange_place(owner, groups) * capacity + rank
    first = lax.axis_index("blk") * blocks

    @pl.loop(0, chunks)
    def _(c):
        for load in loads(c):
            load.wait()
        for b in range(0, CHUNK, 2):
            i = c * CHUNK + b
            rows = []
            for j in range(2):
                tiles = [ext[near_place(ids_ref, k, i + j, first, groups * blocks)] for k in range(3)]
                rows.append(jnp.concatenate(tiles, axis=1))
            mats = [stacked(coeffs[i + j, pl.ds(0, 3)]) for j in range(2)]
            mixed = apart(rows[0], rows[1], jnp.concatenate(mats, axis=0))
            out_ref[pl.ds(i, 2)] = probe_ref[pl.ds(i, 2)].astype(jnp.float32) - mixed
            for j in range(2):
                folded = lax.dot_general(prec[i + j], coeffs[i + j, 3], NT, preferred_element_type=jnp.float32)
                back[i + j] = folded.astype(jnp.bfloat16)
        store(c).start()

    for c in range(chunks):
        store(c).wait()
    first_ref[0] = coeffs[pl.ds(0, CHUNK), 3]
    first_ref[1] = back[pl.ds(0, CHUNK)]


def far_kernel(
    slots_ref, part_ref, far_ref, first_ref, coeffs_ref, back_ref,
    white_ref, parcel_ref, coeffs, back, slot, sems
):
    blocks = part_ref.shape[0]
    chunks = blocks // CHUNK

    def loads(c):
        own = pl.ds(c * CHUNK, CHUNK)
        return (
            pltpu.make_async_copy(coeffs_ref.at[own, 3], coeffs.at[own], sems.at[0, c]),
            pltpu.make_async_copy(back_ref.at[own], back.at[own], sems.at[1, c]),
        )

    slot_copy = pltpu.make_async_copy(slots_ref, slot, sems.at[0, 0])
    slot_copy.start()
    for c in range(1, chunks):
        for load in loads(c):
            load.start()
    parcel_ref[...] = jnp.zeros_like(parcel_ref)
    slot_copy.wait()

    def mix(c, mats):
        for b in range(0, CHUNK, 2):
            i = c * CHUNK + b
            mixed = apart(far_ref[slot[0, i]], far_ref[slot[0, i + 1]], stacked(mats(c, b)))
            white_ref[pl.ds(i, 2)] = (part_ref[pl.ds(i, 2)] - mixed).astype(jnp.bfloat16)

    def send_back(c, mats):
        for b in range(0, CHUNK, 2):
            i = c * CHUNK + b
            terms = apart(white_ref[i], white_ref[i + 1], stacked(mats(c, b)))
            for j in range(2):
                parcel_ref[slot[0, i + j]] = terms[j].astype(jnp.bfloat16)

    def held(mats):
        return lambda c, b: mats[pl.ds(c * CHUNK + b, 2)]

    def ready(c):
        for load in loads(c):
            load.wait()

    mix(0, lambda c, b: first_ref[0, pl.ds(b, 2)])
    ready(1)
    send_back(0, lambda c, b: first_ref[1, pl.ds(b, 2)])
    mix(1, held(coeffs))

    @pl.loop(2, chunks)
    def _(c):
        ready(c)
        send_back(c - 1, held(back))
        mix(c, held(coeffs))

    send_back(chunks - 1, held(back))


def near_back_kernel(
    groups, ids_ref, white_ref, coeffs_ref, prec_ref, base_ref, halo_ref, total, scaled, coeffs, prec, sems
):
    blocks = white_ref.shape[0]
    points = white_ref.shape[2]
    chunks = blocks // CHUNK

    def load_prec(c):
        own = pl.ds(c * CHUNK, CHUNK)
        return pltpu.make_async_copy(prec_ref.at[own], prec.at[own], sems.at[1, c])

    def load_coeffs(c):
        own = pl.ds(c * CHUNK, CHUNK)
        return pltpu.make_async_copy(coeffs_ref.at[own, pl.ds(0, 3)], coeffs.at[own], sems.at[0, c])

    for c in range(chunks):
        load_prec(c).start()
        load_coeffs(c).start()
    total[pl.ds(0, REACH)] = jnp.zeros((REACH,) + total.shape[1:], jnp.float32)
    first = lax.axis_index("blk") * blocks

    def scale(c):
        load_prec(c).wait()
        for b in range(0, CHUNK, 2):
            i = c * CHUNK + b
            tiles = apart(white_ref[i], white_ref[i + 1], stacked(prec[pl.ds(i, 2)])).astype(jnp.bfloat16)
            scaled[pl.ds(i, 2)] = tiles
            total[pl.ds(REACH + i, 2)] = tiles.astype(jnp.float32)

    def back(c):
        load_coeffs(c).wait()
        terms = []
        for b in range(CHUNK + AHEAD):
            if b < CHUNK and b % 2 == 0:
                i = c * CHUNK + b
                terms.extend(apart_back(scaled[pl.ds(i, 2)], stacked(coeffs[pl.ds(i, 2)])))
            if b >= AHEAD:
                i = c * CHUNK + b - AHEAD
                places = [near_place(ids_ref, k, i, first, groups * blocks) for k in range(3)]
                olds = [total[place] for place in places]
                for k in range(3):
                    total[places[k]] = olds[k] - terms[b - AHEAD][:, k * points : (k + 1) * points]

    scale(0)

    @pl.loop(0, chunks - 1)
    def _(c):
        scale(c + 1)
        back(c)

    back(chunks - 1)
    halo_ref[...] = total[pl.ds(0, REACH)].astype(halo_ref.dtype)
    base_ref[...] = total[pl.ds(REACH, blocks)]


def sum_kernel(capacity, all_picks_ref, base_ref, halo_ref, back_ref, out_ref, total, picks_ref, sems):
    groups = all_picks_ref.shape[0]
    picks_copy = pltpu.make_async_copy(all_picks_ref, picks_ref, sems.at[0])
    picks_copy.start()
    blocks = base_ref.shape[0]
    total[pl.ds(0, blocks)] = base_ref[...]
    last = pl.ds(blocks - REACH, REACH)
    total[last] = total[last] + halo_ref[...].astype(jnp.float32)
    picks_copy.wait()

    @pl.loop(0, groups, unroll=8)
    def _(g):
        picks = [picks_ref[g, r] for r in range(capacity)]
        places = [jnp.where(pick > 0, pick - 1, blocks) for pick in picks]
        olds = [total[place] for place in places]
        for r in range(capacity):
            total[places[r]] = olds[r] - back_ref[g * capacity + r].astype(jnp.float32)

    store = pltpu.make_async_copy(total.at[pl.ds(0, blocks)], out_ref, sems.at[1])
    store.start()
    store.wait()


def per_device(probe_vecs, coeffs, cond_prec, neighbours):
    blocks, probes, points = probe_vecs.shape
    groups = lax.axis_size("blk")
    capacity = max(2, blocks // (groups - 1) + 1)
    slots = groups * capacity
    chunks = blocks // CHUNK
    bf16, f32 = jnp.bfloat16, jnp.float32
    tile = (probes, points)
    flops = 2 * blocks * probes * points * points

    def exchange(x):
        groups_of = [exchange_order(groups)]
        return lax.all_to_all(x, "blk", split_axis=0, concat_axis=0, tiled=True, axis_index_groups=groups_of)

    ids = neighbours.T
    sent_ids, tail = pl.pallas_call(
        prep_kernel,
        name="prep",
        out_shape=(
            jax.ShapeDtypeStruct((groups, blocks), jnp.int32),
            jax.ShapeDtypeStruct((REACH,) + tile, bf16),
        ),
        in_specs=[VMEM, HBM],
        out_specs=(VMEM, VMEM),
        scratch_shapes=[pltpu.SemaphoreType.DMA],
        compiler_params=params(8),
    )(ids, in_hbm(probe_vecs))
    halo = passed_along(tail, "blk", 1)
    all_ids = exchange(sent_ids)
    all_ids, halo = lax.optimization_barrier((all_ids, halo))
    outgoing, picks = pl.pallas_call(
        functools.partial(pick_kernel, capacity),
        name="pick_tiles",
        out_shape=(
            jax.ShapeDtypeStruct((slots,) + tile, bf16),
            jax.ShapeDtypeStruct((groups, blocks), jnp.int32),
        ),
        in_specs=[VMEM, HBM],
        out_specs=(HBM, VMEM),
        scratch_shapes=[
            pltpu.VMEM((blocks,) + tile, bf16),
            pltpu.VMEM((slots,) + tile, bf16),
            pltpu.SMEM((groups, blocks), jnp.int32),
            pltpu.SemaphoreType.DMA((2 + STORES,)),
        ],
        compiler_params=params(8),
        cost_estimate=pl.CostEstimate(flops=0, bytes_accessed=2 * slots * 4096, transcendentals=0),
    )(all_ids, in_hbm(probe_vecs))
    arrived = exchange(outgoing.reshape((groups, capacity) + tile)).reshape((slots,) + tile)
    mats = (blocks, points, points)
    part, slot_of, first_mats, back_mats = pl.pallas_call(
        functools.partial(near_forward_kernel, groups, capacity),
        name="near_forward",
        out_shape=(
            jax.ShapeDtypeStruct((blocks,) + tile, f32),
            jax.ShapeDtypeStruct((1, blocks), jnp.int32),
            jax.ShapeDtypeStruct((2, CHUNK, points, points), bf16),
            pltpu.HBM(mats, bf16),
        ),
        in_specs=[SMEM, VMEM, VMEM, VMEM, HBM, HBM],
        out_specs=(VMEM, VMEM, VMEM, HBM),
        scratch_shapes=[
            pltpu.VMEM((REACH + blocks,) + tile, bf16),
            pltpu.VMEM((blocks, 4, points, points), bf16),
            pltpu.VMEM(mats, bf16),
            pltpu.VMEM(mats, bf16),
            pltpu.SemaphoreType.DMA((3, chunks)),
        ],
        compiler_params=params(36),
        cost_estimate=pl.CostEstimate(flops=5 * flops, bytes_accessed=26 * 2**20, transcendentals=0),
    )(ids, ids, halo, probe_vecs, in_hbm(coeffs), in_hbm(cond_prec))
    white, parcel = pl.pallas_call(
        far_kernel,
        name="far_terms",
        out_shape=(
            jax.ShapeDtypeStruct((blocks,) + tile, bf16),
            jax.ShapeDtypeStruct((slots,) + tile, bf16),
        ),
        in_specs=[VMEM, VMEM, VMEM, VMEM, HBM, HBM],
        out_specs=(VMEM, VMEM),
        scratch_shapes=[
            pltpu.VMEM(mats, bf16),
            pltpu.VMEM(mats, bf16),
            pltpu.SMEM((1, blocks), jnp.int32),
            pltpu.SemaphoreType.DMA((2, chunks)),
        ],
        compiler_params=params(24),
        cost_estimate=pl.CostEstimate(flops=2 * flops, bytes_accessed=11 * 2**20, transcendentals=0),
    )(slot_of, part, arrived, first_mats, in_hbm(coeffs), in_hbm(back_mats))
    returned = exchange(parcel.reshape((groups, capacity) + tile)).reshape((slots,) + tile)
    base, halo_back = pl.pallas_call(
        functools.partial(near_back_kernel, groups),
        name="near_back",
        out_shape=(
            jax.ShapeDtypeStruct((blocks,) + tile, f32),
            jax.ShapeDtypeStruct((REACH,) + tile, bf16),
        ),
        in_specs=[SMEM, VMEM, HBM, HBM],
        out_specs=(VMEM, VMEM),
        scratch_shapes=[
            pltpu.VMEM((REACH + blocks,) + tile, f32),
            pltpu.VMEM((blocks,) + tile, bf16),
            pltpu.VMEM((blocks, 3, points, points), bf16),
            pltpu.VMEM(mats, bf16),
            pltpu.SemaphoreType.DMA((2, chunks)),
        ],
        compiler_params=params(28),
        cost_estimate=pl.CostEstimate(flops=4 * flops, bytes_accessed=18 * 2**20, transcendentals=0),
    )(ids, white, in_hbm(coeffs), in_hbm(cond_prec))
    halo_sum = passed_along(halo_back, "blk", -1)
    return pl.pallas_call(
        functools.partial(sum_kernel, capacity),
        name="final_sum",
        out_shape=jax.ShapeDtypeStruct((blocks,) + tile, f32),
        in_specs=[VMEM, VMEM, VMEM, VMEM],
        out_specs=HBM,
        scratch_shapes=[
            pltpu.VMEM((blocks + 1,) + tile, f32),
            pltpu.SMEM((groups, blocks), jnp.int32),
            pltpu.SemaphoreType.DMA((2,)),
        ],
        compiler_params=params(8),
        cost_estimate=pl.CostEstimate(flops=0, bytes_accessed=3 * 2**20, transcendentals=0),
    )(picks, base, halo_sum, returned)


def solution(mesh):
    in_specs = (
        P("blk", None, None),
        P("blk", None, None, None),
        P("blk", None, None),
        P("blk", None),
    )
    return jax.shard_map(
        per_device, mesh=mesh, in_specs=in_specs, out_specs=P("blk", None, None), check_vma=False
    )
```

time: 69.2 us -> 69.4 us (level)
  Pallas kernels: 23.7 us -> 29 us
  waiting for transfers between devices: 15.8 us -> 12.3 us
  local copies, waits for them, and re-layouts: 3.26 us -> 2.4 us
  starting transfers between devices: 11.8 us -> 11 us
    pallas_call x1, Pallas kernels: 5.67 us -> 10.4 us  [per_device(): pl.pallas_call(functools.partial(near_forward_kernel, groups, capacity),...]
    all_to_all x2, waiting for transfers between devices: 13.9 us -> 10.4 us  [exchange(): lax.all_to_all(x, 'blk', split_axis=0, concat_axis=0, tiled=True, axis_in...]
    pallas_call x1, Pallas kernels: 7.31 us -> 9.11 us  [per_device(): pl.pallas_call(functools.partial(near_back_kernel, groups), name='near_ba...]
    slice x2 -> x0, local copies, waits for them, and re-layouts: 1.53 us -> none  [the longest x1 0.84 us: per_device(): halo = passed_along(probe_vecs[blocks - REACH:], 'blk', 1)]
    pallas_call x1 -> x2, Pallas kernels: 6.52 us -> 5.38 us  [the longest x1 4.54 us: per_device(): pl.pallas_call(far_kernel, name='far_terms', out_shape=(jax.ShapeDtypeStr...]
    all_to_all x2, starting transfers between devices: 6.05 us -> 5.27 us  [exchange(): lax.all_to_all(x, 'blk', split_axis=0, concat_axis=0, tiled=True, axis_in...]
    unnamed x6 -> x8, local copies, waits for them, and re-layouts: 1.72 us -> 2.4 us
  transfers between devices with their start and end apart: 4 -> 4, of which waited for: 3 -> 3; matrix products, arithmetic and copies ran while one was open for 1% -> 0% of each run, Pallas kernels for 19% -> 28%
where the time goes in v7:
time: 69.4 us; the launch traced here: 68.9 us
  Pallas kernels  29 us (42%)
  blocking collectives  14 us (20%)
  waiting for transfers between devices  12.3 us (18%)
  starting transfers between devices  11 us (16%)
  local copies, waits for them, and re-layouts  2.4 us (3%)
    all_to_all x1, blocking collectives, exchange(): lax.all_to_all(x, 'blk', split_axis=0, concat_axis=0, tiled=True, axis_in...  14 us
    pallas_call x1, Pallas kernels, per_device(): pl.pallas_call(functools.partial(near_forward_kernel, groups, capacity),...  10.4 us
    all_to_all x2, waiting for transfers between devices, exchange(): lax.all_to_all(x, 'blk', split_axis=0, concat_axis=0, tiled=True, axis_in...  10.4 us
    pallas_call x1, Pallas kernels, per_device(): pl.pallas_call(functools.partial(near_back_kernel, groups), name='near_ba...  9.11 us
    ppermute x2, starting transfers between devices, passed_along(): lax.ppermute(block, axis, [((i - distance) % size, i) for i in range(size)])  5.78 us
    all_to_all x2, starting transfers between devices, exchange(): lax.all_to_all(x, 'blk', split_axis=0, concat_axis=0, tiled=True, axis_in...  5.27 us
    pallas_call x1, Pallas kernels, per_device(): pl.pallas_call(far_kernel, name='far_terms', out_shape=(jax.ShapeDtypeStr...  4.54 us
    unnamed x8, local copies, waits for them, and re-layouts  2.4 us
  transfers between devices with their start and end apart: 4, of which 3 were waited for; matrix products, arithmetic and copies ran while one was open for 0% of the time, Pallas kernels for 28%

profile of v7, /device:TPU:0, one launch (start us, length us, event | category | flops | bytes accessed | tf_op | source)
XLA Modules:
  0.0 68.9 jit_solution(10094726658156507257)
XLA Ops:
  0.0 0.0 copy-start.1
  0.0 0.7 copy-done.1
  0.7 0.8 %prep.1 = (s32[32,128]{1,0:T(8,128)S(1)}, bf16[16,16,128]{2,1,0:T(8,128)(2,1)S(1)}) custom-call(s32[4,128]{1,0:T(4,128)S(1)} %bitcast.12, bf16[128,16,128]{2,1,0:T(8,128)(2,1)} %probe_ref.5), custom_call_target="tpu_custom_call" | custom-call | tf_op jit(solution)/shard_map/prep/pallas_call | solution.py:322
  1.5 0.5 collective-permute-start
  2.0 14.0 %all_to_all.22 = s32[32,1,128]{2,1,0:T(1,128)S(1)} all-to-all(s32[32,1,128]{2,1,0:T(1,128)S(1)} %bitcast.16), channel_id=1, replica_groups={{0,2,4,6,8,10,12,14,16,18,20,22,24,26,28,30,31,29,27,25,23,21,19,17,15,..., dimensions={0} | all-to-all | bytes 32768 | tf_op jit(solution)/shard_map/all_to_all | solution.py:319
  16.1 0.0 collective-permute-done.halo_ref
  16.1 2.0 %pick_tiles.1 = (bf16[160,16,128]{2,1,0:T(8,128)(2,1)}, s32[32,128]{1,0:T(8,128)S(1)}) custom-call(s32[32,128]{1,0:T(8,128)S(1)} %bitcast.11, bf16[128,16,128]{2,1,0:T(8,128)(2,1)} %probe_ref.5), custom_call_target="tpu_custom_call" | custom-call | bytes 1310720 | tf_op jit(solution)/shard_map/pick_tiles/pallas_call | solution.py:337
  18.1 2.6 %all-to-all-start.1 = ((bf16[32,5,16,128]{3,2,1,0:T(8,128)(2,1)}), bf16[32,5,16,128]{3,2,1,0:T(8,128)(2,1)S(1)}, u32[]{:S(2)}, u32[]{:S(2)}) async-start(bf16[32,5,16,128]{3,2,1,0:T(8,128)(2,1)} %bitcast.4), calls=%async_computation.1 | async-start | bytes 1310720 | tf_op jit(solution)/shard_map/all_to_all | solution.py:319
  20.8 0.0 copy-start
  20.8 1.0 %copy-done = bf16[128,16,128]{2,1,0:T(8,128)(2,1)S(1)} copy-done((bf16[128,16,128]{2,1,0:T(8,128)(2,1)S(1)}, bf16[128,16,128]{2,1,0:T(8,128)(2,1)}, u32[]{:S(2)}) %copy-start) | copy-done | bytes 524312
  21.8 0.0 copy-start.2
  21.8 0.7 copy-done.2
  22.5 10.4 %near_forward.1 = (f32[128,16,128]{2,1,0:T(8,128)S(1)}, s32[1,128]{1,0:T(1,128)S(1)}, bf16[2,16,128,128]{3,2,1,0:T(8,128)(2,1)S(1)}, bf16[128,128,128]{2,1,0:T(8,128)(2,1)}) custom-call(s32[4,128]{1,0:T(4,128)S(1)} %bitcast.13, s32[4,128]{1,0:T(4,128)S(1)} %bitcast.14, bf16[16,16,128]{2,1,0:T(8,128)(2,1)S(1)} %collective-permute-done.halo_ref, ...), custom_call_target="tpu_custom_call" | custom-call | flops 335544320 | bytes 27262976 | tf_op jit(solution)/shard_map/near_forward/pallas_call | solution.py:357
  32.9 7.3 %all-to-all-done.1 = bf16[32,5,16,128]{3,2,1,0:T(8,128)(2,1)S(1)} async-done(((bf16[32,5,16,128]{3,2,1,0:T(8,128)(2,1)}), bf16[32,5,16,128]{3,2,1,0:T(8,128)(2,1)S(1)}, u32[]{:S(2)}, u32[]{:S(2)}) %all-to-all-start.1) | async-done | bytes 655392 | tf_op jit(solution)/shard_map/all_to_all | solution.py:319
  40.2 0.0 copy-start.3
  40.2 4.5 %far_terms.1 = (bf16[128,16,128]{2,1,0:T(8,128)(2,1)S(1)}, bf16[160,16,128]{2,1,0:T(8,128)(2,1)}) custom-call(s32[1,128]{1,0:T(1,128)S(1)} %get-tuple-element.24.slots_ref, f32[128,16,128]{2,1,0:T(8,128)S(1)} %get-tuple-element.25.part_ref, bf16[160,16,128]{2,1,0:T(8,128)(2,1)S(1)} %bitcast.9, bf16[2,16,128,128]{3,2,1,0:T(8,128)(2,1)S(1)} %get-tuple-element.27.first_ref, ...), custom_call_target="tpu_custom_call" | custom-call | flops 134217728 | bytes 11534336 | tf_op jit(solution)/shard_map/far_terms/pallas_call | solution.py:378
  44.7 2.6 %all-to-all-start.2 = ((bf16[32,5,16,128]{3,2,1,0:T(8,128)(2,1)}), bf16[32,5,16,128]{3,2,1,0:T(8,128)(2,1)S(1)}, u32[]{:S(2)}, u32[]{:S(2)}) async-start(bf16[32,5,16,128]{3,2,1,0:T(8,128)(2,1)} %bitcast.6), calls=%async_computation.2 | async-start | bytes 1310720 | tf_op jit(solution)/shard_map/all_to_all | solution.py:319
  47.4 0.0 copy-done.3
  47.4 9.1 %near_back.1 = (f32[128,16,128]{2,1,0:T(8,128)S(1)}, bf16[16,16,128]{2,1,0:T(8,128)(2,1)S(1)}) custom-call(s32[4,128]{1,0:T(4,128)S(1)} %bitcast.15, bf16[128,16,128]{2,1,0:T(8,128)(2,1)S(1)} %get-tuple-element.29.white_ref, bf16[128,4,128,128]{3,2,1,0:T(8,128)(2,1)} %coeffs_ref.5, bf16[128,128,128]{2,1,0:T(8,128)(2,1)} %prec_ref.3), custom_call_target="tpu_custom_call" | custom-call | flops 268435456 | bytes 18874368 | tf_op jit(solution)/shard_map/near_back/pallas_call | solution.py:397
  56.5 5.3 %collective-permute-start.1 = (bf16[16,16,128]{2,1,0:T(8,128)(2,1)S(1)}, bf16[16,16,128]{2,1,0:T(8,128)(2,1)S(1)}, u32[]{:S(2)}, u32[]{:S(2)}) collective-permute-start(bf16[16,16,128]{2,1,0:T(8,128)(2,1)S(1)} %get-tuple-element.31), channel_id=1, source_target_pairs={{1,0},{2,1},{3,2},{4,3},{5,4},{6,5},{7,6},{8,7},{9,8},{10,9},{11,1... | collective-permute-start | bytes 196616 | tf_op jit(solution)/shard_map/ppermute | solution.py:30
  61.8 1.9 %collective-permute-done.1.halo_ref = bf16[16,16,128]{2,1,0:T(8,128)(2,1)S(1)} collective-permute-done((bf16[16,16,128]{2,1,0:T(8,128)(2,1)S(1)}, bf16[16,16,128]{2,1,0:T(8,128)(2,1)S(1)}, u32[]{:S(2)}, u32[]{:S(2)}) %collective-permute-start.1) | collective-permute-done | bytes 65568 | tf_op jit(solution)/shard_map/ppermute | solution.py:30
  63.7 3.1 %all-to-all-done.2 = bf16[32,5,16,128]{3,2,1,0:T(8,128)(2,1)S(1)} async-done(((bf16[32,5,16,128]{3,2,1,0:T(8,128)(2,1)}), bf16[32,5,16,128]{3,2,1,0:T(8,128)(2,1)S(1)}, u32[]{:S(2)}, u32[]{:S(2)}) %all-to-all-start.2) | async-done | bytes 655392 | tf_op jit(solution)/shard_map/all_to_all | solution.py:319
  66.8 2.1 %final_sum.1 = f32[128,16,128]{2,1,0:T(8,128)} custom-call(s32[32,128]{1,0:T(8,128)S(1)} %get-tuple-element.22.all_picks_ref, f32[128,16,128]{2,1,0:T(8,128)S(1)} %get-tuple-element.30.base_ref, bf16[16,16,128]{2,1,0:T(8,128)(2,1)S(1)} %collective-permute-done.1.halo_ref, bf16[160,16,128]{2,1,0:T(8,128)(2,1)S(1)} %bitcast.10), custom_call_target="tpu_custom_call" | custom-call | bytes 3145728 | tf_op jit(solution)/shard_map/final_sum/pallas_call | solution.py:417
Async XLA Ops:
  0.0 0.7 copy-start.1
  1.5 14.6 %collective-permute-start = (bf16[16,16,128]{2,1,0:T(8,128)(2,1)S(1)}, bf16[16,16,128]{2,1,0:T(8,128)(2,1)S(1)}, u32[]{:S(2)}, u32[]{:S(2)}) collective-permute-start(bf16[16,16,128]{2,1,0:T(8,128)(2,1)S(1)} %get-tuple-element.20), channel_id=1, source_target_pairs={{31,0},{0,1},{1,2},{2,3},{3,4},{4,5},{5,6},{6,7},{7,8},{8,9},{9,10... | collective-permute-start | bytes 196616 | tf_op jit(solution)/shard_map/ppermute | solution.py:30
  18.1 22.1 %all-to-all-start.1 = ((bf16[32,5,16,128]{3,2,1,0:T(8,128)(2,1)}), bf16[32,5,16,128]{3,2,1,0:T(8,128)(2,1)S(1)}, u32[]{:S(2)}, u32[]{:S(2)}) async-start(bf16[32,5,16,128]{3,2,1,0:T(8,128)(2,1)} %bitcast.4), calls=%async_computation.1 | async-start | bytes 1310720 | tf_op jit(solution)/shard_map/all_to_all | solution.py:319
  20.8 1.0 %copy-start = (bf16[128,16,128]{2,1,0:T(8,128)(2,1)S(1)}, bf16[128,16,128]{2,1,0:T(8,128)(2,1)}, u32[]{:S(2)}) copy-start(bf16[128,16,128]{2,1,0:T(8,128)(2,1)} %probe_ref.5) | copy-start | bytes 1572868
  21.8 0.7 copy-start.2
  40.2 7.2 %copy-start.3 = (s32[128,4]{0,1:T(4,128)S(1)}, s32[128,4]{0,1:T(4,128)}, u32[]{:S(2)}) copy-start(s32[128,4]{0,1:T(4,128)} %param.7) | copy-start | bytes 6148
  44.7 22.1 %all-to-all-start.2 = ((bf16[32,5,16,128]{3,2,1,0:T(8,128)(2,1)}), bf16[32,5,16,128]{3,2,1,0:T(8,128)(2,1)S(1)}, u32[]{:S(2)}, u32[]{:S(2)}) async-start(bf16[32,5,16,128]{3,2,1,0:T(8,128)(2,1)} %bitcast.6), calls=%async_computation.2 | async-start | bytes 1310720 | tf_op jit(solution)/shard_map/all_to_all | solution.py:319
  56.5 7.2 %collective-permute-start.1 = (bf16[16,16,128]{2,1,0:T(8,128)(2,1)S(1)}, bf16[16,16,128]{2,1,0:T(8,128)(2,1)S(1)}, u32[]{:S(2)}, u32[]{:S(2)}) collective-permute-start(bf16[16,16,128]{2,1,0:T(8,128)(2,1)S(1)} %get-tuple-element.31), channel_id=1, source_target_pairs={{1,0},{2,1},{3,2},{4,3},{5,4},{6,5},{7,6},{8,7},{9,8},{10,9},{11,1... | collective-permute-start | bytes 196616 | tf_op jit(solution)/shard_map/ppermute | solution.py:30

commit v8 on v7

--- a/solution.py
+++ b/solution.py
@@ -28,14 +28,6 @@
 def passed_along(block, axis, distance):
     size = lax.axis_size(axis)
     return lax.ppermute(block, axis, [((i - distance) % size, i) for i in range(size)])
-
-
-def exchange_order(groups):
-    return list(range(0, groups, 2)) + list(range(groups - 1, 0, -2))
-
-
-def exchange_place(device, groups):
-    return jnp.where(device % 2 == 0, device // 2, groups - 1 - device // 2)
 
 
 def earlier_matrix(blocks):
@@ -143,7 +135,7 @@
     owner = ids_row_ref[3:4, :] // blocks
     mask = lax.broadcasted_iota(jnp.int32, (groups, blocks), 0) == owner
     rank = jnp.sum(jnp.where(mask, ranks_in(mask, blocks), 0), axis=0, keepdims=True)
-    slot_ref[...] = exchange_place(owner, groups) * capacity + rank
+    slot_ref[...] = owner * capacity + rank
     first = lax.axis_index("blk") * blocks
 
     @pl.loop(0, chunks)
@@ -177,18 +169,21 @@
     blocks = part_ref.shape[0]
     chunks = blocks // CHUNK
 
-    def loads(c):
-        own = pl.ds(c * CHUNK, CHUNK)
-        return (
-            pltpu.make_async_copy(coeffs_ref.at[own, 3], coeffs.at[own], sems.at[0, c]),
-            pltpu.make_async_copy(back_ref.at[own], back.at[own], sems.at[1, c]),
-        )
+    def load_coeffs(c):
+        own = pl.ds(c * CHUNK, CHUNK)
+        return pltpu.make_async_copy(coeffs_ref.at[own, 3], coeffs.at[own], sems.at[0, c])
+
+    def load_back(c):
+        own = pl.ds(c * CHUNK, CHUNK)
+        return pltpu.make_async_copy(back_ref.at[own], back.at[own], sems.at[1, c])
 
     slot_copy = pltpu.make_async_copy(slots_ref, slot, sems.at[0, 0])
     slot_copy.start()
-    for c in range(1, chunks):
-        for load in loads(c):
-            load.start()
+    for c in range(1, chunks + 2):
+        if c < chunks:
+            load_coeffs(c).start()
+        if c >= 3:
+            load_back(c - 2).start()
     parcel_ref[...] = jnp.zeros_like(parcel_ref)
     slot_copy.wait()
 
@@ -208,22 +203,23 @@
     def held(mats):
         return lambda c, b: mats[pl.ds(c * CHUNK + b, 2)]
 
-    def ready(c):
-        for load in loads(c):
-            load.wait()
-
     mix(0, lambda c, b: first_ref[0, pl.ds(b, 2)])
-    ready(1)
+    load_coeffs(1).wait()
     send_back(0, lambda c, b: first_ref[1, pl.ds(b, 2)])
     mix(1, held(coeffs))
-
-    @pl.loop(2, chunks)
+    load_coeffs(2).wait()
+    mix(2, held(coeffs))
+
+    @pl.loop(3, chunks)
     def _(c):
-        ready(c)
-        send_back(c - 1, held(back))
+        load_coeffs(c).wait()
+        load_back(c - 2).wait()
+        send_back(c - 2, held(back))
         mix(c, held(coeffs))
 
-    send_back(chunks - 1, held(back))
+    for c in (chunks - 2, chunks - 1):
+        load_back(c).wait()
+        send_back(c, held(back))
 
 
 def near_back_kernel(
@@ -315,8 +311,7 @@
     flops = 2 * blocks * probes * points * points
 
     def exchange(x):
-        groups_of = [exchange_order(groups)]
-        return lax.all_to_all(x, "blk", split_axis=0, concat_axis=0, tiled=True, axis_index_groups=groups_of)
+        return lax.all_to_all(x, "blk", split_axis=0, concat_axis=0, tiled=True)
 
     ids = neighbours.T
     sent_ids, tail = pl.pallas_call(
@@ -330,7 +325,7 @@
         out_specs=(VMEM, VMEM),
         scratch_shapes=[pltpu.SemaphoreType.DMA],
         compiler_params=params(8),
-    )(ids, in_hbm(probe_vecs))
+    )(in_hbm(ids), in_hbm(probe_vecs))
     halo = passed_along(tail, "blk", 1)
     all_ids = exchange(sent_ids)
     all_ids, halo = lax.optimization_barrier((all_ids, halo))

time: 69.4 us -> 67.1 us (0.967)
  waiting for transfers between devices: 12.3 us -> 9.3 us
  starting transfers between devices: 11 us -> 11.8 us
    all_to_all x2, waiting for transfers between devices: 10.4 us -> 7.39 us  [exchange(): return lax.all_to_all(x, 'blk', split_axis=0, concat_axis=0, tiled=True)]
    all_to_all x2, starting transfers between devices: 5.27 us -> 6.05 us  [exchange(): return lax.all_to_all(x, 'blk', split_axis=0, concat_axis=0, tiled=True)]
    unnamed x8 -> x6, local copies, waits for them, and re-layouts: 2.4 us -> 1.72 us
  transfers between devices with their start and end apart: 4 -> 4, of which waited for: 3 -> 3; matrix products, arithmetic and copies ran while one was open for 0% -> 0% of each run, Pallas kernels for 28% -> 29%
where the time goes in v8:
time: 67.1 us; the launch traced here: 66.6 us
  Pallas kernels  29.6 us (44%)
  blocking collectives  14.1 us (21%)
  starting transfers between devices  11.8 us (18%)
  waiting for transfers between devices  9.3 us (14%)
  local copies, waits for them, and re-layouts  1.72 us (3%)
    all_to_all x1, blocking collectives, exchange(): return lax.all_to_all(x, 'blk', split_axis=0, concat_axis=0, tiled=True)  14.1 us
    pallas_call x1, Pallas kernels, per_device(): pl.pallas_call(functools.partial(near_forward_kernel, groups, capacity),...  10.4 us
    pallas_call x1, Pallas kernels, per_device(): pl.pallas_call(functools.partial(near_back_kernel, groups), name='near_ba...  9.11 us
    all_to_all x2, waiting for transfers between devices, exchange(): return lax.all_to_all(x, 'blk', split_axis=0, concat_axis=0, tiled=True)  7.39 us
    all_to_all x2, starting transfers between devices, exchange(): return lax.all_to_all(x, 'blk', split_axis=0, concat_axis=0, tiled=True)  6.05 us
    ppermute x2, starting transfers between devices, passed_along(): lax.ppermute(block, axis, [((i - distance) % size, i) for i in range(size)])  5.78 us
    pallas_call x1, Pallas kernels, per_device(): pl.pallas_call(far_kernel, name='far_terms', out_shape=(jax.ShapeDtypeStr...  4.46 us
    pallas_call x1, Pallas kernels, per_device(): pl.pallas_call(functools.partial(sum_kernel, capacity), name='final_sum',...  2.1 us
  transfers between devices with their start and end apart: 4, of which 3 were waited for; matrix products, arithmetic and copies ran while one was open for 0% of the time, Pallas kernels for 29%

profile of v8, /device:TPU:0, one launch (start us, length us, event | category | flops | bytes accessed | tf_op | source)
XLA Modules:
  0.0 66.6 jit_solution(5408224118124800430)
XLA Ops:
  0.0 1.5 %prep.1 = (s32[32,128]{1,0:T(8,128)S(1)}, bf16[16,16,128]{2,1,0:T(8,128)(2,1)S(1)}) custom-call(s32[4,128]{1,0:T(4,128)} %bitcast.12, bf16[128,16,128]{2,1,0:T(8,128)(2,1)} %probe_ref.5), custom_call_target="tpu_custom_call" | custom-call | tf_op jit(solution)/shard_map/prep/pallas_call | solution.py:317
  1.5 0.5 collective-permute-start
  2.0 14.1 %all_to_all.22 = s32[32,1,128]{2,1,0:T(1,128)S(1)} all-to-all(s32[32,1,128]{2,1,0:T(1,128)S(1)} %bitcast.16), channel_id=1, replica_groups=mesh['blk'=32] {'blk'}, dimensions={0} | all-to-all | bytes 32768 | tf_op jit(solution)/shard_map/all_to_all | solution.py:314
  16.1 0.0 collective-permute-done.halo_ref
  16.1 2.0 %pick_tiles.1 = (bf16[160,16,128]{2,1,0:T(8,128)(2,1)}, s32[32,128]{1,0:T(8,128)S(1)}) custom-call(s32[32,128]{1,0:T(8,128)S(1)} %bitcast.11, bf16[128,16,128]{2,1,0:T(8,128)(2,1)} %probe_ref.5), custom_call_target="tpu_custom_call" | custom-call | bytes 1310720 | tf_op jit(solution)/shard_map/pick_tiles/pallas_call | solution.py:332
  18.2 2.6 %all-to-all-start.1 = ((bf16[32,5,16,128]{3,2,1,0:T(8,128)(2,1)}), bf16[32,5,16,128]{3,2,1,0:T(8,128)(2,1)S(1)}, u32[]{:S(2)}, u32[]{:S(2)}) async-start(bf16[32,5,16,128]{3,2,1,0:T(8,128)(2,1)} %bitcast.4), calls=%async_computation.1 | async-start | bytes 1310720 | tf_op jit(solution)/shard_map/all_to_all | solution.py:314
  20.8 0.0 copy-start
  20.8 1.0 %copy-done = bf16[128,16,128]{2,1,0:T(8,128)(2,1)S(1)} copy-done((bf16[128,16,128]{2,1,0:T(8,128)(2,1)S(1)}, bf16[128,16,128]{2,1,0:T(8,128)(2,1)}, u32[]{:S(2)}) %copy-start) | copy-done | bytes 524312
  21.9 0.0 copy-start.1
  21.9 0.7 %copy-done.1 = s32[128,4]{0,1:T(4,128)S(1)} copy-done((s32[128,4]{0,1:T(4,128)S(1)}, s32[128,4]{0,1:T(4,128)}, u32[]{:S(2)}) %copy-start.1) | copy-done | bytes 2072
  22.5 10.4 %near_forward.1 = (f32[128,16,128]{2,1,0:T(8,128)S(1)}, s32[1,128]{1,0:T(1,128)S(1)}, bf16[2,16,128,128]{3,2,1,0:T(8,128)(2,1)S(1)}, bf16[128,128,128]{2,1,0:T(8,128)(2,1)}) custom-call(s32[4,128]{1,0:T(4,128)S(1)} %bitcast.13, s32[4,128]{1,0:T(4,128)S(1)} %bitcast.14, bf16[16,16,128]{2,1,0:T(8,128)(2,1)S(1)} %collective-permute-done.halo_ref, ...), custom_call_target="tpu_custom_call" | custom-call | flops 335544320 | bytes 27262976 | tf_op jit(solution)/shard_map/near_forward/pallas_call | solution.py:352
  32.9 5.8 %all-to-all-done.1 = bf16[32,5,16,128]{3,2,1,0:T(8,128)(2,1)S(1)} async-done(((bf16[32,5,16,128]{3,2,1,0:T(8,128)(2,1)}), bf16[32,5,16,128]{3,2,1,0:T(8,128)(2,1)S(1)}, u32[]{:S(2)}, u32[]{:S(2)}) %all-to-all-start.1) | async-done | bytes 655392 | tf_op jit(solution)/shard_map/all_to_all | solution.py:314
  38.7 0.0 copy-start.2
  38.7 4.5 %far_terms.1 = (bf16[128,16,128]{2,1,0:T(8,128)(2,1)S(1)}, bf16[160,16,128]{2,1,0:T(8,128)(2,1)}) custom-call(s32[1,128]{1,0:T(1,128)S(1)} %get-tuple-element.24.slots_ref, f32[128,16,128]{2,1,0:T(8,128)S(1)} %get-tuple-element.25.part_ref, bf16[160,16,128]{2,1,0:T(8,128)(2,1)S(1)} %bitcast.9, bf16[2,16,128,128]{3,2,1,0:T(8,128)(2,1)S(1)} %get-tuple-element.27.first_ref, ...), custom_call_target="tpu_custom_call" | custom-call | flops 134217728 | bytes 11534336 | tf_op jit(solution)/shard_map/far_terms/pallas_call | solution.py:373
  43.2 3.4 %all-to-all-start.2 = ((bf16[32,5,16,128]{3,2,1,0:T(8,128)(2,1)}), bf16[32,5,16,128]{3,2,1,0:T(8,128)(2,1)S(1)}, u32[]{:S(2)}, u32[]{:S(2)}) async-start(bf16[32,5,16,128]{3,2,1,0:T(8,128)(2,1)} %bitcast.6), calls=%async_computation.2 | async-start | bytes 1310720 | tf_op jit(solution)/shard_map/all_to_all | solution.py:314
  46.6 0.0 copy-done.2
  46.6 9.1 %near_back.1 = (f32[128,16,128]{2,1,0:T(8,128)S(1)}, bf16[16,16,128]{2,1,0:T(8,128)(2,1)S(1)}) custom-call(s32[4,128]{1,0:T(4,128)S(1)} %bitcast.15, bf16[128,16,128]{2,1,0:T(8,128)(2,1)S(1)} %get-tuple-element.29.white_ref, bf16[128,4,128,128]{3,2,1,0:T(8,128)(2,1)} %coeffs_ref.5, bf16[128,128,128]{2,1,0:T(8,128)(2,1)} %prec_ref.3), custom_call_target="tpu_custom_call" | custom-call | flops 268435456 | bytes 18874368 | tf_op jit(solution)/shard_map/near_back/pallas_call | solution.py:392
  55.7 5.3 %collective-permute-start.1 = (bf16[16,16,128]{2,1,0:T(8,128)(2,1)S(1)}, bf16[16,16,128]{2,1,0:T(8,128)(2,1)S(1)}, u32[]{:S(2)}, u32[]{:S(2)}) collective-permute-start(bf16[16,16,128]{2,1,0:T(8,128)(2,1)S(1)} %get-tuple-element.31), channel_id=1, source_target_pairs={{1,0},{2,1},{3,2},{4,3},{5,4},{6,5},{7,6},{8,7},{9,8},{10,9},{11,1... | collective-permute-start | bytes 196616 | tf_op jit(solution)/shard_map/ppermute | solution.py:30
  61.0 1.9 %collective-permute-done.1.halo_ref = bf16[16,16,128]{2,1,0:T(8,128)(2,1)S(1)} collective-permute-done((bf16[16,16,128]{2,1,0:T(8,128)(2,1)S(1)}, bf16[16,16,128]{2,1,0:T(8,128)(2,1)S(1)}, u32[]{:S(2)}, u32[]{:S(2)}) %collective-permute-start.1) | collective-permute-done | bytes 65568 | tf_op jit(solution)/shard_map/ppermute | solution.py:30
  62.9 1.6 %all-to-all-done.2 = bf16[32,5,16,128]{3,2,1,0:T(8,128)(2,1)S(1)} async-done(((bf16[32,5,16,128]{3,2,1,0:T(8,128)(2,1)}), bf16[32,5,16,128]{3,2,1,0:T(8,128)(2,1)S(1)}, u32[]{:S(2)}, u32[]{:S(2)}) %all-to-all-start.2) | async-done | bytes 655392 | tf_op jit(solution)/shard_map/all_to_all | solution.py:314
  64.5 2.1 %final_sum.1 = f32[128,16,128]{2,1,0:T(8,128)} custom-call(s32[32,128]{1,0:T(8,128)S(1)} %get-tuple-element.22.all_picks_ref, f32[128,16,128]{2,1,0:T(8,128)S(1)} %get-tuple-element.30.base_ref, bf16[16,16,128]{2,1,0:T(8,128)(2,1)S(1)} %collective-permute-done.1.halo_ref, bf16[160,16,128]{2,1,0:T(8,128)(2,1)S(1)} %bitcast.10), custom_call_target="tpu_custom_call" | custom-call | bytes 3145728 | tf_op jit(solution)/shard_map/final_sum/pallas_call | solution.py:412
Async XLA Ops:
  1.5 14.6 %collective-permute-start = (bf16[16,16,128]{2,1,0:T(8,128)(2,1)S(1)}, bf16[16,16,128]{2,1,0:T(8,128)(2,1)S(1)}, u32[]{:S(2)}, u32[]{:S(2)}) collective-permute-start(bf16[16,16,128]{2,1,0:T(8,128)(2,1)S(1)} %get-tuple-element.20), channel_id=1, source_target_pairs={{31,0},{0,1},{1,2},{2,3},{3,4},{4,5},{5,6},{6,7},{7,8},{8,9},{9,10... | collective-permute-start | bytes 196616 | tf_op jit(solution)/shard_map/ppermute | solution.py:30
  18.2 20.6 %all-to-all-start.1 = ((bf16[32,5,16,128]{3,2,1,0:T(8,128)(2,1)}), bf16[32,5,16,128]{3,2,1,0:T(8,128)(2,1)S(1)}, u32[]{:S(2)}, u32[]{:S(2)}) async-start(bf16[32,5,16,128]{3,2,1,0:T(8,128)(2,1)} %bitcast.4), calls=%async_computation.1 | async-start | bytes 1310720 | tf_op jit(solution)/shard_map/all_to_all | solution.py:314
  20.8 1.0 %copy-start = (bf16[128,16,128]{2,1,0:T(8,128)(2,1)S(1)}, bf16[128,16,128]{2,1,0:T(8,128)(2,1)}, u32[]{:S(2)}) copy-start(bf16[128,16,128]{2,1,0:T(8,128)(2,1)} %probe_ref.5) | copy-start | bytes 1572868
  21.9 0.7 %copy-start.1 = (s32[128,4]{0,1:T(4,128)S(1)}, s32[128,4]{0,1:T(4,128)}, u32[]{:S(2)}) copy-start(s32[128,4]{0,1:T(4,128)} %param.7) | copy-start | bytes 6148
  38.7 7.9 %copy-start.2 = (s32[128,4]{0,1:T(4,128)S(1)}, s32[128,4]{0,1:T(4,128)}, u32[]{:S(2)}) copy-start(s32[128,4]{0,1:T(4,128)} %param.7) | copy-start | bytes 6148
  43.2 21.3 %all-to-all-start.2 = ((bf16[32,5,16,128]{3,2,1,0:T(8,128)(2,1)}), bf16[32,5,16,128]{3,2,1,0:T(8,128)(2,1)S(1)}, u32[]{:S(2)}, u32[]{:S(2)}) async-start(bf16[32,5,16,128]{3,2,1,0:T(8,128)(2,1)} %bitcast.6), calls=%async_computation.2 | async-start | bytes 1310720 | tf_op jit(solution)/shard_map/all_to_all | solution.py:314
  55.7 7.2 %collective-permute-start.1 = (bf16[16,16,128]{2,1,0:T(8,128)(2,1)S(1)}, bf16[16,16,128]{2,1,0:T(8,128)(2,1)S(1)}, u32[]{:S(2)}, u32[]{:S(2)}) collective-permute-start(bf16[16,16,128]{2,1,0:T(8,128)(2,1)S(1)} %get-tuple-element.31), channel_id=1, source_target_pairs={{1,0},{2,1},{3,2},{4,3},{5,4},{6,5},{7,6},{8,7},{9,8},{10,9},{11,1... | collective-permute-start | bytes 196616 | tf_op jit(solution)/shard_map/ppermute | solution.py:30

commit v9 on v8

v9 whole, which is shorter than its diff:
```python
import functools

import jax
import jax.numpy as jnp
from jax import lax
from jax.experimental import pallas as pl
from jax.experimental.pallas import tpu as pltpu
from jax.sharding import PartitionSpec as P

REACH = 16
CHUNK = 16
AHEAD = 4
HELD = 3
STORES = 4
VMEM = pl.BlockSpec(memory_space=pltpu.VMEM)
SMEM = pl.BlockSpec(memory_space=pltpu.SMEM)
HBM = pl.BlockSpec(memory_space=pl.ANY)
NT = (((1,), (1,)), ((), ()))


def params(mib):
    return pltpu.CompilerParams(vmem_limit_bytes=mib * 2**20)


def in_hbm(x):
    return pltpu.with_memory_space_constraint(x, pltpu.HBM)


def passed_along(block, axis, distance):
    size = lax.axis_size(axis)
    return lax.ppermute(block, axis, [((i - distance) % size, i) for i in range(size)])


def earlier_matrix(blocks):
    row = lax.broadcasted_iota(jnp.int32, (blocks, blocks), 0)
    col = lax.broadcasted_iota(jnp.int32, (blocks, blocks), 1)
    return (row < col).astype(jnp.float32).astype(jnp.bfloat16)


def ranks_in(mask, blocks):
    chosen = mask.astype(jnp.float32).astype(jnp.bfloat16)
    return jnp.dot(chosen, earlier_matrix(blocks), preferred_element_type=jnp.float32).astype(jnp.int32)


def prep_kernel(ids_ref, probe_ref, sent_ref, tail_ref, ids, sems):
    blocks = probe_ref.shape[0]
    ids_copy = pltpu.make_async_copy(ids_ref, ids, sems.at[0])
    tail_copy = pltpu.make_async_copy(probe_ref.at[pl.ds(blocks - REACH, REACH)], tail_ref, sems.at[1])
    ids_copy.start()
    tail_copy.start()
    ids_copy.wait()
    sent_ref[...] = jnp.broadcast_to(ids[3:4, :], sent_ref.shape)
    tail_copy.wait()


def pick_kernel(capacity, ids_ref, probe_ref, out_ref, picks_ref, probe, out, picks_smem, sems):
    groups, blocks = ids_ref.shape
    load = pltpu.make_async_copy(probe_ref, probe, sems.at[0])
    load.start()
    me = lax.axis_index("blk")
    local = ids_ref[...] - me * blocks
    mask = (local >= 0) & (local < blocks)
    rank = ranks_in(mask, blocks)
    lane = lax.broadcasted_iota(jnp.int32, (groups, blocks), 1)
    picks = jnp.zeros((groups, blocks), jnp.int32)
    for r in range(capacity):
        found = jnp.sum(jnp.where(mask & (rank == r), local + 1, 0), axis=1, keepdims=True)
        picks = jnp.where(lane == r, found, picks)
    picks_ref[...] = picks
    copy = pltpu.make_async_copy(picks_ref, picks_smem, sems.at[1])
    copy.start()
    copy.wait()
    load.wait()
    part = groups // STORES

    def store(p):
        rows = pl.ds(p * part * capacity, part * capacity)
        return pltpu.make_async_copy(out.at[rows], out_ref.at[rows], sems.at[2 + p])

    for p in range(STORES):

        @pl.loop(p * part, (p + 1) * part, unroll=8)
        def _(g):
            for r in range(capacity):
                out[g * capacity + r] = probe[jnp.maximum(picks_smem[g, r] - 1, 0)]

        store(p).start()
    for p in range(STORES):
        store(p).wait()


def stacked(mats):
    return mats.reshape(-1, mats.shape[-1])


def apart(left0, left1, mats):
    zero = jnp.zeros_like(left0)
    left = jnp.concatenate(
        [jnp.concatenate([left0, zero], axis=1), jnp.concatenate([zero, left1], axis=1)], axis=0
    )
    out = jnp.dot(left, mats, preferred_element_type=jnp.float32)
    return out.reshape((2,) + (left0.shape[0], mats.shape[1]))


def apart_back(lefts, mats):
    rows, half = lefts.shape[1], mats.shape[0] // 2
    out = lax.dot_general(lefts.reshape(2 * rows, lefts.shape[2]), mats, NT, preferred_element_type=jnp.float32)
    return out[:rows, :half], out[rows:, half:]


def near_place(ids_ref, k, i, first, count):
    place = ids_ref[k, i] - first + REACH
    return jnp.where(place >= count, place - count, place)


def near_forward_kernel(
    groups, capacity, ids_ref, ids_row_ref, halo_ref, probe_ref, coeffs_ref, prec_ref,
    part_ref, own_ref, slot_ref, first_ref, mats_ref, ext, coeffs, prec, part, fold, mats, sems
):
    blocks = probe_ref.shape[0]
    chunks = blocks // CHUNK

    def loads(c):
        own = pl.ds(c * CHUNK, CHUNK)
        return (
            pltpu.make_async_copy(coeffs_ref.at[own], coeffs.at[own], sems.at[0, c]),
            pltpu.make_async_copy(prec_ref.at[own], prec.at[own], sems.at[1, c]),
        )

    def store_part(c):
        own = pl.ds(c * CHUNK, CHUNK)
        return pltpu.make_async_copy(part.at[own], part_ref.at[own], sems.at[2, c])

    def store_mats(c):
        own = pl.ds(c * CHUNK, CHUNK)
        return pltpu.make_async_copy(mats.at[own], mats_ref.at[own], sems.at[3, c])

    own_load = pltpu.make_async_copy(probe_ref, ext.at[pl.ds(REACH, blocks)], sems.at[2, 0])
    own_load.start()
    for c in range(chunks):
        for load in loads(c):
            load.start()
    ext[pl.ds(0, REACH)] = halo_ref[...]
    owner = ids_row_ref[3:4, :] // blocks
    mask = lax.broadcasted_iota(jnp.int32, (groups, blocks), 0) == owner
    rank = jnp.sum(jnp.where(mask, ranks_in(mask, blocks), 0), axis=0, keepdims=True)
    slot_ref[...] = owner * capacity + rank
    first = lax.axis_index("blk") * blocks
    own_load.wait()

    def make(c):
        for b in range(0, CHUNK, 2):
            i = c * CHUNK + b
            rows = []
            for j in range(2):
                tiles = [ext[near_place(ids_ref, k, i + j, first, groups * blocks)] for k in range(3)]
                rows.append(jnp.concatenate(tiles, axis=1))
            near = [stacked(coeffs[i + j, pl.ds(0, 3)]) for j in range(2)]
            mixed = apart(rows[0], rows[1], jnp.concatenate(near, axis=0))
            part[pl.ds(i, 2)] = ext[pl.ds(REACH + i, 2)].astype(jnp.float32) - mixed
            for j in range(2):
                folded = lax.dot_general(prec[i + j], coeffs[i + j, 3], NT, preferred_element_type=jnp.float32)
                fold[i + j] = folded.astype(jnp.bfloat16)
        store_part(c).start()

    def use(c):
        for b in range(0, CHUNK, 2):
            i = c * CHUNK + b
            halves = []
            for j in range(2):
                high = part[i + j].astype(jnp.bfloat16)
                low = (part[i + j] - high.astype(jnp.float32)).astype(jnp.bfloat16)
                halves.append(jnp.concatenate([high, low], axis=0))
            both = apart(halves[0], halves[1], stacked(fold[pl.ds(i, 2)]))
            rows = both.shape[1] // 2
            own_ref[pl.ds(i, 2)] = both[:, :rows] + both[:, rows:]
            for j in range(2):
                mat = jnp.dot(coeffs[i + j, 3], fold[i + j], preferred_element_type=jnp.float32)
                mats[i + j] = mat.astype(jnp.bfloat16)
        store_mats(c).start()

    for load in loads(0):
        load.wait()
    make(0)

    @pl.loop(1, chunks)
    def _(c):
        for load in loads(c):
            load.wait()
        use(c - 1)
        make(c)

    use(chunks - 1)
    first_ref[...] = mats[pl.ds(0, HELD * CHUNK)]
    for c in range(chunks):
        store_part(c).wait()
        store_mats(c).wait()


def far_kernel(slots_ref, own_ref, far_ref, first_ref, mats_ref, parcel_ref, mats, slot, sems):
    blocks = own_ref.shape[0]
    chunks = blocks // CHUNK

    def load(c):
        own = pl.ds(c * CHUNK, CHUNK)
        return pltpu.make_async_copy(mats_ref.at[own], mats.at[own], sems.at[c])

    slot_copy = pltpu.make_async_copy(slots_ref, slot, sems.at[0])
    slot_copy.start()
    for c in range(HELD, chunks):
        load(c).start()
    parcel_ref[...] = jnp.zeros_like(parcel_ref)
    slot_copy.wait()

    def send_back(c, pair):
        for b in range(0, CHUNK, 2):
            i = c * CHUNK + b
            terms = own_ref[pl.ds(i, 2)] - apart(far_ref[slot[0, i]], far_ref[slot[0, i + 1]], stacked(pair[pl.ds(i, 2)]))
            for j in range(2):
                parcel_ref[slot[0, i + j]] = terms[j].astype(jnp.bfloat16)

    for c in range(HELD):
        send_back(c, first_ref)

    @pl.loop(HELD, chunks)
    def _(c):
        load(c).wait()
        send_back(c, mats)


def near_back_kernel(
    groups, ids_ref, slot_ref, far_ref, part_ref, coeffs_ref, prec_ref,
    base_ref, halo_ref, total, white, scaled, part, coeffs, prec, sems
):
    blocks = base_ref.shape[0]
    points = base_ref.shape[2]
    chunks = blocks // CHUNK

    def load(c, which):
        own = pl.ds(c * CHUNK, CHUNK)
        source, target = ((part_ref, part), (coeffs_ref, coeffs), (prec_ref, prec))[which]
        return pltpu.make_async_copy(source.at[own], target.at[own], sems.at[which, c])

    for c in range(chunks):
        for which in range(3):
            load(c, which).start()
    total[pl.ds(0, REACH)] = jnp.zeros((REACH,) + total.shape[1:], jnp.float32)
    first = lax.axis_index("blk") * blocks

    def mix(c):
        load(c, 0).wait()
        load(c, 1).wait()
        for b in range(0, CHUNK, 2):
            i = c * CHUNK + b
            mats = jnp.concatenate([coeffs[i, 3], coeffs[i + 1, 3]], axis=0)
            mixed = apart(far_ref[slot_ref[0, i]], far_ref[slot_ref[0, i + 1]], mats)
            white[pl.ds(i, 2)] = (part[pl.ds(i, 2)] - mixed).astype(jnp.bfloat16)

    def scale(c):
        load(c, 2).wait()
        for b in range(0, CHUNK, 2):
            i = c * CHUNK + b
            tiles = apart(white[i], white[i + 1], stacked(prec[pl.ds(i, 2)])).astype(jnp.bfloat16)
            scaled[pl.ds(i, 2)] = tiles
            total[pl.ds(REACH + i, 2)] = tiles.astype(jnp.float32)

    def back(c):
        terms = []
        for b in range(CHUNK + AHEAD):
            if b < CHUNK and b % 2 == 0:
                i = c * CHUNK + b
                mats = [stacked(coeffs[i + j, pl.ds(0, 3)]) for j in range(2)]
                terms.extend(apart_back(scaled[pl.ds(i, 2)], jnp.concatenate(mats, axis=0)))
            if b >= AHEAD:
                i = c * CHUNK + b - AHEAD
                places = [near_place(ids_ref, k, i, first, groups * blocks) for k in range(3)]
                olds = [total[place] for place in places]
                for k in range(3):
                    total[places[k]] = olds[k] - terms[b - AHEAD][:, k * points : (k + 1) * points]

    mix(0)
    scale(0)
    mix(1)

    @pl.loop(0, chunks - 2)
    def _(c):
        back(c)
        scale(c + 1)
        mix(c + 2)

    back(chunks - 2)
    scale(chunks - 1)
    back(chunks - 1)
    halo_ref[...] = total[pl.ds(0, REACH)].astype(halo_ref.dtype)
    base_ref[...] = total[pl.ds(REACH, blocks)]


def sum_kernel(capacity, all_picks_ref, base_ref, halo_ref, back_ref, out_ref, total, picks_ref, sems):
    groups = all_picks_ref.shape[0]
    picks_copy = pltpu.make_async_copy(all_picks_ref, picks_ref, sems.at[0])
    picks_copy.start()
    blocks = base_ref.shape[0]
    total[pl.ds(0, blocks)] = base_ref[...]
    last = pl.ds(blocks - REACH, REACH)
    total[last] = total[last] + halo_ref[...].astype(jnp.float32)
    picks_copy.wait()

    @pl.loop(0, groups, unroll=8)
    def _(g):
        picks = [picks_ref[g, r] for r in range(capacity)]
        places = [jnp.where(pick > 0, pick - 1, blocks) for pick in picks]
        olds = [total[place] for place in places]
        for r in range(capacity):
            total[places[r]] = olds[r] - back_ref[g * capacity + r].astype(jnp.float32)

    store = pltpu.make_async_copy(total.at[pl.ds(0, blocks)], out_ref, sems.at[1])
    store.start()
    store.wait()


def per_device(probe_vecs, coeffs, cond_prec, neighbours):
    blocks, probes, points = probe_vecs.shape
    groups = lax.axis_size("blk")
    capacity = max(2, blocks // (groups - 1) + 1)
    slots = groups * capacity
    chunks = blocks // CHUNK
    bf16, f32 = jnp.bfloat16, jnp.float32
    tile = (probes, points)
    flops = 2 * blocks * probes * points * points

    def exchange(x):
        return lax.all_to_all(x, "blk", split_axis=0, concat_axis=0, tiled=True)

    ids = neighbours.T
    sent_ids, tail = pl.pallas_call(
        prep_kernel,
        name="prep",
        out_shape=(
            jax.ShapeDtypeStruct((groups, blocks), jnp.int32),
            jax.ShapeDtypeStruct((REACH,) + tile, bf16),
        ),
        in_specs=[HBM, HBM],
        out_specs=(VMEM, VMEM),
        scratch_shapes=[pltpu.VMEM(ids.shape, jnp.int32), pltpu.SemaphoreType.DMA((2,))],
        compiler_params=params(8),
    )(in_hbm(ids), in_hbm(probe_vecs))
    halo = passed_along(tail, "blk", 1)
    all_ids = exchange(sent_ids)
    all_ids, halo = lax.optimization_barrier((all_ids, halo))
    outgoing, picks = pl.pallas_call(
        functools.partial(pick_kernel, capacity),
        name="pick_tiles",
        out_shape=(
            jax.ShapeDtypeStruct((slots,) + tile, bf16),
            jax.ShapeDtypeStruct((groups, blocks), jnp.int32),
        ),
        in_specs=[VMEM, HBM],
        out_specs=(HBM, VMEM),
        scratch_shapes=[
            pltpu.VMEM((blocks,) + tile, bf16),
            pltpu.VMEM((slots,) + tile, bf16),
            pltpu.SMEM((groups, blocks), jnp.int32),
            pltpu.SemaphoreType.DMA((2 + STORES,)),
        ],
        compiler_params=params(8),
        cost_estimate=pl.CostEstimate(flops=0, bytes_accessed=2 * slots * 4096, transcendentals=0),
    )(all_ids, in_hbm(probe_vecs))
    arrived = exchange(outgoing.reshape((groups, capacity) + tile)).reshape((slots,) + tile)
    mats = (blocks, points, points)
    all_mats = pltpu.VMEM((blocks, 4, points, points), bf16)
    tiles_f32 = jax.ShapeDtypeStruct((blocks,) + tile, f32)
    part, own_far, slot_of, first_mats, far_mats = pl.pallas_call(
        functools.partial(near_forward_kernel, groups, capacity),
        name="near_forward",
        out_shape=(
            pltpu.HBM((blocks,) + tile, f32),
            tiles_f32,
            jax.ShapeDtypeStruct((1, blocks), jnp.int32),
            jax.ShapeDtypeStruct((HELD * CHUNK, points, points), bf16),
            pltpu.HBM(mats, bf16),
        ),
        in_specs=[SMEM, VMEM, VMEM, HBM, HBM, HBM],
        out_specs=(HBM, VMEM, VMEM, VMEM, HBM),
        scratch_shapes=[
            pltpu.VMEM((REACH + blocks,) + tile, bf16),
            all_mats,
            pltpu.VMEM(mats, bf16),
            pltpu.VMEM((blocks,) + tile, f32),
            pltpu.VMEM(mats, bf16),
            pltpu.VMEM(mats, bf16),
            pltpu.SemaphoreType.DMA((4, chunks)),
        ],
        compiler_params=params(40),
        cost_estimate=pl.CostEstimate(flops=20 * flops, bytes_accessed=28 * 2**20, transcendentals=0),
    )(ids, ids, halo, in_hbm(probe_vecs), in_hbm(coeffs), in_hbm(cond_prec))
    parcel = pl.pallas_call(
        far_kernel,
        name="far_terms",
        out_shape=jax.ShapeDtypeStruct((slots,) + tile, bf16),
        in_specs=[VMEM, VMEM, VMEM, VMEM, HBM],
        out_specs=VMEM,
        scratch_shapes=[
            pltpu.VMEM(mats, bf16),
            pltpu.SMEM((1, blocks), jnp.int32),
            pltpu.SemaphoreType.DMA((chunks,)),
        ],
        compiler_params=params(16),
        cost_estimate=pl.CostEstimate(flops=flops, bytes_accessed=6 * 2**20, transcendentals=0),
    )(slot_of, own_far, arrived, first_mats, in_hbm(far_mats))
    parcel, arrived = lax.optimization_barrier((parcel, arrived))
    returned = exchange(parcel.reshape((groups, capacity) + tile)).reshape((slots,) + tile)
    base, halo_back = pl.pallas_call(
        functools.partial(near_back_kernel, groups),
        name="near_back",
        out_shape=(tiles_f32, jax.ShapeDtypeStruct((REACH,) + tile, bf16)),
        in_specs=[SMEM, SMEM, VMEM, HBM, HBM, HBM],
        out_specs=(VMEM, VMEM),
        scratch_shapes=[
            pltpu.VMEM((REACH + blocks,) + tile, f32),
            pltpu.VMEM((blocks,) + tile, bf16),
            pltpu.VMEM((blocks,) + tile, bf16),
            pltpu.VMEM((blocks,) + tile, f32),
            all_mats,
            pltpu.VMEM(mats, bf16),
            pltpu.SemaphoreType.DMA((3, chunks)),
        ],
        compiler_params=params(36),
        cost_estimate=pl.CostEstimate(flops=5 * flops, bytes_accessed=23 * 2**20, transcendentals=0),
    )(ids, slot_of, arrived, in_hbm(part), in_hbm(coeffs), in_hbm(cond_prec))
    halo_sum = passed_along(halo_back, "blk", -1)
    return pl.pallas_call(
        functools.partial(sum_kernel, capacity),
        name="final_sum",
        out_shape=jax.ShapeDtypeStruct((blocks,) + tile, f32),
        in_specs=[VMEM, VMEM, VMEM, VMEM],
        out_specs=HBM,
        scratch_shapes=[
            pltpu.VMEM((blocks + 1,) + tile, f32),
            pltpu.SMEM((groups, blocks), jnp.int32),
            pltpu.SemaphoreType.DMA((2,)),
        ],
        compiler_params=params(8),
        cost_estimate=pl.CostEstimate(flops=0, bytes_accessed=3 * 2**20, transcendentals=0),
    )(picks, base, halo_sum, returned)


def solution(mesh):
    in_specs = (
        P("blk", None, None),
        P("blk", None, None, None),
        P("blk", None, None),
        P("blk", None),
    )
    return jax.shard_map(
        per_device, mesh=mesh, in_specs=in_specs, out_specs=P("blk", None, None), check_vma=False
    )
```

time: 67.1 us -> 65.6 us (0.978)
  waiting for transfers between devices: 9.3 us -> 7.89 us
  local copies, waits for them, and re-layouts: 1.72 us -> 0.68 us
  Pallas kernels: 29.6 us -> 30.6 us
    pallas_call x1, Pallas kernels: 9.11 us -> 11.4 us  [per_device(): pl.pallas_call(functools.partial(near_back_kernel, groups), name='near_ba...]
    pallas_call x1, Pallas kernels: 4.46 us -> 3.01 us  [per_device(): pl.pallas_call(far_kernel, name='far_terms', out_shape=jax.ShapeDtypeStru...]
    all_to_all x2, waiting for transfers between devices: 7.39 us -> 5.98 us  [exchange(): return lax.all_to_all(x, 'blk', split_axis=0, concat_axis=0, tiled=True)]
    unnamed x6 -> x4, local copies, waits for them, and re-layouts: 1.72 us -> 0.68 us
    pallas_call x1, Pallas kernels: 10.4 us -> 11.2 us  [per_device(): pl.pallas_call(functools.partial(near_forward_kernel, groups, capacity),...]
  transfers between devices with their start and end apart: 4 -> 4, of which waited for: 3 -> 2; matrix products, arithmetic and copies ran while one was open for 0% -> 0% of each run, Pallas kernels for 29% -> 35%
where the time goes in v9:
time: 65.6 us; the launch traced here: 65.2 us
  Pallas kernels  30.6 us (47%)
  blocking collectives  14.1 us (21%)
  starting transfers between devices  11.8 us (18%)
  waiting for transfers between devices  7.89 us (12%)
  local copies, waits for them, and re-layouts  0.68 us (1%)
    all_to_all x1, blocking collectives, exchange(): return lax.all_to_all(x, 'blk', split_axis=0, concat_axis=0, tiled=True)  14.1 us
    pallas_call x1, Pallas kernels, per_device(): pl.pallas_call(functools.partial(near_back_kernel, groups), name='near_ba...  11.4 us
    pallas_call x1, Pallas kernels, per_device(): pl.pallas_call(functools.partial(near_forward_kernel, groups, capacity),...  11.2 us
    all_to_all x2, starting transfers between devices, exchange(): return lax.all_to_all(x, 'blk', split_axis=0, concat_axis=0, tiled=True)  6.05 us
    all_to_all x2, waiting for transfers between devices, exchange(): return lax.all_to_all(x, 'blk', split_axis=0, concat_axis=0, tiled=True)  5.98 us
    ppermute x2, starting transfers between devices, passed_along(): lax.ppermute(block, axis, [((i - distance) % size, i) for i in range(size)])  5.78 us
    pallas_call x1, Pallas kernels, per_device(): pl.pallas_call(far_kernel, name='far_terms', out_shape=jax.ShapeDtypeStru...  3.01 us
    pallas_call x1, Pallas kernels, per_device(): pl.pallas_call(functools.partial(sum_kernel, capacity), name='final_sum',...  2.1 us
  transfers between devices with their start and end apart: 4, of which 2 were waited for; matrix products, arithmetic and copies ran while one was open for 0% of the time, Pallas kernels for 35%

profile of v9, /device:TPU:0, one launch (start us, length us, event | category | flops | bytes accessed | tf_op | source)
XLA Modules:
  0.0 65.2 jit_solution(16444936219741244962)
XLA Ops:
  0.0 0.9 %prep.1 = (s32[32,128]{1,0:T(8,128)S(1)}, bf16[16,16,128]{2,1,0:T(8,128)(2,1)S(1)}) custom-call(s32[4,128]{1,0:T(4,128)} %bitcast.13, bf16[128,16,128]{2,1,0:T(8,128)(2,1)} %probe_ref.5), custom_call_target="tpu_custom_call" | custom-call | tf_op jit(solution)/shard_map/prep/pallas_call | solution.py:335
  0.9 0.5 collective-permute-start
  1.4 14.1 %all_to_all.22 = s32[32,1,128]{2,1,0:T(1,128)S(1)} all-to-all(s32[32,1,128]{2,1,0:T(1,128)S(1)} %bitcast.17), channel_id=1, replica_groups=mesh['blk'=32] {'blk'}, dimensions={0} | all-to-all | bytes 32768 | tf_op jit(solution)/shard_map/all_to_all | solution.py:332
  15.5 0.0 collective-permute-done.halo_ref
  15.5 2.0 %pick_tiles.1 = (bf16[160,16,128]{2,1,0:T(8,128)(2,1)}, s32[32,128]{1,0:T(8,128)S(1)}) custom-call(s32[32,128]{1,0:T(8,128)S(1)} %bitcast.12, bf16[128,16,128]{2,1,0:T(8,128)(2,1)} %probe_ref.5), custom_call_target="tpu_custom_call" | custom-call | bytes 1310720 | tf_op jit(solution)/shard_map/pick_tiles/pallas_call | solution.py:350
  17.5 2.6 %all-to-all-start.1 = ((bf16[32,5,16,128]{3,2,1,0:T(8,128)(2,1)}), bf16[32,5,16,128]{3,2,1,0:T(8,128)(2,1)S(1)}, u32[]{:S(2)}, u32[]{:S(2)}) async-start(bf16[32,5,16,128]{3,2,1,0:T(8,128)(2,1)} %bitcast.4), calls=%async_computation.1 | async-start | bytes 1310720 | tf_op jit(solution)/shard_map/all_to_all | solution.py:332
  20.2 0.0 copy-start
  20.2 0.7 %copy-done = s32[128,4]{0,1:T(4,128)S(1)} copy-done((s32[128,4]{0,1:T(4,128)S(1)}, s32[128,4]{0,1:T(4,128)}, u32[]{:S(2)}) %copy-start) | copy-done | bytes 2072
  20.8 11.2 %near_forward.1 = (f32[128,16,128]{2,1,0:T(8,128)}, f32[128,16,128]{2,1,0:T(8,128)S(1)}, s32[1,128]{1,0:T(1,128)S(1)}, bf16[48,128,128]{2,1,0:T(8,128)(2,1)S(1)}, bf16[128,128,128]{2,1,0:T(8,128)(2,1)}) custom-call(s32[4,128]{1,0:T(4,128)S(1)} %bitcast.14, s32[4,128]{1,0:T(4,128)S(1)} %bitcast.15, bf16[16,16,128]{2,1,0:T(8,128)(2,1)S(1)} %collective-permute-done.halo_ref, ...), custom_call_target="tpu_custom_call" | custom-call | flops 1342177280 | bytes 29360128 | tf_op jit(solution)/shard_map/near_forward/pallas_call | solution.py:372
  32.1 6.0 %all-to-all-done.1 = bf16[32,5,16,128]{3,2,1,0:T(8,128)(2,1)S(1)} async-done(((bf16[32,5,16,128]{3,2,1,0:T(8,128)(2,1)}), bf16[32,5,16,128]{3,2,1,0:T(8,128)(2,1)S(1)}, u32[]{:S(2)}, u32[]{:S(2)}) %all-to-all-start.1) | async-done | bytes 655392 | tf_op jit(solution)/shard_map/all_to_all | solution.py:332
  38.1 0.0 copy-start.1
  38.1 3.0 %far_terms.1 = bf16[160,16,128]{2,1,0:T(8,128)(2,1)} custom-call(s32[1,128]{1,0:T(1,128)S(1)} %get-tuple-element.25.slots_ref.slot_ref, f32[128,16,128]{2,1,0:T(8,128)S(1)} %get-tuple-element.26.own_ref, bf16[160,16,128]{2,1,0:T(8,128)(2,1)S(1)} %bitcast.9, bf16[48,128,128]{2,1,0:T(8,128)(2,1)S(1)} %get-tuple-element.28.first_ref, ...), custom_call_target="tpu_custom_call" | custom-call | flops 67108864 | bytes 6291456 | tf_op jit(solution)/shard_map/far_terms/pallas_call | solution.py:396
  41.1 3.4 %all-to-all-start.2 = ((bf16[32,5,16,128]{3,2,1,0:T(8,128)(2,1)}), bf16[32,5,16,128]{3,2,1,0:T(8,128)(2,1)S(1)}, u32[]{:S(2)}, u32[]{:S(2)}) async-start(bf16[32,5,16,128]{3,2,1,0:T(8,128)(2,1)} %bitcast.6), calls=%async_computation.2 | async-start | bytes 1310720 | tf_op jit(solution)/shard_map/all_to_all | solution.py:332
  44.5 0.0 copy-done.1
  44.5 11.4 %near_back.1 = (f32[128,16,128]{2,1,0:T(8,128)S(1)}, bf16[16,16,128]{2,1,0:T(8,128)(2,1)S(1)}) custom-call(s32[4,128]{1,0:T(4,128)S(1)} %bitcast.16, s32[1,128]{1,0:T(1,128)S(1)} %get-tuple-element.25.slots_ref.slot_ref, bf16[160,16,128]{2,1,0:T(8,128)(2,1)S(1)} %bitcast.10, f32[128,16,128]{2,1,0:T(8,128)} %get-tuple-element.31.part_ref, ...), custom_call_target="tpu_custom_call" | custom-call | flops 335544320 | bytes 24117248 | tf_op jit(solution)/shard_map/near_back/pallas_call | solution.py:412
  55.9 5.3 %collective-permute-start.1 = (bf16[16,16,128]{2,1,0:T(8,128)(2,1)S(1)}, bf16[16,16,128]{2,1,0:T(8,128)(2,1)S(1)}, u32[]{:S(2)}, u32[]{:S(2)}) collective-permute-start(bf16[16,16,128]{2,1,0:T(8,128)(2,1)S(1)} %get-tuple-element.33), channel_id=1, source_target_pairs={{1,0},{2,1},{3,2},{4,3},{5,4},{6,5},{7,6},{8,7},{9,8},{10,9},{11,1... | collective-permute-start | bytes 196616 | tf_op jit(solution)/shard_map/ppermute | solution.py:31
  61.2 1.9 %collective-permute-done.1.halo_ref = bf16[16,16,128]{2,1,0:T(8,128)(2,1)S(1)} collective-permute-done((bf16[16,16,128]{2,1,0:T(8,128)(2,1)S(1)}, bf16[16,16,128]{2,1,0:T(8,128)(2,1)S(1)}, u32[]{:S(2)}, u32[]{:S(2)}) %collective-permute-start.1) | collective-permute-done | bytes 65568 | tf_op jit(solution)/shard_map/ppermute | solution.py:31
  63.1 0.0 all-to-all-done.2
  63.1 2.1 %final_sum.1 = f32[128,16,128]{2,1,0:T(8,128)} custom-call(s32[32,128]{1,0:T(8,128)S(1)} %get-tuple-element.23.all_picks_ref, f32[128,16,128]{2,1,0:T(8,128)S(1)} %get-tuple-element.32.base_ref, bf16[16,16,128]{2,1,0:T(8,128)(2,1)S(1)} %collective-permute-done.1.halo_ref, bf16[160,16,128]{2,1,0:T(8,128)(2,1)S(1)} %bitcast.11), custom_call_target="tpu_custom_call" | custom-call | bytes 3145728 | tf_op jit(solution)/shard_map/final_sum/pallas_call | solution.py:431
Async XLA Ops:
  0.9 14.6 %collective-permute-start = (bf16[16,16,128]{2,1,0:T(8,128)(2,1)S(1)}, bf16[16,16,128]{2,1,0:T(8,128)(2,1)S(1)}, u32[]{:S(2)}, u32[]{:S(2)}) collective-permute-start(bf16[16,16,128]{2,1,0:T(8,128)(2,1)S(1)} %get-tuple-element.21), channel_id=1, source_target_pairs={{31,0},{0,1},{1,2},{2,3},{3,4},{4,5},{5,6},{6,7},{7,8},{8,9},{9,10... | collective-permute-start | bytes 196616 | tf_op jit(solution)/shard_map/ppermute | solution.py:31
  17.5 20.6 %all-to-all-start.1 = ((bf16[32,5,16,128]{3,2,1,0:T(8,128)(2,1)}), bf16[32,5,16,128]{3,2,1,0:T(8,128)(2,1)S(1)}, u32[]{:S(2)}, u32[]{:S(2)}) async-start(bf16[32,5,16,128]{3,2,1,0:T(8,128)(2,1)} %bitcast.4), calls=%async_computation.1 | async-start | bytes 1310720 | tf_op jit(solution)/shard_map/all_to_all | solution.py:332
  20.2 0.7 %copy-start = (s32[128,4]{0,1:T(4,128)S(1)}, s32[128,4]{0,1:T(4,128)}, u32[]{:S(2)}) copy-start(s32[128,4]{0,1:T(4,128)} %param.7) | copy-start | bytes 6148
  38.1 6.5 %copy-start.1 = (s32[128,4]{0,1:T(4,128)S(1)}, s32[128,4]{0,1:T(4,128)}, u32[]{:S(2)}) copy-start(s32[128,4]{0,1:T(4,128)} %param.7) | copy-start | bytes 6148
  41.1 22.0 %all-to-all-start.2 = ((bf16[32,5,16,128]{3,2,1,0:T(8,128)(2,1)}), bf16[32,5,16,128]{3,2,1,0:T(8,128)(2,1)S(1)}, u32[]{:S(2)}, u32[]{:S(2)}) async-start(bf16[32,5,16,128]{3,2,1,0:T(8,128)(2,1)} %bitcast.6), calls=%async_computation.2 | async-start | bytes 1310720 | tf_op jit(solution)/shard_map/all_to_all | solution.py:332
  55.9 7.2 %collective-permute-start.1 = (bf16[16,16,128]{2,1,0:T(8,128)(2,1)S(1)}, bf16[16,16,128]{2,1,0:T(8,128)(2,1)S(1)}, u32[]{:S(2)}, u32[]{:S(2)}) collective-permute-start(bf16[16,16,128]{2,1,0:T(8,128)(2,1)S(1)} %get-tuple-element.33), channel_id=1, source_target_pairs={{1,0},{2,1},{3,2},{4,3},{5,4},{6,5},{7,6},{8,7},{9,8},{10,9},{11,1... | collective-permute-start | bytes 196616 | tf_op jit(solution)/shard_map/ppermute | solution.py:31

commit v10 on v9

--- a/solution.py
+++ b/solution.py
@@ -11,6 +11,7 @@
 CHUNK = 16
 AHEAD = 4
 HELD = 3
+LEAD = 3
 STORES = 4
 VMEM = pl.BlockSpec(memory_space=pltpu.VMEM)
 SMEM = pl.BlockSpec(memory_space=pltpu.SMEM)
@@ -61,12 +62,14 @@
     local = ids_ref[...] - me * blocks
     mask = (local >= 0) & (local < blocks)
     rank = ranks_in(mask, blocks)
-    lane = lax.broadcasted_iota(jnp.int32, (groups, blocks), 1)
-    picks = jnp.zeros((groups, blocks), jnp.int32)
+    row = lax.broadcasted_iota(jnp.int32, (picks_ref.shape[0], groups), 0)
+    ones = jnp.ones((picks_ref.shape[0], blocks), jnp.bfloat16)
+    picks = jnp.zeros(row.shape, jnp.float32)
     for r in range(capacity):
-        found = jnp.sum(jnp.where(mask & (rank == r), local + 1, 0), axis=1, keepdims=True)
-        picks = jnp.where(lane == r, found, picks)
-    picks_ref[...] = picks
+        chosen = jnp.where(mask & (rank == r), local + 1, 0).astype(jnp.float32).astype(jnp.bfloat16)
+        found = lax.dot_general(ones, chosen, NT, preferred_element_type=jnp.float32)
+        picks = jnp.where(row == r, found, picks)
+    picks_ref[:, pl.ds(0, groups)] = picks.astype(jnp.int32)
     copy = pltpu.make_async_copy(picks_ref, picks_smem, sems.at[1])
     copy.start()
     copy.wait()
@@ -82,7 +85,7 @@
         @pl.loop(p * part, (p + 1) * part, unroll=8)
         def _(g):
             for r in range(capacity):
-                out[g * capacity + r] = probe[jnp.maximum(picks_smem[g, r] - 1, 0)]
+                out[g * capacity + r] = probe[jnp.maximum(picks_smem[r, g] - 1, 0)]
 
         store(p).start()
     for p in range(STORES):
@@ -137,9 +140,17 @@
 
     own_load = pltpu.make_async_copy(probe_ref, ext.at[pl.ds(REACH, blocks)], sems.at[2, 0])
     own_load.start()
-    for c in range(chunks):
+
+    def fetch(c):
         for load in loads(c):
             load.start()
+
+    def ready(c):
+        for load in loads(c):
+            load.wait()
+
+    for c in range(LEAD):
+        fetch(c)
     ext[pl.ds(0, REACH)] = halo_ref[...]
     owner = ids_row_ref[3:4, :] // blocks
     mask = lax.broadcasted_iota(jnp.int32, (groups, blocks), 0) == owner
@@ -179,14 +190,18 @@
                 mats[i + j] = mat.astype(jnp.bfloat16)
         store_mats(c).start()
 
-    for load in loads(0):
-        load.wait()
+    ready(0)
+    fetch(LEAD)
     make(0)
 
     @pl.loop(1, chunks)
     def _(c):
-        for load in loads(c):
-            load.wait()
+        ready(c)
+
+        @pl.when(c + LEAD < chunks)
+        def _():
+            fetch(c + LEAD)
+
         use(c - 1)
         make(c)
 
@@ -241,9 +256,12 @@
         source, target = ((part_ref, part), (coeffs_ref, coeffs), (prec_ref, prec))[which]
         return pltpu.make_async_copy(source.at[own], target.at[own], sems.at[which, c])
 
-    for c in range(chunks):
+    def fetch(c):
         for which in range(3):
             load(c, which).start()
+
+    for c in range(LEAD):
+        fetch(c)
     total[pl.ds(0, REACH)] = jnp.zeros((REACH,) + total.shape[1:], jnp.float32)
     first = lax.axis_index("blk") * blocks
 
@@ -279,11 +297,17 @@
                     total[places[k]] = olds[k] - terms[b - AHEAD][:, k * points : (k + 1) * points]
 
     mix(0)
+    fetch(LEAD)
     scale(0)
     mix(1)
+    fetch(LEAD + 1)
 
     @pl.loop(0, chunks - 2)
     def _(c):
+        @pl.when(c + LEAD + 2 < chunks)
+        def _():
+            fetch(c + LEAD + 2)
+
         back(c)
         scale(c + 1)
         mix(c + 2)
@@ -296,7 +320,7 @@
 
 
 def sum_kernel(capacity, all_picks_ref, base_ref, halo_ref, back_ref, out_ref, total, picks_ref, sems):
-    groups = all_picks_ref.shape[0]
+    groups = back_ref.shape[0] // capacity
     picks_copy = pltpu.make_async_copy(all_picks_ref, picks_ref, sems.at[0])
     picks_copy.start()
     blocks = base_ref.shape[0]
@@ -307,7 +331,7 @@
 
     @pl.loop(0, groups, unroll=8)
     def _(g):
-        picks = [picks_ref[g, r] for r in range(capacity)]
+        picks = [picks_ref[r, g] for r in range(capacity)]
         places = [jnp.where(pick > 0, pick - 1, blocks) for pick in picks]
         olds = [total[place] for place in places]
         for r in range(capacity):
@@ -323,6 +347,7 @@
     groups = lax.axis_size("blk")
     capacity = max(2, blocks // (groups - 1) + 1)
     slots = groups * capacity
+    picks_shape = (-(-capacity // 8) * 8, -(-groups // 128) * 128)
     chunks = blocks // CHUNK
     bf16, f32 = jnp.bfloat16, jnp.float32
     tile = (probes, points)
@@ -352,14 +377,14 @@
         name="pick_tiles",
         out_shape=(
             jax.ShapeDtypeStruct((slots,) + tile, bf16),
-            jax.ShapeDtypeStruct((groups, blocks), jnp.int32),
+            jax.ShapeDtypeStruct(picks_shape, jnp.int32),
         ),
         in_specs=[VMEM, HBM],
         out_specs=(HBM, VMEM),
         scratch_shapes=[
             pltpu.VMEM((blocks,) + tile, bf16),
             pltpu.VMEM((slots,) + tile, bf16),
-            pltpu.SMEM((groups, blocks), jnp.int32),
+            pltpu.SMEM(picks_shape, jnp.int32),
             pltpu.SemaphoreType.DMA((2 + STORES,)),
         ],
         compiler_params=params(8),
@@ -436,7 +461,7 @@
         out_specs=HBM,
         scratch_shapes=[
             pltpu.VMEM((blocks + 1,) + tile, f32),
-            pltpu.SMEM((groups, blocks), jnp.int32),
+            pltpu.SMEM(picks_shape, jnp.int32),
             pltpu.SemaphoreType.DMA((2,)),
         ],
         compiler_params=params(8),

time: 65.6 us -> 65.4 us (level)
  no operation moved by 1% of the time
where the time goes in v10:
time: 65.4 us; the launch traced here: 65 us
  Pallas kernels  30.5 us (47%)
  blocking collectives  14.1 us (22%)
  starting transfers between devices  11.8 us (18%)
  waiting for transfers between devices  7.82 us (12%)
  local copies, waits for them, and re-layouts  0.68 us (1%)
    all_to_all x1, blocking collectives, exchange(): return lax.all_to_all(x, 'blk', split_axis=0, concat_axis=0, tiled=True)  14.1 us
    pallas_call x1, Pallas kernels, per_device(): pl.pallas_call(functools.partial(near_back_kernel, groups), name='near_ba...  11.4 us
    pallas_call x1, Pallas kernels, per_device(): pl.pallas_call(functools.partial(near_forward_kernel, groups, capacity),...  11.3 us
    all_to_all x2, starting transfers between devices, exchange(): return lax.all_to_all(x, 'blk', split_axis=0, concat_axis=0, tiled=True)  6.05 us
    all_to_all x2, waiting for transfers between devices, exchange(): return lax.all_to_all(x, 'blk', split_axis=0, concat_axis=0, tiled=True)  5.91 us
    ppermute x2, starting transfers between devices, passed_along(): lax.ppermute(block, axis, [((i - distance) % size, i) for i in range(size)])  5.78 us
    pallas_call x1, Pallas kernels, per_device(): pl.pallas_call(far_kernel, name='far_terms', out_shape=jax.ShapeDtypeStru...  3.01 us
    pallas_call x1, Pallas kernels, per_device(): pl.pallas_call(functools.partial(pick_kernel, capacity), name='pick_tiles...  2.01 us
  transfers between devices with their start and end apart: 4, of which 2 were waited for; matrix products, arithmetic and copies ran while one was open for 0% of the time, Pallas kernels for 35%

profile of v10, /device:TPU:0, one launch (start us, length us, event | category | flops | bytes accessed | tf_op | source)
XLA Modules:
  0.0 65.0 jit_solution(2502301509160431466)
XLA Ops:
  0.0 0.9 %prep.1 = (s32[32,128]{1,0:T(8,128)S(1)}, bf16[16,16,128]{2,1,0:T(8,128)(2,1)S(1)}) custom-call(s32[4,128]{1,0:T(4,128)} %bitcast.13, bf16[128,16,128]{2,1,0:T(8,128)(2,1)} %probe_ref.5), custom_call_target="tpu_custom_call" | custom-call | tf_op jit(solution)/shard_map/prep/pallas_call | solution.py:360
  0.9 0.5 collective-permute-start
  1.4 14.1 %all_to_all.22 = s32[32,1,128]{2,1,0:T(1,128)S(1)} all-to-all(s32[32,1,128]{2,1,0:T(1,128)S(1)} %bitcast.17), channel_id=1, replica_groups=mesh['blk'=32] {'blk'}, dimensions={0} | all-to-all | bytes 32768 | tf_op jit(solution)/shard_map/all_to_all | solution.py:357
  15.5 0.0 collective-permute-done.halo_ref
  15.5 2.0 %pick_tiles.1 = (bf16[160,16,128]{2,1,0:T(8,128)(2,1)}, s32[8,128]{1,0:T(8,128)S(1)}) custom-call(s32[32,128]{1,0:T(8,128)S(1)} %bitcast.12, bf16[128,16,128]{2,1,0:T(8,128)(2,1)} %probe_ref.5), custom_call_target="tpu_custom_call" | custom-call | bytes 1310720 | tf_op jit(solution)/shard_map/pick_tiles/pallas_call | solution.py:375
  17.5 2.6 %all-to-all-start.1 = ((bf16[32,5,16,128]{3,2,1,0:T(8,128)(2,1)}), bf16[32,5,16,128]{3,2,1,0:T(8,128)(2,1)S(1)}, u32[]{:S(2)}, u32[]{:S(2)}) async-start(bf16[32,5,16,128]{3,2,1,0:T(8,128)(2,1)} %bitcast.4), calls=%async_computation.1 | async-start | bytes 1310720 | tf_op jit(solution)/shard_map/all_to_all | solution.py:357
  20.1 0.0 copy-start
  20.1 0.7 %copy-done = s32[128,4]{0,1:T(4,128)S(1)} copy-done((s32[128,4]{0,1:T(4,128)S(1)}, s32[128,4]{0,1:T(4,128)}, u32[]{:S(2)}) %copy-start) | copy-done | bytes 2072
  20.8 11.3 %near_forward.1 = (f32[128,16,128]{2,1,0:T(8,128)}, f32[128,16,128]{2,1,0:T(8,128)S(1)}, s32[1,128]{1,0:T(1,128)S(1)}, bf16[48,128,128]{2,1,0:T(8,128)(2,1)S(1)}, bf16[128,128,128]{2,1,0:T(8,128)(2,1)}) custom-call(s32[4,128]{1,0:T(4,128)S(1)} %bitcast.14, s32[4,128]{1,0:T(4,128)S(1)} %bitcast.15, bf16[16,16,128]{2,1,0:T(8,128)(2,1)S(1)} %collective-permute-done.halo_ref, ...), custom_call_target="tpu_custom_call" | custom-call | flops 1342177280 | bytes 29360128 | tf_op jit(solution)/shard_map/near_forward/pallas_call | solution.py:397
  32.1 5.9 %all-to-all-done.1 = bf16[32,5,16,128]{3,2,1,0:T(8,128)(2,1)S(1)} async-done(((bf16[32,5,16,128]{3,2,1,0:T(8,128)(2,1)}), bf16[32,5,16,128]{3,2,1,0:T(8,128)(2,1)S(1)}, u32[]{:S(2)}, u32[]{:S(2)}) %all-to-all-start.1) | async-done | bytes 655392 | tf_op jit(solution)/shard_map/all_to_all | solution.py:357
  38.0 0.0 copy-start.1
  38.0 3.0 %far_terms.1 = bf16[160,16,128]{2,1,0:T(8,128)(2,1)} custom-call(s32[1,128]{1,0:T(1,128)S(1)} %get-tuple-element.25.slots_ref.slot_ref, f32[128,16,128]{2,1,0:T(8,128)S(1)} %get-tuple-element.26.own_ref, bf16[160,16,128]{2,1,0:T(8,128)(2,1)S(1)} %bitcast.9, bf16[48,128,128]{2,1,0:T(8,128)(2,1)S(1)} %get-tuple-element.28.first_ref, ...), custom_call_target="tpu_custom_call" | custom-call | flops 67108864 | bytes 6291456 | tf_op jit(solution)/shard_map/far_terms/pallas_call | solution.py:421
  41.1 3.4 %all-to-all-start.2 = ((bf16[32,5,16,128]{3,2,1,0:T(8,128)(2,1)}), bf16[32,5,16,128]{3,2,1,0:T(8,128)(2,1)S(1)}, u32[]{:S(2)}, u32[]{:S(2)}) async-start(bf16[32,5,16,128]{3,2,1,0:T(8,128)(2,1)} %bitcast.6), calls=%async_computation.2 | async-start | bytes 1310720 | tf_op jit(solution)/shard_map/all_to_all | solution.py:357
  44.5 0.0 copy-done.1
  44.5 11.4 %near_back.1 = (f32[128,16,128]{2,1,0:T(8,128)S(1)}, bf16[16,16,128]{2,1,0:T(8,128)(2,1)S(1)}) custom-call(s32[4,128]{1,0:T(4,128)S(1)} %bitcast.16, s32[1,128]{1,0:T(1,128)S(1)} %get-tuple-element.25.slots_ref.slot_ref, bf16[160,16,128]{2,1,0:T(8,128)(2,1)S(1)} %bitcast.10, f32[128,16,128]{2,1,0:T(8,128)} %get-tuple-element.31.part_ref, ...), custom_call_target="tpu_custom_call" | custom-call | flops 335544320 | bytes 24117248 | tf_op jit(solution)/shard_map/near_back/pallas_call | solution.py:437
  55.9 5.3 %collective-permute-start.1 = (bf16[16,16,128]{2,1,0:T(8,128)(2,1)S(1)}, bf16[16,16,128]{2,1,0:T(8,128)(2,1)S(1)}, u32[]{:S(2)}, u32[]{:S(2)}) collective-permute-start(bf16[16,16,128]{2,1,0:T(8,128)(2,1)S(1)} %get-tuple-element.33), channel_id=1, source_target_pairs={{1,0},{2,1},{3,2},{4,3},{5,4},{6,5},{7,6},{8,7},{9,8},{10,9},{11,1... | collective-permute-start | bytes 196616 | tf_op jit(solution)/shard_map/ppermute | solution.py:32
  61.1 1.9 %collective-permute-done.1.halo_ref = bf16[16,16,128]{2,1,0:T(8,128)(2,1)S(1)} collective-permute-done((bf16[16,16,128]{2,1,0:T(8,128)(2,1)S(1)}, bf16[16,16,128]{2,1,0:T(8,128)(2,1)S(1)}, u32[]{:S(2)}, u32[]{:S(2)}) %collective-permute-start.1) | collective-permute-done | bytes 65568 | tf_op jit(solution)/shard_map/ppermute | solution.py:32
  63.1 0.0 all-to-all-done.2
  63.1 2.0 %final_sum.1 = f32[128,16,128]{2,1,0:T(8,128)} custom-call(s32[8,128]{1,0:T(8,128)S(1)} %get-tuple-element.23.all_picks_ref, f32[128,16,128]{2,1,0:T(8,128)S(1)} %get-tuple-element.32.base_ref, bf16[16,16,128]{2,1,0:T(8,128)(2,1)S(1)} %collective-permute-done.1.halo_ref, bf16[160,16,128]{2,1,0:T(8,128)(2,1)S(1)} %bitcast.11), custom_call_target="tpu_custom_call" | custom-call | bytes 3145728 | tf_op jit(solution)/shard_map/final_sum/pallas_call | solution.py:456
Async XLA Ops:
  0.9 14.6 %collective-permute-start = (bf16[16,16,128]{2,1,0:T(8,128)(2,1)S(1)}, bf16[16,16,128]{2,1,0:T(8,128)(2,1)S(1)}, u32[]{:S(2)}, u32[]{:S(2)}) collective-permute-start(bf16[16,16,128]{2,1,0:T(8,128)(2,1)S(1)} %get-tuple-element.21), channel_id=1, source_target_pairs={{31,0},{0,1},{1,2},{2,3},{3,4},{4,5},{5,6},{6,7},{7,8},{8,9},{9,10... | collective-permute-start | bytes 196616 | tf_op jit(solution)/shard_map/ppermute | solution.py:32
  17.5 20.6 %all-to-all-start.1 = ((bf16[32,5,16,128]{3,2,1,0:T(8,128)(2,1)}), bf16[32,5,16,128]{3,2,1,0:T(8,128)(2,1)S(1)}, u32[]{:S(2)}, u32[]{:S(2)}) async-start(bf16[32,5,16,128]{3,2,1,0:T(8,128)(2,1)} %bitcast.4), calls=%async_computation.1 | async-start | bytes 1310720 | tf_op jit(solution)/shard_map/all_to_all | solution.py:357
  20.1 0.7 %copy-start = (s32[128,4]{0,1:T(4,128)S(1)}, s32[128,4]{0,1:T(4,128)}, u32[]{:S(2)}) copy-start(s32[128,4]{0,1:T(4,128)} %param.7) | copy-start | bytes 6148
  38.0 6.5 %copy-start.1 = (s32[128,4]{0,1:T(4,128)S(1)}, s32[128,4]{0,1:T(4,128)}, u32[]{:S(2)}) copy-start(s32[128,4]{0,1:T(4,128)} %param.7) | copy-start | bytes 6148
  41.1 22.0 %all-to-all-start.2 = ((bf16[32,5,16,128]{3,2,1,0:T(8,128)(2,1)}), bf16[32,5,16,128]{3,2,1,0:T(8,128)(2,1)S(1)}, u32[]{:S(2)}, u32[]{:S(2)}) async-start(bf16[32,5,16,128]{3,2,1,0:T(8,128)(2,1)} %bitcast.6), calls=%async_computation.2 | async-start | bytes 1310720 | tf_op jit(solution)/shard_map/all_to_all | solution.py:357
  55.9 7.2 %collective-permute-start.1 = (bf16[16,16,128]{2,1,0:T(8,128)(2,1)S(1)}, bf16[16,16,128]{2,1,0:T(8,128)(2,1)S(1)}, u32[]{:S(2)}, u32[]{:S(2)}) collective-permute-start(bf16[16,16,128]{2,1,0:T(8,128)(2,1)S(1)} %get-tuple-element.33), channel_id=1, source_target_pairs={{1,0},{2,1},{3,2},{4,3},{5,4},{6,5},{7,6},{8,7},{9,8},{10,9},{11,1... | collective-permute-start | bytes 196616 | tf_op jit(solution)/shard_map/ppermute | solution.py:32

commit v11 on v10

--- a/solution.py
+++ b/solution.py
@@ -105,6 +105,20 @@
     return out.reshape((2,) + (left0.shape[0], mats.shape[1]))
 
 
+def apart4(lefts, mats):
+    zero = jnp.zeros_like(lefts[0])
+    rows = zero.shape[0]
+    left = jnp.concatenate(
+        [jnp.concatenate([x, zero] if j % 2 == 0 else [zero, x], axis=1) for j, x in enumerate(lefts)], axis=0
+    )
+    right = jnp.concatenate(
+        [jnp.concatenate([mats[0], mats[1]], axis=0), jnp.concatenate([mats[2], mats[3]], axis=0)], axis=1
+    )
+    out = jnp.dot(left, right, preferred_element_type=jnp.float32)
+    half = right.shape[1] // 2
+    return [out[j * rows : (j + 1) * rows, (j // 2) * half : (j // 2 + 1) * half] for j in range(4)]
+
+
 def apart_back(lefts, mats):
     rows, half = lefts.shape[1], mats.shape[0] // 2
     out = lax.dot_general(lefts.reshape(2 * rows, lefts.shape[2]), mats, NT, preferred_element_type=jnp.float32)
@@ -228,11 +242,11 @@
     slot_copy.wait()
 
     def send_back(c, pair):
-        for b in range(0, CHUNK, 2):
+        for b in range(0, CHUNK, 4):
             i = c * CHUNK + b
-            terms = own_ref[pl.ds(i, 2)] - apart(far_ref[slot[0, i]], far_ref[slot[0, i + 1]], stacked(pair[pl.ds(i, 2)]))
-            for j in range(2):
-                parcel_ref[slot[0, i + j]] = terms[j].astype(jnp.bfloat16)
+            mixed = apart4([far_ref[slot[0, i + j]] for j in range(4)], [pair[i + j] for j in range(4)])
+            for j in range(4):
+                parcel_ref[slot[0, i + j]] = (own_ref[i + j] - mixed[j]).astype(jnp.bfloat16)
 
     for c in range(HELD):
         send_back(c, first_ref)
@@ -253,11 +267,16 @@
 
     def load(c, which):
         own = pl.ds(c * CHUNK, CHUNK)
-        source, target = ((part_ref, part), (coeffs_ref, coeffs), (prec_ref, prec))[which]
-        return pltpu.make_async_copy(source.at[own], target.at[own], sems.at[which, c])
+        source, target = (
+            (part_ref.at[own], part.at[own]),
+            (coeffs_ref.at[own, 3], coeffs.at[own, 3]),
+            (prec_ref.at[own], prec.at[own]),
+            (coeffs_ref.at[own, pl.ds(0, 3)], coeffs.at[own, pl.ds(0, 3)]),
+        )[which]
+        return pltpu.make_async_copy(source, target, sems.at[which, c])
 
     def fetch(c):
-        for which in range(3):
+        for which in range(4):
             load(c, which).start()
 
     for c in range(LEAD):
@@ -268,21 +287,23 @@
     def mix(c):
         load(c, 0).wait()
         load(c, 1).wait()
-        for b in range(0, CHUNK, 2):
+        for b in range(0, CHUNK, 4):
             i = c * CHUNK + b
-            mats = jnp.concatenate([coeffs[i, 3], coeffs[i + 1, 3]], axis=0)
-            mixed = apart(far_ref[slot_ref[0, i]], far_ref[slot_ref[0, i + 1]], mats)
-            white[pl.ds(i, 2)] = (part[pl.ds(i, 2)] - mixed).astype(jnp.bfloat16)
+            mixed = apart4([far_ref[slot_ref[0, i + j]] for j in range(4)], [coeffs[i + j, 3] for j in range(4)])
+            for j in range(4):
+                white[i + j] = (part[i + j] - mixed[j]).astype(jnp.bfloat16)
 
     def scale(c):
         load(c, 2).wait()
-        for b in range(0, CHUNK, 2):
+        for b in range(0, CHUNK, 4):
             i = c * CHUNK + b
-            tiles = apart(white[i], white[i + 1], stacked(prec[pl.ds(i, 2)])).astype(jnp.bfloat16)
-            scaled[pl.ds(i, 2)] = tiles
-            total[pl.ds(REACH + i, 2)] = tiles.astype(jnp.float32)
+            tiles = apart4([white[i + j] for j in range(4)], [prec[i + j] for j in range(4)])
+            for j in range(4):
+                scaled[i + j] = tiles[j].astype(jnp.bfloat16)
+                total[REACH + i + j] = scaled[i + j].astype(jnp.float32)
 
     def back(c):
+        load(c, 3).wait()
         terms = []
         for b in range(CHUNK + AHEAD):
             if b < CHUNK and b % 2 == 0:
@@ -447,7 +468,7 @@
             pltpu.VMEM((blocks,) + tile, f32),
             all_mats,
             pltpu.VMEM(mats, bf16),
-            pltpu.SemaphoreType.DMA((3, chunks)),
+            pltpu.SemaphoreType.DMA((4, chunks)),
         ],
         compiler_params=params(36),
         cost_estimate=pl.CostEstimate(flops=5 * flops, bytes_accessed=23 * 2**20, transcendentals=0),

time: 65.4 us -> 65.2 us (level)
  no operation moved by 1% of the time
where the time goes in v11:
time: 65.2 us; the launch traced here: 64.7 us
  Pallas kernels  30.3 us (46%)
  blocking collectives  14.1 us (22%)
  starting transfers between devices  11.8 us (18%)
  waiting for transfers between devices  7.82 us (12%)
  local copies, waits for them, and re-layouts  0.68 us (1%)
    all_to_all x1, blocking collectives, exchange(): return lax.all_to_all(x, 'blk', split_axis=0, concat_axis=0, tiled=True)  14.1 us
    pallas_call x1, Pallas kernels, per_device(): pl.pallas_call(functools.partial(near_forward_kernel, groups, capacity),...  11.3 us
    pallas_call x1, Pallas kernels, per_device(): pl.pallas_call(functools.partial(near_back_kernel, groups), name='near_ba...  11.1 us
    all_to_all x2, starting transfers between devices, exchange(): return lax.all_to_all(x, 'blk', split_axis=0, concat_axis=0, tiled=True)  6.05 us
    all_to_all x2, waiting for transfers between devices, exchange(): return lax.all_to_all(x, 'blk', split_axis=0, concat_axis=0, tiled=True)  5.91 us
    ppermute x2, starting transfers between devices, passed_along(): lax.ppermute(block, axis, [((i - distance) % size, i) for i in range(size)])  5.78 us
    pallas_call x1, Pallas kernels, per_device(): pl.pallas_call(far_kernel, name='far_terms', out_shape=jax.ShapeDtypeStru...  3.04 us
    pallas_call x1, Pallas kernels, per_device(): pl.pallas_call(functools.partial(pick_kernel, capacity), name='pick_tiles...  2.01 us
  transfers between devices with their start and end apart: 4, of which 2 were waited for; matrix products, arithmetic and copies ran while one was open for 0% of the time, Pallas kernels for 35%

profile of v11, /device:TPU:0, one launch (start us, length us, event | category | flops | bytes accessed | tf_op | source)
XLA Modules:
  0.0 64.7 jit_solution(735504664954794742)
XLA Ops:
  0.0 0.9 %prep.1 = (s32[32,128]{1,0:T(8,128)S(1)}, bf16[16,16,128]{2,1,0:T(8,128)(2,1)S(1)}) custom-call(s32[4,128]{1,0:T(4,128)} %bitcast.13, bf16[128,16,128]{2,1,0:T(8,128)(2,1)} %probe_ref.5), custom_call_target="tpu_custom_call" | custom-call | tf_op jit(solution)/shard_map/prep/pallas_call | solution.py:381
  0.9 0.5 collective-permute-start
  1.4 14.1 %all_to_all.22 = s32[32,1,128]{2,1,0:T(1,128)S(1)} all-to-all(s32[32,1,128]{2,1,0:T(1,128)S(1)} %bitcast.17), channel_id=1, replica_groups=mesh['blk'=32] {'blk'}, dimensions={0} | all-to-all | bytes 32768 | tf_op jit(solution)/shard_map/all_to_all | solution.py:378
  15.5 0.0 collective-permute-done.halo_ref
  15.5 2.0 %pick_tiles.1 = (bf16[160,16,128]{2,1,0:T(8,128)(2,1)}, s32[8,128]{1,0:T(8,128)S(1)}) custom-call(s32[32,128]{1,0:T(8,128)S(1)} %bitcast.12, bf16[128,16,128]{2,1,0:T(8,128)(2,1)} %probe_ref.5), custom_call_target="tpu_custom_call" | custom-call | bytes 1310720 | tf_op jit(solution)/shard_map/pick_tiles/pallas_call | solution.py:396
  17.5 2.6 %all-to-all-start.1 = ((bf16[32,5,16,128]{3,2,1,0:T(8,128)(2,1)}), bf16[32,5,16,128]{3,2,1,0:T(8,128)(2,1)S(1)}, u32[]{:S(2)}, u32[]{:S(2)}) async-start(bf16[32,5,16,128]{3,2,1,0:T(8,128)(2,1)} %bitcast.4), calls=%async_computation.1 | async-start | bytes 1310720 | tf_op jit(solution)/shard_map/all_to_all | solution.py:378
  20.1 0.0 copy-start
  20.1 0.7 %copy-done = s32[128,4]{0,1:T(4,128)S(1)} copy-done((s32[128,4]{0,1:T(4,128)S(1)}, s32[128,4]{0,1:T(4,128)}, u32[]{:S(2)}) %copy-start) | copy-done | bytes 2072
  20.8 11.3 %near_forward.1 = (f32[128,16,128]{2,1,0:T(8,128)}, f32[128,16,128]{2,1,0:T(8,128)S(1)}, s32[1,128]{1,0:T(1,128)S(1)}, bf16[48,128,128]{2,1,0:T(8,128)(2,1)S(1)}, bf16[128,128,128]{2,1,0:T(8,128)(2,1)}) custom-call(s32[4,128]{1,0:T(4,128)S(1)} %bitcast.14, s32[4,128]{1,0:T(4,128)S(1)} %bitcast.15, bf16[16,16,128]{2,1,0:T(8,128)(2,1)S(1)} %collective-permute-done.halo_ref, ...), custom_call_target="tpu_custom_call" | custom-call | flops 1342177280 | bytes 29360128 | tf_op jit(solution)/shard_map/near_forward/pallas_call | solution.py:418
  32.1 5.9 %all-to-all-done.1 = bf16[32,5,16,128]{3,2,1,0:T(8,128)(2,1)S(1)} async-done(((bf16[32,5,16,128]{3,2,1,0:T(8,128)(2,1)}), bf16[32,5,16,128]{3,2,1,0:T(8,128)(2,1)S(1)}, u32[]{:S(2)}, u32[]{:S(2)}) %all-to-all-start.1) | async-done | bytes 655392 | tf_op jit(solution)/shard_map/all_to_all | solution.py:378
  38.0 0.0 copy-start.1
  38.0 3.0 %far_terms.1 = bf16[160,16,128]{2,1,0:T(8,128)(2,1)} custom-call(s32[1,128]{1,0:T(1,128)S(1)} %get-tuple-element.25.slots_ref.slot_ref, f32[128,16,128]{2,1,0:T(8,128)S(1)} %get-tuple-element.26.own_ref, bf16[160,16,128]{2,1,0:T(8,128)(2,1)S(1)} %bitcast.9, bf16[48,128,128]{2,1,0:T(8,128)(2,1)S(1)} %get-tuple-element.28.first_ref, ...), custom_call_target="tpu_custom_call" | custom-call | flops 67108864 | bytes 6291456 | tf_op jit(solution)/shard_map/far_terms/pallas_call | solution.py:442
  41.1 3.4 %all-to-all-start.2 = ((bf16[32,5,16,128]{3,2,1,0:T(8,128)(2,1)}), bf16[32,5,16,128]{3,2,1,0:T(8,128)(2,1)S(1)}, u32[]{:S(2)}, u32[]{:S(2)}) async-start(bf16[32,5,16,128]{3,2,1,0:T(8,128)(2,1)} %bitcast.6), calls=%async_computation.2 | async-start | bytes 1310720 | tf_op jit(solution)/shard_map/all_to_all | solution.py:378
  44.5 0.0 copy-done.1
  44.5 11.1 %near_back.1 = (f32[128,16,128]{2,1,0:T(8,128)S(1)}, bf16[16,16,128]{2,1,0:T(8,128)(2,1)S(1)}) custom-call(s32[4,128]{1,0:T(4,128)S(1)} %bitcast.16, s32[1,128]{1,0:T(1,128)S(1)} %get-tuple-element.25.slots_ref.slot_ref, bf16[160,16,128]{2,1,0:T(8,128)(2,1)S(1)} %bitcast.10, f32[128,16,128]{2,1,0:T(8,128)} %get-tuple-element.31.part_ref, ...), custom_call_target="tpu_custom_call" | custom-call | flops 335544320 | bytes 24117248 | tf_op jit(solution)/shard_map/near_back/pallas_call | solution.py:458
  55.6 5.3 %collective-permute-start.1 = (bf16[16,16,128]{2,1,0:T(8,128)(2,1)S(1)}, bf16[16,16,128]{2,1,0:T(8,128)(2,1)S(1)}, u32[]{:S(2)}, u32[]{:S(2)}) collective-permute-start(bf16[16,16,128]{2,1,0:T(8,128)(2,1)S(1)} %get-tuple-element.33), channel_id=1, source_target_pairs={{1,0},{2,1},{3,2},{4,3},{5,4},{6,5},{7,6},{8,7},{9,8},{10,9},{11,1... | collective-permute-start | bytes 196616 | tf_op jit(solution)/shard_map/ppermute | solution.py:32
  60.9 1.9 %collective-permute-done.1.halo_ref = bf16[16,16,128]{2,1,0:T(8,128)(2,1)S(1)} collective-permute-done((bf16[16,16,128]{2,1,0:T(8,128)(2,1)S(1)}, bf16[16,16,128]{2,1,0:T(8,128)(2,1)S(1)}, u32[]{:S(2)}, u32[]{:S(2)}) %collective-permute-start.1) | collective-permute-done | bytes 65568 | tf_op jit(solution)/shard_map/ppermute | solution.py:32
  62.8 0.0 all-to-all-done.2
  62.8 2.0 %final_sum.1 = f32[128,16,128]{2,1,0:T(8,128)} custom-call(s32[8,128]{1,0:T(8,128)S(1)} %get-tuple-element.23.all_picks_ref, f32[128,16,128]{2,1,0:T(8,128)S(1)} %get-tuple-element.32.base_ref, bf16[16,16,128]{2,1,0:T(8,128)(2,1)S(1)} %collective-permute-done.1.halo_ref, bf16[160,16,128]{2,1,0:T(8,128)(2,1)S(1)} %bitcast.11), custom_call_target="tpu_custom_call" | custom-call | bytes 3145728 | tf_op jit(solution)/shard_map/final_sum/pallas_call | solution.py:477
Async XLA Ops:
  0.9 14.6 %collective-permute-start = (bf16[16,16,128]{2,1,0:T(8,128)(2,1)S(1)}, bf16[16,16,128]{2,1,0:T(8,128)(2,1)S(1)}, u32[]{:S(2)}, u32[]{:S(2)}) collective-permute-start(bf16[16,16,128]{2,1,0:T(8,128)(2,1)S(1)} %get-tuple-element.21), channel_id=1, source_target_pairs={{31,0},{0,1},{1,2},{2,3},{3,4},{4,5},{5,6},{6,7},{7,8},{8,9},{9,10... | collective-permute-start | bytes 196616 | tf_op jit(solution)/shard_map/ppermute | solution.py:32
  17.5 20.6 %all-to-all-start.1 = ((bf16[32,5,16,128]{3,2,1,0:T(8,128)(2,1)}), bf16[32,5,16,128]{3,2,1,0:T(8,128)(2,1)S(1)}, u32[]{:S(2)}, u32[]{:S(2)}) async-start(bf16[32,5,16,128]{3,2,1,0:T(8,128)(2,1)} %bitcast.4), calls=%async_computation.1 | async-start | bytes 1310720 | tf_op jit(solution)/shard_map/all_to_all | solution.py:378
  20.1 0.7 %copy-start = (s32[128,4]{0,1:T(4,128)S(1)}, s32[128,4]{0,1:T(4,128)}, u32[]{:S(2)}) copy-start(s32[128,4]{0,1:T(4,128)} %param.7) | copy-start | bytes 6148
  38.0 6.5 %copy-start.1 = (s32[128,4]{0,1:T(4,128)S(1)}, s32[128,4]{0,1:T(4,128)}, u32[]{:S(2)}) copy-start(s32[128,4]{0,1:T(4,128)} %param.7) | copy-start | bytes 6148
  41.1 21.7 %all-to-all-start.2 = ((bf16[32,5,16,128]{3,2,1,0:T(8,128)(2,1)}), bf16[32,5,16,128]{3,2,1,0:T(8,128)(2,1)S(1)}, u32[]{:S(2)}, u32[]{:S(2)}) async-start(bf16[32,5,16,128]{3,2,1,0:T(8,128)(2,1)} %bitcast.6), calls=%async_computation.2 | async-start | bytes 1310720 | tf_op jit(solution)/shard_map/all_to_all | solution.py:378
  55.6 7.2 %collective-permute-start.1 = (bf16[16,16,128]{2,1,0:T(8,128)(2,1)S(1)}, bf16[16,16,128]{2,1,0:T(8,128)(2,1)S(1)}, u32[]{:S(2)}, u32[]{:S(2)}) collective-permute-start(bf16[16,16,128]{2,1,0:T(8,128)(2,1)S(1)} %get-tuple-element.33), channel_id=1, source_target_pairs={{1,0},{2,1},{3,2},{4,3},{5,4},{6,5},{7,6},{8,7},{9,8},{10,9},{11,1... | collective-permute-start | bytes 196616 | tf_op jit(solution)/shard_map/ppermute | solution.py:32

commit v12 on v11

--- a/solution.py
+++ b/solution.py
@@ -9,7 +9,8 @@
 
 REACH = 16
 CHUNK = 16
-AHEAD = 4
+AHEAD = 8
+WIDTH = 8
 HELD = 3
 LEAD = 3
 STORES = 4
@@ -119,6 +120,17 @@
     return [out[j * rows : (j + 1) * rows, (j // 2) * half : (j // 2 + 1) * half] for j in range(4)]
 
 
+def streamed(tiles, mats):
+    rows = tiles[0].shape[0]
+    size = mats.shape[1]
+    out = lax.dot_general(stacked(mats), jnp.concatenate(tiles, axis=0), NT, preferred_element_type=jnp.float32)
+    owner = lax.broadcasted_iota(jnp.int32, (size, rows * len(tiles)), 1) // rows
+    kept = out[:size]
+    for j in range(1, len(tiles)):
+        kept = jnp.where(owner == j, out[j * size : (j + 1) * size], kept)
+    return kept.T.reshape(len(tiles), rows, size)
+
+
 def apart_back(lefts, mats):
     rows, half = lefts.shape[1], mats.shape[0] // 2
     out = lax.dot_general(lefts.reshape(2 * rows, lefts.shape[2]), mats, NT, preferred_element_type=jnp.float32)
@@ -184,7 +196,7 @@
             mixed = apart(rows[0], rows[1], jnp.concatenate(near, axis=0))
             part[pl.ds(i, 2)] = ext[pl.ds(REACH + i, 2)].astype(jnp.float32) - mixed
             for j in range(2):
-                folded = lax.dot_general(prec[i + j], coeffs[i + j, 3], NT, preferred_element_type=jnp.float32)
+                folded = lax.dot_general(coeffs[i + j, 3], prec[i + j], NT, preferred_element_type=jnp.float32)
                 fold[i + j] = folded.astype(jnp.bfloat16)
         store_part(c).start()
 
@@ -195,12 +207,12 @@
             for j in range(2):
                 high = part[i + j].astype(jnp.bfloat16)
                 low = (part[i + j] - high.astype(jnp.float32)).astype(jnp.bfloat16)
-                halves.append(jnp.concatenate([high, low], axis=0))
-            both = apart(halves[0], halves[1], stacked(fold[pl.ds(i, 2)]))
-            rows = both.shape[1] // 2
-            own_ref[pl.ds(i, 2)] = both[:, :rows] + both[:, rows:]
+                halves.append(jnp.concatenate([high, low], axis=0)[None])
+            both = apart_back(jnp.concatenate(halves, axis=0), stacked(fold[pl.ds(i, 2)]))
             for j in range(2):
-                mat = jnp.dot(coeffs[i + j, 3], fold[i + j], preferred_element_type=jnp.float32)
+                rows = both[j].shape[0] // 2
+                own_ref[i + j] = both[j][:rows] + both[j][rows:]
+                mat = lax.dot_general(fold[i + j], coeffs[i + j, 3], NT, preferred_element_type=jnp.float32)
                 mats[i + j] = mat.astype(jnp.bfloat16)
         store_mats(c).start()
 
@@ -242,10 +254,10 @@
     slot_copy.wait()
 
     def send_back(c, pair):
-        for b in range(0, CHUNK, 4):
+        for b in range(0, CHUNK, WIDTH):
             i = c * CHUNK + b
-            mixed = apart4([far_ref[slot[0, i + j]] for j in range(4)], [pair[i + j] for j in range(4)])
-            for j in range(4):
+            mixed = streamed([far_ref[slot[0, i + j]] for j in range(WIDTH)], pair[pl.ds(i, WIDTH)])
+            for j in range(WIDTH):
                 parcel_ref[slot[0, i + j]] = (own_ref[i + j] - mixed[j]).astype(jnp.bfloat16)
 
     for c in range(HELD):
@@ -262,7 +274,6 @@
     base_ref, halo_ref, total, white, scaled, part, coeffs, prec, sems
 ):
     blocks = base_ref.shape[0]
-    points = base_ref.shape[2]
     chunks = blocks // CHUNK
 
     def load(c, which):
@@ -306,16 +317,16 @@
         load(c, 3).wait()
         terms = []
         for b in range(CHUNK + AHEAD):
-            if b < CHUNK and b % 2 == 0:
+            if b < CHUNK and b % WIDTH == 0:
                 i = c * CHUNK + b
-                mats = [stacked(coeffs[i + j, pl.ds(0, 3)]) for j in range(2)]
-                terms.extend(apart_back(scaled[pl.ds(i, 2)], jnp.concatenate(mats, axis=0)))
+                tiles = [scaled[i + j] for j in range(WIDTH)]
+                terms.append([streamed(tiles, coeffs[pl.ds(i, WIDTH), k]) for k in range(3)])
             if b >= AHEAD:
                 i = c * CHUNK + b - AHEAD
                 places = [near_place(ids_ref, k, i, first, groups * blocks) for k in range(3)]
                 olds = [total[place] for place in places]
                 for k in range(3):
-                    total[places[k]] = olds[k] - terms[b - AHEAD][:, k * points : (k + 1) * points]
+                    total[places[k]] = olds[k] - terms[(b - AHEAD) // WIDTH][k][(b - AHEAD) % WIDTH]
 
     mix(0)
     fetch(LEAD)

time: 65.2 us -> 66.4 us (1.018)
  Pallas kernels: 30.3 us -> 33.6 us
  waiting for transfers between devices: 7.82 us -> 5.73 us
    pallas_call x1, Pallas kernels: 11.3 us -> 13.4 us  [per_device(): pl.pallas_call(functools.partial(near_forward_kernel, groups, capacity),...]
    all_to_all x2, waiting for transfers between devices: 5.91 us -> 3.82 us  [exchange(): return lax.all_to_all(x, 'blk', split_axis=0, concat_axis=0, tiled=True)]
    pallas_call x1, Pallas kernels: 3.04 us -> 4.06 us  [per_device(): pl.pallas_call(far_kernel, name='far_terms', out_shape=jax.ShapeDtypeStru...]
  transfers between devices with their start and end apart: 4 -> 4, of which waited for: 2 -> 2; matrix products, arithmetic and copies ran while one was open for 0% -> 0% of each run, Pallas kernels for 35% -> 37%
where the time goes in v12:
time: 66.4 us; the launch traced here: 66 us
  Pallas kernels  33.6 us (51%)
  blocking collectives  14.1 us (21%)
  starting transfers between devices  11.8 us (18%)
  waiting for transfers between devices  5.73 us (9%)
  local copies, waits for them, and re-layouts  0.68 us (1%)
    all_to_all x1, blocking collectives, exchange(): return lax.all_to_all(x, 'blk', split_axis=0, concat_axis=0, tiled=True)  14.1 us
    pallas_call x1, Pallas kernels, per_device(): pl.pallas_call(functools.partial(near_forward_kernel, groups, capacity),...  13.4 us
    pallas_call x1, Pallas kernels, per_device(): pl.pallas_call(functools.partial(near_back_kernel, groups), name='near_ba...  11.3 us
    all_to_all x2, starting transfers between devices, exchange(): return lax.all_to_all(x, 'blk', split_axis=0, concat_axis=0, tiled=True)  6.05 us
    ppermute x2, starting transfers between devices, passed_along(): lax.ppermute(block, axis, [((i - distance) % size, i) for i in range(size)])  5.79 us
    pallas_call x1, Pallas kernels, per_device(): pl.pallas_call(far_kernel, name='far_terms', out_shape=jax.ShapeDtypeStru...  4.06 us
    all_to_all x2, waiting for transfers between devices, exchange(): return lax.all_to_all(x, 'blk', split_axis=0, concat_axis=0, tiled=True)  3.82 us
    pallas_call x1, Pallas kernels, per_device(): pl.pallas_call(functools.partial(pick_kernel, capacity), name='pick_tiles...  2.01 us
  transfers between devices with their start and end apart: 4, of which 2 were waited for; matrix products, arithmetic and copies ran while one was open for 0% of the time, Pallas kernels for 37%

profile of v12, /device:TPU:0, one launch (start us, length us, event | category | flops | bytes accessed | tf_op | source)
XLA Modules:
  0.0 66.0 jit_solution(1831532767927193830)
XLA Ops:
  0.0 0.9 %prep.1 = (s32[32,128]{1,0:T(8,128)S(1)}, bf16[16,16,128]{2,1,0:T(8,128)(2,1)S(1)}) custom-call(s32[4,128]{1,0:T(4,128)} %bitcast.13, bf16[128,16,128]{2,1,0:T(8,128)(2,1)} %probe_ref.5), custom_call_target="tpu_custom_call" | custom-call | tf_op jit(solution)/shard_map/prep/pallas_call | solution.py:392
  0.9 0.5 collective-permute-start
  1.4 14.1 %all_to_all.22 = s32[32,1,128]{2,1,0:T(1,128)S(1)} all-to-all(s32[32,1,128]{2,1,0:T(1,128)S(1)} %bitcast.17), channel_id=1, replica_groups=mesh['blk'=32] {'blk'}, dimensions={0} | all-to-all | bytes 32768 | tf_op jit(solution)/shard_map/all_to_all | solution.py:389
  15.5 0.0 collective-permute-done.halo_ref
  15.5 2.0 %pick_tiles.1 = (bf16[160,16,128]{2,1,0:T(8,128)(2,1)}, s32[8,128]{1,0:T(8,128)S(1)}) custom-call(s32[32,128]{1,0:T(8,128)S(1)} %bitcast.12, bf16[128,16,128]{2,1,0:T(8,128)(2,1)} %probe_ref.5), custom_call_target="tpu_custom_call" | custom-call | bytes 1310720 | tf_op jit(solution)/shard_map/pick_tiles/pallas_call | solution.py:407
  17.5 2.6 %all-to-all-start.1 = ((bf16[32,5,16,128]{3,2,1,0:T(8,128)(2,1)}), bf16[32,5,16,128]{3,2,1,0:T(8,128)(2,1)S(1)}, u32[]{:S(2)}, u32[]{:S(2)}) async-start(bf16[32,5,16,128]{3,2,1,0:T(8,128)(2,1)} %bitcast.4), calls=%async_computation.1 | async-start | bytes 1310720 | tf_op jit(solution)/shard_map/all_to_all | solution.py:389
  20.1 0.0 copy-start
  20.1 0.7 %copy-done = s32[128,4]{0,1:T(4,128)S(1)} copy-done((s32[128,4]{0,1:T(4,128)S(1)}, s32[128,4]{0,1:T(4,128)}, u32[]{:S(2)}) %copy-start) | copy-done | bytes 2072
  20.8 13.4 %near_forward.1 = (f32[128,16,128]{2,1,0:T(8,128)}, f32[128,16,128]{2,1,0:T(8,128)S(1)}, s32[1,128]{1,0:T(1,128)S(1)}, bf16[48,128,128]{2,1,0:T(8,128)(2,1)S(1)}, bf16[128,128,128]{2,1,0:T(8,128)(2,1)}) custom-call(s32[4,128]{1,0:T(4,128)S(1)} %bitcast.14, s32[4,128]{1,0:T(4,128)S(1)} %bitcast.15, bf16[16,16,128]{2,1,0:T(8,128)(2,1)S(1)} %collective-permute-done.halo_ref, ...), custom_call_target="tpu_custom_call" | custom-call | flops 1342177280 | bytes 29360128 | tf_op jit(solution)/shard_map/near_forward/pallas_call | solution.py:429
  34.2 3.8 %all-to-all-done.1 = bf16[32,5,16,128]{3,2,1,0:T(8,128)(2,1)S(1)} async-done(((bf16[32,5,16,128]{3,2,1,0:T(8,128)(2,1)}), bf16[32,5,16,128]{3,2,1,0:T(8,128)(2,1)S(1)}, u32[]{:S(2)}, u32[]{:S(2)}) %all-to-all-start.1) | async-done | bytes 655392 | tf_op jit(solution)/shard_map/all_to_all | solution.py:389
  38.0 0.0 copy-start.1
  38.0 4.1 %far_terms.1 = bf16[160,16,128]{2,1,0:T(8,128)(2,1)} custom-call(s32[1,128]{1,0:T(1,128)S(1)} %get-tuple-element.25.slots_ref.slot_ref, f32[128,16,128]{2,1,0:T(8,128)S(1)} %get-tuple-element.26.own_ref, bf16[160,16,128]{2,1,0:T(8,128)(2,1)S(1)} %bitcast.9, bf16[48,128,128]{2,1,0:T(8,128)(2,1)S(1)} %get-tuple-element.28.first_ref, ...), custom_call_target="tpu_custom_call" | custom-call | flops 67108864 | bytes 6291456 | tf_op jit(solution)/shard_map/far_terms/pallas_call | solution.py:453
  42.1 3.4 %all-to-all-start.2 = ((bf16[32,5,16,128]{3,2,1,0:T(8,128)(2,1)}), bf16[32,5,16,128]{3,2,1,0:T(8,128)(2,1)S(1)}, u32[]{:S(2)}, u32[]{:S(2)}) async-start(bf16[32,5,16,128]{3,2,1,0:T(8,128)(2,1)} %bitcast.6), calls=%async_computation.2 | async-start | bytes 1310720 | tf_op jit(solution)/shard_map/all_to_all | solution.py:389
  45.5 0.0 copy-done.1
  45.5 11.3 %near_back.1 = (f32[128,16,128]{2,1,0:T(8,128)S(1)}, bf16[16,16,128]{2,1,0:T(8,128)(2,1)S(1)}) custom-call(s32[4,128]{1,0:T(4,128)S(1)} %bitcast.16, s32[1,128]{1,0:T(1,128)S(1)} %get-tuple-element.25.slots_ref.slot_ref, bf16[160,16,128]{2,1,0:T(8,128)(2,1)S(1)} %bitcast.10, f32[128,16,128]{2,1,0:T(8,128)} %get-tuple-element.31.part_ref, ...), custom_call_target="tpu_custom_call" | custom-call | flops 335544320 | bytes 24117248 | tf_op jit(solution)/shard_map/near_back/pallas_call | solution.py:469
  56.8 5.3 %collective-permute-start.1 = (bf16[16,16,128]{2,1,0:T(8,128)(2,1)S(1)}, bf16[16,16,128]{2,1,0:T(8,128)(2,1)S(1)}, u32[]{:S(2)}, u32[]{:S(2)}) collective-permute-start(bf16[16,16,128]{2,1,0:T(8,128)(2,1)S(1)} %get-tuple-element.33), channel_id=1, source_target_pairs={{1,0},{2,1},{3,2},{4,3},{5,4},{6,5},{7,6},{8,7},{9,8},{10,9},{11,1... | collective-permute-start | bytes 196616 | tf_op jit(solution)/shard_map/ppermute | solution.py:33
  62.1 1.9 %collective-permute-done.1.halo_ref = bf16[16,16,128]{2,1,0:T(8,128)(2,1)S(1)} collective-permute-done((bf16[16,16,128]{2,1,0:T(8,128)(2,1)S(1)}, bf16[16,16,128]{2,1,0:T(8,128)(2,1)S(1)}, u32[]{:S(2)}, u32[]{:S(2)}) %collective-permute-start.1) | collective-permute-done | bytes 65568 | tf_op jit(solution)/shard_map/ppermute | solution.py:33
  64.0 0.0 all-to-all-done.2
  64.0 2.0 %final_sum.1 = f32[128,16,128]{2,1,0:T(8,128)} custom-call(s32[8,128]{1,0:T(8,128)S(1)} %get-tuple-element.23.all_picks_ref, f32[128,16,128]{2,1,0:T(8,128)S(1)} %get-tuple-element.32.base_ref, bf16[16,16,128]{2,1,0:T(8,128)(2,1)S(1)} %collective-permute-done.1.halo_ref, bf16[160,16,128]{2,1,0:T(8,128)(2,1)S(1)} %bitcast.11), custom_call_target="tpu_custom_call" | custom-call | bytes 3145728 | tf_op jit(solution)/shard_map/final_sum/pallas_call | solution.py:488
Async XLA Ops:
  0.9 14.6 %collective-permute-start = (bf16[16,16,128]{2,1,0:T(8,128)(2,1)S(1)}, bf16[16,16,128]{2,1,0:T(8,128)(2,1)S(1)}, u32[]{:S(2)}, u32[]{:S(2)}) collective-permute-start(bf16[16,16,128]{2,1,0:T(8,128)(2,1)S(1)} %get-tuple-element.21), channel_id=1, source_target_pairs={{31,0},{0,1},{1,2},{2,3},{3,4},{4,5},{5,6},{6,7},{7,8},{8,9},{9,10... | collective-permute-start | bytes 196616 | tf_op jit(solution)/shard_map/ppermute | solution.py:33
  17.5 20.6 %all-to-all-start.1 = ((bf16[32,5,16,128]{3,2,1,0:T(8,128)(2,1)}), bf16[32,5,16,128]{3,2,1,0:T(8,128)(2,1)S(1)}, u32[]{:S(2)}, u32[]{:S(2)}) async-start(bf16[32,5,16,128]{3,2,1,0:T(8,128)(2,1)} %bitcast.4), calls=%async_computation.1 | async-start | bytes 1310720 | tf_op jit(solution)/shard_map/all_to_all | solution.py:389
  20.1 0.7 %copy-start = (s32[128,4]{0,1:T(4,128)S(1)}, s32[128,4]{0,1:T(4,128)}, u32[]{:S(2)}) copy-start(s32[128,4]{0,1:T(4,128)} %param.7) | copy-start | bytes 6148
  38.0 7.5 %copy-start.1 = (s32[128,4]{0,1:T(4,128)S(1)}, s32[128,4]{0,1:T(4,128)}, u32[]{:S(2)}) copy-start(s32[128,4]{0,1:T(4,128)} %param.7) | copy-start | bytes 6148
  42.1 21.9 %all-to-all-start.2 = ((bf16[32,5,16,128]{3,2,1,0:T(8,128)(2,1)}), bf16[32,5,16,128]{3,2,1,0:T(8,128)(2,1)S(1)}, u32[]{:S(2)}, u32[]{:S(2)}) async-start(bf16[32,5,16,128]{3,2,1,0:T(8,128)(2,1)} %bitcast.6), calls=%async_computation.2 | async-start | bytes 1310720 | tf_op jit(solution)/shard_map/all_to_all | solution.py:389
  56.8 7.2 %collective-permute-start.1 = (bf16[16,16,128]{2,1,0:T(8,128)(2,1)S(1)}, bf16[16,16,128]{2,1,0:T(8,128)(2,1)S(1)}, u32[]{:S(2)}, u32[]{:S(2)}) collective-permute-start(bf16[16,16,128]{2,1,0:T(8,128)(2,1)S(1)} %get-tuple-element.33), channel_id=1, source_target_pairs={{1,0},{2,1},{3,2},{4,3},{5,4},{6,5},{7,6},{8,7},{9,8},{10,9},{11,1... | collective-permute-start | bytes 196616 | tf_op jit(solution)/shard_map/ppermute | solution.py:33

commit v13 on v11

--- a/solution.py
+++ b/solution.py
@@ -250,19 +250,19 @@
 
     for c in range(HELD):
         send_back(c, first_ref)
-
-    @pl.loop(HELD, chunks)
-    def _(c):
-        load(c).wait()
-        send_back(c, mats)
+    middle = (HELD + chunks) // 2
+    for part in (range(HELD, middle), range(middle, chunks)):
+        for c in part:
+            load(c).wait()
+        for c in part:
+            send_back(c, mats)
 
 
 def near_back_kernel(
-    groups, ids_ref, slot_ref, far_ref, part_ref, coeffs_ref, prec_ref,
-    base_ref, halo_ref, total, white, scaled, part, coeffs, prec, sems
+    groups, all_ids_ref, slots_ref, far_ref, part_ref, coeffs_ref, prec_ref,
+    total, halo_ref, white, scaled, part, coeffs, prec, ids_ref, slot_ref, sems
 ):
-    blocks = base_ref.shape[0]
-    points = base_ref.shape[2]
+    blocks, _, points = white.shape
     chunks = blocks // CHUNK
 
     def load(c, which):
@@ -279,7 +279,14 @@
         for which in range(4):
             load(c, which).start()
 
-    for c in range(LEAD):
+    for which in range(3):
+        load(0, which).start()
+    ids_copy = pltpu.make_async_copy(all_ids_ref, ids_ref, sems.at[4, 0])
+    slot_copy = pltpu.make_async_copy(slots_ref, slot_ref, sems.at[4, 1])
+    ids_copy.start()
+    slot_copy.start()
+    load(0, 3).start()
+    for c in range(1, LEAD):
         fetch(c)
     total[pl.ds(0, REACH)] = jnp.zeros((REACH,) + total.shape[1:], jnp.float32)
     first = lax.axis_index("blk") * blocks
@@ -317,6 +324,8 @@
                 for k in range(3):
                     total[places[k]] = olds[k] - terms[b - AHEAD][:, k * points : (k + 1) * points]
 
+    ids_copy.wait()
+    slot_copy.wait()
     mix(0)
     fetch(LEAD)
     scale(0)
@@ -337,15 +346,14 @@
     scale(chunks - 1)
     back(chunks - 1)
     halo_ref[...] = total[pl.ds(0, REACH)].astype(halo_ref.dtype)
-    base_ref[...] = total[pl.ds(REACH, blocks)]
 
 
 def sum_kernel(capacity, all_picks_ref, base_ref, halo_ref, back_ref, out_ref, total, picks_ref, sems):
     groups = back_ref.shape[0] // capacity
     picks_copy = pltpu.make_async_copy(all_picks_ref, picks_ref, sems.at[0])
     picks_copy.start()
-    blocks = base_ref.shape[0]
-    total[pl.ds(0, blocks)] = base_ref[...]
+    blocks = out_ref.shape[0]
+    total[pl.ds(0, blocks)] = base_ref[pl.ds(REACH, blocks)]
     last = pl.ds(blocks - REACH, REACH)
     total[last] = total[last] + halo_ref[...].astype(jnp.float32)
     picks_copy.wait()
@@ -458,17 +466,21 @@
     base, halo_back = pl.pallas_call(
         functools.partial(near_back_kernel, groups),
         name="near_back",
-        out_shape=(tiles_f32, jax.ShapeDtypeStruct((REACH,) + tile, bf16)),
-        in_specs=[SMEM, SMEM, VMEM, HBM, HBM, HBM],
+        out_shape=(
+            jax.ShapeDtypeStruct((REACH + blocks,) + tile, f32),
+            jax.ShapeDtypeStruct((REACH,) + tile, bf16),
+        ),
+        in_specs=[VMEM, VMEM, VMEM, HBM, HBM, HBM],
         out_specs=(VMEM, VMEM),
         scratch_shapes=[
-            pltpu.VMEM((REACH + blocks,) + tile, f32),
             pltpu.VMEM((blocks,) + tile, bf16),
             pltpu.VMEM((blocks,) + tile, bf16),
             pltpu.VMEM((blocks,) + tile, f32),
             all_mats,
             pltpu.VMEM(mats, bf16),
-            pltpu.SemaphoreType.DMA((4, chunks)),
+            pltpu.SMEM(ids.shape, jnp.int32),
+            pltpu.SMEM((1, blocks), jnp.int32),
+            pltpu.SemaphoreType.DMA((5, chunks)),
         ],
         compiler_params=params(36),
         cost_estimate=pl.CostEstimate(flops=5 * flops, bytes_accessed=23 * 2**20, transcendentals=0),

time: 65.2 us -> 64.8 us (level)
  Pallas kernels: 30.3 us -> 29.6 us
  transfers between devices with their start and end apart: 4 -> 4, of which waited for: 2 -> 3; matrix products, arithmetic and copies ran while one was open for 0% -> 0% of each run, Pallas kernels for 35% -> 34%
where the time goes in v13:
time: 64.8 us; the launch traced here: 64.4 us
  Pallas kernels  29.6 us (46%)
  blocking collectives  14.1 us (22%)
  starting transfers between devices  11.8 us (18%)
  waiting for transfers between devices  8.06 us (12%)
  local copies, waits for them, and re-layouts  0.68 us (1%)
    all_to_all x1, blocking collectives, exchange(): return lax.all_to_all(x, 'blk', split_axis=0, concat_axis=0, tiled=True)  14.1 us
    pallas_call x1, Pallas kernels, per_device(): pl.pallas_call(functools.partial(near_forward_kernel, groups, capacity),...  11.3 us
    pallas_call x1, Pallas kernels, per_device(): pl.pallas_call(functools.partial(near_back_kernel, groups), name='near_ba...  10.5 us
    all_to_all x2, waiting for transfers between devices, exchange(): return lax.all_to_all(x, 'blk', split_axis=0, concat_axis=0, tiled=True)  6.15 us
    all_to_all x2, starting transfers between devices, exchange(): return lax.all_to_all(x, 'blk', split_axis=0, concat_axis=0, tiled=True)  6.06 us
    ppermute x2, starting transfers between devices, passed_along(): lax.ppermute(block, axis, [((i - distance) % size, i) for i in range(size)])  5.77 us
    pallas_call x1, Pallas kernels, per_device(): pl.pallas_call(far_kernel, name='far_terms', out_shape=jax.ShapeDtypeStru...  2.99 us
    pallas_call x1, Pallas kernels, per_device(): pl.pallas_call(functools.partial(pick_kernel, capacity), name='pick_tiles...  2.01 us
  transfers between devices with their start and end apart: 4, of which 3 were waited for; matrix products, arithmetic and copies ran while one was open for 0% of the time, Pallas kernels for 34%

profile of v13, /device:TPU:0, one launch (start us, length us, event | category | flops | bytes accessed | tf_op | source)
XLA Modules:
  0.0 64.4 jit_solution(4104828944280595142)
XLA Ops:
  0.0 0.9 %prep.1 = (s32[32,128]{1,0:T(8,128)S(1)}, bf16[16,16,128]{2,1,0:T(8,128)(2,1)S(1)}) custom-call(s32[4,128]{1,0:T(4,128)} %bitcast.13, bf16[128,16,128]{2,1,0:T(8,128)(2,1)} %probe_ref.5), custom_call_target="tpu_custom_call" | custom-call | tf_op jit(solution)/shard_map/prep/pallas_call | solution.py:389
  0.9 0.5 collective-permute-start
  1.4 14.1 %all_to_all.22 = s32[32,1,128]{2,1,0:T(1,128)S(1)} all-to-all(s32[32,1,128]{2,1,0:T(1,128)S(1)} %bitcast.17), channel_id=1, replica_groups=mesh['blk'=32] {'blk'}, dimensions={0} | all-to-all | bytes 32768 | tf_op jit(solution)/shard_map/all_to_all | solution.py:386
  15.5 0.0 collective-permute-done.halo_ref
  15.5 2.0 %pick_tiles.1 = (bf16[160,16,128]{2,1,0:T(8,128)(2,1)}, s32[8,128]{1,0:T(8,128)S(1)}) custom-call(s32[32,128]{1,0:T(8,128)S(1)} %bitcast.12, bf16[128,16,128]{2,1,0:T(8,128)(2,1)} %probe_ref.5), custom_call_target="tpu_custom_call" | custom-call | bytes 1310720 | tf_op jit(solution)/shard_map/pick_tiles/pallas_call | solution.py:404
  17.5 2.6 %all-to-all-start.1 = ((bf16[32,5,16,128]{3,2,1,0:T(8,128)(2,1)}), bf16[32,5,16,128]{3,2,1,0:T(8,128)(2,1)S(1)}, u32[]{:S(2)}, u32[]{:S(2)}) async-start(bf16[32,5,16,128]{3,2,1,0:T(8,128)(2,1)} %bitcast.4), calls=%async_computation.1 | async-start | bytes 1310720 | tf_op jit(solution)/shard_map/all_to_all | solution.py:386
  20.1 0.0 copy-start
  20.1 0.7 %copy-done = s32[128,4]{0,1:T(4,128)S(1)} copy-done((s32[128,4]{0,1:T(4,128)S(1)}, s32[128,4]{0,1:T(4,128)}, u32[]{:S(2)}) %copy-start) | copy-done | bytes 2072
  20.8 11.3 %near_forward.1 = (f32[128,16,128]{2,1,0:T(8,128)}, f32[128,16,128]{2,1,0:T(8,128)S(1)}, s32[1,128]{1,0:T(1,128)S(1)}, bf16[48,128,128]{2,1,0:T(8,128)(2,1)S(1)}, bf16[128,128,128]{2,1,0:T(8,128)(2,1)}) custom-call(s32[4,128]{1,0:T(4,128)S(1)} %bitcast.14, s32[4,128]{1,0:T(4,128)S(1)} %bitcast.15, bf16[16,16,128]{2,1,0:T(8,128)(2,1)S(1)} %collective-permute-done.halo_ref, ...), custom_call_target="tpu_custom_call" | custom-call | flops 1342177280 | bytes 29360128 | tf_op jit(solution)/shard_map/near_forward/pallas_call | solution.py:426
  32.1 5.9 %all-to-all-done.1 = bf16[32,5,16,128]{3,2,1,0:T(8,128)(2,1)S(1)} async-done(((bf16[32,5,16,128]{3,2,1,0:T(8,128)(2,1)}), bf16[32,5,16,128]{3,2,1,0:T(8,128)(2,1)S(1)}, u32[]{:S(2)}, u32[]{:S(2)}) %all-to-all-start.1) | async-done | bytes 655392 | tf_op jit(solution)/shard_map/all_to_all | solution.py:386
  38.0 0.0 copy-start.1
  38.0 3.0 %far_terms.1 = bf16[160,16,128]{2,1,0:T(8,128)(2,1)} custom-call(s32[1,128]{1,0:T(1,128)S(1)} %get-tuple-element.25.slots_ref, f32[128,16,128]{2,1,0:T(8,128)S(1)} %get-tuple-element.26.own_ref, bf16[160,16,128]{2,1,0:T(8,128)(2,1)S(1)} %bitcast.9, bf16[48,128,128]{2,1,0:T(8,128)(2,1)S(1)} %get-tuple-element.28.first_ref, ...), custom_call_target="tpu_custom_call" | custom-call | flops 67108864 | bytes 6291456 | tf_op jit(solution)/shard_map/far_terms/pallas_call | solution.py:450
  41.0 3.4 %all-to-all-start.2 = ((bf16[32,5,16,128]{3,2,1,0:T(8,128)(2,1)}), bf16[32,5,16,128]{3,2,1,0:T(8,128)(2,1)S(1)}, u32[]{:S(2)}, u32[]{:S(2)}) async-start(bf16[32,5,16,128]{3,2,1,0:T(8,128)(2,1)} %bitcast.6), calls=%async_computation.2 | async-start | bytes 1310720 | tf_op jit(solution)/shard_map/all_to_all | solution.py:386
  44.5 0.0 copy-done.1
  44.5 10.5 %near_back.1 = (f32[144,16,128]{2,1,0:T(8,128)S(1)}, bf16[16,16,128]{2,1,0:T(8,128)(2,1)S(1)}) custom-call(s32[4,128]{1,0:T(4,128)S(1)} %bitcast.16, s32[1,128]{1,0:T(1,128)S(1)} %get-tuple-element.25.slots_ref, bf16[160,16,128]{2,1,0:T(8,128)(2,1)S(1)} %bitcast.10, f32[128,16,128]{2,1,0:T(8,128)} %get-tuple-element.31.part_ref, ...), custom_call_target="tpu_custom_call" | custom-call | flops 335544320 | bytes 24117248 | tf_op jit(solution)/shard_map/near_back/pallas_call | solution.py:466
  55.0 5.3 %collective-permute-start.1 = (bf16[16,16,128]{2,1,0:T(8,128)(2,1)S(1)}, bf16[16,16,128]{2,1,0:T(8,128)(2,1)S(1)}, u32[]{:S(2)}, u32[]{:S(2)}) collective-permute-start(bf16[16,16,128]{2,1,0:T(8,128)(2,1)S(1)} %get-tuple-element.33), channel_id=1, source_target_pairs={{1,0},{2,1},{3,2},{4,3},{5,4},{6,5},{7,6},{8,7},{9,8},{10,9},{11,1... | collective-permute-start | bytes 196616 | tf_op jit(solution)/shard_map/ppermute | solution.py:32
  60.3 1.9 %collective-permute-done.1.halo_ref = bf16[16,16,128]{2,1,0:T(8,128)(2,1)S(1)} collective-permute-done((bf16[16,16,128]{2,1,0:T(8,128)(2,1)S(1)}, bf16[16,16,128]{2,1,0:T(8,128)(2,1)S(1)}, u32[]{:S(2)}, u32[]{:S(2)}) %collective-permute-start.1) | collective-permute-done | bytes 65568 | tf_op jit(solution)/shard_map/ppermute | solution.py:32
  62.2 0.2 all-to-all-done.2
  62.4 2.0 %final_sum.1 = f32[128,16,128]{2,1,0:T(8,128)} custom-call(s32[8,128]{1,0:T(8,128)S(1)} %get-tuple-element.23.all_picks_ref, f32[144,16,128]{2,1,0:T(8,128)S(1)} %get-tuple-element.32.base_ref, bf16[16,16,128]{2,1,0:T(8,128)(2,1)S(1)} %collective-permute-done.1.halo_ref, bf16[160,16,128]{2,1,0:T(8,128)(2,1)S(1)} %bitcast.11), custom_call_target="tpu_custom_call" | custom-call | bytes 3145728 | tf_op jit(solution)/shard_map/final_sum/pallas_call | solution.py:489
Async XLA Ops:
  0.9 14.6 %collective-permute-start = (bf16[16,16,128]{2,1,0:T(8,128)(2,1)S(1)}, bf16[16,16,128]{2,1,0:T(8,128)(2,1)S(1)}, u32[]{:S(2)}, u32[]{:S(2)}) collective-permute-start(bf16[16,16,128]{2,1,0:T(8,128)(2,1)S(1)} %get-tuple-element.21), channel_id=1, source_target_pairs={{31,0},{0,1},{1,2},{2,3},{3,4},{4,5},{5,6},{6,7},{7,8},{8,9},{9,10... | collective-permute-start | bytes 196616 | tf_op jit(solution)/shard_map/ppermute | solution.py:32
  17.5 20.6 %all-to-all-start.1 = ((bf16[32,5,16,128]{3,2,1,0:T(8,128)(2,1)}), bf16[32,5,16,128]{3,2,1,0:T(8,128)(2,1)S(1)}, u32[]{:S(2)}, u32[]{:S(2)}) async-start(bf16[32,5,16,128]{3,2,1,0:T(8,128)(2,1)} %bitcast.4), calls=%async_computation.1 | async-start | bytes 1310720 | tf_op jit(solution)/shard_map/all_to_all | solution.py:386
  20.1 0.7 %copy-start = (s32[128,4]{0,1:T(4,128)S(1)}, s32[128,4]{0,1:T(4,128)}, u32[]{:S(2)}) copy-start(s32[128,4]{0,1:T(4,128)} %param.7) | copy-start | bytes 6148
  38.0 6.4 %copy-start.1 = (s32[128,4]{0,1:T(4,128)S(1)}, s32[128,4]{0,1:T(4,128)}, u32[]{:S(2)}) copy-start(s32[128,4]{0,1:T(4,128)} %param.7) | copy-start | bytes 6148
  41.0 21.3 %all-to-all-start.2 = ((bf16[32,5,16,128]{3,2,1,0:T(8,128)(2,1)}), bf16[32,5,16,128]{3,2,1,0:T(8,128)(2,1)S(1)}, u32[]{:S(2)}, u32[]{:S(2)}) async-start(bf16[32,5,16,128]{3,2,1,0:T(8,128)(2,1)} %bitcast.6), calls=%async_computation.2 | async-start | bytes 1310720 | tf_op jit(solution)/shard_map/all_to_all | solution.py:386
  55.0 7.2 %collective-permute-start.1 = (bf16[16,16,128]{2,1,0:T(8,128)(2,1)S(1)}, bf16[16,16,128]{2,1,0:T(8,128)(2,1)S(1)}, u32[]{:S(2)}, u32[]{:S(2)}) collective-permute-start(bf16[16,16,128]{2,1,0:T(8,128)(2,1)S(1)} %get-tuple-element.33), channel_id=1, source_target_pairs={{1,0},{2,1},{3,2},{4,3},{5,4},{6,5},{7,6},{8,7},{9,8},{10,9},{11,1... | collective-permute-start | bytes 196616 | tf_op jit(solution)/shard_map/ppermute | solution.py:32

commit v14 on v13

--- a/solution.py
+++ b/solution.py
@@ -43,18 +43,21 @@
     return jnp.dot(chosen, earlier_matrix(blocks), preferred_element_type=jnp.float32).astype(jnp.int32)
 
 
-def prep_kernel(ids_ref, probe_ref, sent_ref, tail_ref, ids, sems):
+def prep_kernel(ids_ref, probe_ref, sent_ref, tail_ref, scalars_ref, ids, sems):
     blocks = probe_ref.shape[0]
     ids_copy = pltpu.make_async_copy(ids_ref, ids, sems.at[0])
     tail_copy = pltpu.make_async_copy(probe_ref.at[pl.ds(blocks - REACH, REACH)], tail_ref, sems.at[1])
+    scalars_copy = pltpu.make_async_copy(ids_ref, scalars_ref, sems.at[2])
     ids_copy.start()
     tail_copy.start()
+    scalars_copy.start()
     ids_copy.wait()
     sent_ref[...] = jnp.broadcast_to(ids[3:4, :], sent_ref.shape)
     tail_copy.wait()
-
-
-def pick_kernel(capacity, ids_ref, probe_ref, out_ref, picks_ref, probe, out, picks_smem, sems):
+    scalars_copy.wait()
+
+
+def pick_kernel(capacity, ids_ref, probe_ref, out_ref, picks_smem, probe, out, picks_ref, sems):
     groups, blocks = ids_ref.shape
     load = pltpu.make_async_copy(probe_ref, probe, sems.at[0])
     load.start()
@@ -132,7 +135,7 @@
 
 def near_forward_kernel(
     groups, capacity, ids_ref, ids_row_ref, halo_ref, probe_ref, coeffs_ref, prec_ref,
-    part_ref, own_ref, slot_ref, first_ref, mats_ref, ext, coeffs, prec, part, fold, mats, sems
+    part_ref, own_ref, slot_ref, first_ref, mats_ref, ext, coeffs, prec, part, fold, mats, slots, sems
 ):
     blocks = probe_ref.shape[0]
     chunks = blocks // CHUNK
@@ -169,8 +172,11 @@
     owner = ids_row_ref[3:4, :] // blocks
     mask = lax.broadcasted_iota(jnp.int32, (groups, blocks), 0) == owner
     rank = jnp.sum(jnp.where(mask, ranks_in(mask, blocks), 0), axis=0, keepdims=True)
-    slot_ref[...] = owner * capacity + rank
+    slots[...] = owner * capacity + rank
+    slot_copy = pltpu.make_async_copy(slots, slot_ref, sems.at[2, 1])
+    slot_copy.start()
     first = lax.axis_index("blk") * blocks
+    slot_copy.wait()
     own_load.wait()
 
     def make(c):
@@ -226,7 +232,7 @@
         store_mats(c).wait()
 
 
-def far_kernel(slots_ref, own_ref, far_ref, first_ref, mats_ref, parcel_ref, mats, slot, sems):
+def far_kernel(slot, own_ref, far_ref, first_ref, mats_ref, parcel_ref, mats, sems):
     blocks = own_ref.shape[0]
     chunks = blocks // CHUNK
 
@@ -234,12 +240,9 @@
         own = pl.ds(c * CHUNK, CHUNK)
         return pltpu.make_async_copy(mats_ref.at[own], mats.at[own], sems.at[c])
 
-    slot_copy = pltpu.make_async_copy(slots_ref, slot, sems.at[0])
-    slot_copy.start()
     for c in range(HELD, chunks):
         load(c).start()
     parcel_ref[...] = jnp.zeros_like(parcel_ref)
-    slot_copy.wait()
 
     def send_back(c, pair):
         for b in range(0, CHUNK, 4):
@@ -259,8 +262,8 @@
 
 
 def near_back_kernel(
-    groups, all_ids_ref, slots_ref, far_ref, part_ref, coeffs_ref, prec_ref,
-    total, halo_ref, white, scaled, part, coeffs, prec, ids_ref, slot_ref, sems
+    groups, ids_ref, slot_ref, far_ref, part_ref, coeffs_ref, prec_ref,
+    total, halo_ref, white, scaled, part, coeffs, prec, sems
 ):
     blocks, _, points = white.shape
     chunks = blocks // CHUNK
@@ -281,10 +284,6 @@
 
     for which in range(3):
         load(0, which).start()
-    ids_copy = pltpu.make_async_copy(all_ids_ref, ids_ref, sems.at[4, 0])
-    slot_copy = pltpu.make_async_copy(slots_ref, slot_ref, sems.at[4, 1])
-    ids_copy.start()
-    slot_copy.start()
     load(0, 3).start()
     for c in range(1, LEAD):
         fetch(c)
@@ -324,8 +323,6 @@
                 for k in range(3):
                     total[places[k]] = olds[k] - terms[b - AHEAD][:, k * points : (k + 1) * points]
 
-    ids_copy.wait()
-    slot_copy.wait()
     mix(0)
     fetch(LEAD)
     scale(0)
@@ -348,15 +345,12 @@
     halo_ref[...] = total[pl.ds(0, REACH)].astype(halo_ref.dtype)
 
 
-def sum_kernel(capacity, all_picks_ref, base_ref, halo_ref, back_ref, out_ref, total, picks_ref, sems):
+def sum_kernel(capacity, picks_ref, base_ref, halo_ref, back_ref, out_ref, total, sem):
     groups = back_ref.shape[0] // capacity
-    picks_copy = pltpu.make_async_copy(all_picks_ref, picks_ref, sems.at[0])
-    picks_copy.start()
     blocks = out_ref.shape[0]
     total[pl.ds(0, blocks)] = base_ref[pl.ds(REACH, blocks)]
     last = pl.ds(blocks - REACH, REACH)
     total[last] = total[last] + halo_ref[...].astype(jnp.float32)
-    picks_copy.wait()
 
     @pl.loop(0, groups, unroll=8)
     def _(g):
@@ -366,7 +360,7 @@
         for r in range(capacity):
             total[places[r]] = olds[r] - back_ref[g * capacity + r].astype(jnp.float32)
 
-    store = pltpu.make_async_copy(total.at[pl.ds(0, blocks)], out_ref, sems.at[1])
+    store = pltpu.make_async_copy(total.at[pl.ds(0, blocks)], out_ref, sem)
     store.start()
     store.wait()
 
@@ -386,16 +380,17 @@
         return lax.all_to_all(x, "blk", split_axis=0, concat_axis=0, tiled=True)
 
     ids = neighbours.T
-    sent_ids, tail = pl.pallas_call(
+    sent_ids, tail, scalar_ids = pl.pallas_call(
         prep_kernel,
         name="prep",
         out_shape=(
             jax.ShapeDtypeStruct((groups, blocks), jnp.int32),
             jax.ShapeDtypeStruct((REACH,) + tile, bf16),
+            pltpu.SMEM(ids.shape, jnp.int32),
         ),
         in_specs=[HBM, HBM],
-        out_specs=(VMEM, VMEM),
-        scratch_shapes=[pltpu.VMEM(ids.shape, jnp.int32), pltpu.SemaphoreType.DMA((2,))],
+        out_specs=(VMEM, VMEM, SMEM),
+        scratch_shapes=[pltpu.VMEM(ids.shape, jnp.int32), pltpu.SemaphoreType.DMA((3,))],
         compiler_params=params(8),
     )(in_hbm(ids), in_hbm(probe_vecs))
     halo = passed_along(tail, "blk", 1)
@@ -406,14 +401,14 @@
         name="pick_tiles",
         out_shape=(
             jax.ShapeDtypeStruct((slots,) + tile, bf16),
-            jax.ShapeDtypeStruct(picks_shape, jnp.int32),
+            pltpu.SMEM(picks_shape, jnp.int32),
         ),
         in_specs=[VMEM, HBM],
-        out_specs=(HBM, VMEM),
+        out_specs=(HBM, SMEM),
         scratch_shapes=[
             pltpu.VMEM((blocks,) + tile, bf16),
             pltpu.VMEM((slots,) + tile, bf16),
-            pltpu.SMEM(picks_shape, jnp.int32),
+            pltpu.VMEM(picks_shape, jnp.int32),
             pltpu.SemaphoreType.DMA((2 + STORES,)),
         ],
         compiler_params=params(8),
@@ -429,12 +424,12 @@
         out_shape=(
             pltpu.HBM((blocks,) + tile, f32),
             tiles_f32,
-            jax.ShapeDtypeStruct((1, blocks), jnp.int32),
+            pltpu.SMEM((1, blocks), jnp.int32),
             jax.ShapeDtypeStruct((HELD * CHUNK, points, points), bf16),
             pltpu.HBM(mats, bf16),
         ),
         in_specs=[SMEM, VMEM, VMEM, HBM, HBM, HBM],
-        out_specs=(HBM, VMEM, VMEM, VMEM, HBM),
+        out_specs=(HBM, VMEM, SMEM, VMEM, HBM),
         scratch_shapes=[
             pltpu.VMEM((REACH + blocks,) + tile, bf16),
             all_mats,
@@ -442,20 +437,20 @@
             pltpu.VMEM((blocks,) + tile, f32),
             pltpu.VMEM(mats, bf16),
             pltpu.VMEM(mats, bf16),
+            pltpu.VMEM((1, blocks), jnp.int32),
             pltpu.SemaphoreType.DMA((4, chunks)),
         ],
         compiler_params=params(40),
         cost_estimate=pl.CostEstimate(flops=20 * flops, bytes_accessed=28 * 2**20, transcendentals=0),
-    )(ids, ids, halo, in_hbm(probe_vecs), in_hbm(coeffs), in_hbm(cond_prec))
+    )(scalar_ids, ids, halo, in_hbm(probe_vecs), in_hbm(coeffs), in_hbm(cond_prec))
     parcel = pl.pallas_call(
         far_kernel,
         name="far_terms",
         out_shape=jax.ShapeDtypeStruct((slots,) + tile, bf16),
-        in_specs=[VMEM, VMEM, VMEM, VMEM, HBM],
+        in_specs=[SMEM, VMEM, VMEM, VMEM, HBM],
         out_specs=VMEM,
         scratch_shapes=[
             pltpu.VMEM(mats, bf16),
-            pltpu.SMEM((1, blocks), jnp.int32),
             pltpu.SemaphoreType.DMA((chunks,)),
         ],
         compiler_params=params(16),
@@ -470,7 +465,7 @@
             jax.ShapeDtypeStruct((REACH + blocks,) + tile, f32),
             jax.ShapeDtypeStruct((REACH,) + tile, bf16),
         ),
-        in_specs=[VMEM, VMEM, VMEM, HBM, HBM, HBM],
+        in_specs=[SMEM, SMEM, VMEM, HBM, HBM, HBM],
         out_specs=(VMEM, VMEM),
         scratch_shapes=[
             pltpu.VMEM((blocks,) + tile, bf16),
@@ -478,24 +473,21 @@
             pltpu.VMEM((blocks,) + tile, f32),
             all_mats,
             pltpu.VMEM(mats, bf16),
-            pltpu.SMEM(ids.shape, jnp.int32),
-            pltpu.SMEM((1, blocks), jnp.int32),
-            pltpu.SemaphoreType.DMA((5, chunks)),
+            pltpu.SemaphoreType.DMA((4, chunks)),
         ],
         compiler_params=params(36),
         cost_estimate=pl.CostEstimate(flops=5 * flops, bytes_accessed=23 * 2**20, transcendentals=0),
-    )(ids, slot_of, arrived, in_hbm(part), in_hbm(coeffs), in_hbm(cond_prec))
+    )(scalar_ids, slot_of, arrived, in_hbm(part), in_hbm(coeffs), in_hbm(cond_prec))
     halo_sum = passed_along(halo_back, "blk", -1)
     return pl.pallas_call(
         functools.partial(sum_kernel, capacity),
         name="final_sum",
         out_shape=jax.ShapeDtypeStruct((blocks,) + tile, f32),
-        in_specs=[VMEM, VMEM, VMEM, VMEM],
+        in_specs=[SMEM, VMEM, VMEM, VMEM],
         out_specs=HBM,
         scratch_shapes=[
             pltpu.VMEM((blocks + 1,) + tile, f32),
-            pltpu.SMEM(picks_shape, jnp.int32),
-            pltpu.SemaphoreType.DMA((2,)),
+            pltpu.SemaphoreType.DMA,
         ],
         compiler_params=params(8),
         cost_estimate=pl.CostEstimate(flops=0, bytes_accessed=3 * 2**20, transcendentals=0),

time: 64.8 us -> 64.6 us (level)
  Pallas kernels: 29.6 us -> 28.8 us
  transfers between devices with their start and end apart: 4 -> 4, of which waited for: 3 -> 3; matrix products, arithmetic and copies ran while one was open for 0% -> 0% of each run, Pallas kernels for 34% -> 33%
where the time goes in v14:
time: 64.6 us; the launch traced here: 64.1 us
  Pallas kernels  28.8 us (45%)
  blocking collectives  14.1 us (22%)
  starting transfers between devices  11.8 us (18%)
  waiting for transfers between devices  8.68 us (13%)
  local copies, waits for them, and re-layouts  0.68 us (1%)
    all_to_all x1, blocking collectives, exchange(): return lax.all_to_all(x, 'blk', split_axis=0, concat_axis=0, tiled=True)  14.1 us
    pallas_call x1, Pallas kernels, per_device(): pl.pallas_call(functools.partial(near_forward_kernel, groups, capacity),...  10.7 us
    pallas_call x1, Pallas kernels, per_device(): pl.pallas_call(functools.partial(near_back_kernel, groups), name='near_ba...  10.4 us
    all_to_all x2, waiting for transfers between devices, exchange(): return lax.all_to_all(x, 'blk', split_axis=0, concat_axis=0, tiled=True)  6.77 us
    all_to_all x2, starting transfers between devices, exchange(): return lax.all_to_all(x, 'blk', split_axis=0, concat_axis=0, tiled=True)  6.05 us
    ppermute x2, starting transfers between devices, passed_along(): lax.ppermute(block, axis, [((i - distance) % size, i) for i in range(size)])  5.77 us
    pallas_call x1, Pallas kernels, per_device(): pl.pallas_call(far_kernel, name='far_terms', out_shape=jax.ShapeDtypeStru...  3.27 us
    pallas_call x1, Pallas kernels, per_device(): pl.pallas_call(functools.partial(pick_kernel, capacity), name='pick_tiles...  2.05 us
  transfers between devices with their start and end apart: 4, of which 3 were waited for; matrix products, arithmetic and copies ran while one was open for 0% of the time, Pallas kernels for 33%

profile of v14, /device:TPU:0, one launch (start us, length us, event | category | flops | bytes accessed | tf_op | source)
XLA Modules:
  0.0 64.1 jit_solution(13838165102710078962)
XLA Ops:
  0.0 0.9 %prep.1 = (s32[32,128]{1,0:T(8,128)S(1)}, bf16[16,16,128]{2,1,0:T(8,128)(2,1)S(1)}, s32[4,128]{1,0:T(4,128)S(4)}) custom-call(s32[4,128]{1,0:T(4,128)} %bitcast.14, bf16[128,16,128]{2,1,0:T(8,128)(2,1)} %probe_ref.5), custom_call_target="tpu_custom_call" | custom-call | tf_op jit(solution)/shard_map/prep/pallas_call | solution.py:383
  0.9 0.5 collective-permute-start
  1.4 14.1 %all_to_all.22 = s32[32,1,128]{2,1,0:T(1,128)S(1)} all-to-all(s32[32,1,128]{2,1,0:T(1,128)S(1)} %bitcast.13), channel_id=1, replica_groups=mesh['blk'=32] {'blk'}, dimensions={0} | all-to-all | bytes 32768 | tf_op jit(solution)/shard_map/all_to_all | solution.py:380
  15.5 0.0 collective-permute-done.halo_ref
  15.5 2.0 %pick_tiles.1 = (bf16[160,16,128]{2,1,0:T(8,128)(2,1)}, s32[8,128]{1,0:T(8,128)S(4)}) custom-call(s32[32,128]{1,0:T(8,128)S(1)} %bitcast.12, bf16[128,16,128]{2,1,0:T(8,128)(2,1)} %probe_ref.5), custom_call_target="tpu_custom_call" | custom-call | bytes 1310720 | tf_op jit(solution)/shard_map/pick_tiles/pallas_call | solution.py:399
  17.5 2.6 %all-to-all-start.1 = ((bf16[32,5,16,128]{3,2,1,0:T(8,128)(2,1)}), bf16[32,5,16,128]{3,2,1,0:T(8,128)(2,1)S(1)}, u32[]{:S(2)}, u32[]{:S(2)}) async-start(bf16[32,5,16,128]{3,2,1,0:T(8,128)(2,1)} %bitcast.4), calls=%async_computation.1 | async-start | bytes 1310720 | tf_op jit(solution)/shard_map/all_to_all | solution.py:380
  20.2 0.0 copy-start
  20.2 0.7 %copy-done = s32[128,4]{0,1:T(4,128)S(1)} copy-done((s32[128,4]{0,1:T(4,128)S(1)}, s32[128,4]{0,1:T(4,128)}, u32[]{:S(2)}) %copy-start) | copy-done | bytes 2072
  20.9 10.7 %near_forward.1 = (f32[128,16,128]{2,1,0:T(8,128)}, f32[128,16,128]{2,1,0:T(8,128)S(1)}, s32[1,128]{1,0:T(1,128)S(4)}, bf16[48,128,128]{2,1,0:T(8,128)(2,1)S(1)}, bf16[128,128,128]{2,1,0:T(8,128)(2,1)}) custom-call(s32[4,128]{1,0:T(4,128)S(4)} %get-tuple-element.25.ids_ref, s32[4,128]{1,0:T(4,128)S(1)} %bitcast.15, ...), custom_call_target="tpu_custom_call" | custom-call | flops 1342177280 | bytes 29360128 | tf_op jit(solution)/shard_map/near_forward/pallas_call | solution.py:421
  31.6 6.5 %all-to-all-done.1 = bf16[32,5,16,128]{3,2,1,0:T(8,128)(2,1)S(1)} async-done(((bf16[32,5,16,128]{3,2,1,0:T(8,128)(2,1)}), bf16[32,5,16,128]{3,2,1,0:T(8,128)(2,1)S(1)}, u32[]{:S(2)}, u32[]{:S(2)}) %all-to-all-start.1) | async-done | bytes 655392 | tf_op jit(solution)/shard_map/all_to_all | solution.py:380
  38.1 3.3 %far_terms.1 = bf16[160,16,128]{2,1,0:T(8,128)(2,1)} custom-call(s32[1,128]{1,0:T(1,128)S(4)} %get-tuple-element.27.slot.slot_ref, f32[128,16,128]{2,1,0:T(8,128)S(1)} %get-tuple-element.28.own_ref, bf16[160,16,128]{2,1,0:T(8,128)(2,1)S(1)} %bitcast.9, bf16[48,128,128]{2,1,0:T(8,128)(2,1)S(1)} %get-tuple-element.30.first_ref, ...), custom_call_target="tpu_custom_call" | custom-call | flops 67108864 | bytes 6291456 | tf_op jit(solution)/shard_map/far_terms/pallas_call | solution.py:446
  41.4 3.4 %all-to-all-start.2 = ((bf16[32,5,16,128]{3,2,1,0:T(8,128)(2,1)}), bf16[32,5,16,128]{3,2,1,0:T(8,128)(2,1)S(1)}, u32[]{:S(2)}, u32[]{:S(2)}) async-start(bf16[32,5,16,128]{3,2,1,0:T(8,128)(2,1)} %bitcast.6), calls=%async_computation.2 | async-start | bytes 1310720 | tf_op jit(solution)/shard_map/all_to_all | solution.py:380
  44.8 10.4 %near_back.1 = (f32[144,16,128]{2,1,0:T(8,128)S(1)}, bf16[16,16,128]{2,1,0:T(8,128)(2,1)S(1)}) custom-call(s32[4,128]{1,0:T(4,128)S(4)} %get-tuple-element.25.ids_ref, s32[1,128]{1,0:T(1,128)S(4)} %get-tuple-element.27.slot.slot_ref, bf16[160,16,128]{2,1,0:T(8,128)(2,1)S(1)} %bitcast.10, f32[128,16,128]{2,1,0:T(8,128)} %get-tuple-element.33.part_ref, ...), custom_call_target="tpu_custom_call" | custom-call | flops 335544320 | bytes 24117248 | tf_op jit(solution)/shard_map/near_back/pallas_call | solution.py:461
  55.3 5.3 %collective-permute-start.1 = (bf16[16,16,128]{2,1,0:T(8,128)(2,1)S(1)}, bf16[16,16,128]{2,1,0:T(8,128)(2,1)S(1)}, u32[]{:S(2)}, u32[]{:S(2)}) collective-permute-start(bf16[16,16,128]{2,1,0:T(8,128)(2,1)S(1)} %get-tuple-element.35), channel_id=1, source_target_pairs={{1,0},{2,1},{3,2},{4,3},{5,4},{6,5},{7,6},{8,7},{9,8},{10,9},{11,1... | collective-permute-start | bytes 196616 | tf_op jit(solution)/shard_map/ppermute | solution.py:32
  60.5 1.9 %collective-permute-done.1.halo_ref = bf16[16,16,128]{2,1,0:T(8,128)(2,1)S(1)} collective-permute-done((bf16[16,16,128]{2,1,0:T(8,128)(2,1)S(1)}, bf16[16,16,128]{2,1,0:T(8,128)(2,1)S(1)}, u32[]{:S(2)}, u32[]{:S(2)}) %collective-permute-start.1) | collective-permute-done | bytes 65568 | tf_op jit(solution)/shard_map/ppermute | solution.py:32
  62.4 0.3 all-to-all-done.2
  62.7 1.4 %final_sum.1 = f32[128,16,128]{2,1,0:T(8,128)} custom-call(s32[8,128]{1,0:T(8,128)S(4)} %get-tuple-element.24.picks_ref, f32[144,16,128]{2,1,0:T(8,128)S(1)} %get-tuple-element.34.base_ref, bf16[16,16,128]{2,1,0:T(8,128)(2,1)S(1)} %collective-permute-done.1.halo_ref, bf16[160,16,128]{2,1,0:T(8,128)(2,1)S(1)} %bitcast.11), custom_call_target="tpu_custom_call" | custom-call | bytes 3145728 | tf_op jit(solution)/shard_map/final_sum/pallas_call | solution.py:482
Async XLA Ops:
  0.9 14.6 %collective-permute-start = (bf16[16,16,128]{2,1,0:T(8,128)(2,1)S(1)}, bf16[16,16,128]{2,1,0:T(8,128)(2,1)S(1)}, u32[]{:S(2)}, u32[]{:S(2)}) collective-permute-start(bf16[16,16,128]{2,1,0:T(8,128)(2,1)S(1)} %get-tuple-element.22), channel_id=1, source_target_pairs={{31,0},{0,1},{1,2},{2,3},{3,4},{4,5},{5,6},{6,7},{7,8},{8,9},{9,10... | collective-permute-start | bytes 196616 | tf_op jit(solution)/shard_map/ppermute | solution.py:32
  17.5 20.6 %all-to-all-start.1 = ((bf16[32,5,16,128]{3,2,1,0:T(8,128)(2,1)}), bf16[32,5,16,128]{3,2,1,0:T(8,128)(2,1)S(1)}, u32[]{:S(2)}, u32[]{:S(2)}) async-start(bf16[32,5,16,128]{3,2,1,0:T(8,128)(2,1)} %bitcast.4), calls=%async_computation.1 | async-start | bytes 1310720 | tf_op jit(solution)/shard_map/all_to_all | solution.py:380
  20.2 0.7 %copy-start = (s32[128,4]{0,1:T(4,128)S(1)}, s32[128,4]{0,1:T(4,128)}, u32[]{:S(2)}) copy-start(s32[128,4]{0,1:T(4,128)} %param.7) | copy-start | bytes 6148
  41.4 21.3 %all-to-all-start.2 = ((bf16[32,5,16,128]{3,2,1,0:T(8,128)(2,1)}), bf16[32,5,16,128]{3,2,1,0:T(8,128)(2,1)S(1)}, u32[]{:S(2)}, u32[]{:S(2)}) async-start(bf16[32,5,16,128]{3,2,1,0:T(8,128)(2,1)} %bitcast.6), calls=%async_computation.2 | async-start | bytes 1310720 | tf_op jit(solution)/shard_map/all_to_all | solution.py:380
  55.3 7.2 %collective-permute-start.1 = (bf16[16,16,128]{2,1,0:T(8,128)(2,1)S(1)}, bf16[16,16,128]{2,1,0:T(8,128)(2,1)S(1)}, u32[]{:S(2)}, u32[]{:S(2)}) collective-permute-start(bf16[16,16,128]{2,1,0:T(8,128)(2,1)S(1)} %get-tuple-element.35), channel_id=1, source_target_pairs={{1,0},{2,1},{3,2},{4,3},{5,4},{6,5},{7,6},{8,7},{9,8},{10,9},{11,1... | collective-permute-start | bytes 196616 | tf_op jit(solution)/shard_map/ppermute | solution.py:32

commit v15 on v14

--- a/solution.py
+++ b/solution.py
@@ -253,11 +253,11 @@
 
     for c in range(HELD):
         send_back(c, first_ref)
-    middle = (HELD + chunks) // 2
-    for part in (range(HELD, middle), range(middle, chunks)):
-        for c in part:
+    for c in range(HELD, chunks, 2):
+        piece = range(c, min(c + 2, chunks))
+        for c in piece:
             load(c).wait()
-        for c in part:
+        for c in piece:
             send_back(c, mats)
 
 

time: 64.6 us -> 64.5 us (level)
  no operation moved by 1% of the time
where the time goes in v15:
time: 64.5 us; the launch traced here: 64.1 us
  Pallas kernels  28.8 us (45%)
  blocking collectives  14.1 us (22%)
  starting transfers between devices  11.8 us (18%)
  waiting for transfers between devices  8.66 us (13%)
  local copies, waits for them, and re-layouts  0.68 us (1%)
    all_to_all x1, blocking collectives, exchange(): return lax.all_to_all(x, 'blk', split_axis=0, concat_axis=0, tiled=True)  14.1 us
    pallas_call x1, Pallas kernels, per_device(): pl.pallas_call(functools.partial(near_forward_kernel, groups, capacity),...  10.8 us
    pallas_call x1, Pallas kernels, per_device(): pl.pallas_call(functools.partial(near_back_kernel, groups), name='near_ba...  10.4 us
    all_to_all x2, waiting for transfers between devices, exchange(): return lax.all_to_all(x, 'blk', split_axis=0, concat_axis=0, tiled=True)  6.75 us
    all_to_all x2, starting transfers between devices, exchange(): return lax.all_to_all(x, 'blk', split_axis=0, concat_axis=0, tiled=True)  6.05 us
    ppermute x2, starting transfers between devices, passed_along(): lax.ppermute(block, axis, [((i - distance) % size, i) for i in range(size)])  5.8 us
    pallas_call x1, Pallas kernels, per_device(): pl.pallas_call(far_kernel, name='far_terms', out_shape=jax.ShapeDtypeStru...  3.25 us
    pallas_call x1, Pallas kernels, per_device(): pl.pallas_call(functools.partial(pick_kernel, capacity), name='pick_tiles...  2.05 us
  transfers between devices with their start and end apart: 4, of which 3 were waited for; matrix products, arithmetic and copies ran while one was open for 0% of the time, Pallas kernels for 33%

profile of v15, /device:TPU:0, one launch (start us, length us, event | category | flops | bytes accessed | tf_op | source)
XLA Modules:
  0.0 64.1 jit_solution(718399508933508260)
XLA Ops:
  0.0 0.9 %prep.1 = (s32[32,128]{1,0:T(8,128)S(1)}, bf16[16,16,128]{2,1,0:T(8,128)(2,1)S(1)}, s32[4,128]{1,0:T(4,128)S(4)}) custom-call(s32[4,128]{1,0:T(4,128)} %bitcast.14, bf16[128,16,128]{2,1,0:T(8,128)(2,1)} %probe_ref.5), custom_call_target="tpu_custom_call" | custom-call | tf_op jit(solution)/shard_map/prep/pallas_call | solution.py:383
  0.9 0.5 collective-permute-start
  1.4 14.1 %all_to_all.22 = s32[32,1,128]{2,1,0:T(1,128)S(1)} all-to-all(s32[32,1,128]{2,1,0:T(1,128)S(1)} %bitcast.13), channel_id=1, replica_groups=mesh['blk'=32] {'blk'}, dimensions={0} | all-to-all | bytes 32768 | tf_op jit(solution)/shard_map/all_to_all | solution.py:380
  15.5 0.0 collective-permute-done.halo_ref
  15.5 2.0 %pick_tiles.1 = (bf16[160,16,128]{2,1,0:T(8,128)(2,1)}, s32[8,128]{1,0:T(8,128)S(4)}) custom-call(s32[32,128]{1,0:T(8,128)S(1)} %bitcast.12, bf16[128,16,128]{2,1,0:T(8,128)(2,1)} %probe_ref.5), custom_call_target="tpu_custom_call" | custom-call | bytes 1310720 | tf_op jit(solution)/shard_map/pick_tiles/pallas_call | solution.py:399
  17.5 2.6 %all-to-all-start.1 = ((bf16[32,5,16,128]{3,2,1,0:T(8,128)(2,1)}), bf16[32,5,16,128]{3,2,1,0:T(8,128)(2,1)S(1)}, u32[]{:S(2)}, u32[]{:S(2)}) async-start(bf16[32,5,16,128]{3,2,1,0:T(8,128)(2,1)} %bitcast.4), calls=%async_computation.1 | async-start | bytes 1310720 | tf_op jit(solution)/shard_map/all_to_all | solution.py:380
  20.2 0.0 copy-start
  20.2 0.7 %copy-done = s32[128,4]{0,1:T(4,128)S(1)} copy-done((s32[128,4]{0,1:T(4,128)S(1)}, s32[128,4]{0,1:T(4,128)}, u32[]{:S(2)}) %copy-start) | copy-done | bytes 2072
  20.9 10.8 %near_forward.1 = (f32[128,16,128]{2,1,0:T(8,128)}, f32[128,16,128]{2,1,0:T(8,128)S(1)}, s32[1,128]{1,0:T(1,128)S(4)}, bf16[48,128,128]{2,1,0:T(8,128)(2,1)S(1)}, bf16[128,128,128]{2,1,0:T(8,128)(2,1)}) custom-call(s32[4,128]{1,0:T(4,128)S(4)} %get-tuple-element.25.ids_ref, s32[4,128]{1,0:T(4,128)S(1)} %bitcast.15, ...), custom_call_target="tpu_custom_call" | custom-call | flops 1342177280 | bytes 29360128 | tf_op jit(solution)/shard_map/near_forward/pallas_call | solution.py:421
  31.6 6.5 %all-to-all-done.1 = bf16[32,5,16,128]{3,2,1,0:T(8,128)(2,1)S(1)} async-done(((bf16[32,5,16,128]{3,2,1,0:T(8,128)(2,1)}), bf16[32,5,16,128]{3,2,1,0:T(8,128)(2,1)S(1)}, u32[]{:S(2)}, u32[]{:S(2)}) %all-to-all-start.1) | async-done | bytes 655392 | tf_op jit(solution)/shard_map/all_to_all | solution.py:380
  38.1 3.3 %far_terms.1 = bf16[160,16,128]{2,1,0:T(8,128)(2,1)} custom-call(s32[1,128]{1,0:T(1,128)S(4)} %get-tuple-element.27.slot.slot_ref, f32[128,16,128]{2,1,0:T(8,128)S(1)} %get-tuple-element.28.own_ref, bf16[160,16,128]{2,1,0:T(8,128)(2,1)S(1)} %bitcast.9, bf16[48,128,128]{2,1,0:T(8,128)(2,1)S(1)} %get-tuple-element.30.first_ref, ...), custom_call_target="tpu_custom_call" | custom-call | flops 67108864 | bytes 6291456 | tf_op jit(solution)/shard_map/far_terms/pallas_call | solution.py:446
  41.4 3.4 %all-to-all-start.2 = ((bf16[32,5,16,128]{3,2,1,0:T(8,128)(2,1)}), bf16[32,5,16,128]{3,2,1,0:T(8,128)(2,1)S(1)}, u32[]{:S(2)}, u32[]{:S(2)}) async-start(bf16[32,5,16,128]{3,2,1,0:T(8,128)(2,1)} %bitcast.6), calls=%async_computation.2 | async-start | bytes 1310720 | tf_op jit(solution)/shard_map/all_to_all | solution.py:380
  44.8 10.4 %near_back.1 = (f32[144,16,128]{2,1,0:T(8,128)S(1)}, bf16[16,16,128]{2,1,0:T(8,128)(2,1)S(1)}) custom-call(s32[4,128]{1,0:T(4,128)S(4)} %get-tuple-element.25.ids_ref, s32[1,128]{1,0:T(1,128)S(4)} %get-tuple-element.27.slot.slot_ref, bf16[160,16,128]{2,1,0:T(8,128)(2,1)S(1)} %bitcast.10, f32[128,16,128]{2,1,0:T(8,128)} %get-tuple-element.33.part_ref, ...), custom_call_target="tpu_custom_call" | custom-call | flops 335544320 | bytes 24117248 | tf_op jit(solution)/shard_map/near_back/pallas_call | solution.py:461
  55.2 5.3 %collective-permute-start.1 = (bf16[16,16,128]{2,1,0:T(8,128)(2,1)S(1)}, bf16[16,16,128]{2,1,0:T(8,128)(2,1)S(1)}, u32[]{:S(2)}, u32[]{:S(2)}) collective-permute-start(bf16[16,16,128]{2,1,0:T(8,128)(2,1)S(1)} %get-tuple-element.35), channel_id=1, source_target_pairs={{1,0},{2,1},{3,2},{4,3},{5,4},{6,5},{7,6},{8,7},{9,8},{10,9},{11,1... | collective-permute-start | bytes 196616 | tf_op jit(solution)/shard_map/ppermute | solution.py:32
  60.5 1.9 %collective-permute-done.1.halo_ref = bf16[16,16,128]{2,1,0:T(8,128)(2,1)S(1)} collective-permute-done((bf16[16,16,128]{2,1,0:T(8,128)(2,1)S(1)}, bf16[16,16,128]{2,1,0:T(8,128)(2,1)S(1)}, u32[]{:S(2)}, u32[]{:S(2)}) %collective-permute-start.1) | collective-permute-done | bytes 65568 | tf_op jit(solution)/shard_map/ppermute | solution.py:32
  62.4 0.3 all-to-all-done.2
  62.7 1.4 %final_sum.1 = f32[128,16,128]{2,1,0:T(8,128)} custom-call(s32[8,128]{1,0:T(8,128)S(4)} %get-tuple-element.24.picks_ref, f32[144,16,128]{2,1,0:T(8,128)S(1)} %get-tuple-element.34.base_ref, bf16[16,16,128]{2,1,0:T(8,128)(2,1)S(1)} %collective-permute-done.1.halo_ref, bf16[160,16,128]{2,1,0:T(8,128)(2,1)S(1)} %bitcast.11), custom_call_target="tpu_custom_call" | custom-call | bytes 3145728 | tf_op jit(solution)/shard_map/final_sum/pallas_call | solution.py:482
Async XLA Ops:
  0.9 14.6 %collective-permute-start = (bf16[16,16,128]{2,1,0:T(8,128)(2,1)S(1)}, bf16[16,16,128]{2,1,0:T(8,128)(2,1)S(1)}, u32[]{:S(2)}, u32[]{:S(2)}) collective-permute-start(bf16[16,16,128]{2,1,0:T(8,128)(2,1)S(1)} %get-tuple-element.22), channel_id=1, source_target_pairs={{31,0},{0,1},{1,2},{2,3},{3,4},{4,5},{5,6},{6,7},{7,8},{8,9},{9,10... | collective-permute-start | bytes 196616 | tf_op jit(solution)/shard_map/ppermute | solution.py:32
  17.5 20.6 %all-to-all-start.1 = ((bf16[32,5,16,128]{3,2,1,0:T(8,128)(2,1)}), bf16[32,5,16,128]{3,2,1,0:T(8,128)(2,1)S(1)}, u32[]{:S(2)}, u32[]{:S(2)}) async-start(bf16[32,5,16,128]{3,2,1,0:T(8,128)(2,1)} %bitcast.4), calls=%async_computation.1 | async-start | bytes 1310720 | tf_op jit(solution)/shard_map/all_to_all | solution.py:380
  20.2 0.7 %copy-start = (s32[128,4]{0,1:T(4,128)S(1)}, s32[128,4]{0,1:T(4,128)}, u32[]{:S(2)}) copy-start(s32[128,4]{0,1:T(4,128)} %param.7) | copy-start | bytes 6148
  41.4 21.3 %all-to-all-start.2 = ((bf16[32,5,16,128]{3,2,1,0:T(8,128)(2,1)}), bf16[32,5,16,128]{3,2,1,0:T(8,128)(2,1)S(1)}, u32[]{:S(2)}, u32[]{:S(2)}) async-start(bf16[32,5,16,128]{3,2,1,0:T(8,128)(2,1)} %bitcast.6), calls=%async_computation.2 | async-start | bytes 1310720 | tf_op jit(solution)/shard_map/all_to_all | solution.py:380
  55.2 7.2 %collective-permute-start.1 = (bf16[16,16,128]{2,1,0:T(8,128)(2,1)S(1)}, bf16[16,16,128]{2,1,0:T(8,128)(2,1)S(1)}, u32[]{:S(2)}, u32[]{:S(2)}) collective-permute-start(bf16[16,16,128]{2,1,0:T(8,128)(2,1)S(1)} %get-tuple-element.35), channel_id=1, source_target_pairs={{1,0},{2,1},{3,2},{4,3},{5,4},{6,5},{7,6},{8,7},{9,8},{10,9},{11,1... | collective-permute-start | bytes 196616 | tf_op jit(solution)/shard_map/ppermute | solution.py:32

commit v16 on v15

--- a/solution.py
+++ b/solution.py
@@ -83,14 +83,16 @@
         rows = pl.ds(p * part * capacity, part * capacity)
         return pltpu.make_async_copy(out.at[rows], out_ref.at[rows], sems.at[2 + p])
 
-    for p in range(STORES):
-
-        @pl.loop(p * part, (p + 1) * part, unroll=8)
-        def _(g):
-            for r in range(capacity):
-                out[g * capacity + r] = probe[jnp.maximum(picks_smem[r, g] - 1, 0)]
+    @pl.loop(0, STORES)
+    def _(p):
+        @pl.loop(p * part, (p + 1) * part, step=4)
+        def _(first):
+            for j in range(4):
+                for r in range(capacity):
+                    out[(first + j) * capacity + r] = probe[jnp.maximum(picks_smem[r, first + j] - 1, 0)]
 
         store(p).start()
+
     for p in range(STORES):
         store(p).wait()
 
@@ -242,7 +244,6 @@
 
     for c in range(HELD, chunks):
         load(c).start()
-    parcel_ref[...] = jnp.zeros_like(parcel_ref)
 
     def send_back(c, pair):
         for b in range(0, CHUNK, 4):
@@ -251,14 +252,14 @@
             for j in range(4):
                 parcel_ref[slot[0, i + j]] = (own_ref[i + j] - mixed[j]).astype(jnp.bfloat16)
 
-    for c in range(HELD):
+    @pl.loop(0, HELD)
+    def _(c):
         send_back(c, first_ref)
-    for c in range(HELD, chunks, 2):
-        piece = range(c, min(c + 2, chunks))
-        for c in piece:
-            load(c).wait()
-        for c in piece:
-            send_back(c, mats)
+
+    @pl.loop(HELD, chunks)
+    def _(c):
+        load(c).wait()
+        send_back(c, mats)
 
 
 def near_back_kernel(
@@ -348,11 +349,15 @@
 def sum_kernel(capacity, picks_ref, base_ref, halo_ref, back_ref, out_ref, total, sem):
     groups = back_ref.shape[0] // capacity
     blocks = out_ref.shape[0]
-    total[pl.ds(0, blocks)] = base_ref[pl.ds(REACH, blocks)]
+
+    @pl.loop(0, blocks, unroll=8)
+    def _(i):
+        total[i] = base_ref[REACH + i]
+
     last = pl.ds(blocks - REACH, REACH)
     total[last] = total[last] + halo_ref[...].astype(jnp.float32)
 
-    @pl.loop(0, groups, unroll=8)
+    @pl.loop(0, groups, unroll=4)
     def _(g):
         picks = [picks_ref[r, g] for r in range(capacity)]
         places = [jnp.where(pick > 0, pick - 1, blocks) for pick in picks]

time: 64.5 us -> 64.5 us (level)
  no operation moved by 1% of the time
where the time goes in v16:
time: 64.5 us; the launch traced here: 64.1 us
  Pallas kernels  28.7 us (44%)
  blocking collectives  14.1 us (22%)
  starting transfers between devices  11.8 us (18%)
  waiting for transfers between devices  8.71 us (14%)
  local copies, waits for them, and re-layouts  0.68 us (1%)
    all_to_all x1, blocking collectives, exchange(): return lax.all_to_all(x, 'blk', split_axis=0, concat_axis=0, tiled=True)  14.1 us
    pallas_call x1, Pallas kernels, per_device(): pl.pallas_call(functools.partial(near_forward_kernel, groups, capacity),...  10.7 us
    pallas_call x1, Pallas kernels, per_device(): pl.pallas_call(functools.partial(near_back_kernel, groups), name='near_ba...  10.4 us
    all_to_all x2, waiting for transfers between devices, exchange(): return lax.all_to_all(x, 'blk', split_axis=0, concat_axis=0, tiled=True)  6.8 us
    all_to_all x2, starting transfers between devices, exchange(): return lax.all_to_all(x, 'blk', split_axis=0, concat_axis=0, tiled=True)  6.05 us
    ppermute x2, starting transfers between devices, passed_along(): lax.ppermute(block, axis, [((i - distance) % size, i) for i in range(size)])  5.78 us
    pallas_call x1, Pallas kernels, per_device(): pl.pallas_call(far_kernel, name='far_terms', out_shape=jax.ShapeDtypeStru...  3.03 us
    pallas_call x1, Pallas kernels, per_device(): pl.pallas_call(functools.partial(pick_kernel, capacity), name='pick_tiles...  2.17 us
  transfers between devices with their start and end apart: 4, of which 3 were waited for; matrix products, arithmetic and copies ran while one was open for 0% of the time, Pallas kernels for 33%

profile of v16, /device:TPU:0, one launch (start us, length us, event | category | flops | bytes accessed | tf_op | source)
XLA Modules:
  0.0 64.1 jit_solution(10878916807513813177)
XLA Ops:
  0.0 0.9 %prep.1 = (s32[32,128]{1,0:T(8,128)S(1)}, bf16[16,16,128]{2,1,0:T(8,128)(2,1)S(1)}, s32[4,128]{1,0:T(4,128)S(4)}) custom-call(s32[4,128]{1,0:T(4,128)} %bitcast.14, bf16[128,16,128]{2,1,0:T(8,128)(2,1)} %probe_ref.5), custom_call_target="tpu_custom_call" | custom-call | tf_op jit(solution)/shard_map/prep/pallas_call | solution.py:388
  0.9 0.5 collective-permute-start
  1.4 14.1 %all_to_all.22 = s32[32,1,128]{2,1,0:T(1,128)S(1)} all-to-all(s32[32,1,128]{2,1,0:T(1,128)S(1)} %bitcast.13), channel_id=1, replica_groups=mesh['blk'=32] {'blk'}, dimensions={0} | all-to-all | bytes 32768 | tf_op jit(solution)/shard_map/all_to_all | solution.py:385
  15.5 0.0 collective-permute-done.halo_ref
  15.5 2.2 %pick_tiles.1 = (bf16[160,16,128]{2,1,0:T(8,128)(2,1)}, s32[8,128]{1,0:T(8,128)S(4)}) custom-call(s32[32,128]{1,0:T(8,128)S(1)} %bitcast.12, bf16[128,16,128]{2,1,0:T(8,128)(2,1)} %probe_ref.5), custom_call_target="tpu_custom_call" | custom-call | bytes 1310720 | tf_op jit(solution)/shard_map/pick_tiles/pallas_call | solution.py:404
  17.7 2.6 %all-to-all-start.1 = ((bf16[32,5,16,128]{3,2,1,0:T(8,128)(2,1)}), bf16[32,5,16,128]{3,2,1,0:T(8,128)(2,1)S(1)}, u32[]{:S(2)}, u32[]{:S(2)}) async-start(bf16[32,5,16,128]{3,2,1,0:T(8,128)(2,1)} %bitcast.4), calls=%async_computation.1 | async-start | bytes 1310720 | tf_op jit(solution)/shard_map/all_to_all | solution.py:385
  20.3 0.0 copy-start
  20.3 0.7 %copy-done = s32[128,4]{0,1:T(4,128)S(1)} copy-done((s32[128,4]{0,1:T(4,128)S(1)}, s32[128,4]{0,1:T(4,128)}, u32[]{:S(2)}) %copy-start) | copy-done | bytes 2072
  21.0 10.7 %near_forward.1 = (f32[128,16,128]{2,1,0:T(8,128)}, f32[128,16,128]{2,1,0:T(8,128)S(1)}, s32[1,128]{1,0:T(1,128)S(4)}, bf16[48,128,128]{2,1,0:T(8,128)(2,1)S(1)}, bf16[128,128,128]{2,1,0:T(8,128)(2,1)}) custom-call(s32[4,128]{1,0:T(4,128)S(4)} %get-tuple-element.25.ids_ref, s32[4,128]{1,0:T(4,128)S(1)} %bitcast.15, ...), custom_call_target="tpu_custom_call" | custom-call | flops 1342177280 | bytes 29360128 | tf_op jit(solution)/shard_map/near_forward/pallas_call | solution.py:426
  31.7 6.5 %all-to-all-done.1 = bf16[32,5,16,128]{3,2,1,0:T(8,128)(2,1)S(1)} async-done(((bf16[32,5,16,128]{3,2,1,0:T(8,128)(2,1)}), bf16[32,5,16,128]{3,2,1,0:T(8,128)(2,1)S(1)}, u32[]{:S(2)}, u32[]{:S(2)}) %all-to-all-start.1) | async-done | bytes 655392 | tf_op jit(solution)/shard_map/all_to_all | solution.py:385
  38.2 3.0 %far_terms.1 = bf16[160,16,128]{2,1,0:T(8,128)(2,1)} custom-call(s32[1,128]{1,0:T(1,128)S(4)} %get-tuple-element.27.slot.slot_ref, f32[128,16,128]{2,1,0:T(8,128)S(1)} %get-tuple-element.28.own_ref, bf16[160,16,128]{2,1,0:T(8,128)(2,1)S(1)} %bitcast.9, bf16[48,128,128]{2,1,0:T(8,128)(2,1)S(1)} %get-tuple-element.30.first_ref, ...), custom_call_target="tpu_custom_call" | custom-call | flops 67108864 | bytes 6291456 | tf_op jit(solution)/shard_map/far_terms/pallas_call | solution.py:451
  41.3 3.4 %all-to-all-start.2 = ((bf16[32,5,16,128]{3,2,1,0:T(8,128)(2,1)}), bf16[32,5,16,128]{3,2,1,0:T(8,128)(2,1)S(1)}, u32[]{:S(2)}, u32[]{:S(2)}) async-start(bf16[32,5,16,128]{3,2,1,0:T(8,128)(2,1)} %bitcast.6), calls=%async_computation.2 | async-start | bytes 1310720 | tf_op jit(solution)/shard_map/all_to_all | solution.py:385
  44.7 10.4 %near_back.1 = (f32[144,16,128]{2,1,0:T(8,128)S(1)}, bf16[16,16,128]{2,1,0:T(8,128)(2,1)S(1)}) custom-call(s32[4,128]{1,0:T(4,128)S(4)} %get-tuple-element.25.ids_ref, s32[1,128]{1,0:T(1,128)S(4)} %get-tuple-element.27.slot.slot_ref, bf16[160,16,128]{2,1,0:T(8,128)(2,1)S(1)} %bitcast.10, f32[128,16,128]{2,1,0:T(8,128)} %get-tuple-element.33.part_ref, ...), custom_call_target="tpu_custom_call" | custom-call | flops 335544320 | bytes 24117248 | tf_op jit(solution)/shard_map/near_back/pallas_call | solution.py:466
  55.1 5.3 %collective-permute-start.1 = (bf16[16,16,128]{2,1,0:T(8,128)(2,1)S(1)}, bf16[16,16,128]{2,1,0:T(8,128)(2,1)S(1)}, u32[]{:S(2)}, u32[]{:S(2)}) collective-permute-start(bf16[16,16,128]{2,1,0:T(8,128)(2,1)S(1)} %get-tuple-element.35), channel_id=1, source_target_pairs={{1,0},{2,1},{3,2},{4,3},{5,4},{6,5},{7,6},{8,7},{9,8},{10,9},{11,1... | collective-permute-start | bytes 196616 | tf_op jit(solution)/shard_map/ppermute | solution.py:32
  60.4 1.9 %collective-permute-done.1.halo_ref = bf16[16,16,128]{2,1,0:T(8,128)(2,1)S(1)} collective-permute-done((bf16[16,16,128]{2,1,0:T(8,128)(2,1)S(1)}, bf16[16,16,128]{2,1,0:T(8,128)(2,1)S(1)}, u32[]{:S(2)}, u32[]{:S(2)}) %collective-permute-start.1) | collective-permute-done | bytes 65568 | tf_op jit(solution)/shard_map/ppermute | solution.py:32
  62.3 0.3 all-to-all-done.2
  62.6 1.5 %final_sum.1 = f32[128,16,128]{2,1,0:T(8,128)} custom-call(s32[8,128]{1,0:T(8,128)S(4)} %get-tuple-element.24.picks_ref, f32[144,16,128]{2,1,0:T(8,128)S(1)} %get-tuple-element.34.base_ref, bf16[16,16,128]{2,1,0:T(8,128)(2,1)S(1)} %collective-permute-done.1.halo_ref, bf16[160,16,128]{2,1,0:T(8,128)(2,1)S(1)} %bitcast.11), custom_call_target="tpu_custom_call" | custom-call | bytes 3145728 | tf_op jit(solution)/shard_map/final_sum/pallas_call | solution.py:487
Async XLA Ops:
  0.9 14.6 %collective-permute-start = (bf16[16,16,128]{2,1,0:T(8,128)(2,1)S(1)}, bf16[16,16,128]{2,1,0:T(8,128)(2,1)S(1)}, u32[]{:S(2)}, u32[]{:S(2)}) collective-permute-start(bf16[16,16,128]{2,1,0:T(8,128)(2,1)S(1)} %get-tuple-element.22), channel_id=1, source_target_pairs={{31,0},{0,1},{1,2},{2,3},{3,4},{4,5},{5,6},{6,7},{7,8},{8,9},{9,10... | collective-permute-start | bytes 196616 | tf_op jit(solution)/shard_map/ppermute | solution.py:32
  17.7 20.6 %all-to-all-start.1 = ((bf16[32,5,16,128]{3,2,1,0:T(8,128)(2,1)}), bf16[32,5,16,128]{3,2,1,0:T(8,128)(2,1)S(1)}, u32[]{:S(2)}, u32[]{:S(2)}) async-start(bf16[32,5,16,128]{3,2,1,0:T(8,128)(2,1)} %bitcast.4), calls=%async_computation.1 | async-start | bytes 1310720 | tf_op jit(solution)/shard_map/all_to_all | solution.py:385
  20.3 0.7 %copy-start = (s32[128,4]{0,1:T(4,128)S(1)}, s32[128,4]{0,1:T(4,128)}, u32[]{:S(2)}) copy-start(s32[128,4]{0,1:T(4,128)} %param.7) | copy-start | bytes 6148
  41.3 21.3 %all-to-all-start.2 = ((bf16[32,5,16,128]{3,2,1,0:T(8,128)(2,1)}), bf16[32,5,16,128]{3,2,1,0:T(8,128)(2,1)S(1)}, u32[]{:S(2)}, u32[]{:S(2)}) async-start(bf16[32,5,16,128]{3,2,1,0:T(8,128)(2,1)} %bitcast.6), calls=%async_computation.2 | async-start | bytes 1310720 | tf_op jit(solution)/shard_map/all_to_all | solution.py:385
  55.1 7.2 %collective-permute-start.1 = (bf16[16,16,128]{2,1,0:T(8,128)(2,1)S(1)}, bf16[16,16,128]{2,1,0:T(8,128)(2,1)S(1)}, u32[]{:S(2)}, u32[]{:S(2)}) collective-permute-start(bf16[16,16,128]{2,1,0:T(8,128)(2,1)S(1)} %get-tuple-element.35), channel_id=1, source_target_pairs={{1,0},{2,1},{3,2},{4,3},{5,4},{6,5},{7,6},{8,7},{9,8},{10,9},{11,1... | collective-permute-start | bytes 196616 | tf_op jit(solution)/shard_map/ppermute | solution.py:32

commit v17 on v15

--- a/solution.py
+++ b/solution.py
@@ -242,7 +242,6 @@
 
     for c in range(HELD, chunks):
         load(c).start()
-    parcel_ref[...] = jnp.zeros_like(parcel_ref)
 
     def send_back(c, pair):
         for b in range(0, CHUNK, 4):
@@ -251,14 +250,14 @@
             for j in range(4):
                 parcel_ref[slot[0, i + j]] = (own_ref[i + j] - mixed[j]).astype(jnp.bfloat16)
 
-    for c in range(HELD):
+    @pl.loop(0, HELD)
+    def _(c):
         send_back(c, first_ref)
-    for c in range(HELD, chunks, 2):
-        piece = range(c, min(c + 2, chunks))
-        for c in piece:
-            load(c).wait()
-        for c in piece:
-            send_back(c, mats)
+
+    @pl.loop(HELD, chunks)
+    def _(c):
+        load(c).wait()
+        send_back(c, mats)
 
 
 def near_back_kernel(
@@ -348,19 +347,18 @@
 def sum_kernel(capacity, picks_ref, base_ref, halo_ref, back_ref, out_ref, total, sem):
     groups = back_ref.shape[0] // capacity
     blocks = out_ref.shape[0]
-    total[pl.ds(0, blocks)] = base_ref[pl.ds(REACH, blocks)]
-    last = pl.ds(blocks - REACH, REACH)
-    total[last] = total[last] + halo_ref[...].astype(jnp.float32)
+    last = pl.ds(blocks, REACH)
+    total[last] = base_ref[last] + halo_ref[...].astype(jnp.float32)
 
     @pl.loop(0, groups, unroll=8)
     def _(g):
         picks = [picks_ref[r, g] for r in range(capacity)]
-        places = [jnp.where(pick > 0, pick - 1, blocks) for pick in picks]
+        places = [jnp.where(pick > 0, pick + (REACH - 1), 0) for pick in picks]
         olds = [total[place] for place in places]
         for r in range(capacity):
             total[places[r]] = olds[r] - back_ref[g * capacity + r].astype(jnp.float32)
 
-    store = pltpu.make_async_copy(total.at[pl.ds(0, blocks)], out_ref, sem)
+    store = pltpu.make_async_copy(total.at[pl.ds(REACH, blocks)], out_ref, sem)
     store.start()
     store.wait()
 
@@ -479,19 +477,21 @@
         cost_estimate=pl.CostEstimate(flops=5 * flops, bytes_accessed=23 * 2**20, transcendentals=0),
     )(scalar_ids, slot_of, arrived, in_hbm(part), in_hbm(coeffs), in_hbm(cond_prec))
     halo_sum = passed_along(halo_back, "blk", -1)
-    return pl.pallas_call(
+    result, _ = pl.pallas_call(
         functools.partial(sum_kernel, capacity),
         name="final_sum",
-        out_shape=jax.ShapeDtypeStruct((blocks,) + tile, f32),
+        out_shape=(
+            jax.ShapeDtypeStruct((blocks,) + tile, f32),
+            jax.ShapeDtypeStruct((REACH + blocks,) + tile, f32),
+        ),
         in_specs=[SMEM, VMEM, VMEM, VMEM],
-        out_specs=HBM,
-        scratch_shapes=[
-            pltpu.VMEM((blocks + 1,) + tile, f32),
-            pltpu.SemaphoreType.DMA,
-        ],
+        out_specs=(HBM, VMEM),
+        scratch_shapes=[pltpu.SemaphoreType.DMA],
+        input_output_aliases={1: 1},
         compiler_params=params(8),
         cost_estimate=pl.CostEstimate(flops=0, bytes_accessed=3 * 2**20, transcendentals=0),
     )(picks, base, halo_sum, returned)
+    return result
 
 
 def solution(mesh):

time: 64.5 us -> 64.3 us (level)
  no operation moved by 1% of the time
where the time goes in v17:
time: 64.3 us; the launch traced here: 63.8 us
  Pallas kernels  28.5 us (44%)
  blocking collectives  14.1 us (22%)
  starting transfers between devices  11.8 us (18%)
  waiting for transfers between devices  8.67 us (13%)
  local copies, waits for them, and re-layouts  0.68 us (1%)
    all_to_all x1, blocking collectives, exchange(): return lax.all_to_all(x, 'blk', split_axis=0, concat_axis=0, tiled=True)  14.1 us
    pallas_call x1, Pallas kernels, per_device(): pl.pallas_call(functools.partial(near_forward_kernel, groups, capacity),...  10.8 us
    pallas_call x1, Pallas kernels, per_device(): pl.pallas_call(functools.partial(near_back_kernel, groups), name='near_ba...  10.4 us
    all_to_all x2, waiting for transfers between devices, exchange(): return lax.all_to_all(x, 'blk', split_axis=0, concat_axis=0, tiled=True)  6.76 us
    all_to_all x2, starting transfers between devices, exchange(): return lax.all_to_all(x, 'blk', split_axis=0, concat_axis=0, tiled=True)  6.05 us
    ppermute x2, starting transfers between devices, passed_along(): lax.ppermute(block, axis, [((i - distance) % size, i) for i in range(size)])  5.78 us
    pallas_call x1, Pallas kernels, per_device(): pl.pallas_call(far_kernel, name='far_terms', out_shape=jax.ShapeDtypeStru...  3.03 us
    pallas_call x1, Pallas kernels, per_device(): pl.pallas_call(functools.partial(pick_kernel, capacity), name='pick_tiles...  2.05 us
  transfers between devices with their start and end apart: 4, of which 3 were waited for; matrix products, arithmetic and copies ran while one was open for 0% of the time, Pallas kernels for 33%

profile of v17, /device:TPU:0, one launch (start us, length us, event | category | flops | bytes accessed | tf_op | source)
XLA Modules:
  0.0 63.8 jit_solution(955630090216766830)
XLA Ops:
  0.0 0.9 %prep.1 = (s32[32,128]{1,0:T(8,128)S(1)}, bf16[16,16,128]{2,1,0:T(8,128)(2,1)S(1)}, s32[4,128]{1,0:T(4,128)S(4)}) custom-call(s32[4,128]{1,0:T(4,128)} %bitcast.14, bf16[128,16,128]{2,1,0:T(8,128)(2,1)} %probe_ref.5), custom_call_target="tpu_custom_call" | custom-call | tf_op jit(solution)/shard_map/prep/pallas_call | solution.py:381
  0.9 0.5 collective-permute-start
  1.4 14.1 %all_to_all.22 = s32[32,1,128]{2,1,0:T(1,128)S(1)} all-to-all(s32[32,1,128]{2,1,0:T(1,128)S(1)} %bitcast.13), channel_id=1, replica_groups=mesh['blk'=32] {'blk'}, dimensions={0} | all-to-all | bytes 32768 | tf_op jit(solution)/shard_map/all_to_all | solution.py:378
  15.5 0.0 collective-permute-done.halo_ref
  15.5 2.0 %pick_tiles.1 = (bf16[160,16,128]{2,1,0:T(8,128)(2,1)}, s32[8,128]{1,0:T(8,128)S(4)}) custom-call(s32[32,128]{1,0:T(8,128)S(1)} %bitcast.12, bf16[128,16,128]{2,1,0:T(8,128)(2,1)} %probe_ref.5), custom_call_target="tpu_custom_call" | custom-call | bytes 1310720 | tf_op jit(solution)/shard_map/pick_tiles/pallas_call | solution.py:397
  17.5 2.6 %all-to-all-start.1 = ((bf16[32,5,16,128]{3,2,1,0:T(8,128)(2,1)}), bf16[32,5,16,128]{3,2,1,0:T(8,128)(2,1)S(1)}, u32[]{:S(2)}, u32[]{:S(2)}) async-start(bf16[32,5,16,128]{3,2,1,0:T(8,128)(2,1)} %bitcast.4), calls=%async_computation.1 | async-start | bytes 1310720 | tf_op jit(solution)/shard_map/all_to_all | solution.py:378
  20.2 0.0 copy-start
  20.2 0.7 %copy-done = s32[128,4]{0,1:T(4,128)S(1)} copy-done((s32[128,4]{0,1:T(4,128)S(1)}, s32[128,4]{0,1:T(4,128)}, u32[]{:S(2)}) %copy-start) | copy-done | bytes 2072
  20.9 10.8 %near_forward.1 = (f32[128,16,128]{2,1,0:T(8,128)}, f32[128,16,128]{2,1,0:T(8,128)S(1)}, s32[1,128]{1,0:T(1,128)S(4)}, bf16[48,128,128]{2,1,0:T(8,128)(2,1)S(1)}, bf16[128,128,128]{2,1,0:T(8,128)(2,1)}) custom-call(s32[4,128]{1,0:T(4,128)S(4)} %get-tuple-element.26.ids_ref, s32[4,128]{1,0:T(4,128)S(1)} %bitcast.15, ...), custom_call_target="tpu_custom_call" | custom-call | flops 1342177280 | bytes 29360128 | tf_op jit(solution)/shard_map/near_forward/pallas_call | solution.py:419
  31.6 6.5 %all-to-all-done.1 = bf16[32,5,16,128]{3,2,1,0:T(8,128)(2,1)S(1)} async-done(((bf16[32,5,16,128]{3,2,1,0:T(8,128)(2,1)}), bf16[32,5,16,128]{3,2,1,0:T(8,128)(2,1)S(1)}, u32[]{:S(2)}, u32[]{:S(2)}) %all-to-all-start.1) | async-done | bytes 655392 | tf_op jit(solution)/shard_map/all_to_all | solution.py:378
  38.1 3.0 %far_terms.1 = bf16[160,16,128]{2,1,0:T(8,128)(2,1)} custom-call(s32[1,128]{1,0:T(1,128)S(4)} %get-tuple-element.28.slot.slot_ref, f32[128,16,128]{2,1,0:T(8,128)S(1)} %get-tuple-element.29.own_ref, bf16[160,16,128]{2,1,0:T(8,128)(2,1)S(1)} %bitcast.9, bf16[48,128,128]{2,1,0:T(8,128)(2,1)S(1)} %get-tuple-element.31.first_ref, ...), custom_call_target="tpu_custom_call" | custom-call | flops 67108864 | bytes 6291456 | tf_op jit(solution)/shard_map/far_terms/pallas_call | solution.py:444
  41.1 3.4 %all-to-all-start.2 = ((bf16[32,5,16,128]{3,2,1,0:T(8,128)(2,1)}), bf16[32,5,16,128]{3,2,1,0:T(8,128)(2,1)S(1)}, u32[]{:S(2)}, u32[]{:S(2)}) async-start(bf16[32,5,16,128]{3,2,1,0:T(8,128)(2,1)} %bitcast.6), calls=%async_computation.2 | async-start | bytes 1310720 | tf_op jit(solution)/shard_map/all_to_all | solution.py:378
  44.6 10.4 %near_back.1 = (f32[144,16,128]{2,1,0:T(8,128)S(1)}, bf16[16,16,128]{2,1,0:T(8,128)(2,1)S(1)}) custom-call(s32[4,128]{1,0:T(4,128)S(4)} %get-tuple-element.26.ids_ref, s32[1,128]{1,0:T(1,128)S(4)} %get-tuple-element.28.slot.slot_ref, bf16[160,16,128]{2,1,0:T(8,128)(2,1)S(1)} %bitcast.10, f32[128,16,128]{2,1,0:T(8,128)} %get-tuple-element.34.part_ref, ...), custom_call_target="tpu_custom_call" | custom-call | flops 335544320 | bytes 24117248 | tf_op jit(solution)/shard_map/near_back/pallas_call | solution.py:459
  55.0 5.3 %collective-permute-start.1 = (bf16[16,16,128]{2,1,0:T(8,128)(2,1)S(1)}, bf16[16,16,128]{2,1,0:T(8,128)(2,1)S(1)}, u32[]{:S(2)}, u32[]{:S(2)}) collective-permute-start(bf16[16,16,128]{2,1,0:T(8,128)(2,1)S(1)} %get-tuple-element.36), channel_id=1, source_target_pairs={{1,0},{2,1},{3,2},{4,3},{5,4},{6,5},{7,6},{8,7},{9,8},{10,9},{11,1... | collective-permute-start | bytes 196616 | tf_op jit(solution)/shard_map/ppermute | solution.py:32
  60.3 1.9 %collective-permute-done.1.halo_ref = bf16[16,16,128]{2,1,0:T(8,128)(2,1)S(1)} collective-permute-done((bf16[16,16,128]{2,1,0:T(8,128)(2,1)S(1)}, bf16[16,16,128]{2,1,0:T(8,128)(2,1)S(1)}, u32[]{:S(2)}, u32[]{:S(2)}) %collective-permute-start.1) | collective-permute-done | bytes 65568 | tf_op jit(solution)/shard_map/ppermute | solution.py:32
  62.2 0.3 all-to-all-done.2
  62.5 1.4 %final_sum.1 = (f32[128,16,128]{2,1,0:T(8,128)}, f32[144,16,128]{2,1,0:T(8,128)S(1)}) custom-call(s32[8,128]{1,0:T(8,128)S(4)} %get-tuple-element.25.picks_ref, f32[144,16,128]{2,1,0:T(8,128)S(1)} %get-tuple-element.35.base_ref, bf16[16,16,128]{2,1,0:T(8,128)(2,1)S(1)} %collective-permute-done.1.halo_ref, ...), custom_call_target="tpu_custom_call", output_to_operand_aliasing={{1}: (1, {})} | custom-call | bytes 3145728 | tf_op jit(solution)/shard_map/final_sum/pallas_call | solution.py:480
Async XLA Ops:
  0.9 14.6 %collective-permute-start = (bf16[16,16,128]{2,1,0:T(8,128)(2,1)S(1)}, bf16[16,16,128]{2,1,0:T(8,128)(2,1)S(1)}, u32[]{:S(2)}, u32[]{:S(2)}) collective-permute-start(bf16[16,16,128]{2,1,0:T(8,128)(2,1)S(1)} %get-tuple-element.23), channel_id=1, source_target_pairs={{31,0},{0,1},{1,2},{2,3},{3,4},{4,5},{5,6},{6,7},{7,8},{8,9},{9,10... | collective-permute-start | bytes 196616 | tf_op jit(solution)/shard_map/ppermute | solution.py:32
  17.5 20.6 %all-to-all-start.1 = ((bf16[32,5,16,128]{3,2,1,0:T(8,128)(2,1)}), bf16[32,5,16,128]{3,2,1,0:T(8,128)(2,1)S(1)}, u32[]{:S(2)}, u32[]{:S(2)}) async-start(bf16[32,5,16,128]{3,2,1,0:T(8,128)(2,1)} %bitcast.4), calls=%async_computation.1 | async-start | bytes 1310720 | tf_op jit(solution)/shard_map/all_to_all | solution.py:378
  20.2 0.7 %copy-start = (s32[128,4]{0,1:T(4,128)S(1)}, s32[128,4]{0,1:T(4,128)}, u32[]{:S(2)}) copy-start(s32[128,4]{0,1:T(4,128)} %param.7) | copy-start | bytes 6148
  41.1 21.3 %all-to-all-start.2 = ((bf16[32,5,16,128]{3,2,1,0:T(8,128)(2,1)}), bf16[32,5,16,128]{3,2,1,0:T(8,128)(2,1)S(1)}, u32[]{:S(2)}, u32[]{:S(2)}) async-start(bf16[32,5,16,128]{3,2,1,0:T(8,128)(2,1)} %bitcast.6), calls=%async_computation.2 | async-start | bytes 1310720 | tf_op jit(solution)/shard_map/all_to_all | solution.py:378
  55.0 7.2 %collective-permute-start.1 = (bf16[16,16,128]{2,1,0:T(8,128)(2,1)S(1)}, bf16[16,16,128]{2,1,0:T(8,128)(2,1)S(1)}, u32[]{:S(2)}, u32[]{:S(2)}) collective-permute-start(bf16[16,16,128]{2,1,0:T(8,128)(2,1)S(1)} %get-tuple-element.36), channel_id=1, source_target_pairs={{1,0},{2,1},{3,2},{4,3},{5,4},{6,5},{7,6},{8,7},{9,8},{10,9},{11,1... | collective-permute-start | bytes 196616 | tf_op jit(solution)/shard_map/ppermute | solution.py:32

commit v18 on v17

--- a/solution.py
+++ b/solution.py
@@ -412,7 +412,7 @@
         compiler_params=params(8),
         cost_estimate=pl.CostEstimate(flops=0, bytes_accessed=2 * slots * 4096, transcendentals=0),
     )(all_ids, in_hbm(probe_vecs))
-    arrived = exchange(outgoing.reshape((groups, capacity) + tile)).reshape((slots,) + tile)
+    arrived = exchange(outgoing.reshape(groups, capacity * probes, points)).reshape((slots,) + tile)
     mats = (blocks, points, points)
     all_mats = pltpu.VMEM((blocks, 4, points, points), bf16)
     tiles_f32 = jax.ShapeDtypeStruct((blocks,) + tile, f32)
@@ -455,7 +455,7 @@
         cost_estimate=pl.CostEstimate(flops=flops, bytes_accessed=6 * 2**20, transcendentals=0),
     )(slot_of, own_far, arrived, first_mats, in_hbm(far_mats))
     parcel, arrived = lax.optimization_barrier((parcel, arrived))
-    returned = exchange(parcel.reshape((groups, capacity) + tile)).reshape((slots,) + tile)
+    returned = exchange(parcel.reshape(groups, capacity * probes, points)).reshape((slots,) + tile)
     base, halo_back = pl.pallas_call(
         functools.partial(near_back_kernel, groups),
         name="near_back",

time: 64.3 us -> 64.3 us (level)
  no operation moved by 1% of the time
where the time goes in v18:
time: 64.3 us; the launch traced here: 63.8 us
  Pallas kernels  28.5 us (44%)
  blocking collectives  14.1 us (22%)
  starting transfers between devices  11.8 us (18%)
  waiting for transfers between devices  8.67 us (13%)
  local copies, waits for them, and re-layouts  0.68 us (1%)
    all_to_all x1, blocking collectives, exchange(): return lax.all_to_all(x, 'blk', split_axis=0, concat_axis=0, tiled=True)  14.1 us
    pallas_call x1, Pallas kernels, per_device(): pl.pallas_call(functools.partial(near_forward_kernel, groups, capacity),...  10.8 us
    pallas_call x1, Pallas kernels, per_device(): pl.pallas_call(functools.partial(near_back_kernel, groups), name='near_ba...  10.4 us
    all_to_all x2, waiting for transfers between devices, exchange(): return lax.all_to_all(x, 'blk', split_axis=0, concat_axis=0, tiled=True)  6.76 us
    all_to_all x2, starting transfers between devices, exchange(): return lax.all_to_all(x, 'blk', split_axis=0, concat_axis=0, tiled=True)  6.06 us
    ppermute x2, starting transfers between devices, passed_along(): lax.ppermute(block, axis, [((i - distance) % size, i) for i in range(size)])  5.78 us
    pallas_call x1, Pallas kernels, per_device(): pl.pallas_call(far_kernel, name='far_terms', out_shape=jax.ShapeDtypeStru...  3.02 us
    pallas_call x1, Pallas kernels, per_device(): pl.pallas_call(functools.partial(pick_kernel, capacity), name='pick_tiles...  2.05 us
  transfers between devices with their start and end apart: 4, of which 3 were waited for; matrix products, arithmetic and copies ran while one was open for 0% of the time, Pallas kernels for 33%

profile of v18, /device:TPU:0, one launch (start us, length us, event | category | flops | bytes accessed | tf_op | source)
XLA Modules:
  0.0 63.8 jit_solution(955630090216766830)
XLA Ops:
  0.0 0.9 %prep.1 = (s32[32,128]{1,0:T(8,128)S(1)}, bf16[16,16,128]{2,1,0:T(8,128)(2,1)S(1)}, s32[4,128]{1,0:T(4,128)S(4)}) custom-call(s32[4,128]{1,0:T(4,128)} %bitcast.14, bf16[128,16,128]{2,1,0:T(8,128)(2,1)} %probe_ref.5), custom_call_target="tpu_custom_call" | custom-call | tf_op jit(solution)/shard_map/prep/pallas_call | solution.py:381
  0.9 0.5 collective-permute-start
  1.4 14.1 %all_to_all.22 = s32[32,1,128]{2,1,0:T(1,128)S(1)} all-to-all(s32[32,1,128]{2,1,0:T(1,128)S(1)} %bitcast.13), channel_id=1, replica_groups=mesh['blk'=32] {'blk'}, dimensions={0} | all-to-all | bytes 32768 | tf_op jit(solution)/shard_map/all_to_all | solution.py:378
  15.5 0.0 collective-permute-done.halo_ref
  15.5 2.0 %pick_tiles.1 = (bf16[160,16,128]{2,1,0:T(8,128)(2,1)}, s32[8,128]{1,0:T(8,128)S(4)}) custom-call(s32[32,128]{1,0:T(8,128)S(1)} %bitcast.12, bf16[128,16,128]{2,1,0:T(8,128)(2,1)} %probe_ref.5), custom_call_target="tpu_custom_call" | custom-call | bytes 1310720 | tf_op jit(solution)/shard_map/pick_tiles/pallas_call | solution.py:397
  17.5 2.6 %all-to-all-start.1 = ((bf16[32,80,128]{2,1,0:T(8,128)(2,1)}), bf16[32,80,128]{2,1,0:T(8,128)(2,1)S(1)}, u32[]{:S(2)}, u32[]{:S(2)}) async-start(bf16[32,80,128]{2,1,0:T(8,128)(2,1)} %bitcast.4), calls=%async_computation.1 | async-start | bytes 1310720 | tf_op jit(solution)/shard_map/all_to_all | solution.py:378
  20.2 0.0 copy-start
  20.2 0.7 %copy-done = s32[128,4]{0,1:T(4,128)S(1)} copy-done((s32[128,4]{0,1:T(4,128)S(1)}, s32[128,4]{0,1:T(4,128)}, u32[]{:S(2)}) %copy-start) | copy-done | bytes 2072
  20.9 10.8 %near_forward.1 = (f32[128,16,128]{2,1,0:T(8,128)}, f32[128,16,128]{2,1,0:T(8,128)S(1)}, s32[1,128]{1,0:T(1,128)S(4)}, bf16[48,128,128]{2,1,0:T(8,128)(2,1)S(1)}, bf16[128,128,128]{2,1,0:T(8,128)(2,1)}) custom-call(s32[4,128]{1,0:T(4,128)S(4)} %get-tuple-element.26.ids_ref, s32[4,128]{1,0:T(4,128)S(1)} %bitcast.15, ...), custom_call_target="tpu_custom_call" | custom-call | flops 1342177280 | bytes 29360128 | tf_op jit(solution)/shard_map/near_forward/pallas_call | solution.py:419
  31.6 6.5 %all-to-all-done.1 = bf16[32,80,128]{2,1,0:T(8,128)(2,1)S(1)} async-done(((bf16[32,80,128]{2,1,0:T(8,128)(2,1)}), bf16[32,80,128]{2,1,0:T(8,128)(2,1)S(1)}, u32[]{:S(2)}, u32[]{:S(2)}) %all-to-all-start.1) | async-done | bytes 655392 | tf_op jit(solution)/shard_map/all_to_all | solution.py:378
  38.1 3.0 %far_terms.1 = bf16[160,16,128]{2,1,0:T(8,128)(2,1)} custom-call(s32[1,128]{1,0:T(1,128)S(4)} %get-tuple-element.28.slot.slot_ref, f32[128,16,128]{2,1,0:T(8,128)S(1)} %get-tuple-element.29.own_ref, bf16[160,16,128]{2,1,0:T(8,128)(2,1)S(1)} %bitcast.9, bf16[48,128,128]{2,1,0:T(8,128)(2,1)S(1)} %get-tuple-element.31.first_ref, ...), custom_call_target="tpu_custom_call" | custom-call | flops 67108864 | bytes 6291456 | tf_op jit(solution)/shard_map/far_terms/pallas_call | solution.py:444
  41.1 3.4 %all-to-all-start.2 = ((bf16[32,80,128]{2,1,0:T(8,128)(2,1)}), bf16[32,80,128]{2,1,0:T(8,128)(2,1)S(1)}, u32[]{:S(2)}, u32[]{:S(2)}) async-start(bf16[32,80,128]{2,1,0:T(8,128)(2,1)} %bitcast.6), calls=%async_computation.2 | async-start | bytes 1310720 | tf_op jit(solution)/shard_map/all_to_all | solution.py:378
  44.6 10.4 %near_back.1 = (f32[144,16,128]{2,1,0:T(8,128)S(1)}, bf16[16,16,128]{2,1,0:T(8,128)(2,1)S(1)}) custom-call(s32[4,128]{1,0:T(4,128)S(4)} %get-tuple-element.26.ids_ref, s32[1,128]{1,0:T(1,128)S(4)} %get-tuple-element.28.slot.slot_ref, bf16[160,16,128]{2,1,0:T(8,128)(2,1)S(1)} %bitcast.10, f32[128,16,128]{2,1,0:T(8,128)} %get-tuple-element.34.part_ref, ...), custom_call_target="tpu_custom_call" | custom-call | flops 335544320 | bytes 24117248 | tf_op jit(solution)/shard_map/near_back/pallas_call | solution.py:459
  55.0 5.3 %collective-permute-start.1 = (bf16[16,16,128]{2,1,0:T(8,128)(2,1)S(1)}, bf16[16,16,128]{2,1,0:T(8,128)(2,1)S(1)}, u32[]{:S(2)}, u32[]{:S(2)}) collective-permute-start(bf16[16,16,128]{2,1,0:T(8,128)(2,1)S(1)} %get-tuple-element.36), channel_id=1, source_target_pairs={{1,0},{2,1},{3,2},{4,3},{5,4},{6,5},{7,6},{8,7},{9,8},{10,9},{11,1... | collective-permute-start | bytes 196616 | tf_op jit(solution)/shard_map/ppermute | solution.py:32
  60.3 1.9 %collective-permute-done.1.halo_ref = bf16[16,16,128]{2,1,0:T(8,128)(2,1)S(1)} collective-permute-done((bf16[16,16,128]{2,1,0:T(8,128)(2,1)S(1)}, bf16[16,16,128]{2,1,0:T(8,128)(2,1)S(1)}, u32[]{:S(2)}, u32[]{:S(2)}) %collective-permute-start.1) | collective-permute-done | bytes 65568 | tf_op jit(solution)/shard_map/ppermute | solution.py:32
  62.2 0.3 all-to-all-done.2
  62.5 1.4 %final_sum.1 = (f32[128,16,128]{2,1,0:T(8,128)}, f32[144,16,128]{2,1,0:T(8,128)S(1)}) custom-call(s32[8,128]{1,0:T(8,128)S(4)} %get-tuple-element.25.picks_ref, f32[144,16,128]{2,1,0:T(8,128)S(1)} %get-tuple-element.35.base_ref, bf16[16,16,128]{2,1,0:T(8,128)(2,1)S(1)} %collective-permute-done.1.halo_ref, ...), custom_call_target="tpu_custom_call", output_to_operand_aliasing={{1}: (1, {})} | custom-call | bytes 3145728 | tf_op jit(solution)/shard_map/final_sum/pallas_call | solution.py:480
Async XLA Ops:
  0.9 14.6 %collective-permute-start = (bf16[16,16,128]{2,1,0:T(8,128)(2,1)S(1)}, bf16[16,16,128]{2,1,0:T(8,128)(2,1)S(1)}, u32[]{:S(2)}, u32[]{:S(2)}) collective-permute-start(bf16[16,16,128]{2,1,0:T(8,128)(2,1)S(1)} %get-tuple-element.23), channel_id=1, source_target_pairs={{31,0},{0,1},{1,2},{2,3},{3,4},{4,5},{5,6},{6,7},{7,8},{8,9},{9,10... | collective-permute-start | bytes 196616 | tf_op jit(solution)/shard_map/ppermute | solution.py:32
  17.5 20.6 %all-to-all-start.1 = ((bf16[32,80,128]{2,1,0:T(8,128)(2,1)}), bf16[32,80,128]{2,1,0:T(8,128)(2,1)S(1)}, u32[]{:S(2)}, u32[]{:S(2)}) async-start(bf16[32,80,128]{2,1,0:T(8,128)(2,1)} %bitcast.4), calls=%async_computation.1 | async-start | bytes 1310720 | tf_op jit(solution)/shard_map/all_to_all | solution.py:378
  20.2 0.7 %copy-start = (s32[128,4]{0,1:T(4,128)S(1)}, s32[128,4]{0,1:T(4,128)}, u32[]{:S(2)}) copy-start(s32[128,4]{0,1:T(4,128)} %param.7) | copy-start | bytes 6148
  41.1 21.3 %all-to-all-start.2 = ((bf16[32,80,128]{2,1,0:T(8,128)(2,1)}), bf16[32,80,128]{2,1,0:T(8,128)(2,1)S(1)}, u32[]{:S(2)}, u32[]{:S(2)}) async-start(bf16[32,80,128]{2,1,0:T(8,128)(2,1)} %bitcast.6), calls=%async_computation.2 | async-start | bytes 1310720 | tf_op jit(solution)/shard_map/all_to_all | solution.py:378
  55.0 7.2 %collective-permute-start.1 = (bf16[16,16,128]{2,1,0:T(8,128)(2,1)S(1)}, bf16[16,16,128]{2,1,0:T(8,128)(2,1)S(1)}, u32[]{:S(2)}, u32[]{:S(2)}) collective-permute-start(bf16[16,16,128]{2,1,0:T(8,128)(2,1)S(1)} %get-tuple-element.36), channel_id=1, source_target_pairs={{1,0},{2,1},{3,2},{4,3},{5,4},{6,5},{7,6},{8,7},{9,8},{10,9},{11,1... | collective-permute-start | bytes 196616 | tf_op jit(solution)/shard_map/ppermute | solution.py:32

commit v19 on v18

--- a/solution.py
+++ b/solution.py
@@ -65,14 +65,11 @@
     local = ids_ref[...] - me * blocks
     mask = (local >= 0) & (local < blocks)
     rank = ranks_in(mask, blocks)
-    row = lax.broadcasted_iota(jnp.int32, (picks_ref.shape[0], groups), 0)
-    ones = jnp.ones((picks_ref.shape[0], blocks), jnp.bfloat16)
-    picks = jnp.zeros(row.shape, jnp.float32)
-    for r in range(capacity):
-        chosen = jnp.where(mask & (rank == r), local + 1, 0).astype(jnp.float32).astype(jnp.bfloat16)
-        found = lax.dot_general(ones, chosen, NT, preferred_element_type=jnp.float32)
-        picks = jnp.where(row == r, found, picks)
-    picks_ref[:, pl.ds(0, groups)] = picks.astype(jnp.int32)
+    chosen = [jnp.where(mask & (rank == r), local + 1, 0).astype(jnp.float32) for r in range(capacity)]
+    chosen = jnp.concatenate(chosen, axis=0).astype(jnp.bfloat16)
+    ones = jnp.ones((8, blocks), jnp.bfloat16)
+    found = lax.dot_general(ones, chosen, NT, preferred_element_type=jnp.float32)
+    picks_ref[:, pl.ds(0, groups * capacity)] = found[:1].astype(jnp.int32)
     copy = pltpu.make_async_copy(picks_ref, picks_smem, sems.at[1])
     copy.start()
     copy.wait()
@@ -88,7 +85,7 @@
         @pl.loop(p * part, (p + 1) * part, unroll=8)
         def _(g):
             for r in range(capacity):
-                out[g * capacity + r] = probe[jnp.maximum(picks_smem[r, g] - 1, 0)]
+                out[g * capacity + r] = probe[jnp.maximum(picks_smem[0, r * groups + g] - 1, 0)]
 
         store(p).start()
     for p in range(STORES):
@@ -352,7 +349,7 @@
 
     @pl.loop(0, groups, unroll=8)
     def _(g):
-        picks = [picks_ref[r, g] for r in range(capacity)]
+        picks = [picks_ref[0, r * groups + g] for r in range(capacity)]
         places = [jnp.where(pick > 0, pick + (REACH - 1), 0) for pick in picks]
         olds = [total[place] for place in places]
         for r in range(capacity):
@@ -368,7 +365,7 @@
     groups = lax.axis_size("blk")
     capacity = max(2, blocks // (groups - 1) + 1)
     slots = groups * capacity
-    picks_shape = (-(-capacity // 8) * 8, -(-groups // 128) * 128)
+    picks_shape = (1, -(-slots // 128) * 128)
     chunks = blocks // CHUNK
     bf16, f32 = jnp.bfloat16, jnp.float32
     tile = (probes, points)

time: 64.3 us -> 64.2 us (level)
  no operation moved by 1% of the time
where the time goes in v19:
time: 64.2 us; the launch traced here: 63.8 us
  Pallas kernels  28.5 us (44%)
  blocking collectives  14.1 us (22%)
  starting transfers between devices  11.8 us (18%)
  waiting for transfers between devices  8.67 us (14%)
  local copies, waits for them, and re-layouts  0.68 us (1%)
    all_to_all x1, blocking collectives, exchange(): return lax.all_to_all(x, 'blk', split_axis=0, concat_axis=0, tiled=True)  14.1 us
    pallas_call x1, Pallas kernels, per_device(): pl.pallas_call(functools.partial(near_forward_kernel, groups, capacity),...  10.8 us
    pallas_call x1, Pallas kernels, per_device(): pl.pallas_call(functools.partial(near_back_kernel, groups), name='near_ba...  10.4 us
    all_to_all x2, waiting for transfers between devices, exchange(): return lax.all_to_all(x, 'blk', split_axis=0, concat_axis=0, tiled=True)  6.76 us
    all_to_all x2, starting transfers between devices, exchange(): return lax.all_to_all(x, 'blk', split_axis=0, concat_axis=0, tiled=True)  6.05 us
    ppermute x2, starting transfers between devices, passed_along(): lax.ppermute(block, axis, [((i - distance) % size, i) for i in range(size)])  5.78 us
    pallas_call x1, Pallas kernels, per_device(): pl.pallas_call(far_kernel, name='far_terms', out_shape=jax.ShapeDtypeStru...  3.02 us
    pallas_call x1, Pallas kernels, per_device(): pl.pallas_call(functools.partial(pick_kernel, capacity), name='pick_tiles...  2.05 us
  transfers between devices with their start and end apart: 4, of which 3 were waited for; matrix products, arithmetic and copies ran while one was open for 0% of the time, Pallas kernels for 33%

profile of v19, /device:TPU:0, one launch (start us, length us, event | category | flops | bytes accessed | tf_op | source)
XLA Modules:
  0.0 63.8 jit_solution(8519178726324070676)
XLA Ops:
  0.0 0.9 %prep.1 = (s32[32,128]{1,0:T(8,128)S(1)}, bf16[16,16,128]{2,1,0:T(8,128)(2,1)S(1)}, s32[4,128]{1,0:T(4,128)S(4)}) custom-call(s32[4,128]{1,0:T(4,128)} %bitcast.14, bf16[128,16,128]{2,1,0:T(8,128)(2,1)} %probe_ref.5), custom_call_target="tpu_custom_call" | custom-call | tf_op jit(solution)/shard_map/prep/pallas_call | solution.py:378
  0.9 0.5 collective-permute-start
  1.4 14.1 %all_to_all.22 = s32[32,1,128]{2,1,0:T(1,128)S(1)} all-to-all(s32[32,1,128]{2,1,0:T(1,128)S(1)} %bitcast.13), channel_id=1, replica_groups=mesh['blk'=32] {'blk'}, dimensions={0} | all-to-all | bytes 32768 | tf_op jit(solution)/shard_map/all_to_all | solution.py:375
  15.5 0.0 collective-permute-done.halo_ref
  15.5 2.0 %pick_tiles.1 = (bf16[160,16,128]{2,1,0:T(8,128)(2,1)}, s32[1,256]{1,0:T(1,128)S(4)}) custom-call(s32[32,128]{1,0:T(8,128)S(1)} %bitcast.12, bf16[128,16,128]{2,1,0:T(8,128)(2,1)} %probe_ref.5), custom_call_target="tpu_custom_call" | custom-call | bytes 1310720 | tf_op jit(solution)/shard_map/pick_tiles/pallas_call | solution.py:394
  17.5 2.6 %all-to-all-start.1 = ((bf16[32,80,128]{2,1,0:T(8,128)(2,1)}), bf16[32,80,128]{2,1,0:T(8,128)(2,1)S(1)}, u32[]{:S(2)}, u32[]{:S(2)}) async-start(bf16[32,80,128]{2,1,0:T(8,128)(2,1)} %bitcast.4), calls=%async_computation.1 | async-start | bytes 1310720 | tf_op jit(solution)/shard_map/all_to_all | solution.py:375
  20.2 0.0 copy-start
  20.2 0.7 %copy-done = s32[128,4]{0,1:T(4,128)S(1)} copy-done((s32[128,4]{0,1:T(4,128)S(1)}, s32[128,4]{0,1:T(4,128)}, u32[]{:S(2)}) %copy-start) | copy-done | bytes 2072
  20.9 10.8 %near_forward.1 = (f32[128,16,128]{2,1,0:T(8,128)}, f32[128,16,128]{2,1,0:T(8,128)S(1)}, s32[1,128]{1,0:T(1,128)S(4)}, bf16[48,128,128]{2,1,0:T(8,128)(2,1)S(1)}, bf16[128,128,128]{2,1,0:T(8,128)(2,1)}) custom-call(s32[4,128]{1,0:T(4,128)S(4)} %get-tuple-element.26.ids_ref, s32[4,128]{1,0:T(4,128)S(1)} %bitcast.15, ...), custom_call_target="tpu_custom_call" | custom-call | flops 1342177280 | bytes 29360128 | tf_op jit(solution)/shard_map/near_forward/pallas_call | solution.py:416
  31.6 6.5 %all-to-all-done.1 = bf16[32,80,128]{2,1,0:T(8,128)(2,1)S(1)} async-done(((bf16[32,80,128]{2,1,0:T(8,128)(2,1)}), bf16[32,80,128]{2,1,0:T(8,128)(2,1)S(1)}, u32[]{:S(2)}, u32[]{:S(2)}) %all-to-all-start.1) | async-done | bytes 655392 | tf_op jit(solution)/shard_map/all_to_all | solution.py:375
  38.1 3.0 %far_terms.1 = bf16[160,16,128]{2,1,0:T(8,128)(2,1)} custom-call(s32[1,128]{1,0:T(1,128)S(4)} %get-tuple-element.28.slot.slot_ref, f32[128,16,128]{2,1,0:T(8,128)S(1)} %get-tuple-element.29.own_ref, bf16[160,16,128]{2,1,0:T(8,128)(2,1)S(1)} %bitcast.9, bf16[48,128,128]{2,1,0:T(8,128)(2,1)S(1)} %get-tuple-element.31.first_ref, ...), custom_call_target="tpu_custom_call" | custom-call | flops 67108864 | bytes 6291456 | tf_op jit(solution)/shard_map/far_terms/pallas_call | solution.py:441
  41.1 3.4 %all-to-all-start.2 = ((bf16[32,80,128]{2,1,0:T(8,128)(2,1)}), bf16[32,80,128]{2,1,0:T(8,128)(2,1)S(1)}, u32[]{:S(2)}, u32[]{:S(2)}) async-start(bf16[32,80,128]{2,1,0:T(8,128)(2,1)} %bitcast.6), calls=%async_computation.2 | async-start | bytes 1310720 | tf_op jit(solution)/shard_map/all_to_all | solution.py:375
  44.6 10.4 %near_back.1 = (f32[144,16,128]{2,1,0:T(8,128)S(1)}, bf16[16,16,128]{2,1,0:T(8,128)(2,1)S(1)}) custom-call(s32[4,128]{1,0:T(4,128)S(4)} %get-tuple-element.26.ids_ref, s32[1,128]{1,0:T(1,128)S(4)} %get-tuple-element.28.slot.slot_ref, bf16[160,16,128]{2,1,0:T(8,128)(2,1)S(1)} %bitcast.10, f32[128,16,128]{2,1,0:T(8,128)} %get-tuple-element.34.part_ref, ...), custom_call_target="tpu_custom_call" | custom-call | flops 335544320 | bytes 24117248 | tf_op jit(solution)/shard_map/near_back/pallas_call | solution.py:456
  55.0 5.3 %collective-permute-start.1 = (bf16[16,16,128]{2,1,0:T(8,128)(2,1)S(1)}, bf16[16,16,128]{2,1,0:T(8,128)(2,1)S(1)}, u32[]{:S(2)}, u32[]{:S(2)}) collective-permute-start(bf16[16,16,128]{2,1,0:T(8,128)(2,1)S(1)} %get-tuple-element.36), channel_id=1, source_target_pairs={{1,0},{2,1},{3,2},{4,3},{5,4},{6,5},{7,6},{8,7},{9,8},{10,9},{11,1... | collective-permute-start | bytes 196616 | tf_op jit(solution)/shard_map/ppermute | solution.py:32
  60.3 1.9 %collective-permute-done.1.halo_ref = bf16[16,16,128]{2,1,0:T(8,128)(2,1)S(1)} collective-permute-done((bf16[16,16,128]{2,1,0:T(8,128)(2,1)S(1)}, bf16[16,16,128]{2,1,0:T(8,128)(2,1)S(1)}, u32[]{:S(2)}, u32[]{:S(2)}) %collective-permute-start.1) | collective-permute-done | bytes 65568 | tf_op jit(solution)/shard_map/ppermute | solution.py:32
  62.2 0.3 all-to-all-done.2
  62.5 1.3 %final_sum.1 = (f32[128,16,128]{2,1,0:T(8,128)}, f32[144,16,128]{2,1,0:T(8,128)S(1)}) custom-call(s32[1,256]{1,0:T(1,128)S(4)} %get-tuple-element.25.picks_ref, f32[144,16,128]{2,1,0:T(8,128)S(1)} %get-tuple-element.35.base_ref, bf16[16,16,128]{2,1,0:T(8,128)(2,1)S(1)} %collective-permute-done.1.halo_ref, ...), custom_call_target="tpu_custom_call", output_to_operand_aliasing={{1}: (1, {})} | custom-call | bytes 3145728 | tf_op jit(solution)/shard_map/final_sum/pallas_call | solution.py:477
Async XLA Ops:
  0.9 14.6 %collective-permute-start = (bf16[16,16,128]{2,1,0:T(8,128)(2,1)S(1)}, bf16[16,16,128]{2,1,0:T(8,128)(2,1)S(1)}, u32[]{:S(2)}, u32[]{:S(2)}) collective-permute-start(bf16[16,16,128]{2,1,0:T(8,128)(2,1)S(1)} %get-tuple-element.23), channel_id=1, source_target_pairs={{31,0},{0,1},{1,2},{2,3},{3,4},{4,5},{5,6},{6,7},{7,8},{8,9},{9,10... | collective-permute-start | bytes 196616 | tf_op jit(solution)/shard_map/ppermute | solution.py:32
  17.5 20.6 %all-to-all-start.1 = ((bf16[32,80,128]{2,1,0:T(8,128)(2,1)}), bf16[32,80,128]{2,1,0:T(8,128)(2,1)S(1)}, u32[]{:S(2)}, u32[]{:S(2)}) async-start(bf16[32,80,128]{2,1,0:T(8,128)(2,1)} %bitcast.4), calls=%async_computation.1 | async-start | bytes 1310720 | tf_op jit(solution)/shard_map/all_to_all | solution.py:375
  20.2 0.7 %copy-start = (s32[128,4]{0,1:T(4,128)S(1)}, s32[128,4]{0,1:T(4,128)}, u32[]{:S(2)}) copy-start(s32[128,4]{0,1:T(4,128)} %param.7) | copy-start | bytes 6148
  41.1 21.3 %all-to-all-start.2 = ((bf16[32,80,128]{2,1,0:T(8,128)(2,1)}), bf16[32,80,128]{2,1,0:T(8,128)(2,1)S(1)}, u32[]{:S(2)}, u32[]{:S(2)}) async-start(bf16[32,80,128]{2,1,0:T(8,128)(2,1)} %bitcast.6), calls=%async_computation.2 | async-start | bytes 1310720 | tf_op jit(solution)/shard_map/all_to_all | solution.py:375
  55.0 7.2 %collective-permute-start.1 = (bf16[16,16,128]{2,1,0:T(8,128)(2,1)S(1)}, bf16[16,16,128]{2,1,0:T(8,128)(2,1)S(1)}, u32[]{:S(2)}, u32[]{:S(2)}) collective-permute-start(bf16[16,16,128]{2,1,0:T(8,128)(2,1)S(1)} %get-tuple-element.36), channel_id=1, source_target_pairs={{1,0},{2,1},{3,2},{4,3},{5,4},{6,5},{7,6},{8,7},{9,8},{10,9},{11,1... | collective-permute-start | bytes 196616 | tf_op jit(solution)/shard_map/ppermute | solution.py:32

commit v20 on v18

--- a/solution.py
+++ b/solution.py
@@ -12,7 +12,7 @@
 AHEAD = 4
 HELD = 3
 LEAD = 3
-STORES = 4
+STORES = 2
 VMEM = pl.BlockSpec(memory_space=pltpu.VMEM)
 SMEM = pl.BlockSpec(memory_space=pltpu.SMEM)
 HBM = pl.BlockSpec(memory_space=pl.ANY)

time: 64.3 us -> 64.4 us (level)
  no operation moved by 1% of the time
where the time goes in v20:
time: 64.4 us; the launch traced here: 63.9 us
  Pallas kernels  28.6 us (44%)
  blocking collectives  14.1 us (22%)
  starting transfers between devices  11.8 us (18%)
  waiting for transfers between devices  8.66 us (13%)
  local copies, waits for them, and re-layouts  0.68 us (1%)
    all_to_all x1, blocking collectives, exchange(): return lax.all_to_all(x, 'blk', split_axis=0, concat_axis=0, tiled=True)  14.1 us
    pallas_call x1, Pallas kernels, per_device(): pl.pallas_call(functools.partial(near_forward_kernel, groups, capacity),...  10.7 us
    pallas_call x1, Pallas kernels, per_device(): pl.pallas_call(functools.partial(near_back_kernel, groups), name='near_ba...  10.4 us
    all_to_all x2, waiting for transfers between devices, exchange(): return lax.all_to_all(x, 'blk', split_axis=0, concat_axis=0, tiled=True)  6.76 us
    all_to_all x2, starting transfers between devices, exchange(): return lax.all_to_all(x, 'blk', split_axis=0, concat_axis=0, tiled=True)  6.05 us
    ppermute x2, starting transfers between devices, passed_along(): lax.ppermute(block, axis, [((i - distance) % size, i) for i in range(size)])  5.79 us
    pallas_call x1, Pallas kernels, per_device(): pl.pallas_call(far_kernel, name='far_terms', out_shape=jax.ShapeDtypeStru...  3.02 us
    pallas_call x1, Pallas kernels, per_device(): pl.pallas_call(functools.partial(pick_kernel, capacity), name='pick_tiles...  2.16 us
  transfers between devices with their start and end apart: 4, of which 3 were waited for; matrix products, arithmetic and copies ran while one was open for 0% of the time, Pallas kernels for 33%

profile of v20, /device:TPU:0, one launch (start us, length us, event | category | flops | bytes accessed | tf_op | source)
XLA Modules:
  0.0 63.9 jit_solution(894011717224741729)
XLA Ops:
  0.0 0.9 %prep.1 = (s32[32,128]{1,0:T(8,128)S(1)}, bf16[16,16,128]{2,1,0:T(8,128)(2,1)S(1)}, s32[4,128]{1,0:T(4,128)S(4)}) custom-call(s32[4,128]{1,0:T(4,128)} %bitcast.14, bf16[128,16,128]{2,1,0:T(8,128)(2,1)} %probe_ref.5), custom_call_target="tpu_custom_call" | custom-call | tf_op jit(solution)/shard_map/prep/pallas_call | solution.py:381
  0.9 0.5 collective-permute-start
  1.4 14.1 %all_to_all.22 = s32[32,1,128]{2,1,0:T(1,128)S(1)} all-to-all(s32[32,1,128]{2,1,0:T(1,128)S(1)} %bitcast.13), channel_id=1, replica_groups=mesh['blk'=32] {'blk'}, dimensions={0} | all-to-all | bytes 32768 | tf_op jit(solution)/shard_map/all_to_all | solution.py:378
  15.5 0.0 collective-permute-done.halo_ref
  15.5 2.2 %pick_tiles.1 = (bf16[160,16,128]{2,1,0:T(8,128)(2,1)}, s32[8,128]{1,0:T(8,128)S(4)}) custom-call(s32[32,128]{1,0:T(8,128)S(1)} %bitcast.12, bf16[128,16,128]{2,1,0:T(8,128)(2,1)} %probe_ref.5), custom_call_target="tpu_custom_call" | custom-call | bytes 1310720 | tf_op jit(solution)/shard_map/pick_tiles/pallas_call | solution.py:397
  17.6 2.6 %all-to-all-start.1 = ((bf16[32,80,128]{2,1,0:T(8,128)(2,1)}), bf16[32,80,128]{2,1,0:T(8,128)(2,1)S(1)}, u32[]{:S(2)}, u32[]{:S(2)}) async-start(bf16[32,80,128]{2,1,0:T(8,128)(2,1)} %bitcast.4), calls=%async_computation.1 | async-start | bytes 1310720 | tf_op jit(solution)/shard_map/all_to_all | solution.py:378
  20.3 0.0 copy-start
  20.3 0.7 %copy-done = s32[128,4]{0,1:T(4,128)S(1)} copy-done((s32[128,4]{0,1:T(4,128)S(1)}, s32[128,4]{0,1:T(4,128)}, u32[]{:S(2)}) %copy-start) | copy-done | bytes 2072
  21.0 10.7 %near_forward.1 = (f32[128,16,128]{2,1,0:T(8,128)}, f32[128,16,128]{2,1,0:T(8,128)S(1)}, s32[1,128]{1,0:T(1,128)S(4)}, bf16[48,128,128]{2,1,0:T(8,128)(2,1)S(1)}, bf16[128,128,128]{2,1,0:T(8,128)(2,1)}) custom-call(s32[4,128]{1,0:T(4,128)S(4)} %get-tuple-element.26.ids_ref, s32[4,128]{1,0:T(4,128)S(1)} %bitcast.15, ...), custom_call_target="tpu_custom_call" | custom-call | flops 1342177280 | bytes 29360128 | tf_op jit(solution)/shard_map/near_forward/pallas_call | solution.py:419
  31.7 6.5 %all-to-all-done.1 = bf16[32,80,128]{2,1,0:T(8,128)(2,1)S(1)} async-done(((bf16[32,80,128]{2,1,0:T(8,128)(2,1)}), bf16[32,80,128]{2,1,0:T(8,128)(2,1)S(1)}, u32[]{:S(2)}, u32[]{:S(2)}) %all-to-all-start.1) | async-done | bytes 655392 | tf_op jit(solution)/shard_map/all_to_all | solution.py:378
  38.2 3.0 %far_terms.1 = bf16[160,16,128]{2,1,0:T(8,128)(2,1)} custom-call(s32[1,128]{1,0:T(1,128)S(4)} %get-tuple-element.28.slot.slot_ref, f32[128,16,128]{2,1,0:T(8,128)S(1)} %get-tuple-element.29.own_ref, bf16[160,16,128]{2,1,0:T(8,128)(2,1)S(1)} %bitcast.9, bf16[48,128,128]{2,1,0:T(8,128)(2,1)S(1)} %get-tuple-element.31.first_ref, ...), custom_call_target="tpu_custom_call" | custom-call | flops 67108864 | bytes 6291456 | tf_op jit(solution)/shard_map/far_terms/pallas_call | solution.py:444
  41.2 3.4 %all-to-all-start.2 = ((bf16[32,80,128]{2,1,0:T(8,128)(2,1)}), bf16[32,80,128]{2,1,0:T(8,128)(2,1)S(1)}, u32[]{:S(2)}, u32[]{:S(2)}) async-start(bf16[32,80,128]{2,1,0:T(8,128)(2,1)} %bitcast.6), calls=%async_computation.2 | async-start | bytes 1310720 | tf_op jit(solution)/shard_map/all_to_all | solution.py:378
  44.7 10.4 %near_back.1 = (f32[144,16,128]{2,1,0:T(8,128)S(1)}, bf16[16,16,128]{2,1,0:T(8,128)(2,1)S(1)}) custom-call(s32[4,128]{1,0:T(4,128)S(4)} %get-tuple-element.26.ids_ref, s32[1,128]{1,0:T(1,128)S(4)} %get-tuple-element.28.slot.slot_ref, bf16[160,16,128]{2,1,0:T(8,128)(2,1)S(1)} %bitcast.10, f32[128,16,128]{2,1,0:T(8,128)} %get-tuple-element.34.part_ref, ...), custom_call_target="tpu_custom_call" | custom-call | flops 335544320 | bytes 24117248 | tf_op jit(solution)/shard_map/near_back/pallas_call | solution.py:459
  55.1 5.3 %collective-permute-start.1 = (bf16[16,16,128]{2,1,0:T(8,128)(2,1)S(1)}, bf16[16,16,128]{2,1,0:T(8,128)(2,1)S(1)}, u32[]{:S(2)}, u32[]{:S(2)}) collective-permute-start(bf16[16,16,128]{2,1,0:T(8,128)(2,1)S(1)} %get-tuple-element.36), channel_id=1, source_target_pairs={{1,0},{2,1},{3,2},{4,3},{5,4},{6,5},{7,6},{8,7},{9,8},{10,9},{11,1... | collective-permute-start | bytes 196616 | tf_op jit(solution)/shard_map/ppermute | solution.py:32
  60.4 1.9 %collective-permute-done.1.halo_ref = bf16[16,16,128]{2,1,0:T(8,128)(2,1)S(1)} collective-permute-done((bf16[16,16,128]{2,1,0:T(8,128)(2,1)S(1)}, bf16[16,16,128]{2,1,0:T(8,128)(2,1)S(1)}, u32[]{:S(2)}, u32[]{:S(2)}) %collective-permute-start.1) | collective-permute-done | bytes 65568 | tf_op jit(solution)/shard_map/ppermute | solution.py:32
  62.3 0.3 all-to-all-done.2
  62.6 1.4 %final_sum.1 = (f32[128,16,128]{2,1,0:T(8,128)}, f32[144,16,128]{2,1,0:T(8,128)S(1)}) custom-call(s32[8,128]{1,0:T(8,128)S(4)} %get-tuple-element.25.picks_ref, f32[144,16,128]{2,1,0:T(8,128)S(1)} %get-tuple-element.35.base_ref, bf16[16,16,128]{2,1,0:T(8,128)(2,1)S(1)} %collective-permute-done.1.halo_ref, ...), custom_call_target="tpu_custom_call", output_to_operand_aliasing={{1}: (1, {})} | custom-call | bytes 3145728 | tf_op jit(solution)/shard_map/final_sum/pallas_call | solution.py:480
Async XLA Ops:
  0.9 14.6 %collective-permute-start = (bf16[16,16,128]{2,1,0:T(8,128)(2,1)S(1)}, bf16[16,16,128]{2,1,0:T(8,128)(2,1)S(1)}, u32[]{:S(2)}, u32[]{:S(2)}) collective-permute-start(bf16[16,16,128]{2,1,0:T(8,128)(2,1)S(1)} %get-tuple-element.23), channel_id=1, source_target_pairs={{31,0},{0,1},{1,2},{2,3},{3,4},{4,5},{5,6},{6,7},{7,8},{8,9},{9,10... | collective-permute-start | bytes 196616 | tf_op jit(solution)/shard_map/ppermute | solution.py:32
  17.6 20.6 %all-to-all-start.1 = ((bf16[32,80,128]{2,1,0:T(8,128)(2,1)}), bf16[32,80,128]{2,1,0:T(8,128)(2,1)S(1)}, u32[]{:S(2)}, u32[]{:S(2)}) async-start(bf16[32,80,128]{2,1,0:T(8,128)(2,1)} %bitcast.4), calls=%async_computation.1 | async-start | bytes 1310720 | tf_op jit(solution)/shard_map/all_to_all | solution.py:378
  20.3 0.7 %copy-start = (s32[128,4]{0,1:T(4,128)S(1)}, s32[128,4]{0,1:T(4,128)}, u32[]{:S(2)}) copy-start(s32[128,4]{0,1:T(4,128)} %param.7) | copy-start | bytes 6148
  41.2 21.3 %all-to-all-start.2 = ((bf16[32,80,128]{2,1,0:T(8,128)(2,1)}), bf16[32,80,128]{2,1,0:T(8,128)(2,1)S(1)}, u32[]{:S(2)}, u32[]{:S(2)}) async-start(bf16[32,80,128]{2,1,0:T(8,128)(2,1)} %bitcast.6), calls=%async_computation.2 | async-start | bytes 1310720 | tf_op jit(solution)/shard_map/all_to_all | solution.py:378
  55.1 7.2 %collective-permute-start.1 = (bf16[16,16,128]{2,1,0:T(8,128)(2,1)S(1)}, bf16[16,16,128]{2,1,0:T(8,128)(2,1)S(1)}, u32[]{:S(2)}, u32[]{:S(2)}) collective-permute-start(bf16[16,16,128]{2,1,0:T(8,128)(2,1)S(1)} %get-tuple-element.36), channel_id=1, source_target_pairs={{1,0},{2,1},{3,2},{4,3},{5,4},{6,5},{7,6},{8,7},{9,8},{10,9},{11,1... | collective-permute-start | bytes 196616 | tf_op jit(solution)/shard_map/ppermute | solution.py:32
